TPU v7x, 32 devices: a whole 2x2x4 slice. The times are simulated.
32 devices in a mesh: aux: 8 (over z, core), vir: 2 (over x), outer: 2 (over y).
Axes of the slice: x: 2, y: 2, z: 4, core: 2. Of those that a mesh axis runs over, the one named last changes fastest.
Arguments:
- factors: bfloat16 [128, 256, 2048], P(('aux', 'outer'), None, 'vir'), may hold values from -0.125 to 0.125
- trials: float32 [4, 256, 2048], P('vir', None, 'aux'), may hold values from -6 to 6
Outputs:
- sigma: float32 [4, 256, 2048], P('vir', 'outer', 'aux')
All inputs are finite; a program needn't handle non-finite values.
Results may differ from a plain program's by a relative error of at most 0.004.
Values may be sent and summed in bfloat16 or wider, within the bound.
No kernel may reach another device: no remote copies, remote signals or barrier semaphores. Data moves between devices by JAX's collectives and lax.ppermute only.
A program may use at most 64 MiB of HBM per device.

v0:
```python
import jax
import jax.numpy as jnp
from jax import lax
from jax.sharding import PartitionSpec as P


def per_device(factors, trials):
    trial_b = trials.astype(jnp.bfloat16)
    gathered = lax.all_gather(trial_b, "aux", axis=2, tiled=True)
    columns = lax.all_gather(factors, "vir", axis=2, tiled=True)
    pairs = jnp.einsum(
        "qib,mjb->mqij", columns, gathered, preferred_element_type=jnp.float32
    ).astype(jnp.bfloat16)
    stacked = jnp.einsum("mqij,qja->mia", pairs, columns, preferred_element_type=jnp.float32)
    slices = lax.psum_scatter(stacked, "aux", scatter_dimension=2, tiled=True)
    return lax.psum_scatter(slices, "outer", scatter_dimension=1, tiled=True)


def solution(mesh):
    placed = (P(("aux", "outer"), None, "vir"), P("vir", None, "aux"))
    return jax.shard_map(
        per_device, mesh=mesh, in_specs=placed, out_specs=P("vir", "outer", "aux"), check_vma=False
    )
```

profile of v0, /device:TPU:0, one launch (start us, length us, event | category | flops | bytes accessed | tf_op | source)
XLA Modules:
  0.0 235.9 jit_solution(4994720477463511270)
XLA Ops:
  6.5 0.0 all-gather.3.cloned.1.call-start
  6.5 1.8 convert_element_type.9
  8.3 0.0 all-gather.3.cloned.1.call-update
  8.3 0.0 all-gather.5.cloned.1.call-start
  8.4 0.7 all-gather.5.cloned.1.call-update
  9.1 0.0 reduce-scatter.3.cloned.1.call-start
  9.1 33.4 %all-gather.3.cloned.1.call-done = bf16[2,256,2048]{2,1,0:T(8,128)(2,1)} async-done(((bf16[2,256,256]{2,1,0:T(8,128)(2,1)}), bf16[2,256,2048]{2,1,0:T(8,128)(2,1)}) %all-gather.3.cloned.1.call-update) | async-done | bytes 2097168 | tf_op jit(solution)/shard_map/all_gather | solution.py:9
  42.5 104.6 %all-gather.5.cloned.1.call-done = bf16[8,256,2048]{2,1,0:T(8,128)(2,1)} async-done(((bf16[8,256,1024]{2,1,0:T(8,128)(2,1)}), bf16[8,256,2048]{2,1,0:T(8,128)(2,1)}) %all-gather.5.cloned.1.call-update) | async-done | bytes 8388624 | tf_op jit(solution)/shard_map/all_gather | solution.py:10
  147.2 17.2 %fusion.4 = f32[2,256,2048]{2,1,0:T(8,128)} fusion(bf16[8,256,2048]{2,1,0:T(8,128)(2,1)} %all-gather.5.cloned.1.call-done, bf16[2,256,2048]{2,1,0:T(8,128)(2,1)} %all-gather.3.cloned.1.call-done), kind=kOutput, calls=%fused_computation.4 | convolution fusion | flops 8590983168 | bytes 14680064 | tf_op jit(solution)/shard_map/mqij,qja->mia/dot_general | solution.py:14
  164.4 0.0 reduce-scatter.3.cloned.1.call-update
  164.4 0.0 reduce-scatter.5.cloned.1.call-start
  164.5 50.1 %reduce-scatter.3.cloned.1.call-done = f32[2,256,256]{2,1,0:T(8,128)} async-done(((f32[2,256,2048]{2,1,0:T(8,128)}), f32[2,256,256]{2,1,0:T(8,128)}) %reduce-scatter.3.cloned.1.call-update) | async-done | bytes 524304 | tf_op jit(solution)/shard_map/reduce_scatter | solution.py:15
  214.6 0.0 reduce-scatter.5.cloned.1.call-update
  214.6 14.8 %reduce-scatter.5.cloned.1.call-done = f32[2,128,256]{2,1,0:T(8,128)} async-done(((f32[2,256,256]{2,1,0:T(8,128)}), f32[2,128,256]{2,1,0:T(8,128)}) %reduce-scatter.5.cloned.1.call-update) | async-done | bytes 262160 | tf_op jit(solution)/shard_map/reduce_scatter | solution.py:16
Async XLA Ops:
  6.5 36.0 %all-gather.3.cloned.1.call-start = ((), (), s32[]{:S(2)}) async-start(), calls=%async_computation.2 | async-start | bytes 2359296 | tf_op jit(solution)/shard_map/all_gather | solution.py:9
  8.3 138.8 %all-gather.5.cloned.1.call-start = ((), (), s32[]{:S(2)}) async-start(), calls=%async_computation.3 | async-start | bytes 12582912 | tf_op jit(solution)/shard_map/all_gather | solution.py:10
  9.1 205.5 %reduce-scatter.3.cloned.1.call-start = ((), (), s32[]{:S(2)}) async-start(), calls=%async_computation.4 | async-start | bytes 4718592 | tf_op jit(solution)/shard_map/reduce_scatter | solution.py:15
  164.4 65.0 %reduce-scatter.5.cloned.1.call-start = ((), (), s32[]{:S(2)}) async-start(), calls=%async_computation.5 | async-start | bytes 786432 | tf_op jit(solution)/shard_map/reduce_scatter | solution.py:16
Sparse Core Ops, SparseCore 0:
  8.9 33.5 all-gather.2
  44.1 103.0 all-gather.4
  164.5 50.0 reduce-scatter.2
  216.7 12.6 reduce-scatter.4
where the time goes:
time: 236 us
  waiting for transfers between devices  204 us (86%)
  matrix products  17.2 us (7%)
  between operations  13.1 us (6%)
    all_gather x1, waiting for transfers between devices, per_device(): columns = lax.all_gather(factors, 'vir', axis=2, tiled=True)  105 us
    reduce_scatter x1, waiting for transfers between devices, per_device(): slices = lax.psum_scatter(stacked, 'aux', scatter_dimension=2, tiled=True)  50.1 us
    all_gather x1, waiting for transfers between devices, per_device(): gathered = lax.all_gather(trial_b, 'aux', axis=2, tiled=True)  33.4 us
    dot_general x1, matrix products, per_device(): jnp.einsum('mqij,qja->mia', pairs, columns, preferred_element_type=jnp.fl...  17.2 us
    reduce_scatter x1, waiting for transfers between devices, per_device(): return lax.psum_scatter(slices, 'outer', scatter_dimension=1, tiled=True)  14.8 us
  transfers between devices with their start and end apart: 4, of which 4 were waited for; matrix products, arithmetic and copies ran while one was open for 0% of the time, Pallas kernels for 0%

commit v1 on v0

v1 whole, which is shorter than its diff:
```python
import jax
import jax.numpy as jnp
from jax import lax
from jax.sharding import PartitionSpec as P

CORES = 2
PIECES = 2


def plain(factors, trials):
    trial_b = trials.astype(jnp.bfloat16)
    gathered = lax.all_gather(trial_b, "aux", axis=2, tiled=True)
    columns = lax.all_gather(factors, "vir", axis=2, tiled=True)
    pairs = jnp.einsum(
        "qib,mjb->mqij", columns, gathered, preferred_element_type=jnp.float32
    ).astype(jnp.bfloat16)
    stacked = jnp.einsum("mqij,qja->mia", pairs, columns, preferred_element_type=jnp.float32)
    slices = lax.psum_scatter(stacked, "aux", scatter_dimension=2, tiled=True)
    return lax.psum_scatter(slices, "outer", scatter_dimension=1, tiled=True)


def shift(array, axis, size, step, stride=1):
    count = size // stride
    pairs = [
        (i, (i // stride + step) % count * stride + i % stride) for i in range(size)
    ]
    return lax.ppermute(array, axis, pairs)


def sibling(array, size):
    return lax.ppermute(array, "aux", [(i, i ^ 1) for i in range(size)])


def part(array, index, size, axis):
    return lax.dynamic_slice_in_dim(array, index * size, size, axis)


def per_device(na, nv, no, factors, trials):
    f32, bf16 = jnp.float32, jnp.bfloat16
    nq, rows, width = factors.shape
    nm, _, cols = trials.shape
    nz = na // CORES
    a, v, o = (lax.axis_index(name) for name in ("aux", "vir", "outer"))
    z, c = a // CORES, a % CORES
    half_m, take = nm // CORES, nq // nv
    block, total = CORES * cols, nv * width

    trial_b = trials.astype(bf16)
    given = sibling(part(trial_b, 1 - c, half_m, 0), na)
    kept = part(trial_b, c, half_m, 0)
    mine = jnp.where(
        c == 0,
        jnp.concatenate([kept, given], axis=2),
        jnp.concatenate([given, kept], axis=2),
    )
    streams = [mine] + [shift(mine, "vir", nv, -r) for r in range(1, nv)]

    sends = [part(factors, (v - r) % nv, take, 0) for r in range(nv)]
    chunks = []
    for k in range(take):
        group = [sends[0][k : k + 1]]
        for r in range(1, nv):
            group.append(shift(sends[r][k : k + 1], "vir", nv, -r))
        group = [jnp.concatenate([g, sibling(g, na)], axis=0) for g in group]
        chunks.append(jnp.concatenate(group, axis=2))

    vectors = []
    for s in streams:
        whole = jnp.zeros((half_m, rows, total), bf16)
        for t in range(nz):
            at = ((z - t) % nz * block - v * width) % total
            whole = lax.dynamic_update_slice_in_dim(whole, s, at, 2)
            if t < nz - 1:
                s = shift(s, "aux", na, 1, CORES)
        vectors.append(whole)

    def pair(chunk, vec):
        return jnp.einsum("qib,mjb->mqij", chunk, vec, preferred_element_type=f32).astype(bf16)

    def expand(p, chunk):
        return jnp.einsum("mqij,qja->mia", p, chunk, preferred_element_type=f32)

    sums = []
    for vec in vectors:
        one = expand(pair(chunks[-1], vec), chunks[-1])
        if len(chunks) > 1:
            early = jnp.concatenate(chunks[:-1], axis=0)
            one += expand(pair(early, vec), early)
        sums.append(one)
    s = jnp.stack(sums).reshape(nv, half_m, no, PIECES, 2, rows // (no * PIECES * 2), total)

    def over_vir(x):
        got = x[0]
        for r in range(1, nv):
            got += jnp.roll(shift(x[r].astype(bf16), "vir", nv, r).astype(f32), -r * width, axis=-1)
        return got

    def over_outer(x, axis):
        got = lax.dynamic_index_in_dim(x, o, axis, False)
        for r in range(1, no):
            sent = lax.dynamic_index_in_dim(x, (o + r) % no, axis, False).astype(bf16)
            got += shift(sent, "outer", no, r).astype(f32)
        return got

    out = []
    for p in range(PIECES):
        one = over_outer(over_vir(s[:, :, :, p, 0]), 1)
        two = over_vir(over_outer(s[:, :, :, p, 1], 2))
        u = jnp.concatenate([one, two], axis=1)

        def to(zz):
            return lax.dynamic_slice_in_dim(u, (zz * block - v * width) % total, block, 2)

        got = to(z)
        for t in range(1, nz):
            got += shift(to((z + t) % nz).astype(bf16), "aux", na, t, CORES).astype(f32)
        out.append(got)
    done = jnp.concatenate(out, axis=1)
    there = sibling(part(done, 1 - c, cols, 2), na)
    here = part(done, c, cols, 2)
    return jnp.where(
        c == 0, jnp.concatenate([here, there], axis=0), jnp.concatenate([there, here], axis=0)
    )


def solution(mesh):
    na, nv, no = (mesh.shape[name] for name in ("aux", "vir", "outer"))

    def step(factors, trials):
        nq, rows, width = factors.shape
        nm, _, cols = trials.shape
        fits = na % CORES == 0 and nm % CORES == 0 and nq % nv == 0
        fits = fits and width % (CORES * cols) == 0 and rows % (no * PIECES * 2 * 16) == 0
        if fits:
            return per_device(na, nv, no, factors, trials)
        return plain(factors, trials)

    placed = (P(("aux", "outer"), None, "vir"), P("vir", None, "aux"))
    return jax.shard_map(
        step, mesh=mesh, in_specs=placed, out_specs=P("vir", "outer", "aux"), check_vma=False
    )
```

time: 236 us -> 155 us (0.66)
  waiting for transfers between devices: 204 us -> 52.8 us
  local copies, waits for them, and re-layouts: 0 us -> 33.4 us
  starting transfers between devices: 0.12 us -> 30.4 us
  between operations: 13.1 us -> 0.69 us
  matrix products: 17.2 us -> 28.2 us
  other arithmetic: 1.77 us -> 8.58 us
    all_gather x2 -> x0, waiting for transfers between devices: 138 us -> none  [the longest x1 105 us: per_device(): columns = lax.all_gather(factors, 'vir', axis=2, tiled=True)]
    reduce_scatter x2 -> x0, waiting for transfers between devices: 64.9 us -> none  [the longest x1 50.1 us: per_device(): slices = lax.psum_scatter(stacked, 'aux', scatter_dimension=2, tiled=True)]
    ppermute x0 -> x35, waiting for transfers between devices: none -> 52.8 us  [the longest x25 50 us: shift(): return lax.ppermute(array, axis, pairs)]
    ppermute x0 -> x35, starting transfers between devices: none -> 30.4 us  [the longest x25 29.1 us: shift(): return lax.ppermute(array, axis, pairs)]
    dynamic_update_slice x0 -> x8, local copies, waits for them, and re-layouts: none -> 25.6 us  [per_device(): whole = lax.dynamic_update_slice_in_dim(whole, s, at, 2)]
    dot_general x1 -> x4, matrix products: 17.2 us -> 28.2 us  [expand(): return jnp.einsum('mqij,qja->mia', p, chunk, preferred_element_type=f32)]
    concatenate x0 -> x2, other arithmetic: none -> 5.5 us  [the longest x1 5.47 us: per_device(): early = jnp.concatenate(chunks[:-1], axis=0)]
    slice x0 -> x5, local copies, waits for them, and re-layouts: none -> 4.03 us  [the longest x1 3.91 us: per_device(): group = [sends[0][k:k + 1]]]
  transfers between devices with their start and end apart: 4 -> 35, of which waited for: 4 -> 17; matrix products, arithmetic and copies ran while one was open for 0% -> 38% of each run, Pallas kernels for 0% -> 0%
where the time goes in v1:
time: 155 us; the launch traced here: 154 us
  waiting for transfers between devices  52.8 us (34%)
  local copies, waits for them, and re-layouts  33.4 us (22%)
  starting transfers between devices  30.4 us (20%)
  matrix products  28.2 us (18%)
  other arithmetic  8.58 us (6%)
    ppermute x25, waiting for transfers between devices, shift(): return lax.ppermute(array, axis, pairs)  50 us
    ppermute x25, starting transfers between devices, shift(): return lax.ppermute(array, axis, pairs)  29.1 us
    dot_general x4, matrix products, expand(): return jnp.einsum('mqij,qja->mia', p, chunk, preferred_element_type=f32)  28.2 us
    dynamic_update_slice x8, local copies, waits for them, and re-layouts, per_device(): whole = lax.dynamic_update_slice_in_dim(whole, s, at, 2)  25.6 us
    concatenate x1, other arithmetic, per_device(): early = jnp.concatenate(chunks[:-1], axis=0)  5.47 us
    slice x1, local copies, waits for them, and re-layouts, per_device(): group = [sends[0][k:k + 1]]  3.91 us
  transfers between devices with their start and end apart: 35, of which 17 were waited for; matrix products, arithmetic and copies ran while one was open for 38% of the time, Pallas kernels for 0%

profile of v1, /device:TPU:0, one launch (start us, length us, event | category | flops | bytes accessed | tf_op | source)
XLA Modules:
  0.0 154.1 jit_solution(6813861586622238623)
XLA Ops:
  0.0 3.9 %constant_dynamic-slice_fusion.5 = (bf16[1,256,1024]{2,1,0:T(8,128)(2,1)}, bf16[1,256,1024]{2,1,0:T(8,128)(2,1)}, bf16[1,256,1024]{2,1,0:T(8,128)(2,1)S(1)}, bf1...) fusion(bf16[8,256,1024]{2,1,0:T(8,128)(2,1)} %param.2, ...), kind=kLoop, calls=%fused_computation.101 | loop fusion | bytes 8388640 | tf_op jit(solution)/shard_map/slice | solution.py:61
  3.9 2.9 %collective-permute-start.14 = (bf16[1,256,1024]{2,1,0:T(8,128)(2,1)}, bf16[1,256,1024]{2,1,0:T(8,128)(2,1)}, u32[]{:S(2)}, u32[]{:S(2)}) collective-permute-start(bf16[1,256,1024]{2,1,0:T(8,128)(2,1)} %get-tuple-element.13), channel_id=1, source_target_pairs={{0,2},{2,0},{1,3},{3,1},{4,6},{6,4},{5,7},{7,5},{8,10},{10,8},{9,1... | collective-permute-start | bytes 1572872 | tf_op jit(solution)/shard_map/ppermute | solution.py:27
  7.5 1.4 collective-permute-done
  9.1 1.6 %collective-permute-start.1 = (bf16[1,256,512]{2,1,0:T(8,128)(2,1)S(1)}, bf16[1,256,512]{2,1,0:T(8,128)(2,1)S(1)}, u32[]{:S(2)}, u32[]{:S(2)}) collective-permute-start(bf16[1,256,512]{2,1,0:T(8,128)(2,1)S(1)} %maximum_select_fusion.1), channel_id=1, source_target_pairs={{0,8},{4,12},{8,16},{12,20},{16,24},{20,28},{24,0},{28,4},{1,9},{5... | collective-permute-start | bytes 786440 | tf_op jit(solution)/shard_map/ppermute | solution.py:27
  11.2 1.5 collective-permute-start.11
  12.7 6.6 %collective-permute-done.1 = bf16[1,256,512]{2,1,0:T(8,128)(2,1)S(1)} collective-permute-done((bf16[1,256,512]{2,1,0:T(8,128)(2,1)S(1)}, bf16[1,256,512]{2,1,0:T(8,128)(2,1)S(1)}, u32[]{:S(2)}, u32[]{:S(2)}) %collective-permute-start.1) | collective-permute-done | bytes 262176 | tf_op jit(solution)/shard_map/ppermute | solution.py:27
  19.3 6.1 %collective-permute-done.16 = bf16[1,256,512]{2,1,0:T(8,128)(2,1)S(1)} collective-permute-done((bf16[1,256,512]{2,1,0:T(8,128)(2,1)S(1)}, bf16[1,256,512]{2,1,0:T(8,128)(2,1)S(1)}, u32[]{:S(2)}, u32[]{:S(2)}) %collective-permute-start.16) | collective-permute-done | bytes 262176 | tf_op jit(solution)/shard_map/ppermute | solution.py:27
  25.4 2.1 %collective-permute-start.8 = (bf16[1,256,1024]{2,1,0:T(8,128)(2,1)S(1)}, bf16[1,256,1024]{2,1,0:T(8,128)(2,1)}, u32[]{:S(2)}, u32[]{:S(2)}) collective-permute-start(bf16[1,256,1024]{2,1,0:T(8,128)(2,1)S(1)} %get-tuple-element.10), channel_id=1, source_target_pairs={{0,2},{2,0},{1,3},{3,1},{4,6},{6,4},{5,7},{7,5},{8,10},{10,8},{9,1... | collective-permute-start | bytes 1572872 | tf_op jit(solution)/shard_map/ppermute | solution.py:27
  27.5 1.6 %collective-permute-start.2 = (bf16[1,256,512]{2,1,0:T(8,128)(2,1)S(1)}, bf16[1,256,512]{2,1,0:T(8,128)(2,1)S(1)}, u32[]{:S(2)}, u32[]{:S(2)}) collective-permute-start(bf16[1,256,512]{2,1,0:T(8,128)(2,1)S(1)} %collective-permute-done.1), channel_id=1, source_target_pairs={{0,8},{4,12},{8,16},{12,20},{16,24},{20,28},{24,0},{28,4},{1,9},{5... | collective-permute-start | bytes 786440 | tf_op jit(solution)/shard_map/ppermute | solution.py:27
  29.1 1.6 %collective-permute-start.17 = (bf16[1,256,512]{2,1,0:T(8,128)(2,1)S(1)}, bf16[1,256,512]{2,1,0:T(8,128)(2,1)S(1)}, u32[]{:S(2)}, u32[]{:S(2)}) collective-permute-start(bf16[1,256,512]{2,1,0:T(8,128)(2,1)S(1)} %collective-permute-done.16), channel_id=1, source_target_pairs={{0,8},{4,12},{8,16},{12,20},{16,24},{20,28},{24,0},{28,4},{1,9},{5... | collective-permute-start | bytes 786440 | tf_op jit(solution)/shard_map/ppermute | solution.py:27
  30.7 7.9 %collective-permute-done.2 = bf16[1,256,512]{2,1,0:T(8,128)(2,1)S(1)} collective-permute-done((bf16[1,256,512]{2,1,0:T(8,128)(2,1)S(1)}, bf16[1,256,512]{2,1,0:T(8,128)(2,1)S(1)}, u32[]{:S(2)}, u32[]{:S(2)}) %collective-permute-start.2) | collective-permute-done | bytes 262176 | tf_op jit(solution)/shard_map/ppermute | solution.py:27
  38.5 5.6 %collective-permute-done.17 = bf16[1,256,512]{2,1,0:T(8,128)(2,1)S(1)} collective-permute-done((bf16[1,256,512]{2,1,0:T(8,128)(2,1)S(1)}, bf16[1,256,512]{2,1,0:T(8,128)(2,1)S(1)}, u32[]{:S(2)}, u32[]{:S(2)}) %collective-permute-start.17) | collective-permute-done | bytes 262176 | tf_op jit(solution)/shard_map/ppermute | solution.py:27
  44.3 0.8 copy-done.4
  45.4 1.8 %collective-permute-done.8 = bf16[1,256,1024]{2,1,0:T(8,128)(2,1)} collective-permute-done((bf16[1,256,1024]{2,1,0:T(8,128)(2,1)S(1)}, bf16[1,256,1024]{2,1,0:T(8,128)(2,1)}, u32[]{:S(2)}, u32[]{:S(2)}) %collective-permute-start.8) | collective-permute-done | bytes 524320 | tf_op jit(solution)/shard_map/ppermute | solution.py:27
  47.2 2.0 %collective-permute-done.3 = bf16[1,256,512]{2,1,0:T(8,128)(2,1)S(1)} collective-permute-done((bf16[1,256,512]{2,1,0:T(8,128)(2,1)S(1)}, bf16[1,256,512]{2,1,0:T(8,128)(2,1)S(1)}, u32[]{:S(2)}, u32[]{:S(2)}) %collective-permute-start.3) | collective-permute-done | bytes 262176 | tf_op jit(solution)/shard_map/ppermute | solution.py:27
  49.2 3.2 %collective-permute-done.18 = bf16[1,256,512]{2,1,0:T(8,128)(2,1)S(1)} collective-permute-done((bf16[1,256,512]{2,1,0:T(8,128)(2,1)S(1)}, bf16[1,256,512]{2,1,0:T(8,128)(2,1)S(1)}, u32[]{:S(2)}, u32[]{:S(2)}) %collective-permute-start.18) | collective-permute-done | bytes 262176 | tf_op jit(solution)/shard_map/ppermute | solution.py:27
  53.2 1.1 broadcast.35.clone
  54.3 3.4 %dynamic_update_slice.32 = bf16[256,2048]{1,0:T(8,128)(2,1)} dynamic-update-slice(bf16[256,2048]{1,0:T(8,128)(2,1)} %broadcast.35.clone, bf16[256,512]{1,0:T(8,128)(2,1)S(1)} %maximum_select_fusion, s32[]{:T(128)} %constant.192.clone.1, s32[]{:T(128)S(6)} %select_n.221) | dynamic-update-slice | bytes 524292 | tf_op jit(solution)/shard_map/dynamic_update_slice | solution.py:72
  57.8 3.5 %dynamic_update_slice.36 = bf16[256,2048]{1,0:T(8,128)(2,1)S(1)} dynamic-update-slice(bf16[256,2048]{1,0:T(8,128)(2,1)S(1)} %broadcast.35.clone.1, bf16[256,512]{1,0:T(8,128)(2,1)} %bitcast.143, s32[]{:T(128)} %constant.192.clone.1, s32[]{:T(128)S(6)} %select_n.221) | dynamic-update-slice | bytes 524292 | tf_op jit(solution)/shard_map/dynamic_update_slice | solution.py:72
  61.2 2.9 %dynamic_update_slice.33 = bf16[256,2048]{1,0:T(8,128)(2,1)} dynamic-update-slice(bf16[256,2048]{1,0:T(8,128)(2,1)} %dynamic_update_slice.32, bf16[256,512]{1,0:T(8,128)(2,1)} %bitcast.142, s32[]{:T(128)} %constant.192.clone.1, s32[]{:T(128)S(6)} %select_n.226) | dynamic-update-slice | bytes 524292 | tf_op jit(solution)/shard_map/dynamic_update_slice | solution.py:72
  64.1 3.1 %dynamic_update_slice.37 = bf16[256,2048]{1,0:T(8,128)(2,1)S(1)} dynamic-update-slice(bf16[256,2048]{1,0:T(8,128)(2,1)S(1)} %dynamic_update_slice.36, bf16[256,512]{1,0:T(8,128)(2,1)} %bitcast.146, s32[]{:T(128)} %constant.192.clone.1, s32[]{:T(128)S(6)} %select_n.226) | dynamic-update-slice | bytes 524292 | tf_op jit(solution)/shard_map/dynamic_update_slice | solution.py:72
  67.2 3.5 %dynamic_update_slice.34 = bf16[256,2048]{1,0:T(8,128)(2,1)} dynamic-update-slice(bf16[256,2048]{1,0:T(8,128)(2,1)} %dynamic_update_slice.33, bf16[256,512]{1,0:T(8,128)(2,1)} %bitcast.144, s32[]{:T(128)} %constant.192.clone.1, s32[]{:T(128)S(6)} %select_n.229) | dynamic-update-slice | bytes 524292 | tf_op jit(solution)/shard_map/dynamic_update_slice | solution.py:72
  70.7 2.4 %dynamic_update_slice.38 = bf16[256,2048]{1,0:T(8,128)(2,1)S(1)} dynamic-update-slice(bf16[256,2048]{1,0:T(8,128)(2,1)S(1)} %dynamic_update_slice.37, bf16[256,512]{1,0:T(8,128)(2,1)S(1)} %bitcast.141, s32[]{:T(128)} %constant.192.clone.1, s32[]{:T(128)S(6)} %select_n.229) | dynamic-update-slice | bytes 524292 | tf_op jit(solution)/shard_map/dynamic_update_slice | solution.py:72
  73.1 3.5 %dynamic_update_slice.35 = bf16[256,2048]{1,0:T(8,128)(2,1)} dynamic-update-slice(bf16[256,2048]{1,0:T(8,128)(2,1)} %dynamic_update_slice.34, bf16[256,512]{1,0:T(8,128)(2,1)} %bitcast.145, s32[]{:T(128)} %constant.192.clone.1, s32[]{:T(128)S(6)} %select_n.232) | dynamic-update-slice | bytes 524292 | tf_op jit(solution)/shard_map/dynamic_update_slice | solution.py:72
  77.2 5.5 %maximum_maximum_fusion = bf16[6,256,2048]{2,1,0:T(8,128)(2,1)} fusion(bf16[1,256,1024]{2,1,0:T(8,128)(2,1)} %collective-permute-done.15, bf16[1,256,1024]{2,1,0:T(8,128)(2,1)} %collective-permute-done.14, bf16[1,256,1024]{2,1,0:T(8,128)(2,1)S(1)} %copy-done.3, bf16[1,256,1024]{2,1,0:T(8,128)(2,1)S(1)} %get-tuple-element.14, ...), kind=kLoop, calls=%fused_computation | loop fusion | flops 75497472 | bytes 12582912 | tf_op jit(solution)/shard_map/concatenate | solution.py:87
  82.6 9.7 %convolution_bitcast_fusion.1 = f32[256,2048]{1,0:T(8,128)} fusion(bf16[6,256,2048]{2,1,0:T(8,128)(2,1)} %maximum_maximum_fusion, bf16[256,2048]{1,0:T(8,128)(2,1)} %dynamic_update_slice.35), kind=kOutput, calls=%fused_computation.2 | convolution fusion | flops 3221618688 | bytes 9437184 | tf_op jit(solution)/shard_map/mqij,qja->mia/dot_general | solution.py:81
  92.3 3.4 %dynamic_update_slice.39 = bf16[256,2048]{1,0:T(8,128)(2,1)S(1)} dynamic-update-slice(bf16[256,2048]{1,0:T(8,128)(2,1)S(1)} %dynamic_update_slice.38, bf16[256,512]{1,0:T(8,128)(2,1)} %bitcast.19, s32[]{:T(128)} %constant.192.clone.1, s32[]{:T(128)S(6)} %select_n.232) | dynamic-update-slice | bytes 524292 | tf_op jit(solution)/shard_map/dynamic_update_slice | solution.py:72
  95.8 9.4 %convolution_bitcast_fusion = f32[256,2048]{1,0:T(8,128)} fusion(bf16[6,256,2048]{2,1,0:T(8,128)(2,1)} %maximum_maximum_fusion, bf16[256,2048]{1,0:T(8,128)(2,1)S(1)} %dynamic_update_slice.39), kind=kOutput, calls=%fused_computation.1 | convolution fusion | flops 3221618688 | bytes 9437184 | tf_op jit(solution)/shard_map/mqij,qja->mia/dot_general | solution.py:81
  105.1 4.4 %fusion.1 = f32[256,2048]{1,0:T(8,128)S(1)} fusion(f32[256,2048]{1,0:T(8,128)} %convolution_bitcast_fusion, bf16[256,2048]{1,0:T(8,128)(2,1)S(1)} %dynamic_update_slice.39, bf16[1,256,1024]{2,1,0:T(8,128)(2,1)} %collective-permute-done.6, bf16[1,256,1024]{2,1,0:T(8,128)(2,1)} %collective-permute-done.5, bf16[1,256,1024]{2,1,0:T(8,128)(2,1)} %collective-permute-done.4, ...), kind=kOutput, calls=%fused_computation.6 | convolution fusion | flops 1091174400 | bytes 7340032 | tf_op jit(solution)/shard_map/mqij,qja->mia/dot_general | solution.py:81
  109.6 1.3 copy-done
  111.2 4.7 %fusion = f32[256,2048]{1,0:T(8,128)S(1)} fusion(f32[256,2048]{1,0:T(8,128)} %convolution_bitcast_fusion.1, bf16[256,2048]{1,0:T(8,128)(2,1)} %dynamic_update_slice.35, bf16[1,256,1024]{2,1,0:T(8,128)(2,1)} %collective-permute-done.6, bf16[1,256,1024]{2,1,0:T(8,128)(2,1)} %collective-permute-done.5, bf16[1,256,1024]{2,1,0:T(8,128)(2,1)} %collective-permute-done.4, ...), kind=kOutput, calls=%fused_computation.5 | convolution fusion | flops 1091174400 | bytes 7340032 | tf_op jit(solution)/shard_map/mqij,qja->mia/dot_general | solution.py:81
  115.9 1.8 %collective-permute-start.20 = (bf16[1,2,32,2048]{3,2,1,0:T(8,128)(2,1)S(1)}, bf16[1,2,32,2048]{3,2,1,0:T(8,128)(2,1)S(1)}, u32[]{:S(2)}, u32[]{:S(2)}) collective-permute-start(bf16[1,2,32,2048]{3,2,1,0:T(8,128)(2,1)S(1)} %get-tuple-element.18), channel_id=1, source_target_pairs={{0,2},{2,0},{1,3},{3,1},{4,6},{6,4},{5,7},{7,5},{8,10},{10,8},{9,1... | collective-permute-start | bytes 786440 | tf_op jit(solution)/shard_map/ppermute | solution.py:27
  117.7 1.2 fusion.25
  118.9 1.6 %collective-permute-start.22 = (bf16[2,1,32,2048]{3,2,0,1:T(8,128)(2,1)S(1)}, bf16[2,1,32,2048]{3,2,0,1:T(8,128)(2,1)S(1)}, u32[]{:S(2)}, u32[]{:S(2)}) collective-permute-start(bf16[2,1,32,2048]{3,2,0,1:T(8,128)(2,1)S(1)} %get-tuple-element.6), channel_id=1, source_target_pairs={{0,1},{1,0},{2,3},{3,2},{4,5},{5,4},{6,7},{7,6},{8,9},{9,8},{10,11... | collective-permute-start | bytes 786440 | tf_op jit(solution)/shard_map/ppermute | solution.py:27
  121.0 3.9 %collective-permute-done.20 = bf16[1,2,32,2048]{3,2,1,0:T(8,128)(2,1)S(1)} collective-permute-done((bf16[1,2,32,2048]{3,2,1,0:T(8,128)(2,1)S(1)}, bf16[1,2,32,2048]{3,2,1,0:T(8,128)(2,1)S(1)}, u32[]{:S(2)}, u32[]{:S(2)}) %collective-permute-start.20) | collective-permute-done | bytes 262176 | tf_op jit(solution)/shard_map/ppermute | solution.py:27
  125.2 1.6 %collective-permute-start.21 = (bf16[1,32,2048]{2,1,0:T(8,128)(2,1)S(1)}, bf16[1,32,2048]{2,1,0:T(8,128)(2,1)S(1)}, u32[]{:S(2)}, u32[]{:S(2)}) collective-permute-start(bf16[1,32,2048]{2,1,0:T(8,128)(2,1)S(1)} %fusion.28), channel_id=1, source_target_pairs={{0,1},{1,0},{2,3},{3,2},{4,5},{5,4},{6,7},{7,6},{8,9},{9,8},{10,11... | collective-permute-start | bytes 393224 | tf_op jit(solution)/shard_map/ppermute | solution.py:27
  126.8 1.4 collective-permute-done.22
  128.7 1.8 %collective-permute-start.28 = (bf16[1,32,2048]{2,1,0:T(8,128)(2,1)S(1)}, bf16[1,32,2048]{2,1,0:T(8,128)(2,1)S(1)}, u32[]{:S(2)}, u32[]{:S(2)}) collective-permute-start(bf16[1,32,2048]{2,1,0:T(8,128)(2,1)S(1)} %fusion.29), channel_id=1, source_target_pairs={{0,1},{1,0},{2,3},{3,2},{4,5},{5,4},{6,7},{7,6},{8,9},{9,8},{10,11... | collective-permute-start | bytes 393224 | tf_op jit(solution)/shard_map/ppermute | solution.py:27
  130.5 3.3 %collective-permute-done.29 = bf16[2,1,32,2048]{3,2,1,0:T(8,128)(2,1)S(1)} collective-permute-done((bf16[2,1,32,2048]{3,2,1,0:T(8,128)(2,1)S(1)}, bf16[2,1,32,2048]{3,2,1,0:T(8,128)(2,1)S(1)}, u32[]{:S(2)}, u32[]{:S(2)}) %collective-permute-start.29) | collective-permute-done | bytes 262176 | tf_op jit(solution)/shard_map/ppermute | solution.py:27
  134.3 2.3 %collective-permute-done.21 = bf16[1,32,2048]{2,1,0:T(8,128)(2,1)S(1)} collective-permute-done((bf16[1,32,2048]{2,1,0:T(8,128)(2,1)S(1)}, bf16[1,32,2048]{2,1,0:T(8,128)(2,1)S(1)}, u32[]{:S(2)}, u32[]{:S(2)}) %collective-permute-start.21) | collective-permute-done | bytes 131104 | tf_op jit(solution)/shard_map/ppermute | solution.py:27
  136.8 3.7 %collective-permute-start.26 = (bf16[1,64,512]{2,1,0:T(8,128)(2,1)S(1)}, bf16[1,64,512]{2,1,0:T(8,128)(2,1)S(1)}, u32[]{:S(2)}, u32[]{:S(2)}) collective-permute-start(bf16[1,64,512]{2,1,0:T(8,128)(2,1)S(1)} %get-tuple-element.24), channel_id=1, source_target_pairs={{0,24},{4,28},{8,0},{12,4},{16,8},{20,12},{24,16},{28,20},{1,25},{... | collective-permute-start | bytes 196616 | tf_op jit(solution)/shard_map/ppermute | solution.py:27
  141.4 3.2 %collective-permute-start.33 = (bf16[1,64,512]{2,1,0:T(8,128)(2,1)S(1)}, bf16[1,64,512]{2,1,0:T(8,128)(2,1)S(1)}, u32[]{:S(2)}, u32[]{:S(2)}) collective-permute-start(bf16[1,64,512]{2,1,0:T(8,128)(2,1)S(1)} %get-tuple-element.21), channel_id=1, source_target_pairs={{0,24},{4,28},{8,0},{12,4},{16,8},{20,12},{24,16},{28,20},{1,25},{... | collective-permute-start | bytes 196616 | tf_op jit(solution)/shard_map/ppermute | solution.py:27
  144.6 1.1 collective-permute-start.32
  145.7 2.3 %collective-permute-done.25 = bf16[1,64,512]{2,1,0:T(8,128)(2,1)S(1)} collective-permute-done((bf16[1,64,512]{2,1,0:T(8,128)(2,1)S(1)}, bf16[1,64,512]{2,1,0:T(8,128)(2,1)S(1)}, u32[]{:S(2)}, u32[]{:S(2)}) %collective-permute-start.25) | collective-permute-done | bytes 65568 | tf_op jit(solution)/shard_map/ppermute | solution.py:27
  148.7 1.4 collective-permute-done.32
  150.1 1.7 %collective-permute-done.31 = bf16[1,64,512]{2,1,0:T(8,128)(2,1)S(1)} collective-permute-done((bf16[1,64,512]{2,1,0:T(8,128)(2,1)S(1)}, bf16[1,64,512]{2,1,0:T(8,128)(2,1)S(1)}, u32[]{:S(2)}, u32[]{:S(2)}) %collective-permute-start.31) | collective-permute-done | bytes 65568 | tf_op jit(solution)/shard_map/ppermute | solution.py:27
  152.0 1.3 collective-permute-done.34
  153.4 0.7 maximum_select_fusion.2
  (91 shorter events, 6.8 us)
Async XLA Ops:
  0.0 6.9 %copy-start.5 = (f32[2,256,256]{2,1,0:T(8,128)S(1)}, f32[2,256,256]{2,1,0:T(8,128)}, u32[]{:S(2)}) copy-start(f32[2,256,256]{2,1,0:T(8,128)} %param.3) | copy-start | bytes 1572868
  3.9 23.6 %collective-permute-start.14 = (bf16[1,256,1024]{2,1,0:T(8,128)(2,1)}, bf16[1,256,1024]{2,1,0:T(8,128)(2,1)}, u32[]{:S(2)}, u32[]{:S(2)}) collective-permute-start(bf16[1,256,1024]{2,1,0:T(8,128)(2,1)} %get-tuple-element.13), channel_id=1, source_target_pairs={{0,2},{2,0},{1,3},{3,1},{4,6},{6,4},{5,7},{7,5},{8,10},{10,8},{9,1... | collective-permute-start | bytes 1572872 | tf_op jit(solution)/shard_map/ppermute | solution.py:27
  6.9 22.2 %collective-permute-start.13 = (bf16[1,256,1024]{2,1,0:T(8,128)(2,1)S(1)}, bf16[1,256,1024]{2,1,0:T(8,128)(2,1)S(1)}, u32[]{:S(2)}, u32[]{:S(2)}) collective-permute-start(bf16[1,256,1024]{2,1,0:T(8,128)(2,1)S(1)} %get-tuple-element.14), channel_id=1, source_target_pairs={{0,4},{4,0},{8,12},{12,8},{16,20},{20,16},{24,28},{28,24},{1,5},{5... | collective-permute-start | bytes 1572872 | tf_op jit(solution)/shard_map/ppermute | solution.py:31
  6.9 2.0 %collective-permute-start = (bf16[1,256,256]{2,1,0:T(8,128)(2,1)S(1)}, bf16[1,256,256]{2,1,0:T(8,128)(2,1)S(1)}, u32[]{:S(2)}, u32[]{:S(2)}) collective-permute-start(bf16[1,256,256]{2,1,0:T(8,128)(2,1)S(1)} %get-tuple-element.32), channel_id=1, source_target_pairs={{0,4},{4,0},{8,12},{12,8},{16,20},{20,16},{24,28},{28,24},{1,5},{5... | collective-permute-start | bytes 393224 | tf_op jit(solution)/shard_map/ppermute | solution.py:31
  9.1 10.3 %collective-permute-start.1 = (bf16[1,256,512]{2,1,0:T(8,128)(2,1)S(1)}, bf16[1,256,512]{2,1,0:T(8,128)(2,1)S(1)}, u32[]{:S(2)}, u32[]{:S(2)}) collective-permute-start(bf16[1,256,512]{2,1,0:T(8,128)(2,1)S(1)} %maximum_select_fusion.1), channel_id=1, source_target_pairs={{0,8},{4,12},{8,16},{12,20},{16,24},{20,28},{24,0},{28,4},{1,9},{5... | collective-permute-start | bytes 786440 | tf_op jit(solution)/shard_map/ppermute | solution.py:27
  10.7 14.7 %collective-permute-start.16 = (bf16[1,256,512]{2,1,0:T(8,128)(2,1)S(1)}, bf16[1,256,512]{2,1,0:T(8,128)(2,1)S(1)}, u32[]{:S(2)}, u32[]{:S(2)}) collective-permute-start(bf16[1,256,512]{2,1,0:T(8,128)(2,1)S(1)} %maximum_select_fusion.1), channel_id=1, source_target_pairs={{0,2},{2,0},{1,3},{3,1},{4,6},{6,4},{5,7},{7,5},{8,10},{10,8},{9,1... | collective-permute-start | bytes 786440 | tf_op jit(solution)/shard_map/ppermute | solution.py:27
  11.2 32.9 %collective-permute-start.11 = (bf16[1,256,1024]{2,1,0:T(8,128)(2,1)}, bf16[1,256,1024]{2,1,0:T(8,128)(2,1)}, u32[]{:S(2)}, u32[]{:S(2)}) collective-permute-start(bf16[1,256,1024]{2,1,0:T(8,128)(2,1)} %get-tuple-element.8), channel_id=1, source_target_pairs={{0,2},{2,0},{1,3},{3,1},{4,6},{6,4},{5,7},{7,5},{8,10},{10,8},{9,1... | collective-permute-start | bytes 1572872 | tf_op jit(solution)/shard_map/ppermute | solution.py:27
  19.3 38.3 %copy-start.8 = (bf16[1,256,512]{2,1,0:T(8,128)(2,1)}, bf16[1,256,512]{2,1,0:T(8,128)(2,1)S(1)}, u32[]{:S(2)}) copy-start(bf16[1,256,512]{2,1,0:T(8,128)(2,1)S(1)} %collective-permute-done.1) | copy-start | bytes 786436
  19.3 24.9 %collective-permute-start.10 = (bf16[1,256,1024]{2,1,0:T(8,128)(2,1)S(1)}, bf16[1,256,1024]{2,1,0:T(8,128)(2,1)S(1)}, u32[]{:S(2)}, u32[]{:S(2)}) collective-permute-start(bf16[1,256,1024]{2,1,0:T(8,128)(2,1)S(1)} %get-tuple-element.9), channel_id=1, source_target_pairs={{0,4},{4,0},{8,12},{12,8},{16,20},{20,16},{24,28},{28,24},{1,5},{5... | collective-permute-start | bytes 1572872 | tf_op jit(solution)/shard_map/ppermute | solution.py:31
  25.4 26.9 %copy-start.9 = (bf16[1,256,512]{2,1,0:T(8,128)(2,1)}, bf16[1,256,512]{2,1,0:T(8,128)(2,1)S(1)}, u32[]{:S(2)}) copy-start(bf16[1,256,512]{2,1,0:T(8,128)(2,1)S(1)} %collective-permute-done.16) | copy-start | bytes 786436
  25.4 21.7 %collective-permute-start.8 = (bf16[1,256,1024]{2,1,0:T(8,128)(2,1)S(1)}, bf16[1,256,1024]{2,1,0:T(8,128)(2,1)}, u32[]{:S(2)}, u32[]{:S(2)}) collective-permute-start(bf16[1,256,1024]{2,1,0:T(8,128)(2,1)S(1)} %get-tuple-element.10), channel_id=1, source_target_pairs={{0,2},{2,0},{1,3},{3,1},{4,6},{6,4},{5,7},{7,5},{8,10},{10,8},{9,1... | collective-permute-start | bytes 1572872 | tf_op jit(solution)/shard_map/ppermute | solution.py:27
  27.5 11.0 %collective-permute-start.2 = (bf16[1,256,512]{2,1,0:T(8,128)(2,1)S(1)}, bf16[1,256,512]{2,1,0:T(8,128)(2,1)S(1)}, u32[]{:S(2)}, u32[]{:S(2)}) collective-permute-start(bf16[1,256,512]{2,1,0:T(8,128)(2,1)S(1)} %collective-permute-done.1), channel_id=1, source_target_pairs={{0,8},{4,12},{8,16},{12,20},{16,24},{20,28},{24,0},{28,4},{1,9},{5... | collective-permute-start | bytes 786440 | tf_op jit(solution)/shard_map/ppermute | solution.py:27
  29.1 28.6 %copy-start.2 = (bf16[1,256,1024]{2,1,0:T(8,128)(2,1)}, bf16[1,256,1024]{2,1,0:T(8,128)(2,1)S(1)}, u32[]{:S(2)}) copy-start(bf16[1,256,1024]{2,1,0:T(8,128)(2,1)S(1)} %collective-permute-done.13) | copy-start | bytes 1572868
  29.1 15.1 %collective-permute-start.17 = (bf16[1,256,512]{2,1,0:T(8,128)(2,1)S(1)}, bf16[1,256,512]{2,1,0:T(8,128)(2,1)S(1)}, u32[]{:S(2)}, u32[]{:S(2)}) collective-permute-start(bf16[1,256,512]{2,1,0:T(8,128)(2,1)S(1)} %collective-permute-done.16), channel_id=1, source_target_pairs={{0,8},{4,12},{8,16},{12,20},{16,24},{20,28},{24,0},{28,4},{1,9},{5... | collective-permute-start | bytes 786440 | tf_op jit(solution)/shard_map/ppermute | solution.py:27
  38.5 13.8 %copy-start.10 = (bf16[1,256,512]{2,1,0:T(8,128)(2,1)}, bf16[1,256,512]{2,1,0:T(8,128)(2,1)S(1)}, u32[]{:S(2)}) copy-start(bf16[1,256,512]{2,1,0:T(8,128)(2,1)S(1)} %collective-permute-done.2) | copy-start | bytes 786436
  38.5 10.6 %collective-permute-start.3 = (bf16[1,256,512]{2,1,0:T(8,128)(2,1)S(1)}, bf16[1,256,512]{2,1,0:T(8,128)(2,1)S(1)}, u32[]{:S(2)}, u32[]{:S(2)}) collective-permute-start(bf16[1,256,512]{2,1,0:T(8,128)(2,1)S(1)} %collective-permute-done.2), channel_id=1, source_target_pairs={{0,8},{4,12},{8,16},{12,20},{16,24},{20,28},{24,0},{28,4},{1,9},{5... | collective-permute-start | bytes 786440 | tf_op jit(solution)/shard_map/ppermute | solution.py:27
  44.2 8.2 %copy-start.12 = (bf16[1,256,512]{2,1,0:T(8,128)(2,1)}, bf16[1,256,512]{2,1,0:T(8,128)(2,1)S(1)}, u32[]{:S(2)}) copy-start(bf16[1,256,512]{2,1,0:T(8,128)(2,1)S(1)} %collective-permute-done.17) | copy-start | bytes 786436
  44.2 8.2 %collective-permute-start.18 = (bf16[1,256,512]{2,1,0:T(8,128)(2,1)S(1)}, bf16[1,256,512]{2,1,0:T(8,128)(2,1)S(1)}, u32[]{:S(2)}, u32[]{:S(2)}) collective-permute-start(bf16[1,256,512]{2,1,0:T(8,128)(2,1)S(1)} %collective-permute-done.17), channel_id=1, source_target_pairs={{0,8},{4,12},{8,16},{12,20},{16,24},{20,28},{24,0},{28,4},{1,9},{5... | collective-permute-start | bytes 786440 | tf_op jit(solution)/shard_map/ppermute | solution.py:27
  44.2 32.4 %collective-permute-start.7 = (bf16[1,256,1024]{2,1,0:T(8,128)(2,1)S(1)}, bf16[1,256,1024]{2,1,0:T(8,128)(2,1)}, u32[]{:S(2)}, u32[]{:S(2)}) collective-permute-start(bf16[1,256,1024]{2,1,0:T(8,128)(2,1)S(1)} %get-tuple-element.11), channel_id=1, source_target_pairs={{0,4},{4,0},{8,12},{12,8},{16,20},{20,16},{24,28},{28,24},{1,5},{5... | collective-permute-start | bytes 1572872 | tf_op jit(solution)/shard_map/ppermute | solution.py:31
  44.3 0.8 copy-start.4
  45.1 31.6 %collective-permute-start.5 = (bf16[1,256,1024]{2,1,0:T(8,128)(2,1)}, bf16[1,256,1024]{2,1,0:T(8,128)(2,1)}, u32[]{:S(2)}, u32[]{:S(2)}) collective-permute-start(bf16[1,256,1024]{2,1,0:T(8,128)(2,1)} %get-tuple-element.12), channel_id=1, source_target_pairs={{0,2},{2,0},{1,3},{3,1},{4,6},{6,4},{5,7},{7,5},{8,10},{10,8},{9,1... | collective-permute-start | bytes 1572872 | tf_op jit(solution)/shard_map/ppermute | solution.py:27
  47.2 29.9 %collective-permute-start.15 = (bf16[1,256,1024]{2,1,0:T(8,128)(2,1)}, bf16[1,256,1024]{2,1,0:T(8,128)(2,1)}, u32[]{:S(2)}, u32[]{:S(2)}) collective-permute-start(bf16[1,256,1024]{2,1,0:T(8,128)(2,1)} %collective-permute-done.14), channel_id=1, source_target_pairs={{0,4},{4,0},{8,12},{12,8},{16,20},{20,16},{24,28},{28,24},{1,5},{5... | collective-permute-start | bytes 1572872 | tf_op jit(solution)/shard_map/ppermute | solution.py:31
  49.1 3.2 %copy-start.11 = (bf16[1,256,512]{2,1,0:T(8,128)(2,1)}, bf16[1,256,512]{2,1,0:T(8,128)(2,1)S(1)}, u32[]{:S(2)}) copy-start(bf16[1,256,512]{2,1,0:T(8,128)(2,1)S(1)} %collective-permute-done.3) | copy-start | bytes 786436
  49.1 28.0 %collective-permute-start.12 = (bf16[1,256,1024]{2,1,0:T(8,128)(2,1)}, bf16[1,256,1024]{2,1,0:T(8,128)(2,1)}, u32[]{:S(2)}, u32[]{:S(2)}) collective-permute-start(bf16[1,256,1024]{2,1,0:T(8,128)(2,1)} %collective-permute-done.11), channel_id=1, source_target_pairs={{0,4},{4,0},{8,12},{12,8},{16,20},{20,16},{24,28},{28,24},{1,5},{5... | collective-permute-start | bytes 1572872 | tf_op jit(solution)/shard_map/ppermute | solution.py:31
  52.3 0.7 copy-start.6
  52.4 24.8 %collective-permute-start.9 = (bf16[1,256,1024]{2,1,0:T(8,128)(2,1)}, bf16[1,256,1024]{2,1,0:T(8,128)(2,1)}, u32[]{:S(2)}, u32[]{:S(2)}) collective-permute-start(bf16[1,256,1024]{2,1,0:T(8,128)(2,1)} %collective-permute-done.8), channel_id=1, source_target_pairs={{0,4},{4,0},{8,12},{12,8},{16,20},{20,16},{24,28},{28,24},{1,5},{5... | collective-permute-start | bytes 1572872 | tf_op jit(solution)/shard_map/ppermute | solution.py:31
  53.1 17.6 %copy-start.7 = (bf16[1,256,512]{2,1,0:T(8,128)(2,1)S(1)}, bf16[1,256,512]{2,1,0:T(8,128)(2,1)}, u32[]{:S(2)}) copy-start(bf16[1,256,512]{2,1,0:T(8,128)(2,1)} %copy-done.6) | copy-start | bytes 786436
  57.6 19.5 %copy-start.3 = (bf16[1,256,1024]{2,1,0:T(8,128)(2,1)S(1)}, bf16[1,256,1024]{2,1,0:T(8,128)(2,1)}, u32[]{:S(2)}) copy-start(bf16[1,256,1024]{2,1,0:T(8,128)(2,1)} %copy-done.2) | copy-start | bytes 1572868
  76.6 28.5 %collective-permute-start.4 = (bf16[1,256,1024]{2,1,0:T(8,128)(2,1)}, bf16[1,256,1024]{2,1,0:T(8,128)(2,1)}, u32[]{:S(2)}, u32[]{:S(2)}) collective-permute-start(bf16[1,256,1024]{2,1,0:T(8,128)(2,1)} %get-tuple-element.7), channel_id=1, source_target_pairs={{0,4},{4,0},{8,12},{12,8},{16,20},{20,16},{24,28},{28,24},{1,5},{5... | collective-permute-start | bytes 1572872 | tf_op jit(solution)/shard_map/ppermute | solution.py:31
  76.6 28.5 %collective-permute-start.6 = (bf16[1,256,1024]{2,1,0:T(8,128)(2,1)}, bf16[1,256,1024]{2,1,0:T(8,128)(2,1)}, u32[]{:S(2)}, u32[]{:S(2)}) collective-permute-start(bf16[1,256,1024]{2,1,0:T(8,128)(2,1)} %collective-permute-done.5), channel_id=1, source_target_pairs={{0,4},{4,0},{8,12},{12,8},{16,20},{20,16},{24,28},{28,24},{1,5},{5... | collective-permute-start | bytes 1572872 | tf_op jit(solution)/shard_map/ppermute | solution.py:31
  77.1 15.2 %collective-permute-start.19 = (bf16[1,256,512]{2,1,0:T(8,128)(2,1)S(1)}, bf16[1,256,512]{2,1,0:T(8,128)(2,1)}, u32[]{:S(2)}, u32[]{:S(2)}) collective-permute-start(bf16[1,256,512]{2,1,0:T(8,128)(2,1)S(1)} %copy-done.7), channel_id=1, source_target_pairs={{0,8},{4,12},{8,16},{12,20},{16,24},{20,28},{24,0},{28,4},{1,9},{5... | collective-permute-start | bytes 786440 | tf_op jit(solution)/shard_map/ppermute | solution.py:27
  109.5 1.4 copy-start
  110.9 10.1 %collective-permute-start.27 = (bf16[1,2,32,2048]{3,2,1,0:T(8,128)(2,1)S(1)}, bf16[1,2,32,2048]{3,2,1,0:T(8,128)(2,1)S(1)}, u32[]{:S(2)}, u32[]{:S(2)}) collective-permute-start(bf16[1,2,32,2048]{3,2,1,0:T(8,128)(2,1)S(1)} %get-tuple-element.17), channel_id=1, source_target_pairs={{0,2},{2,0},{1,3},{3,1},{4,6},{6,4},{5,7},{7,5},{8,10},{10,8},{9,1... | collective-permute-start | bytes 786440 | tf_op jit(solution)/shard_map/ppermute | solution.py:27
  115.9 9.1 %collective-permute-start.20 = (bf16[1,2,32,2048]{3,2,1,0:T(8,128)(2,1)S(1)}, bf16[1,2,32,2048]{3,2,1,0:T(8,128)(2,1)S(1)}, u32[]{:S(2)}, u32[]{:S(2)}) collective-permute-start(bf16[1,2,32,2048]{3,2,1,0:T(8,128)(2,1)S(1)} %get-tuple-element.18), channel_id=1, source_target_pairs={{0,2},{2,0},{1,3},{3,1},{4,6},{6,4},{5,7},{7,5},{8,10},{10,8},{9,1... | collective-permute-start | bytes 786440 | tf_op jit(solution)/shard_map/ppermute | solution.py:27
  117.7 10.5 %copy-start.1 = (f32[256,2048]{1,0:T(8,128)S(1)}, f32[256,2048]{1,0:T(8,128)}, u32[]{:S(2)}) copy-start(f32[256,2048]{1,0:T(8,128)} %copy-done) | copy-start | bytes 6291460
  118.9 9.3 %collective-permute-start.22 = (bf16[2,1,32,2048]{3,2,0,1:T(8,128)(2,1)S(1)}, bf16[2,1,32,2048]{3,2,0,1:T(8,128)(2,1)S(1)}, u32[]{:S(2)}, u32[]{:S(2)}) collective-permute-start(bf16[2,1,32,2048]{3,2,0,1:T(8,128)(2,1)S(1)} %get-tuple-element.6), channel_id=1, source_target_pairs={{0,1},{1,0},{2,3},{3,2},{4,5},{5,4},{6,7},{7,6},{8,9},{9,8},{10,11... | collective-permute-start | bytes 786440 | tf_op jit(solution)/shard_map/ppermute | solution.py:27
  120.5 13.3 %collective-permute-start.29 = (bf16[2,1,32,2048]{3,2,1,0:T(8,128)(2,1)S(1)}, bf16[2,1,32,2048]{3,2,1,0:T(8,128)(2,1)S(1)}, u32[]{:S(2)}, u32[]{:S(2)}) collective-permute-start(bf16[2,1,32,2048]{3,2,1,0:T(8,128)(2,1)S(1)} %get-tuple-element.5), channel_id=1, source_target_pairs={{0,1},{1,0},{2,3},{3,2},{4,5},{5,4},{6,7},{7,6},{8,9},{9,8},{10,11... | collective-permute-start | bytes 786440 | tf_op jit(solution)/shard_map/ppermute | solution.py:27
  125.2 11.4 %collective-permute-start.21 = (bf16[1,32,2048]{2,1,0:T(8,128)(2,1)S(1)}, bf16[1,32,2048]{2,1,0:T(8,128)(2,1)S(1)}, u32[]{:S(2)}, u32[]{:S(2)}) collective-permute-start(bf16[1,32,2048]{2,1,0:T(8,128)(2,1)S(1)} %fusion.28), channel_id=1, source_target_pairs={{0,1},{1,0},{2,3},{3,2},{4,5},{5,4},{6,7},{7,6},{8,9},{9,8},{10,11... | collective-permute-start | bytes 393224 | tf_op jit(solution)/shard_map/ppermute | solution.py:27
  128.3 6.0 %collective-permute-start.23 = (bf16[1,32,2048]{2,1,0:T(8,128)(2,1)S(1)}, bf16[1,32,2048]{2,1,0:T(8,128)(2,1)S(1)}, u32[]{:S(2)}, u32[]{:S(2)}) collective-permute-start(bf16[1,32,2048]{2,1,0:T(8,128)(2,1)S(1)} %fusion.30), channel_id=1, source_target_pairs={{0,2},{2,0},{1,3},{3,1},{4,6},{6,4},{5,7},{7,5},{8,10},{10,8},{9,1... | collective-permute-start | bytes 393224 | tf_op jit(solution)/shard_map/ppermute | solution.py:27
  128.7 12.5 %collective-permute-start.28 = (bf16[1,32,2048]{2,1,0:T(8,128)(2,1)S(1)}, bf16[1,32,2048]{2,1,0:T(8,128)(2,1)S(1)}, u32[]{:S(2)}, u32[]{:S(2)}) collective-permute-start(bf16[1,32,2048]{2,1,0:T(8,128)(2,1)S(1)} %fusion.29), channel_id=1, source_target_pairs={{0,1},{1,0},{2,3},{3,2},{4,5},{5,4},{6,7},{7,6},{8,9},{9,8},{10,11... | collective-permute-start | bytes 393224 | tf_op jit(solution)/shard_map/ppermute | solution.py:27
  133.9 7.2 %collective-permute-start.30 = (bf16[1,32,2048]{2,1,0:T(8,128)(2,1)S(1)}, bf16[1,32,2048]{2,1,0:T(8,128)(2,1)S(1)}, u32[]{:S(2)}, u32[]{:S(2)}) collective-permute-start(bf16[1,32,2048]{2,1,0:T(8,128)(2,1)S(1)} %fusion.31), channel_id=1, source_target_pairs={{0,2},{2,0},{1,3},{3,1},{4,6},{6,4},{5,7},{7,5},{8,10},{10,8},{9,1... | collective-permute-start | bytes 393224 | tf_op jit(solution)/shard_map/ppermute | solution.py:27
  136.8 8.9 %collective-permute-start.26 = (bf16[1,64,512]{2,1,0:T(8,128)(2,1)S(1)}, bf16[1,64,512]{2,1,0:T(8,128)(2,1)S(1)}, u32[]{:S(2)}, u32[]{:S(2)}) collective-permute-start(bf16[1,64,512]{2,1,0:T(8,128)(2,1)S(1)} %get-tuple-element.24), channel_id=1, source_target_pairs={{0,24},{4,28},{8,0},{12,4},{16,8},{20,12},{24,16},{28,20},{1,25},{... | collective-permute-start | bytes 196616 | tf_op jit(solution)/shard_map/ppermute | solution.py:27
  140.4 7.6 %collective-permute-start.25 = (bf16[1,64,512]{2,1,0:T(8,128)(2,1)S(1)}, bf16[1,64,512]{2,1,0:T(8,128)(2,1)S(1)}, u32[]{:S(2)}, u32[]{:S(2)}) collective-permute-start(bf16[1,64,512]{2,1,0:T(8,128)(2,1)S(1)} %get-tuple-element.23), channel_id=1, source_target_pairs={{0,16},{4,20},{8,24},{12,28},{16,0},{20,4},{24,8},{28,12},{1,17},{... | collective-permute-start | bytes 196616 | tf_op jit(solution)/shard_map/ppermute | solution.py:27
  140.5 7.6 %collective-permute-start.24 = (bf16[1,64,512]{2,1,0:T(8,128)(2,1)S(1)}, bf16[1,64,512]{2,1,0:T(8,128)(2,1)S(1)}, u32[]{:S(2)}, u32[]{:S(2)}) collective-permute-start(bf16[1,64,512]{2,1,0:T(8,128)(2,1)S(1)} %get-tuple-element.22), channel_id=1, source_target_pairs={{0,8},{4,12},{8,16},{12,20},{16,24},{20,28},{24,0},{28,4},{1,9},{5... | collective-permute-start | bytes 196616 | tf_op jit(solution)/shard_map/ppermute | solution.py:27
  141.4 7.3 %collective-permute-start.33 = (bf16[1,64,512]{2,1,0:T(8,128)(2,1)S(1)}, bf16[1,64,512]{2,1,0:T(8,128)(2,1)S(1)}, u32[]{:S(2)}, u32[]{:S(2)}) collective-permute-start(bf16[1,64,512]{2,1,0:T(8,128)(2,1)S(1)} %get-tuple-element.21), channel_id=1, source_target_pairs={{0,24},{4,28},{8,0},{12,4},{16,8},{20,12},{24,16},{28,20},{1,25},{... | collective-permute-start | bytes 196616 | tf_op jit(solution)/shard_map/ppermute | solution.py:27
  144.6 5.5 %collective-permute-start.32 = (bf16[1,64,512]{2,1,0:T(8,128)(2,1)S(1)}, bf16[1,64,512]{2,1,0:T(8,128)(2,1)S(1)}, u32[]{:S(2)}, u32[]{:S(2)}) collective-permute-start(bf16[1,64,512]{2,1,0:T(8,128)(2,1)S(1)} %get-tuple-element.20), channel_id=1, source_target_pairs={{0,16},{4,20},{8,24},{12,28},{16,0},{20,4},{24,8},{28,12},{1,17},{... | collective-permute-start | bytes 196616 | tf_op jit(solution)/shard_map/ppermute | solution.py:27
  145.7 6.1 %collective-permute-start.31 = (bf16[1,64,512]{2,1,0:T(8,128)(2,1)S(1)}, bf16[1,64,512]{2,1,0:T(8,128)(2,1)S(1)}, u32[]{:S(2)}, u32[]{:S(2)}) collective-permute-start(bf16[1,64,512]{2,1,0:T(8,128)(2,1)S(1)} %get-tuple-element.19), channel_id=1, source_target_pairs={{0,8},{4,12},{8,16},{12,20},{16,24},{20,28},{24,0},{28,4},{1,9},{5... | collective-permute-start | bytes 196616 | tf_op jit(solution)/shard_map/ppermute | solution.py:27
  151.9 1.4 collective-permute-start.34

commit v2 on v0

v2 whole, which is shorter than its diff:
```python
import functools

import jax
import jax.numpy as jnp
from jax import lax
from jax.experimental import pallas as pl
from jax.experimental.pallas import tpu as pltpu
from jax.sharding import PartitionSpec as P

CORES = 2
PIECES = 2
VMEM_LIMIT = 48 * 2**20
F32, BF16 = jnp.float32, jnp.bfloat16
VMEM = pl.BlockSpec(memory_space=pltpu.VMEM)
SMEM = pl.BlockSpec(memory_space=pltpu.SMEM)


def plain(factors, trials):
    trial_b = trials.astype(jnp.bfloat16)
    gathered = lax.all_gather(trial_b, "aux", axis=2, tiled=True)
    columns = lax.all_gather(factors, "vir", axis=2, tiled=True)
    pairs = jnp.einsum(
        "qib,mjb->mqij", columns, gathered, preferred_element_type=jnp.float32
    ).astype(jnp.bfloat16)
    stacked = jnp.einsum("mqij,qja->mia", pairs, columns, preferred_element_type=jnp.float32)
    slices = lax.psum_scatter(stacked, "aux", scatter_dimension=2, tiled=True)
    return lax.psum_scatter(slices, "outer", scatter_dimension=1, tiled=True)


def shift(array, axis, size, step, stride=1):
    count = size // stride
    pairs = [
        (i, (i // stride + step) % count * stride + i % stride) for i in range(size)
    ]
    return lax.ppermute(array, axis, pairs)


def sibling(array, size):
    return lax.ppermute(array, "aux", [(i, i ^ 1) for i in range(size)])


def part(array, index, size, axis):
    return lax.dynamic_slice_in_dim(array, index * size, size, axis)


def dot_nt(a, b):
    return lax.dot_general(a, b, (((1,), (1,)), ((), ())), preferred_element_type=F32)


def assemble(where, blocks, groups, rows, total):
    nt, ns = len(blocks), len(blocks[0])
    _, share, block = blocks[0][0].shape

    def body(at, *refs):
        out = refs[-1]
        for t in range(nt):
            col = pl.multiple_of(at[t], block)
            for s in range(ns):
                row = pl.multiple_of(at[nt + s], share)
                for g in range(groups):
                    out[g, pl.ds(row, share), pl.ds(col, block)] = refs[t * ns + s][g]

    flat = [b for row in blocks for b in row]
    moved = 2 * groups * rows * total * 2
    return pl.pallas_call(
        body,
        out_shape=jax.ShapeDtypeStruct((groups, rows, total), BF16),
        in_specs=[SMEM] + [VMEM] * len(flat),
        out_specs=VMEM,
        cost_estimate=pl.CostEstimate(flops=0, bytes_accessed=moved, transcendentals=0),
        compiler_params=pltpu.CompilerParams(vmem_limit_bytes=VMEM_LIMIT),
        name="assemble",
    )(where, *flat)


def early_sums(parts, vectors):
    groups, rows, total = vectors.shape
    flat = [p for side in parts for p in side]
    nr = len(parts[0])
    steps, _, width = flat[0].shape

    def body(*refs):
        vec, out = refs[len(flat)], refs[-1]

        @pl.when(pl.program_id(0) == 0)
        def _():
            out[...] = jnp.zeros_like(out)

        for g in range(groups):
            pairs = []
            for side in range(len(parts)):
                acc = None
                for r in range(nr):
                    term = dot_nt(refs[side * nr + r][0], vec[g, :, r * width : (r + 1) * width])
                    acc = term if acc is None else acc + term
                pairs.append(acc.astype(BF16))
            for r in range(nr):
                cols = slice(r * width, (r + 1) * width)
                acc = out[g, :, cols]
                for side, pair in enumerate(pairs):
                    acc = acc + jnp.dot(pair, refs[side * nr + r][0], preferred_element_type=F32)
                out[g, :, cols] = acc

    work = 4 * len(parts) * steps * groups * rows * rows * total
    moved = sum(2 * p.size for p in flat) + 2 * vectors.size + 4 * vectors.size
    return pl.pallas_call(
        body,
        grid=(steps,),
        out_shape=jax.ShapeDtypeStruct((groups, rows, total), F32),
        in_specs=[pl.BlockSpec((1, rows, width), lambda k: (k, 0, 0)) for _ in flat]
        + [pl.BlockSpec((groups, rows, total), lambda k: (0, 0, 0))],
        out_specs=pl.BlockSpec((groups, rows, total), lambda k: (0, 0, 0)),
        cost_estimate=pl.CostEstimate(flops=work, bytes_accessed=moved, transcendentals=0),
        compiler_params=pltpu.CompilerParams(vmem_limit_bytes=VMEM_LIMIT),
        name="early_sums",
    )(*flat, vectors)


def last_sums(piece, o, parts, vectors, early, no, nv):
    groups, rows, total = vectors.shape
    flat = [p for side in parts for p in side]
    nr = len(parts[0])
    width = total // nr
    per = groups // nv
    own = rows // no
    small = own // (PIECES * 2)
    more = [] if early is None else [early.reshape(groups, no, PIECES, 2, small, total)]

    def body(*refs):
        me = refs[0][0]
        ins = refs[1 : 1 + len(flat)]
        vec = refs[1 + len(flat)]
        before = refs[2 + len(flat)] if more else None
        send_x, keep_x, send_y, keep_y, acc = refs[-5:]

        def piece_rows(ref):
            found = []
            for oo in range(no):
                at = oo * own + piece * 2 * small
                found.append(ref[0, at : at + 2 * small, :])
            return jnp.concatenate(found, axis=0)

        left = [piece_rows(ref) for ref in ins]
        for g in range(groups):
            pairs = []
            for side in range(len(parts)):
                total_p = None
                for r in range(nr):
                    term = dot_nt(left[side * nr + r], vec[g, :, r * width : (r + 1) * width])
                    total_p = term if total_p is None else total_p + term
                pairs.append(total_p.astype(BF16))
            v = g // per
            for r in range(nr):
                got = None
                for side, pair in enumerate(pairs):
                    term = jnp.dot(pair, ins[side * nr + r][0], preferred_element_type=F32)
                    got = term if got is None else got + term
                got = got.reshape(no, 2, small, width)
                if before is not None:
                    got = got + before[g, :, 0, :, :, r * width : (r + 1) * width]
                to = (r - v) % nr * width
                cols = slice(to, to + width)
                if v == 0:
                    keep_x[g, :, :, cols] = got[:, 0]
                else:
                    send_x[g - per, :, :, cols] = got[:, 0].astype(BF16)
                acc[:, g, :, cols] = got[:, 1]
        keep_y[...] = acc[me]
        for s in range(1, no):
            send_y[s - 1] = acc[lax.rem(me + s, no)].astype(BF16)

    work = 4 * len(parts) * groups * rows * rows * total // PIECES
    moved = sum(2 * p.size for p in flat) + 2 * vectors.size + 2 * vectors.size
    early_spec = [
        pl.BlockSpec((groups, no, 1, 2, small, total), lambda k: (0, 0, piece, 0, 0, 0)) for _ in more
    ]

    def whole(*shape):
        return pl.BlockSpec(shape, lambda k: (0,) * len(shape))

    shapes = [
        ((groups - per, no, small, total), BF16),
        ((per, no, small, total), F32),
        ((no - 1, groups, small, total), BF16),
        ((groups, small, total), F32),
    ]
    return pl.pallas_call(
        body,
        grid=(1,),
        out_shape=[jax.ShapeDtypeStruct(s, d) for s, d in shapes],
        in_specs=[SMEM] + [whole(*p.shape) for p in flat] + [whole(*vectors.shape)] + early_spec,
        out_specs=[whole(*s) for s, _ in shapes],
        scratch_shapes=[pltpu.VMEM((no, groups, small, total), F32)],
        cost_estimate=pl.CostEstimate(flops=work, bytes_accessed=moved, transcendentals=0),
        compiler_params=pltpu.CompilerParams(vmem_limit_bytes=VMEM_LIMIT),
        name="last_sums",
    )(o.reshape(1), *flat, vectors, *more)


def per_device(na, nv, no, factors, trials):
    nq, rows, width = factors.shape
    nm, _, cols = trials.shape
    nz = na // CORES
    a, v, o = (lax.axis_index(name) for name in ("aux", "vir", "outer"))
    z, c = a // CORES, a % CORES
    half_m, take = nm // CORES, nq // nv
    block, total = CORES * cols, nv * width
    own = rows // no
    groups = nv * half_m

    mine = part(trials, o, own, 1).astype(BF16)
    both = jnp.concatenate([mine] + [shift(mine, "vir", nv, -r) for r in range(1, nv)], axis=0)
    both = both.reshape(nv, CORES, half_m, own, cols)
    given = sibling(lax.dynamic_index_in_dim(both, 1 - c, 1, False), na)
    kept = lax.dynamic_index_in_dim(both, c, 1, False)
    whole = jnp.where(
        c == 0,
        jnp.concatenate([kept, given], axis=-1),
        jnp.concatenate([given, kept], axis=-1),
    ).reshape(groups, own, block)

    sizes = [take - 1, 1] if take > 1 else [1]
    sides = []
    first = 0
    held, _ = lax.optimization_barrier((factors, both))
    for size in sizes:
        got = [lax.dynamic_slice_in_dim(held, v * take + first, size, 0)]
        for r in range(1, nv):
            sent = lax.dynamic_slice_in_dim(held, (v - r) % nv * take + first, size, 0)
            got.append(shift(sent, "vir", nv, -r))
        sides.append(got)
        first += size

    blocks = []
    for t in range(nz):
        got = whole if t == 0 else shift(whole, "aux", na, t, CORES)
        blocks.append([got] + [shift(got, "outer", no, -s) for s in range(1, no)])
    where = jnp.stack(
        [((z - t) % nz * block - v * width) % total for t in range(nz)]
        + [(o + s) % no * own for s in range(no)]
    ).astype(jnp.int32)
    vectors = assemble(where, blocks, groups, rows, total)

    early = None
    if take > 1:
        got, vectors = lax.optimization_barrier((sides[0], vectors))
        early = early_sums([got, [sibling(g, na) for g in got]], vectors)
    got, early = lax.optimization_barrier((sides[-1], early))
    last = [got, [sibling(g, na) for g in got]]

    out = []
    for p in range(PIECES):
        send_x, keep_x, send_y, keep_y = last_sums(p, o, last, vectors, early, no, nv)
        one = keep_x
        for r in range(1, nv):
            sent = send_x[(r - 1) * half_m : r * half_m]
            one += shift(sent, "vir", nv, r).astype(F32)
        u_one = lax.dynamic_index_in_dim(one, o, 1, False)
        for s in range(1, no):
            sent = lax.dynamic_index_in_dim(one, (o + s) % no, 1, False).astype(BF16)
            u_one += shift(sent, "outer", no, s).astype(F32)
        two = keep_y
        for s in range(1, no):
            two += shift(send_y[s - 1], "outer", no, s).astype(F32)
        u_two = two[:half_m]
        for r in range(1, nv):
            sent = two[r * half_m : (r + 1) * half_m].astype(BF16)
            u_two += shift(sent, "vir", nv, r).astype(F32)
        u = jnp.concatenate([u_one, u_two], axis=1)

        def to(zz):
            return lax.dynamic_slice_in_dim(u, (zz * block - v * width) % total, block, 2)

        got = to(z)
        for t in range(1, nz):
            got += shift(to((z + t) % nz).astype(BF16), "aux", na, t, CORES).astype(F32)
        out.append(got)
    done = jnp.concatenate(out, axis=1)
    there = sibling(part(done, 1 - c, cols, 2), na)
    here = part(done, c, cols, 2)
    return jnp.where(
        c == 0, jnp.concatenate([here, there], axis=0), jnp.concatenate([there, here], axis=0)
    )


def solution(mesh):
    na, nv, no = (mesh.shape[name] for name in ("aux", "vir", "outer"))

    def step(factors, trials):
        nq, rows, width = factors.shape
        nm, _, cols = trials.shape
        fits = na % CORES == 0 and nm % CORES == 0 and nq % nv == 0
        fits = fits and width % (CORES * cols) == 0 and cols % 128 == 0
        fits = fits and rows % (no * PIECES * 2 * 16) == 0
        if fits:
            return per_device(na, nv, no, factors, trials)
        return plain(factors, trials)

    placed = (P(("aux", "outer"), None, "vir"), P("vir", None, "aux"))
    return jax.shard_map(
        step, mesh=mesh, in_specs=placed, out_specs=P("vir", "outer", "aux"), check_vma=False
    )
```

time: 236 us -> 115 us (0.49)
  waiting for transfers between devices: 204 us -> 42.8 us
  starting transfers between devices: 0.12 us -> 34.4 us
  Pallas kernels: 0 us -> 21.8 us
  matrix products: 17.2 us -> 0 us
  between operations: 13.1 us -> 0.27 us
  local copies, waits for them, and re-layouts: 0 us -> 12.8 us
    all_gather x2 -> x0, waiting for transfers between devices: 138 us -> none  [the longest x1 105 us: per_device(): columns = lax.all_gather(factors, 'vir', axis=2, tiled=True)]
    reduce_scatter x2 -> x0, waiting for transfers between devices: 64.9 us -> none  [the longest x1 50.1 us: per_device(): slices = lax.psum_scatter(stacked, 'aux', scatter_dimension=2, tiled=True)]
    ppermute x0 -> x30, waiting for transfers between devices: none -> 42.8 us  [the longest x24 34.4 us: shift(): return lax.ppermute(array, axis, pairs)]
    ppermute x0 -> x30, starting transfers between devices: none -> 34.4 us  [the longest x24 33.2 us: shift(): return lax.ppermute(array, axis, pairs)]
    pallas_call x0 -> x4, Pallas kernels: none -> 21.8 us  [the longest x1 12.3 us: early_sums(): pl.pallas_call(body, grid=(steps,), out_shape=jax.ShapeDtypeStruct((group...]
    dot_general x1 -> x0, matrix products: 17.2 us -> none  [per_device(): jnp.einsum('mqij,qja->mia', pairs, columns, preferred_element_type=jnp.fl...]
    unnamed x0 -> x26, local copies, waits for them, and re-layouts: none -> 7.16 us
    dynamic_slice x0 -> x2, local copies, waits for them, and re-layouts: none -> 5.41 us  [per_device(): sent = lax.dynamic_slice_in_dim(held, (v - r) % nv * take + first, size, 0)]
  transfers between devices with their start and end apart: 4 -> 30, of which waited for: 4 -> 16; matrix products, arithmetic and copies ran while one was open for 0% -> 3% of each run, Pallas kernels for 0% -> 15%
where the time goes in v2:
time: 115 us
  waiting for transfers between devices  42.8 us (37%)
  starting transfers between devices  34.4 us (30%)
  Pallas kernels  21.8 us (19%)
  local copies, waits for them, and re-layouts  12.8 us (11%)
  other arithmetic  2.69 us (2%)
    ppermute x24, waiting for transfers between devices, shift(): return lax.ppermute(array, axis, pairs)  34.4 us
    ppermute x24, starting transfers between devices, shift(): return lax.ppermute(array, axis, pairs)  33.2 us
    pallas_call x1, Pallas kernels, early_sums(): pl.pallas_call(body, grid=(steps,), out_shape=jax.ShapeDtypeStruct((group...  12.3 us
    pallas_call x2, Pallas kernels, last_sums(): pl.pallas_call(body, grid=(1,), out_shape=[jax.ShapeDtypeStruct(s, d) for...  8.81 us
    ppermute x6, waiting for transfers between devices, sibling(): return lax.ppermute(array, 'aux', [(i, i ^ 1) for i in range(size)])  8.42 us
    unnamed x26, local copies, waits for them, and re-layouts  7.16 us
    dynamic_slice x2, local copies, waits for them, and re-layouts, per_device(): sent = lax.dynamic_slice_in_dim(held, (v - r) % nv * take + first, size, 0)  5.41 us
  transfers between devices with their start and end apart: 30, of which 16 were waited for; matrix products, arithmetic and copies ran while one was open for 3% of the time, Pallas kernels for 15%

profile of v2, /device:TPU:0, one launch (start us, length us, event | category | flops | bytes accessed | tf_op | source)
XLA Modules:
  0.0 114.7 jit_solution(15828558797215773439)
XLA Ops:
  0.0 1.0 copy-done
  1.1 3.0 %collective-permute-start = (bf16[2,128,256]{2,1,0:T(8,128)(2,1)S(1)}, bf16[2,128,256]{2,1,0:T(8,128)(2,1)S(1)}, u32[]{:S(2)}, u32[]{:S(2)}) collective-permute-start(bf16[2,128,256]{2,1,0:T(8,128)(2,1)S(1)} %dynamic-slice_convert_fusion.2), channel_id=1, source_target_pairs={{0,2},{2,0},{1,3},{3,1},{4,6},{6,4},{5,7},{7,5},{8,10},{10,8},{9,1... | collective-permute-start | bytes 393224 | tf_op jit(solution)/shard_map/ppermute | solution.py:35
  4.1 3.5 %collective-permute-done = bf16[2,128,256]{2,1,0:T(8,128)(2,1)S(1)} collective-permute-done((bf16[2,128,256]{2,1,0:T(8,128)(2,1)S(1)}, bf16[2,128,256]{2,1,0:T(8,128)(2,1)S(1)}, u32[]{:S(2)}, u32[]{:S(2)}) %collective-permute-start) | collective-permute-done | bytes 131104 | tf_op jit(solution)/shard_map/ppermute | solution.py:35
  7.6 4.1 %constant_dynamic-slice_fusion = (bf16[3,256,1024]{2,1,0:T(8,128)(2,1)}, bf16[3,256,1024]{2,1,0:T(8,128)(2,1)}) fusion(bf16[8,256,1024]{2,1,0:T(8,128)(2,1)} %param.2, s32[]{:T(128)S(6)} %select_n.182, s32[]{:T(128)S(6)} %select_n.181), kind=kLoop, calls=%fused_computation.62 | loop fusion | bytes 6291464 | tf_op jit(solution)/shard_map/dynamic_slice | solution.py:229
  11.7 1.7 %collective-permute-start.2 = (bf16[3,256,1024]{2,1,0:T(8,128)(2,1)}, bf16[3,256,1024]{2,1,0:T(8,128)(2,1)}, u32[]{:S(2)}, u32[]{:S(2)}) collective-permute-start(bf16[3,256,1024]{2,1,0:T(8,128)(2,1)} %get-tuple-element.35), channel_id=1, source_target_pairs={{0,2},{2,0},{1,3},{3,1},{4,6},{6,4},{5,7},{7,5},{8,10},{10,8},{9,1... | collective-permute-start | bytes 4718600 | tf_op jit(solution)/shard_map/ppermute | solution.py:35
  13.6 1.3 %collective-permute-done.3 = bf16[2,1,128,256]{3,2,0,1:T(8,128)(2,1)S(1)} collective-permute-done((bf16[2,1,128,256]{3,2,0,1:T(8,128)(2,1)S(1)}, bf16[2,1,128,256]{3,2,0,1:T(8,128)(2,1)S(1)}, u32[]{:S(2)}, u32[]{:S(2)}) %collective-permute-start.3) | collective-permute-done | bytes 131104 | tf_op jit(solution)/shard_map/ppermute | solution.py:39
  15.0 3.7 %collective-permute-start.9 = (bf16[2,128,512]{2,1,0:T(8,128)(2,1)S(1)}, bf16[2,128,512]{2,1,0:T(8,128)(2,1)S(1)}, u32[]{:S(2)}, u32[]{:S(2)}) collective-permute-start(bf16[2,128,512]{2,1,0:T(8,128)(2,1)S(1)} %maximum_select_fusion.refs_0_), channel_id=1, source_target_pairs={{0,24},{4,28},{8,0},{12,4},{16,8},{20,12},{24,16},{28,20},{1,25},{... | collective-permute-start | bytes 786440 | tf_op jit(solution)/shard_map/ppermute | solution.py:35
  18.7 1.0 collective-permute-start.7
  19.7 1.5 %collective-permute-start.4 = (bf16[2,128,512]{2,1,0:T(8,128)(2,1)S(1)}, bf16[2,128,512]{2,1,0:T(8,128)(2,1)S(1)}, u32[]{:S(2)}, u32[]{:S(2)}) collective-permute-start(bf16[2,128,512]{2,1,0:T(8,128)(2,1)S(1)} %maximum_select_fusion.refs_0_), channel_id=1, source_target_pairs={{0,1},{1,0},{2,3},{3,2},{4,5},{5,4},{6,7},{7,6},{8,9},{9,8},{10,11... | collective-permute-start | bytes 786440 | tf_op jit(solution)/shard_map/ppermute | solution.py:35
  21.2 4.2 %collective-permute-done.9.refs_6_ = bf16[2,128,512]{2,1,0:T(8,128)(2,1)S(1)} collective-permute-done((bf16[2,128,512]{2,1,0:T(8,128)(2,1)S(1)}, bf16[2,128,512]{2,1,0:T(8,128)(2,1)S(1)}, u32[]{:S(2)}, u32[]{:S(2)}) %collective-permute-start.9) | collective-permute-done | bytes 262176 | tf_op jit(solution)/shard_map/ppermute | solution.py:35
  25.4 1.5 %collective-permute-start.10 = (bf16[2,128,512]{2,1,0:T(8,128)(2,1)S(1)}, bf16[2,128,512]{2,1,0:T(8,128)(2,1)S(1)}, u32[]{:S(2)}, u32[]{:S(2)}) collective-permute-start(bf16[2,128,512]{2,1,0:T(8,128)(2,1)S(1)} %collective-permute-done.9.refs_6_), channel_id=1, source_target_pairs={{0,1},{1,0},{2,3},{3,2},{4,5},{5,4},{6,7},{7,6},{8,9},{9,8},{10,11... | collective-permute-start | bytes 786440 | tf_op jit(solution)/shard_map/ppermute | solution.py:35
  26.9 5.1 %collective-permute-done.5.refs_2_ = bf16[2,128,512]{2,1,0:T(8,128)(2,1)S(1)} collective-permute-done((bf16[2,128,512]{2,1,0:T(8,128)(2,1)S(1)}, bf16[2,128,512]{2,1,0:T(8,128)(2,1)S(1)}, u32[]{:S(2)}, u32[]{:S(2)}) %collective-permute-start.5) | collective-permute-done | bytes 262176 | tf_op jit(solution)/shard_map/ppermute | solution.py:35
  32.0 1.5 %collective-permute-start.6 = (bf16[2,128,512]{2,1,0:T(8,128)(2,1)S(1)}, bf16[2,128,512]{2,1,0:T(8,128)(2,1)S(1)}, u32[]{:S(2)}, u32[]{:S(2)}) collective-permute-start(bf16[2,128,512]{2,1,0:T(8,128)(2,1)S(1)} %collective-permute-done.5.refs_2_), channel_id=1, source_target_pairs={{0,1},{1,0},{2,3},{3,2},{4,5},{5,4},{6,7},{7,6},{8,9},{9,8},{10,11... | collective-permute-start | bytes 786440 | tf_op jit(solution)/shard_map/ppermute | solution.py:35
  33.5 7.8 %collective-permute-done.7.refs_4_ = bf16[2,128,512]{2,1,0:T(8,128)(2,1)S(1)} collective-permute-done((bf16[2,128,512]{2,1,0:T(8,128)(2,1)S(1)}, bf16[2,128,512]{2,1,0:T(8,128)(2,1)S(1)}, u32[]{:S(2)}, u32[]{:S(2)}) %collective-permute-start.7) | collective-permute-done | bytes 262176 | tf_op jit(solution)/shard_map/ppermute | solution.py:35
  41.3 1.5 %collective-permute-start.8 = (bf16[2,128,512]{2,1,0:T(8,128)(2,1)S(1)}, bf16[2,128,512]{2,1,0:T(8,128)(2,1)S(1)}, u32[]{:S(2)}, u32[]{:S(2)}) collective-permute-start(bf16[2,128,512]{2,1,0:T(8,128)(2,1)S(1)} %collective-permute-done.7.refs_4_), channel_id=1, source_target_pairs={{0,1},{1,0},{2,3},{3,2},{4,5},{5,4},{6,7},{7,6},{8,9},{9,8},{10,11... | collective-permute-start | bytes 786440 | tf_op jit(solution)/shard_map/ppermute | solution.py:35
  42.9 5.9 %collective-permute-done.8.refs_5_ = bf16[2,128,512]{2,1,0:T(8,128)(2,1)S(1)} collective-permute-done((bf16[2,128,512]{2,1,0:T(8,128)(2,1)S(1)}, bf16[2,128,512]{2,1,0:T(8,128)(2,1)S(1)}, u32[]{:S(2)}, u32[]{:S(2)}) %collective-permute-start.8) | collective-permute-done | bytes 262176 | tf_op jit(solution)/shard_map/ppermute | solution.py:35
  48.8 0.7 assemble.1.refs_4_.refs_5_
  49.6 1.3 %copy-done.1 = bf16[2,256,2048]{2,1,0:T(8,128)(2,1)} copy-done((bf16[2,256,2048]{2,1,0:T(8,128)(2,1)}, bf16[2,256,2048]{2,1,0:T(8,128)(2,1)S(1)}, u32[]{:S(2)}) %copy-start.1) | copy-done | bytes 2097176
  51.4 1.3 %constant_dynamic-slice_fusion.2 = (bf16[1,256,1024]{2,1,0:T(8,128)(2,1)S(1)}, bf16[1,256,1024]{2,1,0:T(8,128)(2,1)S(1)}) fusion(bf16[8,256,1024]{2,1,0:T(8,128)(2,1)} %param.2, s32[]{:T(128)S(6)} %select_n.180, s32[]{:T(128)S(6)} %select_n.178), kind=kLoop, calls=%fused_computation.64 | loop fusion | bytes 2097160 | tf_op jit(solution)/shard_map/dynamic_slice | solution.py:229
  53.3 1.4 %collective-permute-done.11.refs_2_ = bf16[3,256,1024]{2,1,0:T(8,128)(2,1)} collective-permute-done((bf16[3,256,1024]{2,1,0:T(8,128)(2,1)}, bf16[3,256,1024]{2,1,0:T(8,128)(2,1)}, u32[]{:S(2)}, u32[]{:S(2)}) %collective-permute-start.11) | collective-permute-done | bytes 1572896 | tf_op jit(solution)/shard_map/ppermute | solution.py:39
  54.7 2.2 %collective-permute-done.12.refs_3_ = bf16[3,256,1024]{2,1,0:T(8,128)(2,1)} collective-permute-done((bf16[3,256,1024]{2,1,0:T(8,128)(2,1)}, bf16[3,256,1024]{2,1,0:T(8,128)(2,1)}, u32[]{:S(2)}, u32[]{:S(2)}) %collective-permute-start.12) | collective-permute-done | bytes 1572896 | tf_op jit(solution)/shard_map/ppermute | solution.py:39
  56.9 12.3 %early_sums.1 = f32[2,256,2048]{2,1,0:T(8,128)} custom-call(bf16[3,256,1024]{2,1,0:T(8,128)(2,1)} %get-tuple-element.21.refs_0_, bf16[3,256,1024]{2,1,0:T(8,128)(2,1)} %collective-permute-done.2.refs_1_, bf16[3,256,1024]{2,1,0:T(8,128)(2,1)} %collective-permute-done.11.refs_2_, bf16[3,256,1024]{2,1,0:T(8,128)(2,1)} %collective-permute-done.12.refs_3_, ...), custom_call_target="tpu_custom_call" | custom-call | flops 6442450944 | bytes 12582912 | tf_op jit(solution)/shard_map/early_sums/pallas_call | solution.py:106
  69.8 1.4 %collective-permute-done.13.refs_3_ = bf16[1,256,1024]{2,1,0:T(8,128)(2,1)S(1)} collective-permute-done((bf16[1,256,1024]{2,1,0:T(8,128)(2,1)S(1)}, bf16[1,256,1024]{2,1,0:T(8,128)(2,1)S(1)}, u32[]{:S(2)}, u32[]{:S(2)}) %collective-permute-start.13) | collective-permute-done | bytes 524320 | tf_op jit(solution)/shard_map/ppermute | solution.py:39
  71.2 0.7 collective-permute-done.14.refs_4_
  72.0 4.8 %last_sums.3 = (bf16[1,2,32,2048]{3,2,1,0:T(8,128)(2,1)S(1)}, f32[1,2,32,2048]{3,2,1,0:T(8,128)S(1)}, bf16[1,2,32,2048]{3,2,1,0:T(8,128)(2,1)}, f32[2,32,2048]{2,1,0:T(8,128)S(1)}) custom-call(s32[1]{0:T(128)} %bitcast.refs_0_, bf16[1,256,1024]{2,1,0:T(8,128)(2,1)S(1)} %get-tuple-element.24.refs_1_, ...), custom_call_target="tpu_custom_call" | custom-call | flops 1073741824 | bytes 6291456 | tf_op jit(solution)/shard_map/last_sums/pallas_call | solution.py:187
  76.8 0.8 copy-done.9
  77.6 0.8 copy-done.11
  78.4 1.5 %collective-permute-start.24 = (bf16[2,32,2048]{2,1,0:T(8,128)(2,1)}, bf16[2,32,2048]{2,1,0:T(8,128)(2,1)}, u32[]{:S(2)}, u32[]{:S(2)}) collective-permute-start(bf16[2,32,2048]{2,1,0:T(8,128)(2,1)} %bitcast.17), channel_id=1, source_target_pairs={{0,1},{1,0},{2,3},{3,2},{4,5},{5,4},{6,7},{7,6},{8,9},{9,8},{10,11... | collective-permute-start | bytes 786440 | tf_op jit(solution)/shard_map/ppermute | solution.py:35
  80.5 1.0 copy-done.4
  81.5 1.0 copy-done.6
  82.6 1.0 copy-done.8
  83.6 4.0 %last_sums.2 = (bf16[1,2,32,2048]{3,2,1,0:T(8,128)(2,1)S(1)}, f32[1,2,32,2048]{3,2,1,0:T(8,128)S(1)}, bf16[1,2,32,2048]{3,2,1,0:T(8,128)(2,1)S(1)}, f32[2,32,2048]{2,1,0:T(8,128)S(1)}) custom-call(s32[1]{0:T(128)} %bitcast.refs_0_, bf16[1,256,1024]{2,1,0:T(8,128)(2,1)S(1)} %get-tuple-element.24.refs_1_, bf16[1,256,1024]{2,1,0:T(8,128)(2,1)S(1)} %copy-done.4, ...), custom_call_target="tpu_custom_call" | custom-call | flops 1073741824 | bytes 6291456 | tf_op jit(solution)/shard_map/last_sums/pallas_call | solution.py:187
  88.2 1.5 %collective-permute-start.15 = (bf16[1,2,32,2048]{3,2,1,0:T(8,128)(2,1)S(1)}, bf16[1,2,32,2048]{3,2,1,0:T(8,128)(2,1)S(1)}, u32[]{:S(2)}, u32[]{:S(2)}) collective-permute-start(bf16[1,2,32,2048]{3,2,1,0:T(8,128)(2,1)S(1)} %get-tuple-element.28), channel_id=1, source_target_pairs={{0,2},{2,0},{1,3},{3,1},{4,6},{6,4},{5,7},{7,5},{8,10},{10,8},{9,1... | collective-permute-start | bytes 786440 | tf_op jit(solution)/shard_map/ppermute | solution.py:35
  89.7 1.0 convert_add_fusion
  90.7 0.6 collective-permute-start.25
  91.4 1.6 %collective-permute-start.23 = (bf16[1,32,2048]{2,1,0:T(8,128)(2,1)S(1)}, bf16[1,32,2048]{2,1,0:T(8,128)(2,1)S(1)}, u32[]{:S(2)}, u32[]{:S(2)}) collective-permute-start(bf16[1,32,2048]{2,1,0:T(8,128)(2,1)S(1)} %fusion.1), channel_id=1, source_target_pairs={{0,1},{1,0},{2,3},{3,2},{4,5},{5,4},{6,7},{7,6},{8,9},{9,8},{10,11... | collective-permute-start | bytes 393224 | tf_op jit(solution)/shard_map/ppermute | solution.py:35
  93.0 3.9 %collective-permute-done.17 = bf16[2,32,2048]{2,1,0:T(8,128)(2,1)S(1)} collective-permute-done((bf16[2,32,2048]{2,1,0:T(8,128)(2,1)S(1)}, bf16[2,32,2048]{2,1,0:T(8,128)(2,1)S(1)}, u32[]{:S(2)}, u32[]{:S(2)}) %collective-permute-start.17) | collective-permute-done | bytes 262176 | tf_op jit(solution)/shard_map/ppermute | solution.py:35
  97.0 1.5 %collective-permute-start.18 = (bf16[1,32,2048]{2,1,0:T(8,128)(2,1)S(1)}, bf16[1,32,2048]{2,1,0:T(8,128)(2,1)S(1)}, u32[]{:S(2)}, u32[]{:S(2)}) collective-permute-start(bf16[1,32,2048]{2,1,0:T(8,128)(2,1)S(1)} %slice.27), channel_id=1, source_target_pairs={{0,2},{2,0},{1,3},{3,1},{4,6},{6,4},{5,7},{7,5},{8,10},{10,8},{9,1... | collective-permute-start | bytes 393224 | tf_op jit(solution)/shard_map/ppermute | solution.py:35
  99.2 0.7 collective-permute-done.25
  100.2 2.9 %collective-permute-start.27 = (bf16[1,64,512]{2,1,0:T(8,128)(2,1)S(1)}, bf16[1,64,512]{2,1,0:T(8,128)(2,1)S(1)}, u32[]{:S(2)}, u32[]{:S(2)}) collective-permute-start(bf16[1,64,512]{2,1,0:T(8,128)(2,1)S(1)} %get-tuple-element.40), channel_id=1, source_target_pairs={{0,16},{4,20},{8,24},{12,28},{16,0},{20,4},{24,8},{28,12},{1,17},{... | collective-permute-start | bytes 196616 | tf_op jit(solution)/shard_map/ppermute | solution.py:35
  103.1 0.9 collective-permute-start.28
  104.2 1.1 %collective-permute-start.19 = (bf16[1,64,512]{2,1,0:T(8,128)(2,1)S(1)}, bf16[1,64,512]{2,1,0:T(8,128)(2,1)S(1)}, u32[]{:S(2)}, u32[]{:S(2)}) collective-permute-start(bf16[1,64,512]{2,1,0:T(8,128)(2,1)S(1)} %get-tuple-element.42), channel_id=1, source_target_pairs={{0,8},{4,12},{8,16},{12,20},{16,24},{20,28},{24,0},{28,4},{1,9},{5... | collective-permute-start | bytes 196616 | tf_op jit(solution)/shard_map/ppermute | solution.py:35
  105.4 1.4 %collective-permute-start.20 = (bf16[1,64,512]{2,1,0:T(8,128)(2,1)S(1)}, bf16[1,64,512]{2,1,0:T(8,128)(2,1)S(1)}, u32[]{:S(2)}, u32[]{:S(2)}) collective-permute-start(bf16[1,64,512]{2,1,0:T(8,128)(2,1)S(1)} %get-tuple-element.43), channel_id=1, source_target_pairs={{0,16},{4,20},{8,24},{12,28},{16,0},{20,4},{24,8},{28,12},{1,17},{... | collective-permute-start | bytes 196616 | tf_op jit(solution)/shard_map/ppermute | solution.py:35
  107.0 2.3 %collective-permute-start.21 = (bf16[1,64,512]{2,1,0:T(8,128)(2,1)S(1)}, bf16[1,64,512]{2,1,0:T(8,128)(2,1)S(1)}, u32[]{:S(2)}, u32[]{:S(2)}) collective-permute-start(bf16[1,64,512]{2,1,0:T(8,128)(2,1)S(1)} %get-tuple-element.44), channel_id=1, source_target_pairs={{0,24},{4,28},{8,0},{12,4},{16,8},{20,12},{24,16},{28,20},{1,25},{... | collective-permute-start | bytes 196616 | tf_op jit(solution)/shard_map/ppermute | solution.py:35
  109.4 1.1 collective-permute-done.19
  110.4 2.0 %collective-permute-done.20 = bf16[1,64,512]{2,1,0:T(8,128)(2,1)S(1)} collective-permute-done((bf16[1,64,512]{2,1,0:T(8,128)(2,1)S(1)}, bf16[1,64,512]{2,1,0:T(8,128)(2,1)S(1)}, u32[]{:S(2)}, u32[]{:S(2)}) %collective-permute-start.20) | collective-permute-done | bytes 65568 | tf_op jit(solution)/shard_map/ppermute | solution.py:35
  112.7 1.3 %collective-permute-done.29 = f32[1,128,256]{2,1,0:T(8,128)S(1)} collective-permute-done((f32[1,128,256]{2,1,0:T(8,128)S(1)}, f32[1,128,256]{2,1,0:T(8,128)S(1)}, u32[]{:S(2)}, u32[]{:S(2)}) %collective-permute-start.29) | collective-permute-done | bytes 131104 | tf_op jit(solution)/shard_map/ppermute | solution.py:39
  114.0 0.7 maximum_select_fusion.1
  (67 shorter events, 5.0 us)
Async XLA Ops:
  0.0 1.0 copy-start
  1.1 6.5 %collective-permute-start = (bf16[2,128,256]{2,1,0:T(8,128)(2,1)S(1)}, bf16[2,128,256]{2,1,0:T(8,128)(2,1)S(1)}, u32[]{:S(2)}, u32[]{:S(2)}) collective-permute-start(bf16[2,128,256]{2,1,0:T(8,128)(2,1)S(1)} %dynamic-slice_convert_fusion.2), channel_id=1, source_target_pairs={{0,2},{2,0},{1,3},{3,1},{4,6},{6,4},{5,7},{7,5},{8,10},{10,8},{9,1... | collective-permute-start | bytes 393224 | tf_op jit(solution)/shard_map/ppermute | solution.py:35
  11.7 39.2 %collective-permute-start.2 = (bf16[3,256,1024]{2,1,0:T(8,128)(2,1)}, bf16[3,256,1024]{2,1,0:T(8,128)(2,1)}, u32[]{:S(2)}, u32[]{:S(2)}) collective-permute-start(bf16[3,256,1024]{2,1,0:T(8,128)(2,1)} %get-tuple-element.35), channel_id=1, source_target_pairs={{0,2},{2,0},{1,3},{3,1},{4,6},{6,4},{5,7},{7,5},{8,10},{10,8},{9,1... | collective-permute-start | bytes 4718600 | tf_op jit(solution)/shard_map/ppermute | solution.py:35
  13.5 1.4 %collective-permute-start.3 = (bf16[2,1,128,256]{3,2,0,1:T(8,128)(2,1)S(1)}, bf16[2,1,128,256]{3,2,0,1:T(8,128)(2,1)S(1)}, u32[]{:S(2)}, u32[]{:S(2)}) collective-permute-start(bf16[2,1,128,256]{3,2,0,1:T(8,128)(2,1)S(1)} %get-tuple-element.48), channel_id=1, source_target_pairs={{0,4},{4,0},{8,12},{12,8},{16,20},{20,16},{24,28},{28,24},{1,5},{5... | collective-permute-start | bytes 393224 | tf_op jit(solution)/shard_map/ppermute | solution.py:39
  15.0 10.4 %collective-permute-start.9 = (bf16[2,128,512]{2,1,0:T(8,128)(2,1)S(1)}, bf16[2,128,512]{2,1,0:T(8,128)(2,1)S(1)}, u32[]{:S(2)}, u32[]{:S(2)}) collective-permute-start(bf16[2,128,512]{2,1,0:T(8,128)(2,1)S(1)} %maximum_select_fusion.refs_0_), channel_id=1, source_target_pairs={{0,24},{4,28},{8,0},{12,4},{16,8},{20,12},{24,16},{28,20},{1,25},{... | collective-permute-start | bytes 786440 | tf_op jit(solution)/shard_map/ppermute | solution.py:35
  18.7 13.3 %collective-permute-start.5 = (bf16[2,128,512]{2,1,0:T(8,128)(2,1)S(1)}, bf16[2,128,512]{2,1,0:T(8,128)(2,1)S(1)}, u32[]{:S(2)}, u32[]{:S(2)}) collective-permute-start(bf16[2,128,512]{2,1,0:T(8,128)(2,1)S(1)} %maximum_select_fusion.refs_0_), channel_id=1, source_target_pairs={{0,8},{4,12},{8,16},{12,20},{16,24},{20,28},{24,0},{28,4},{1,9},{5... | collective-permute-start | bytes 786440 | tf_op jit(solution)/shard_map/ppermute | solution.py:35
  18.7 22.6 %collective-permute-start.7 = (bf16[2,128,512]{2,1,0:T(8,128)(2,1)S(1)}, bf16[2,128,512]{2,1,0:T(8,128)(2,1)S(1)}, u32[]{:S(2)}, u32[]{:S(2)}) collective-permute-start(bf16[2,128,512]{2,1,0:T(8,128)(2,1)S(1)} %maximum_select_fusion.refs_0_), channel_id=1, source_target_pairs={{0,16},{4,20},{8,24},{12,28},{16,0},{20,4},{24,8},{28,12},{1,17},{... | collective-permute-start | bytes 786440 | tf_op jit(solution)/shard_map/ppermute | solution.py:35
  19.7 23.2 %collective-permute-start.4 = (bf16[2,128,512]{2,1,0:T(8,128)(2,1)S(1)}, bf16[2,128,512]{2,1,0:T(8,128)(2,1)S(1)}, u32[]{:S(2)}, u32[]{:S(2)}) collective-permute-start(bf16[2,128,512]{2,1,0:T(8,128)(2,1)S(1)} %maximum_select_fusion.refs_0_), channel_id=1, source_target_pairs={{0,1},{1,0},{2,3},{3,2},{4,5},{5,4},{6,7},{7,6},{8,9},{9,8},{10,11... | collective-permute-start | bytes 786440 | tf_op jit(solution)/shard_map/ppermute | solution.py:35
  25.4 17.5 %collective-permute-start.10 = (bf16[2,128,512]{2,1,0:T(8,128)(2,1)S(1)}, bf16[2,128,512]{2,1,0:T(8,128)(2,1)S(1)}, u32[]{:S(2)}, u32[]{:S(2)}) collective-permute-start(bf16[2,128,512]{2,1,0:T(8,128)(2,1)S(1)} %collective-permute-done.9.refs_6_), channel_id=1, source_target_pairs={{0,1},{1,0},{2,3},{3,2},{4,5},{5,4},{6,7},{7,6},{8,9},{9,8},{10,11... | collective-permute-start | bytes 786440 | tf_op jit(solution)/shard_map/ppermute | solution.py:35
  32.0 10.9 %collective-permute-start.6 = (bf16[2,128,512]{2,1,0:T(8,128)(2,1)S(1)}, bf16[2,128,512]{2,1,0:T(8,128)(2,1)S(1)}, u32[]{:S(2)}, u32[]{:S(2)}) collective-permute-start(bf16[2,128,512]{2,1,0:T(8,128)(2,1)S(1)} %collective-permute-done.5.refs_2_), channel_id=1, source_target_pairs={{0,1},{1,0},{2,3},{3,2},{4,5},{5,4},{6,7},{7,6},{8,9},{9,8},{10,11... | collective-permute-start | bytes 786440 | tf_op jit(solution)/shard_map/ppermute | solution.py:35
  41.3 7.5 %collective-permute-start.8 = (bf16[2,128,512]{2,1,0:T(8,128)(2,1)S(1)}, bf16[2,128,512]{2,1,0:T(8,128)(2,1)S(1)}, u32[]{:S(2)}, u32[]{:S(2)}) collective-permute-start(bf16[2,128,512]{2,1,0:T(8,128)(2,1)S(1)} %collective-permute-done.7.refs_4_), channel_id=1, source_target_pairs={{0,1},{1,0},{2,3},{3,2},{4,5},{5,4},{6,7},{7,6},{8,9},{9,8},{10,11... | collective-permute-start | bytes 786440 | tf_op jit(solution)/shard_map/ppermute | solution.py:35
  49.5 1.4 %copy-start.1 = (bf16[2,256,2048]{2,1,0:T(8,128)(2,1)}, bf16[2,256,2048]{2,1,0:T(8,128)(2,1)S(1)}, u32[]{:S(2)}) copy-start(bf16[2,256,2048]{2,1,0:T(8,128)(2,1)S(1)} %assemble.1.refs_4_.refs_5_) | copy-start | bytes 6291460
  50.9 3.8 %collective-permute-start.11 = (bf16[3,256,1024]{2,1,0:T(8,128)(2,1)}, bf16[3,256,1024]{2,1,0:T(8,128)(2,1)}, u32[]{:S(2)}, u32[]{:S(2)}) collective-permute-start(bf16[3,256,1024]{2,1,0:T(8,128)(2,1)} %get-tuple-element.21.refs_0_), channel_id=1, source_target_pairs={{0,4},{4,0},{8,12},{12,8},{16,20},{20,16},{24,28},{28,24},{1,5},{5... | collective-permute-start | bytes 4718600 | tf_op jit(solution)/shard_map/ppermute | solution.py:39
  50.9 6.0 %collective-permute-start.12 = (bf16[3,256,1024]{2,1,0:T(8,128)(2,1)}, bf16[3,256,1024]{2,1,0:T(8,128)(2,1)}, u32[]{:S(2)}, u32[]{:S(2)}) collective-permute-start(bf16[3,256,1024]{2,1,0:T(8,128)(2,1)} %collective-permute-done.2.refs_1_), channel_id=1, source_target_pairs={{0,4},{4,0},{8,12},{12,8},{16,20},{20,16},{24,28},{28,24},{1,5},{5... | collective-permute-start | bytes 4718600 | tf_op jit(solution)/shard_map/ppermute | solution.py:39
  52.7 19.3 %copy-start.2 = (bf16[2,256,2048]{2,1,0:T(8,128)(2,1)S(1)}, bf16[2,256,2048]{2,1,0:T(8,128)(2,1)}, u32[]{:S(2)}) copy-start(bf16[2,256,2048]{2,1,0:T(8,128)(2,1)} %copy-done.1) | copy-start | bytes 6291460
  52.7 16.5 %collective-permute-start.1 = (bf16[1,256,1024]{2,1,0:T(8,128)(2,1)S(1)}, bf16[1,256,1024]{2,1,0:T(8,128)(2,1)S(1)}, u32[]{:S(2)}, u32[]{:S(2)}) collective-permute-start(bf16[1,256,1024]{2,1,0:T(8,128)(2,1)S(1)} %get-tuple-element.37), channel_id=1, source_target_pairs={{0,2},{2,0},{1,3},{3,1},{4,6},{6,4},{5,7},{7,5},{8,10},{10,8},{9,1... | collective-permute-start | bytes 1572872 | tf_op jit(solution)/shard_map/ppermute | solution.py:35
  69.2 7.6 %copy-start.3 = (bf16[1,256,1024]{2,1,0:T(8,128)(2,1)}, bf16[1,256,1024]{2,1,0:T(8,128)(2,1)S(1)}, u32[]{:S(2)}) copy-start(bf16[1,256,1024]{2,1,0:T(8,128)(2,1)S(1)} %collective-permute-done.1.refs_2_) | copy-start | bytes 1572868
  69.2 2.0 %collective-permute-start.13 = (bf16[1,256,1024]{2,1,0:T(8,128)(2,1)S(1)}, bf16[1,256,1024]{2,1,0:T(8,128)(2,1)S(1)}, u32[]{:S(2)}, u32[]{:S(2)}) collective-permute-start(bf16[1,256,1024]{2,1,0:T(8,128)(2,1)S(1)} %get-tuple-element.24.refs_1_), channel_id=1, source_target_pairs={{0,4},{4,0},{8,12},{12,8},{16,20},{20,16},{24,28},{28,24},{1,5},{5... | collective-permute-start | bytes 1572872 | tf_op jit(solution)/shard_map/ppermute | solution.py:39
  69.4 2.5 %collective-permute-start.14 = (bf16[1,256,1024]{2,1,0:T(8,128)(2,1)S(1)}, bf16[1,256,1024]{2,1,0:T(8,128)(2,1)S(1)}, u32[]{:S(2)}, u32[]{:S(2)}) collective-permute-start(bf16[1,256,1024]{2,1,0:T(8,128)(2,1)S(1)} %collective-permute-done.1.refs_2_), channel_id=1, source_target_pairs={{0,4},{4,0},{8,12},{12,8},{16,20},{20,16},{24,28},{28,24},{1,5},{5... | collective-permute-start | bytes 1572872 | tf_op jit(solution)/shard_map/ppermute | solution.py:39
  71.2 5.6 %copy-start.5 = (bf16[1,256,1024]{2,1,0:T(8,128)(2,1)}, bf16[1,256,1024]{2,1,0:T(8,128)(2,1)S(1)}, u32[]{:S(2)}) copy-start(bf16[1,256,1024]{2,1,0:T(8,128)(2,1)S(1)} %collective-permute-done.13.refs_3_) | copy-start | bytes 1572868
  72.0 4.8 %copy-start.7 = (bf16[1,256,1024]{2,1,0:T(8,128)(2,1)}, bf16[1,256,1024]{2,1,0:T(8,128)(2,1)S(1)}, u32[]{:S(2)}) copy-start(bf16[1,256,1024]{2,1,0:T(8,128)(2,1)S(1)} %collective-permute-done.14.refs_4_) | copy-start | bytes 1572868
  76.8 0.8 copy-start.9
  77.6 0.8 copy-start.11
  78.4 11.2 %collective-permute-start.24 = (bf16[2,32,2048]{2,1,0:T(8,128)(2,1)}, bf16[2,32,2048]{2,1,0:T(8,128)(2,1)}, u32[]{:S(2)}, u32[]{:S(2)}) collective-permute-start(bf16[2,32,2048]{2,1,0:T(8,128)(2,1)} %bitcast.17), channel_id=1, source_target_pairs={{0,1},{1,0},{2,3},{3,2},{4,5},{5,4},{6,7},{7,6},{8,9},{9,8},{10,11... | collective-permute-start | bytes 786440 | tf_op jit(solution)/shard_map/ppermute | solution.py:35
  79.9 11.4 %collective-permute-start.22 = (bf16[1,2,32,2048]{3,2,1,0:T(8,128)(2,1)S(1)}, bf16[1,2,32,2048]{3,2,1,0:T(8,128)(2,1)S(1)}, u32[]{:S(2)}, u32[]{:S(2)}) collective-permute-start(bf16[1,2,32,2048]{3,2,1,0:T(8,128)(2,1)S(1)} %get-tuple-element.32), channel_id=1, source_target_pairs={{0,2},{2,0},{1,3},{3,1},{4,6},{6,4},{5,7},{7,5},{8,10},{10,8},{9,1... | collective-permute-start | bytes 786440 | tf_op jit(solution)/shard_map/ppermute | solution.py:35
  80.5 1.0 copy-start.4
  81.5 1.0 copy-start.6
  82.6 1.0 copy-start.8
  83.6 6.1 %copy-start.12 = (f32[2,32,2048]{2,1,0:T(8,128)S(1)}, f32[2,32,2048]{2,1,0:T(8,128)}, u32[]{:S(2)}) copy-start(f32[2,32,2048]{2,1,0:T(8,128)} %copy-done.11) | copy-start | bytes 1572868
  87.6 3.7 %copy-start.10 = (f32[1,2,32,2048]{3,2,1,0:T(8,128)S(1)}, f32[1,2,32,2048]{3,2,1,0:T(8,128)}, u32[]{:S(2)}) copy-start(f32[1,2,32,2048]{3,2,1,0:T(8,128)} %copy-done.9) | copy-start | bytes 1572868
  87.6 9.3 %collective-permute-start.17 = (bf16[2,32,2048]{2,1,0:T(8,128)(2,1)S(1)}, bf16[2,32,2048]{2,1,0:T(8,128)(2,1)S(1)}, u32[]{:S(2)}, u32[]{:S(2)}) collective-permute-start(bf16[2,32,2048]{2,1,0:T(8,128)(2,1)S(1)} %bitcast.28), channel_id=1, source_target_pairs={{0,1},{1,0},{2,3},{3,2},{4,5},{5,4},{6,7},{7,6},{8,9},{9,8},{10,11... | collective-permute-start | bytes 786440 | tf_op jit(solution)/shard_map/ppermute | solution.py:35
  88.2 10.3 %collective-permute-start.15 = (bf16[1,2,32,2048]{3,2,1,0:T(8,128)(2,1)S(1)}, bf16[1,2,32,2048]{3,2,1,0:T(8,128)(2,1)S(1)}, u32[]{:S(2)}, u32[]{:S(2)}) collective-permute-start(bf16[1,2,32,2048]{3,2,1,0:T(8,128)(2,1)S(1)} %get-tuple-element.28), channel_id=1, source_target_pairs={{0,2},{2,0},{1,3},{3,1},{4,6},{6,4},{5,7},{7,5},{8,10},{10,8},{9,1... | collective-permute-start | bytes 786440 | tf_op jit(solution)/shard_map/ppermute | solution.py:35
  90.7 9.2 %collective-permute-start.25 = (bf16[1,32,2048]{2,1,0:T(8,128)(2,1)S(1)}, bf16[1,32,2048]{2,1,0:T(8,128)(2,1)S(1)}, u32[]{:S(2)}, u32[]{:S(2)}) collective-permute-start(bf16[1,32,2048]{2,1,0:T(8,128)(2,1)S(1)} %slice.26), channel_id=1, source_target_pairs={{0,2},{2,0},{1,3},{3,1},{4,6},{6,4},{5,7},{7,5},{8,10},{10,8},{9,1... | collective-permute-start | bytes 393224 | tf_op jit(solution)/shard_map/ppermute | solution.py:35
  91.4 8.5 %collective-permute-start.23 = (bf16[1,32,2048]{2,1,0:T(8,128)(2,1)S(1)}, bf16[1,32,2048]{2,1,0:T(8,128)(2,1)S(1)}, u32[]{:S(2)}, u32[]{:S(2)}) collective-permute-start(bf16[1,32,2048]{2,1,0:T(8,128)(2,1)S(1)} %fusion.1), channel_id=1, source_target_pairs={{0,1},{1,0},{2,3},{3,2},{4,5},{5,4},{6,7},{7,6},{8,9},{9,8},{10,11... | collective-permute-start | bytes 393224 | tf_op jit(solution)/shard_map/ppermute | solution.py:35
  97.0 7.1 %collective-permute-start.18 = (bf16[1,32,2048]{2,1,0:T(8,128)(2,1)S(1)}, bf16[1,32,2048]{2,1,0:T(8,128)(2,1)S(1)}, u32[]{:S(2)}, u32[]{:S(2)}) collective-permute-start(bf16[1,32,2048]{2,1,0:T(8,128)(2,1)S(1)} %slice.27), channel_id=1, source_target_pairs={{0,2},{2,0},{1,3},{3,1},{4,6},{6,4},{5,7},{7,5},{8,10},{10,8},{9,1... | collective-permute-start | bytes 393224 | tf_op jit(solution)/shard_map/ppermute | solution.py:35
  98.6 5.4 %collective-permute-start.16 = (bf16[1,32,2048]{2,1,0:T(8,128)(2,1)S(1)}, bf16[1,32,2048]{2,1,0:T(8,128)(2,1)S(1)}, u32[]{:S(2)}, u32[]{:S(2)}) collective-permute-start(bf16[1,32,2048]{2,1,0:T(8,128)(2,1)S(1)} %fusion), channel_id=1, source_target_pairs={{0,1},{1,0},{2,3},{3,2},{4,5},{5,4},{6,7},{7,6},{8,9},{9,8},{10,11... | collective-permute-start | bytes 393224 | tf_op jit(solution)/shard_map/ppermute | solution.py:35
  100.1 6.8 %collective-permute-start.26 = (bf16[1,64,512]{2,1,0:T(8,128)(2,1)S(1)}, bf16[1,64,512]{2,1,0:T(8,128)(2,1)S(1)}, u32[]{:S(2)}, u32[]{:S(2)}) collective-permute-start(bf16[1,64,512]{2,1,0:T(8,128)(2,1)S(1)} %get-tuple-element.39), channel_id=1, source_target_pairs={{0,8},{4,12},{8,16},{12,20},{16,24},{20,28},{24,0},{28,4},{1,9},{5... | collective-permute-start | bytes 196616 | tf_op jit(solution)/shard_map/ppermute | solution.py:35
  100.2 9.0 %collective-permute-start.27 = (bf16[1,64,512]{2,1,0:T(8,128)(2,1)S(1)}, bf16[1,64,512]{2,1,0:T(8,128)(2,1)S(1)}, u32[]{:S(2)}, u32[]{:S(2)}) collective-permute-start(bf16[1,64,512]{2,1,0:T(8,128)(2,1)S(1)} %get-tuple-element.40), channel_id=1, source_target_pairs={{0,16},{4,20},{8,24},{12,28},{16,0},{20,4},{24,8},{28,12},{1,17},{... | collective-permute-start | bytes 196616 | tf_op jit(solution)/shard_map/ppermute | solution.py:35
  103.1 6.2 %collective-permute-start.28 = (bf16[1,64,512]{2,1,0:T(8,128)(2,1)S(1)}, bf16[1,64,512]{2,1,0:T(8,128)(2,1)S(1)}, u32[]{:S(2)}, u32[]{:S(2)}) collective-permute-start(bf16[1,64,512]{2,1,0:T(8,128)(2,1)S(1)} %get-tuple-element.41), channel_id=1, source_target_pairs={{0,24},{4,28},{8,0},{12,4},{16,8},{20,12},{24,16},{28,20},{1,25},{... | collective-permute-start | bytes 196616 | tf_op jit(solution)/shard_map/ppermute | solution.py:35
  104.2 6.2 %collective-permute-start.19 = (bf16[1,64,512]{2,1,0:T(8,128)(2,1)S(1)}, bf16[1,64,512]{2,1,0:T(8,128)(2,1)S(1)}, u32[]{:S(2)}, u32[]{:S(2)}) collective-permute-start(bf16[1,64,512]{2,1,0:T(8,128)(2,1)S(1)} %get-tuple-element.42), channel_id=1, source_target_pairs={{0,8},{4,12},{8,16},{12,20},{16,24},{20,28},{24,0},{28,4},{1,9},{5... | collective-permute-start | bytes 196616 | tf_op jit(solution)/shard_map/ppermute | solution.py:35
  105.4 7.1 %collective-permute-start.20 = (bf16[1,64,512]{2,1,0:T(8,128)(2,1)S(1)}, bf16[1,64,512]{2,1,0:T(8,128)(2,1)S(1)}, u32[]{:S(2)}, u32[]{:S(2)}) collective-permute-start(bf16[1,64,512]{2,1,0:T(8,128)(2,1)S(1)} %get-tuple-element.43), channel_id=1, source_target_pairs={{0,16},{4,20},{8,24},{12,28},{16,0},{20,4},{24,8},{28,12},{1,17},{... | collective-permute-start | bytes 196616 | tf_op jit(solution)/shard_map/ppermute | solution.py:35
  107.0 5.5 %collective-permute-start.21 = (bf16[1,64,512]{2,1,0:T(8,128)(2,1)S(1)}, bf16[1,64,512]{2,1,0:T(8,128)(2,1)S(1)}, u32[]{:S(2)}, u32[]{:S(2)}) collective-permute-start(bf16[1,64,512]{2,1,0:T(8,128)(2,1)S(1)} %get-tuple-element.44), channel_id=1, source_target_pairs={{0,24},{4,28},{8,0},{12,4},{16,8},{20,12},{24,16},{28,20},{1,25},{... | collective-permute-start | bytes 196616 | tf_op jit(solution)/shard_map/ppermute | solution.py:35
  112.6 1.4 %collective-permute-start.29 = (f32[1,128,256]{2,1,0:T(8,128)S(1)}, f32[1,128,256]{2,1,0:T(8,128)S(1)}, u32[]{:S(2)}, u32[]{:S(2)}) collective-permute-start(f32[1,128,256]{2,1,0:T(8,128)S(1)} %get-tuple-element.46), channel_id=1, source_target_pairs={{0,4},{4,0},{8,12},{12,8},{16,20},{20,16},{24,28},{28,24},{1,5},{5... | collective-permute-start | bytes 393224 | tf_op jit(solution)/shard_map/ppermute | solution.py:39

commit v3 on v0

v3 whole, which is shorter than its diff:
```python
import jax
import jax.numpy as jnp
from jax import lax
from jax.experimental import pallas as pl
from jax.experimental.pallas import tpu as pltpu
from jax.sharding import PartitionSpec as P

CORES = 2
PIECES = 2
VMEM_LIMIT = 8 * 2**20
F32, BF16 = jnp.float32, jnp.bfloat16
VMEM = pl.BlockSpec(memory_space=pltpu.VMEM)
SMEM = pl.BlockSpec(memory_space=pltpu.SMEM)


def plain(factors, trials):
    trial_b = trials.astype(jnp.bfloat16)
    gathered = lax.all_gather(trial_b, "aux", axis=2, tiled=True)
    columns = lax.all_gather(factors, "vir", axis=2, tiled=True)
    pairs = jnp.einsum(
        "qib,mjb->mqij", columns, gathered, preferred_element_type=jnp.float32
    ).astype(jnp.bfloat16)
    stacked = jnp.einsum("mqij,qja->mia", pairs, columns, preferred_element_type=jnp.float32)
    slices = lax.psum_scatter(stacked, "aux", scatter_dimension=2, tiled=True)
    return lax.psum_scatter(slices, "outer", scatter_dimension=1, tiled=True)


def shift(array, axis, size, step, stride=1):
    count = size // stride
    pairs = [
        (i, (i // stride + step) % count * stride + i % stride) for i in range(size)
    ]
    return lax.ppermute(array, axis, pairs)


def sibling(array, size):
    return lax.ppermute(array, "aux", [(i, i ^ 1) for i in range(size)])


def part(array, index, size, axis):
    return lax.dynamic_slice_in_dim(array, index * size, size, axis)


def dot_nt(a, b):
    return lax.dot_general(a, b, (((1,), (1,)), ((), ())), preferred_element_type=F32)


def params():
    return pltpu.CompilerParams(vmem_limit_bytes=VMEM_LIMIT)


def cost(flops, *arrays):
    moved = sum(x.size * x.dtype.itemsize for x in arrays)
    return pl.CostEstimate(flops=flops, bytes_accessed=moved, transcendentals=0)


def assemble(where, blocks, groups, rows, total):
    shape = jax.ShapeDtypeStruct((groups, rows, total), BF16)

    def body(at, *refs):
        out = refs[-1]
        for ref, (_, first, row_slot, col_slot) in zip(refs, blocks):
            many, share, block = ref.shape
            row = pl.multiple_of(at[row_slot], share)
            col = pl.multiple_of(at[col_slot], block)
            for g in range(many):
                out[first + g, pl.ds(row, share), pl.ds(col, block)] = ref[g]

    return pl.pallas_call(
        body,
        out_shape=shape,
        in_specs=[SMEM] + [VMEM] * len(blocks),
        out_specs=VMEM,
        cost_estimate=cost(0, shape, shape),
        compiler_params=params(),
        name="assemble",
    )(where, *[b[0] for b in blocks])


def pairs_of(refs, firsts, count, vec, store):
    groups, rows, _ = vec.shape
    for g in range(groups):
        acc = None
        for r, (ref, first) in enumerate(zip(refs, firsts)):
            width = ref.shape[2]
            left = ref[first : first + count].reshape(count * rows, width)
            term = dot_nt(left, vec[g, :, r * width : (r + 1) * width])
            acc = term if acc is None else acc + term
        acc = acc.astype(BF16)
        for k in range(count):
            store(g, k, acc[k * rows : (k + 1) * rows])


def early_sums(sides, steps, vectors):
    groups, rows, total = vectors.shape
    nr = len(sides[0])
    width = total // nr
    flat = [p for side in sides for p in side]
    shape = jax.ShapeDtypeStruct((groups, rows, total), F32)
    tile = min(width, 512)

    def body(*refs):
        vec, out, held = refs[len(flat) :]
        for s in range(len(sides)):

            def store(g, k, pair, s=s):
                held[s, g * rows : (g + 1) * rows, k * rows : (k + 1) * rows] = pair

            pairs_of(refs[s * nr : (s + 1) * nr], [0] * nr, steps, vec, store)
        for r in range(nr):
            for at in range(0, width, tile):
                acc = None
                for s in range(len(sides)):
                    right = refs[s * nr + r][0:steps, :, at : at + tile]
                    term = jnp.dot(
                        held[s], right.reshape(steps * rows, tile), preferred_element_type=F32
                    )
                    acc = term if acc is None else acc + term
                col = r * width + at
                out[:, :, col : col + tile] = acc.reshape(groups, rows, tile)

    work = 4 * len(sides) * steps * groups * rows * rows * total
    return pl.pallas_call(
        body,
        out_shape=shape,
        in_specs=[VMEM] * (len(flat) + 1),
        out_specs=VMEM,
        scratch_shapes=[pltpu.VMEM((len(sides), groups * rows, steps * rows), BF16)],
        cost_estimate=cost(work, *flat, vectors, shape),
        compiler_params=params(),
        name="early_sums",
    )(*flat, vectors)


def own_pairs(side, firsts, vectors):
    groups, rows, total = vectors.shape
    shape = jax.ShapeDtypeStruct((groups, rows, rows), BF16)

    def body(*refs):
        vec, out = refs[-2:]

        def store(g, _, pair):
            out[g] = pair

        pairs_of(refs[:-2], firsts, 1, vec, store)

    return pl.pallas_call(
        body,
        out_shape=shape,
        in_specs=[VMEM] * (len(side) + 1),
        out_specs=VMEM,
        cost_estimate=cost(2 * groups * rows * rows * total, *side, vectors),
        compiler_params=params(),
        name="own_pairs",
    )(*side, vectors)


def last_sums(piece, o, sides, firsts, pairs, early, no, nv):
    groups, rows, _ = pairs[0].shape
    nr = len(sides[0])
    width = sides[0][0].shape[2]
    total = nr * width
    flat = [p for side in sides for p in side]
    per = groups // nv
    own = rows // no
    small = own // (PIECES * 2)
    more = [] if early is None else [early]
    tile = min(width, 512)

    def body(*refs):
        me = refs[0][0]
        ins = refs[1 : 1 + len(flat)]
        pair_refs = refs[1 + len(flat) : 1 + len(flat) + len(pairs)]
        before = refs[1 + len(flat) + len(pairs)]
        send_x, keep_x, send_y, keep_y, acc = refs[-5:]
        places = [oo * own + piece * 2 * small for oo in range(no)]
        left = [
            jnp.concatenate(
                [ref[g, at : at + 2 * small, :] for g in range(groups) for at in places], axis=0
            )
            for ref in pair_refs
        ]
        for r in range(nr):
            for at in range(0, width, tile):
                got = None
                for s in range(len(sides)):
                    right = ins[s * nr + r][firsts[r], :, at : at + tile]
                    term = jnp.dot(left[s], right, preferred_element_type=F32)
                    got = term if got is None else got + term
                got = got.reshape(groups, no, 2, small, tile)
                for g in range(groups):
                    v = g // per
                    to = (r - v) % nr * width + at
                    cols = slice(to, to + tile)
                    for oo in range(no):
                        half = [got[g, oo, 0], got[g, oo, 1]]
                        if more:
                            col = r * width + at
                            for h in range(2):
                                row = places[oo] + h * small
                                half[h] += before[g, row : row + small, col : col + tile]
                        if v == 0:
                            keep_x[g, oo, :, cols] = half[0]
                        else:
                            send_x[g - per, oo, :, cols] = half[0].astype(BF16)
                        acc[oo, g, :, cols] = half[1]
        keep_y[...] = acc[me]
        for s in range(1, no):
            send_y[s - 1] = acc[lax.rem(me + s, no)].astype(BF16)

    work = 2 * len(sides) * groups * rows * rows * total // PIECES
    shapes = [
        jax.ShapeDtypeStruct((groups - per, no, small, total), BF16),
        jax.ShapeDtypeStruct((per, no, small, total), F32),
        jax.ShapeDtypeStruct((no - 1, groups, small, total), BF16),
        jax.ShapeDtypeStruct((groups, small, total), F32),
    ]
    return pl.pallas_call(
        body,
        out_shape=shapes,
        in_specs=[SMEM] + [VMEM] * (len(flat) + len(pairs) + len(more)),
        out_specs=[VMEM] * len(shapes),
        scratch_shapes=[pltpu.VMEM((no, groups, small, total), F32)],
        cost_estimate=cost(work, *flat, *pairs, *shapes, *shapes),
        compiler_params=params(),
        name="last_sums",
    )(o.reshape(1), *flat, *pairs, *more)


def per_device(na, nv, no, factors, trials):
    nq, rows, width = factors.shape
    nm, _, cols = trials.shape
    nz = na // CORES
    a, v, o = (lax.axis_index(name) for name in ("aux", "vir", "outer"))
    z, c = a // CORES, a % CORES
    half_m, take = nm // CORES, nq // nv
    block, total = CORES * cols, nv * width
    own = rows // no
    groups = nv * half_m
    early_steps = take - 1

    trial_b = trials.astype(BF16)
    mine = part(trial_b, o, own, 1)
    others = [shift(mine, "vir", nv, -r) for r in range(1, nv)]

    def over_cores(x):
        x = x.reshape(x.shape[0] // nm, CORES, half_m, *x.shape[1:])
        given = sibling(lax.dynamic_index_in_dim(x, 1 - c, 1, False), na)
        kept = lax.dynamic_index_in_dim(x, c, 1, False)
        both = jnp.where(
            c == 0,
            jnp.concatenate([kept, given], axis=-1),
            jnp.concatenate([given, kept], axis=-1),
        )
        return both.reshape(-1, *both.shape[2:])

    own_whole = over_cores(trial_b)
    own_part = part(own_whole, o, own, 1)

    held, own_part = lax.optimization_barrier((factors, own_part))
    sizes = [early_steps, 1] if early_steps else [1]
    come, first = [], 0
    for size in sizes:
        got = []
        for r in range(1, nv):
            sent = lax.dynamic_slice_in_dim(held, (v - r) % nv * take + first, size, 0)
            got.append(shift(sent, "vir", nv, -r))
        come.append(got)
        first += size

    their = over_cores(jnp.concatenate(others, axis=0)) if others else None
    blocks = []
    for first, x in ((0, own_part), (half_m, their)):
        for t in range(nz):
            if x is None:
                continue
            if t == 0 and first == 0:
                for s in range(no):
                    blocks.append((part(own_whole, (o + s) % no, own, 1), 0, nz + s, 0))
                continue
            got = x if t == 0 else shift(x, "aux", na, t, CORES)
            blocks.append((got, first, nz, t))
            for s in range(1, no):
                blocks.append((shift(got, "outer", no, -s), first, nz + s, t))
    where = jnp.stack(
        [((z - t) % nz * block - v * width) % total for t in range(nz)]
        + [(o + s) % no * own for s in range(no)]
    ).astype(jnp.int32)
    vectors = assemble(where, blocks, groups, rows, total)

    later, _ = lax.optimization_barrier((factors, blocks[-no][0]))
    kept = lax.dynamic_slice_in_dim(later, v * take, take, 0)
    shown = sibling(kept, na)
    early = None
    if early_steps:
        got, vectors = lax.optimization_barrier((come[0], vectors))
        early = early_sums(
            [[kept] + got, [shown] + [sibling(g, na) for g in got]], early_steps, vectors
        )
    got, early = lax.optimization_barrier((come[-1], early))
    sides = [[kept] + got, [shown] + [sibling(g, na) for g in got]]
    firsts = [early_steps] + [0] * (nv - 1)
    pairs = [own_pairs(side, firsts, vectors) for side in sides]

    out = []
    for p in range(PIECES):
        send_x, keep_x, send_y, keep_y = last_sums(p, o, sides, firsts, pairs, early, no, nv)
        one = keep_x
        for r in range(1, nv):
            sent = send_x[(r - 1) * half_m : r * half_m]
            one += shift(sent, "vir", nv, r).astype(F32)
        u_one = lax.dynamic_index_in_dim(one, o, 1, False)
        for s in range(1, no):
            sent = lax.dynamic_index_in_dim(one, (o + s) % no, 1, False).astype(BF16)
            u_one += shift(sent, "outer", no, s).astype(F32)
        two = keep_y
        for s in range(1, no):
            two += shift(send_y[s - 1], "outer", no, s).astype(F32)
        u_two = two[:half_m]
        for r in range(1, nv):
            sent = two[r * half_m : (r + 1) * half_m].astype(BF16)
            u_two += shift(sent, "vir", nv, r).astype(F32)
        u = jnp.concatenate([u_one, u_two], axis=1)

        def to(zz):
            return lax.dynamic_slice_in_dim(u, (zz * block - v * width) % total, block, 2)

        got = to(z)
        for t in range(1, nz):
            got += shift(to((z + t) % nz).astype(BF16), "aux", na, t, CORES).astype(F32)
        out.append(got)
    done = jnp.concatenate(out, axis=1)
    there = sibling(part(done, 1 - c, cols, 2), na)
    here = part(done, c, cols, 2)
    return jnp.where(
        c == 0, jnp.concatenate([here, there], axis=0), jnp.concatenate([there, here], axis=0)
    )


def solution(mesh):
    na, nv, no = (mesh.shape[name] for name in ("aux", "vir", "outer"))

    def step(factors, trials):
        nq, rows, width = factors.shape
        nm, _, cols = trials.shape
        fits = na % CORES == 0 and nm % CORES == 0 and nq % nv == 0
        fits = fits and width % (CORES * cols) == 0 and cols % 128 == 0
        fits = fits and rows % (no * PIECES * 2 * 16) == 0
        if fits:
            return per_device(na, nv, no, factors, trials)
        return plain(factors, trials)

    placed = (P(("aux", "outer"), None, "vir"), P("vir", None, "aux"))
    return jax.shard_map(
        step, mesh=mesh, in_specs=placed, out_specs=P("vir", "outer", "aux"), check_vma=False
    )
```

time: 236 us -> 159 us (0.67)
  waiting for transfers between devices: 204 us -> 76 us
  starting transfers between devices: 0.12 us -> 41.7 us
  Pallas kernels: 0 us -> 19.2 us
  local copies, waits for them, and re-layouts: 0 us -> 17.4 us
  matrix products: 17.2 us -> 0 us
  between operations: 13.1 us -> 0.32 us
    all_gather x2 -> x0, waiting for transfers between devices: 138 us -> none  [the longest x1 105 us: per_device(): columns = lax.all_gather(factors, 'vir', axis=2, tiled=True)]
    ppermute x0 -> x36, waiting for transfers between devices: none -> 76 us  [the longest x30 70.1 us: shift(): return lax.ppermute(array, axis, pairs)]
    reduce_scatter x2 -> x0, waiting for transfers between devices: 64.9 us -> none  [the longest x1 50.1 us: per_device(): slices = lax.psum_scatter(stacked, 'aux', scatter_dimension=2, tiled=True)]
    ppermute x0 -> x36, starting transfers between devices: none -> 41.7 us  [the longest x30 41 us: shift(): return lax.ppermute(array, axis, pairs)]
    pallas_call x0 -> x6, Pallas kernels: none -> 19.2 us  [the longest x1 9.2 us: early_sums(): pl.pallas_call(body, out_shape=shape, in_specs=[VMEM] * (len(flat) + 1),...]
    dot_general x1 -> x0, matrix products: 17.2 us -> none  [per_device(): jnp.einsum('mqij,qja->mia', pairs, columns, preferred_element_type=jnp.fl...]
    unnamed x0 -> x30, local copies, waits for them, and re-layouts: none -> 11.5 us
    dynamic_slice x0 -> x6, local copies, waits for them, and re-layouts: none -> 5.67 us  [the longest x2 3.85 us: per_device(): sent = lax.dynamic_slice_in_dim(held, (v - r) % nv * take + first, size, 0)]
  transfers between devices with their start and end apart: 4 -> 36, of which waited for: 4 -> 23; matrix products, arithmetic and copies ran while one was open for 0% -> 3% of each run, Pallas kernels for 0% -> 9%
where the time goes in v3:
time: 159 us; the launch traced here: 158 us
  waiting for transfers between devices  76 us (48%)
  starting transfers between devices  41.7 us (26%)
  Pallas kernels  19.2 us (12%)
  local copies, waits for them, and re-layouts  17.4 us (11%)
  other arithmetic  3.75 us (2%)
    ppermute x30, waiting for transfers between devices, shift(): return lax.ppermute(array, axis, pairs)  70.1 us
    ppermute x30, starting transfers between devices, shift(): return lax.ppermute(array, axis, pairs)  41 us
    unnamed x30, local copies, waits for them, and re-layouts  11.5 us
    pallas_call x1, Pallas kernels, early_sums(): pl.pallas_call(body, out_shape=shape, in_specs=[VMEM] * (len(flat) + 1),...  9.2 us
    ppermute x6, waiting for transfers between devices, sibling(): return lax.ppermute(array, 'aux', [(i, i ^ 1) for i in range(size)])  5.84 us
    pallas_call x2, Pallas kernels, last_sums(): pl.pallas_call(body, out_shape=shapes, in_specs=[SMEM] + [VMEM] * (len(fl...  5.8 us
    dynamic_slice x2, local copies, waits for them, and re-layouts, per_device(): sent = lax.dynamic_slice_in_dim(held, (v - r) % nv * take + first, size, 0)  3.85 us
  transfers between devices with their start and end apart: 36, of which 23 were waited for; matrix products, arithmetic and copies ran while one was open for 3% of the time, Pallas kernels for 9%

profile of v3, /device:TPU:0, one launch (start us, length us, event | category | flops | bytes accessed | tf_op | source)
XLA Modules:
  0.0 158.4 jit_solution(6676923855205455623)
XLA Ops:
  0.0 1.1 convert_element_type.93
  2.8 2.8 %constant_dynamic-slice_fusion = bf16[3,256,1024]{2,1,0:T(8,128)(2,1)} fusion(bf16[8,256,1024]{2,1,0:T(8,128)(2,1)} %param.2, s32[]{:T(128)S(6)} %select_n.220), kind=kLoop, calls=%fused_computation.65 | loop fusion | bytes 3145732 | tf_op jit(solution)/shard_map/dynamic_slice | solution.py:266
  5.6 2.8 %collective-permute-start.5 = (bf16[3,256,1024]{2,1,0:T(8,128)(2,1)}, bf16[3,256,1024]{2,1,0:T(8,128)(2,1)}, u32[]{:S(2)}, u32[]{:S(2)}) collective-permute-start(bf16[3,256,1024]{2,1,0:T(8,128)(2,1)} %constant_dynamic-slice_fusion), channel_id=1, source_target_pairs={{0,2},{2,0},{1,3},{3,1},{4,6},{6,4},{5,7},{7,5},{8,10},{10,8},{9,1... | collective-permute-start | bytes 4718600 | tf_op jit(solution)/shard_map/ppermute | solution.py:33
  8.5 37.6 %collective-permute-done = bf16[2,128,256]{2,1,0:T(8,128)(2,1)S(1)} collective-permute-done((bf16[2,128,256]{2,1,0:T(8,128)(2,1)S(1)}, bf16[2,128,256]{2,1,0:T(8,128)(2,1)S(1)}, u32[]{:S(2)}, u32[]{:S(2)}) %collective-permute-start) | collective-permute-done | bytes 131104 | tf_op jit(solution)/shard_map/ppermute | solution.py:33
  46.2 1.2 collective-permute-done.1
  47.5 3.9 %collective-permute-start.2 = (bf16[1,128,512]{2,1,0:T(8,128)(2,1)S(1)}, bf16[1,128,512]{2,1,0:T(8,128)(2,1)S(1)}, u32[]{:S(2)}, u32[]{:S(2)}) collective-permute-start(bf16[1,128,512]{2,1,0:T(8,128)(2,1)S(1)} %maximum_select_fusion.2.refs_8_), channel_id=1, source_target_pairs={{0,24},{4,28},{8,0},{12,4},{16,8},{20,12},{24,16},{28,20},{1,25},{... | collective-permute-start | bytes 393224 | tf_op jit(solution)/shard_map/ppermute | solution.py:33
  51.9 1.6 collective-permute-start.6
  53.4 1.9 %collective-permute-done.2.refs_14_ = bf16[1,128,512]{2,1,0:T(8,128)(2,1)S(1)} collective-permute-done((bf16[1,128,512]{2,1,0:T(8,128)(2,1)S(1)}, bf16[1,128,512]{2,1,0:T(8,128)(2,1)S(1)}, u32[]{:S(2)}, u32[]{:S(2)}) %collective-permute-start.2) | collective-permute-done | bytes 131104 | tf_op jit(solution)/shard_map/ppermute | solution.py:33
  55.3 1.8 %constant_dynamic-slice_fusion.2.refs_0_.refs_1_ = bf16[4,256,1024]{2,1,0:T(8,128)(2,1)S(1)} fusion(bf16[8,256,1024]{2,1,0:T(8,128)(2,1)} %param.2, s32[]{:T(128)S(6)} %select_n.215), kind=kLoop, calls=%fused_computation.67 | loop fusion | bytes 4194308 | tf_op jit(solution)/shard_map/dynamic_slice | solution.py:292
  59.1 2.8 %collective-permute-done.6.refs_2_ = bf16[1,128,512]{2,1,0:T(8,128)(2,1)S(1)} collective-permute-done((bf16[1,128,512]{2,1,0:T(8,128)(2,1)S(1)}, bf16[1,128,512]{2,1,0:T(8,128)(2,1)S(1)}, u32[]{:S(2)}, u32[]{:S(2)}) %collective-permute-start.6) | collective-permute-done | bytes 131104 | tf_op jit(solution)/shard_map/ppermute | solution.py:33
  61.9 2.5 %collective-permute-start.15 = (bf16[1,128,512]{2,1,0:T(8,128)(2,1)S(1)}, bf16[1,128,512]{2,1,0:T(8,128)(2,1)S(1)}, u32[]{:S(2)}, u32[]{:S(2)}) collective-permute-start(bf16[1,128,512]{2,1,0:T(8,128)(2,1)S(1)} %maximum_select_fusion.2.refs_8_), channel_id=1, source_target_pairs={{0,16},{4,20},{8,24},{12,28},{16,0},{20,4},{24,8},{28,12},{1,17},{... | collective-permute-start | bytes 393224 | tf_op jit(solution)/shard_map/ppermute | solution.py:33
  64.4 7.6 %collective-permute-done.8.refs_4_ = bf16[1,128,512]{2,1,0:T(8,128)(2,1)S(1)} collective-permute-done((bf16[1,128,512]{2,1,0:T(8,128)(2,1)S(1)}, bf16[1,128,512]{2,1,0:T(8,128)(2,1)S(1)}, u32[]{:S(2)}, u32[]{:S(2)}) %collective-permute-start.8) | collective-permute-done | bytes 131104 | tf_op jit(solution)/shard_map/ppermute | solution.py:33
  72.0 1.5 collective-permute-start.12
  74.0 1.5 collective-permute-start.7
  75.6 2.9 %collective-permute-done.12.refs_9_ = bf16[1,128,512]{2,1,0:T(8,128)(2,1)S(1)} collective-permute-done((bf16[1,128,512]{2,1,0:T(8,128)(2,1)S(1)}, bf16[1,128,512]{2,1,0:T(8,128)(2,1)S(1)}, u32[]{:S(2)}, u32[]{:S(2)}) %collective-permute-start.12) | collective-permute-done | bytes 131104 | tf_op jit(solution)/shard_map/ppermute | solution.py:33
  78.4 1.5 collective-permute-start.9
  80.0 1.3 collective-permute-done.11.refs_7_
  81.3 1.5 collective-permute-start.14
  82.8 1.3 collective-permute-done.7.refs_3_
  84.7 1.5 collective-permute-start.16
  87.5 1.5 collective-permute-start.17
  89.8 1.7 %collective-permute-done.16.refs_13_ = bf16[1,128,512]{2,1,0:T(8,128)(2,1)} collective-permute-done((bf16[1,128,512]{2,1,0:T(8,128)(2,1)S(1)}, bf16[1,128,512]{2,1,0:T(8,128)(2,1)}, u32[]{:S(2)}, u32[]{:S(2)}) %collective-permute-start.16) | collective-permute-done | bytes 131104 | tf_op jit(solution)/shard_map/ppermute | solution.py:33
  91.5 1.4 collective-permute-done.17.refs_15_
  94.7 1.2 assemble.1.refs_4_.refs_2_
  95.9 1.3 copy-done
  97.3 1.1 constant_dynamic-slice_fusion.1
  98.3 1.6 collective-permute-start.4
  99.9 1.1 collective-permute-done.19.refs_3_
  101.0 1.6 %copy-done.1 = bf16[2,256,2048]{2,1,0:T(8,128)(2,1)S(1)} copy-done((bf16[2,256,2048]{2,1,0:T(8,128)(2,1)S(1)}, bf16[2,256,2048]{2,1,0:T(8,128)(2,1)}, u32[]{:S(2)}) %copy-start.1) | copy-done | bytes 2097176
  102.6 9.2 %early_sums.1.refs_7_ = f32[2,256,2048]{2,1,0:T(8,128)S(1)} custom-call(bf16[4,256,1024]{2,1,0:T(8,128)(2,1)S(1)} %constant_dynamic-slice_fusion.2.refs_0_.refs_1_, bf16[3,256,1024]{2,1,0:T(8,128)(2,1)} %collective-permute-done.5.refs_1_, bf16[4,256,1024]{2,1,0:T(8,128)(2,1)} %collective-permute-done.18.refs_2_.refs_0_.refs_3_, ...), custom_call_target="tpu_custom_call" | custom-call | flops 6442450944 | bytes 13631488 | tf_op jit(solution)/shard_map/early_sums/pallas_call | solution.py:123
  113.5 1.2 collective-permute-done.20.refs_1_.refs_4_
  114.7 2.3 %own_pairs.3.refs_6_ = bf16[2,256,256]{2,1,0:T(8,128)(2,1)S(1)} custom-call(bf16[4,256,1024]{2,1,0:T(8,128)(2,1)} %collective-permute-done.18.refs_2_.refs_0_.refs_3_, bf16[1,256,1024]{2,1,0:T(8,128)(2,1)S(1)} %collective-permute-done.20.refs_1_.refs_4_, bf16[2,256,2048]{2,1,0:T(8,128)(2,1)S(1)} %copy-done.1), custom_call_target="tpu_custom_call" | custom-call | flops 536870912 | bytes 4718592 | tf_op jit(solution)/shard_map/own_pairs/pallas_call | solution.py:147
  117.0 3.3 %last_sums.3 = (bf16[1,2,32,2048]{3,2,1,0:T(8,128)(2,1)S(1)}, f32[1,2,32,2048]{3,2,1,0:T(8,128)S(1)}, bf16[1,2,32,2048]{3,2,1,0:T(8,128)(2,1)}, f32[2,32,2048]{2,1,0:T(8,128)S(1)}) custom-call(s32[1]{0:T(128)} %bitcast.refs_0_, bf16[4,256,1024]{2,1,0:T(8,128)(2,1)S(1)} %constant_dynamic-slice_fusion.2.refs_0_.refs_1_, ...), custom_call_target="tpu_custom_call" | custom-call | flops 536870912 | bytes 8912896 | tf_op jit(solution)/shard_map/last_sums/pallas_call | solution.py:218
  122.6 1.5 collective-permute-start.30
  124.1 1.5 collective-permute-start.28
  125.6 2.2 %copy-done.3 = f32[2,256,2048]{2,1,0:T(8,128)S(1)} copy-done((f32[2,256,2048]{2,1,0:T(8,128)S(1)}, f32[2,256,2048]{2,1,0:T(8,128)}, u32[]{:S(2)}) %copy-start.3) | copy-done | bytes 4194328
  128.8 2.5 %last_sums.2 = (bf16[1,2,32,2048]{3,2,1,0:T(8,128)(2,1)S(1)}, f32[1,2,32,2048]{3,2,1,0:T(8,128)S(1)}, bf16[1,2,32,2048]{3,2,1,0:T(8,128)(2,1)S(1)}, f32[2,32,2048]{2,1,0:T(8,128)S(1)}) custom-call(s32[1]{0:T(128)} %bitcast.refs_0_, bf16[4,256,1024]{2,1,0:T(8,128)(2,1)S(1)} %constant_dynamic-slice_fusion.2.refs_0_.refs_1_, ...), custom_call_target="tpu_custom_call" | custom-call | flops 536870912 | bytes 8912896 | tf_op jit(solution)/shard_map/last_sums/pallas_call | solution.py:218
  132.4 1.0 convert_add_fusion
  133.5 1.6 collective-permute-start.31
  135.1 1.6 %collective-permute-start.29 = (bf16[1,32,2048]{2,1,0:T(8,128)(2,1)S(1)}, bf16[1,32,2048]{2,1,0:T(8,128)(2,1)S(1)}, u32[]{:S(2)}, u32[]{:S(2)}) collective-permute-start(bf16[1,32,2048]{2,1,0:T(8,128)(2,1)S(1)} %fusion.1), channel_id=1, source_target_pairs={{0,1},{1,0},{2,3},{3,2},{4,5},{5,4},{6,7},{7,6},{8,9},{9,8},{10,11... | collective-permute-start | bytes 393224 | tf_op jit(solution)/shard_map/ppermute | solution.py:33
  136.7 3.9 %collective-permute-done.23 = bf16[2,32,2048]{2,1,0:T(8,128)(2,1)S(1)} collective-permute-done((bf16[2,32,2048]{2,1,0:T(8,128)(2,1)S(1)}, bf16[2,32,2048]{2,1,0:T(8,128)(2,1)S(1)}, u32[]{:S(2)}, u32[]{:S(2)}) %collective-permute-start.23) | collective-permute-done | bytes 262176 | tf_op jit(solution)/shard_map/ppermute | solution.py:33
  141.3 1.5 collective-permute-start.22
  143.9 2.9 %collective-permute-start.33 = (bf16[1,64,512]{2,1,0:T(8,128)(2,1)S(1)}, bf16[1,64,512]{2,1,0:T(8,128)(2,1)S(1)}, u32[]{:S(2)}, u32[]{:S(2)}) collective-permute-start(bf16[1,64,512]{2,1,0:T(8,128)(2,1)S(1)} %get-tuple-element.36), channel_id=1, source_target_pairs={{0,16},{4,20},{8,24},{12,28},{16,0},{20,4},{24,8},{28,12},{1,17},{... | collective-permute-start | bytes 196616 | tf_op jit(solution)/shard_map/ppermute | solution.py:33
  146.8 1.5 collective-permute-start.34
  150.7 2.2 %collective-permute-start.27 = (bf16[1,64,512]{2,1,0:T(8,128)(2,1)S(1)}, bf16[1,64,512]{2,1,0:T(8,128)(2,1)S(1)}, u32[]{:S(2)}, u32[]{:S(2)}) collective-permute-start(bf16[1,64,512]{2,1,0:T(8,128)(2,1)S(1)} %get-tuple-element.40), channel_id=1, source_target_pairs={{0,24},{4,28},{8,0},{12,4},{16,8},{20,12},{24,16},{28,20},{1,25},{... | collective-permute-start | bytes 196616 | tf_op jit(solution)/shard_map/ppermute | solution.py:33
  153.0 1.7 %collective-permute-done.25 = bf16[1,64,512]{2,1,0:T(8,128)(2,1)S(1)} collective-permute-done((bf16[1,64,512]{2,1,0:T(8,128)(2,1)S(1)}, bf16[1,64,512]{2,1,0:T(8,128)(2,1)S(1)}, u32[]{:S(2)}, u32[]{:S(2)}) %collective-permute-start.25) | collective-permute-done | bytes 65568 | tf_op jit(solution)/shard_map/ppermute | solution.py:33
  154.7 1.4 collective-permute-done.26
  156.4 1.3 collective-permute-done.35
  (89 shorter events, 20.8 us)
Async XLA Ops:
  1.1 1.5 collective-permute-start.3
  5.6 91.7 %collective-permute-start.5 = (bf16[3,256,1024]{2,1,0:T(8,128)(2,1)}, bf16[3,256,1024]{2,1,0:T(8,128)(2,1)}, u32[]{:S(2)}, u32[]{:S(2)}) collective-permute-start(bf16[3,256,1024]{2,1,0:T(8,128)(2,1)} %constant_dynamic-slice_fusion), channel_id=1, source_target_pairs={{0,2},{2,0},{1,3},{3,1},{4,6},{6,4},{5,7},{7,5},{8,10},{10,8},{9,1... | collective-permute-start | bytes 4718600 | tf_op jit(solution)/shard_map/ppermute | solution.py:33
  8.4 37.7 %collective-permute-start = (bf16[2,128,256]{2,1,0:T(8,128)(2,1)S(1)}, bf16[2,128,256]{2,1,0:T(8,128)(2,1)S(1)}, u32[]{:S(2)}, u32[]{:S(2)}) collective-permute-start(bf16[2,128,256]{2,1,0:T(8,128)(2,1)S(1)} %constant_dynamic-slice_fusion.4), channel_id=1, source_target_pairs={{0,2},{2,0},{1,3},{3,1},{4,6},{6,4},{5,7},{7,5},{8,10},{10,8},{9,1... | collective-permute-start | bytes 393224 | tf_op jit(solution)/shard_map/ppermute | solution.py:33
  46.1 1.3 collective-permute-start.1
  47.5 7.8 %collective-permute-start.2 = (bf16[1,128,512]{2,1,0:T(8,128)(2,1)S(1)}, bf16[1,128,512]{2,1,0:T(8,128)(2,1)S(1)}, u32[]{:S(2)}, u32[]{:S(2)}) collective-permute-start(bf16[1,128,512]{2,1,0:T(8,128)(2,1)S(1)} %maximum_select_fusion.2.refs_8_), channel_id=1, source_target_pairs={{0,24},{4,28},{8,0},{12,4},{16,8},{20,12},{24,16},{28,20},{1,25},{... | collective-permute-start | bytes 393224 | tf_op jit(solution)/shard_map/ppermute | solution.py:33
  51.4 6.7 %collective-permute-start.10 = (bf16[1,128,512]{2,1,0:T(8,128)(2,1)S(1)}, bf16[1,128,512]{2,1,0:T(8,128)(2,1)S(1)}, u32[]{:S(2)}, u32[]{:S(2)}) collective-permute-start(bf16[1,128,512]{2,1,0:T(8,128)(2,1)S(1)} %get-tuple-element.22), channel_id=1, source_target_pairs={{0,24},{4,28},{8,0},{12,4},{16,8},{20,12},{24,16},{28,20},{1,25},{... | collective-permute-start | bytes 393224 | tf_op jit(solution)/shard_map/ppermute | solution.py:33
  51.9 10.0 %collective-permute-start.6 = (bf16[1,128,512]{2,1,0:T(8,128)(2,1)S(1)}, bf16[1,128,512]{2,1,0:T(8,128)(2,1)S(1)}, u32[]{:S(2)}, u32[]{:S(2)}) collective-permute-start(bf16[1,128,512]{2,1,0:T(8,128)(2,1)S(1)} %get-tuple-element.22), channel_id=1, source_target_pairs={{0,8},{4,12},{8,16},{12,20},{16,24},{20,28},{24,0},{28,4},{1,9},{5... | collective-permute-start | bytes 393224 | tf_op jit(solution)/shard_map/ppermute | solution.py:33
  53.4 18.6 %collective-permute-start.8 = (bf16[1,128,512]{2,1,0:T(8,128)(2,1)S(1)}, bf16[1,128,512]{2,1,0:T(8,128)(2,1)S(1)}, u32[]{:S(2)}, u32[]{:S(2)}) collective-permute-start(bf16[1,128,512]{2,1,0:T(8,128)(2,1)S(1)} %get-tuple-element.22), channel_id=1, source_target_pairs={{0,16},{4,20},{8,24},{12,28},{16,0},{20,4},{24,8},{28,12},{1,17},{... | collective-permute-start | bytes 393224 | tf_op jit(solution)/shard_map/ppermute | solution.py:33
  57.1 42.8 %collective-permute-start.18 = (bf16[4,256,1024]{2,1,0:T(8,128)(2,1)S(1)}, bf16[4,256,1024]{2,1,0:T(8,128)(2,1)}, u32[]{:S(2)}, u32[]{:S(2)}) collective-permute-start(bf16[4,256,1024]{2,1,0:T(8,128)(2,1)S(1)} %constant_dynamic-slice_fusion.2.refs_0_.refs_1_), channel_id=1, source_target_pairs={{0,4},{4,0},{8,12},{12,8},{16,20},{20,16},{24,28},{28,24},{1,5},{5... | collective-permute-start | bytes 6291464 | tf_op jit(solution)/shard_map/ppermute | solution.py:37
  58.1 15.4 %collective-permute-start.13 = (bf16[1,128,512]{2,1,0:T(8,128)(2,1)S(1)}, bf16[1,128,512]{2,1,0:T(8,128)(2,1)S(1)}, u32[]{:S(2)}, u32[]{:S(2)}) collective-permute-start(bf16[1,128,512]{2,1,0:T(8,128)(2,1)S(1)} %maximum_select_fusion.2.refs_8_), channel_id=1, source_target_pairs={{0,8},{4,12},{8,16},{12,20},{16,24},{20,28},{24,0},{28,4},{1,9},{5... | collective-permute-start | bytes 393224 | tf_op jit(solution)/shard_map/ppermute | solution.py:33
  61.9 12.2 %collective-permute-start.15 = (bf16[1,128,512]{2,1,0:T(8,128)(2,1)S(1)}, bf16[1,128,512]{2,1,0:T(8,128)(2,1)S(1)}, u32[]{:S(2)}, u32[]{:S(2)}) collective-permute-start(bf16[1,128,512]{2,1,0:T(8,128)(2,1)S(1)} %maximum_select_fusion.2.refs_8_), channel_id=1, source_target_pairs={{0,16},{4,20},{8,24},{12,28},{16,0},{20,4},{24,8},{28,12},{1,17},{... | collective-permute-start | bytes 393224 | tf_op jit(solution)/shard_map/ppermute | solution.py:33
  72.0 6.4 %collective-permute-start.12 = (bf16[1,128,512]{2,1,0:T(8,128)(2,1)S(1)}, bf16[1,128,512]{2,1,0:T(8,128)(2,1)S(1)}, u32[]{:S(2)}, u32[]{:S(2)}) collective-permute-start(bf16[1,128,512]{2,1,0:T(8,128)(2,1)S(1)} %maximum_select_fusion.2.refs_8_), channel_id=1, source_target_pairs={{0,1},{1,0},{2,3},{3,2},{4,5},{5,4},{6,7},{7,6},{8,9},{9,8},{10,11... | collective-permute-start | bytes 393224 | tf_op jit(solution)/shard_map/ppermute | solution.py:33
  73.5 7.7 %collective-permute-start.11 = (bf16[1,128,512]{2,1,0:T(8,128)(2,1)S(1)}, bf16[1,128,512]{2,1,0:T(8,128)(2,1)S(1)}, u32[]{:S(2)}, u32[]{:S(2)}) collective-permute-start(bf16[1,128,512]{2,1,0:T(8,128)(2,1)S(1)} %collective-permute-done.10.refs_6_), channel_id=1, source_target_pairs={{0,1},{1,0},{2,3},{3,2},{4,5},{5,4},{6,7},{7,6},{8,9},{9,8},{10,11... | collective-permute-start | bytes 393224 | tf_op jit(solution)/shard_map/ppermute | solution.py:33
  74.0 10.0 %collective-permute-start.7 = (bf16[1,128,512]{2,1,0:T(8,128)(2,1)S(1)}, bf16[1,128,512]{2,1,0:T(8,128)(2,1)S(1)}, u32[]{:S(2)}, u32[]{:S(2)}) collective-permute-start(bf16[1,128,512]{2,1,0:T(8,128)(2,1)S(1)} %collective-permute-done.6.refs_2_), channel_id=1, source_target_pairs={{0,1},{1,0},{2,3},{3,2},{4,5},{5,4},{6,7},{7,6},{8,9},{9,8},{10,11... | collective-permute-start | bytes 393224 | tf_op jit(solution)/shard_map/ppermute | solution.py:33
  78.4 8.4 %collective-permute-start.9 = (bf16[1,128,512]{2,1,0:T(8,128)(2,1)S(1)}, bf16[1,128,512]{2,1,0:T(8,128)(2,1)S(1)}, u32[]{:S(2)}, u32[]{:S(2)}) collective-permute-start(bf16[1,128,512]{2,1,0:T(8,128)(2,1)S(1)} %collective-permute-done.8.refs_4_), channel_id=1, source_target_pairs={{0,1},{1,0},{2,3},{3,2},{4,5},{5,4},{6,7},{7,6},{8,9},{9,8},{10,11... | collective-permute-start | bytes 393224 | tf_op jit(solution)/shard_map/ppermute | solution.py:33
  81.3 8.5 %collective-permute-start.14 = (bf16[1,128,512]{2,1,0:T(8,128)(2,1)S(1)}, bf16[1,128,512]{2,1,0:T(8,128)(2,1)}, u32[]{:S(2)}, u32[]{:S(2)}) collective-permute-start(bf16[1,128,512]{2,1,0:T(8,128)(2,1)S(1)} %collective-permute-done.13.refs_10_), channel_id=1, source_target_pairs={{0,1},{1,0},{2,3},{3,2},{4,5},{5,4},{6,7},{7,6},{8,9},{9,8},{10,11... | collective-permute-start | bytes 393224 | tf_op jit(solution)/shard_map/ppermute | solution.py:33
  84.7 6.8 %collective-permute-start.16 = (bf16[1,128,512]{2,1,0:T(8,128)(2,1)S(1)}, bf16[1,128,512]{2,1,0:T(8,128)(2,1)}, u32[]{:S(2)}, u32[]{:S(2)}) collective-permute-start(bf16[1,128,512]{2,1,0:T(8,128)(2,1)S(1)} %collective-permute-done.15.refs_12_), channel_id=1, source_target_pairs={{0,1},{1,0},{2,3},{3,2},{4,5},{5,4},{6,7},{7,6},{8,9},{9,8},{10,11... | collective-permute-start | bytes 393224 | tf_op jit(solution)/shard_map/ppermute | solution.py:33
  87.5 5.4 %collective-permute-start.17 = (bf16[1,128,512]{2,1,0:T(8,128)(2,1)S(1)}, bf16[1,128,512]{2,1,0:T(8,128)(2,1)}, u32[]{:S(2)}, u32[]{:S(2)}) collective-permute-start(bf16[1,128,512]{2,1,0:T(8,128)(2,1)S(1)} %collective-permute-done.2.refs_14_), channel_id=1, source_target_pairs={{0,1},{1,0},{2,3},{3,2},{4,5},{5,4},{6,7},{7,6},{8,9},{9,8},{10,11... | collective-permute-start | bytes 393224 | tf_op jit(solution)/shard_map/ppermute | solution.py:33
  92.9 0.9 copy-start.11
  93.8 0.9 copy-start.13
  95.9 1.3 copy-start
  97.3 3.8 %collective-permute-start.19 = (bf16[3,256,1024]{2,1,0:T(8,128)(2,1)}, bf16[3,256,1024]{2,1,0:T(8,128)(2,1)}, u32[]{:S(2)}, u32[]{:S(2)}) collective-permute-start(bf16[3,256,1024]{2,1,0:T(8,128)(2,1)} %collective-permute-done.5.refs_1_), channel_id=1, source_target_pairs={{0,4},{4,0},{8,12},{12,8},{16,20},{20,16},{24,28},{28,24},{1,5},{5... | collective-permute-start | bytes 4718600 | tf_op jit(solution)/shard_map/ppermute | solution.py:37
  98.3 14.4 %collective-permute-start.4 = (bf16[1,256,1024]{2,1,0:T(8,128)(2,1)S(1)}, bf16[1,256,1024]{2,1,0:T(8,128)(2,1)S(1)}, u32[]{:S(2)}, u32[]{:S(2)}) collective-permute-start(bf16[1,256,1024]{2,1,0:T(8,128)(2,1)S(1)} %constant_dynamic-slice_fusion.1), channel_id=1, source_target_pairs={{0,2},{2,0},{1,3},{3,1},{4,6},{6,4},{5,7},{7,5},{8,10},{10,8},{9,1... | collective-permute-start | bytes 1572872 | tf_op jit(solution)/shard_map/ppermute | solution.py:33
  101.0 1.6 %copy-start.1 = (bf16[2,256,2048]{2,1,0:T(8,128)(2,1)S(1)}, bf16[2,256,2048]{2,1,0:T(8,128)(2,1)}, u32[]{:S(2)}) copy-start(bf16[2,256,2048]{2,1,0:T(8,128)(2,1)} %copy-done) | copy-start | bytes 6291460
  111.8 5.2 %copy-start.2 = (f32[2,256,2048]{2,1,0:T(8,128)}, f32[2,256,2048]{2,1,0:T(8,128)S(1)}, u32[]{:S(2)}) copy-start(f32[2,256,2048]{2,1,0:T(8,128)S(1)} %early_sums.1.refs_7_) | copy-start | bytes 12582916
  112.7 1.9 %collective-permute-start.20 = (bf16[1,256,1024]{2,1,0:T(8,128)(2,1)S(1)}, bf16[1,256,1024]{2,1,0:T(8,128)(2,1)S(1)}, u32[]{:S(2)}, u32[]{:S(2)}) collective-permute-start(bf16[1,256,1024]{2,1,0:T(8,128)(2,1)S(1)} %collective-permute-done.4.refs_1_.refs_2_), channel_id=1, source_target_pairs={{0,4},{4,0},{8,12},{12,8},{16,20},{20,16},{24,28},{28,24},{1,5},{5... | collective-permute-start | bytes 1572872 | tf_op jit(solution)/shard_map/ppermute | solution.py:37
  117.0 3.3 %copy-start.4 = (bf16[2,256,256]{2,1,0:T(8,128)(2,1)}, bf16[2,256,256]{2,1,0:T(8,128)(2,1)S(1)}, u32[]{:S(2)}) copy-start(bf16[2,256,256]{2,1,0:T(8,128)(2,1)S(1)} %own_pairs.3.refs_6_) | copy-start | bytes 786436
  120.3 0.8 copy-start.6
  121.1 0.8 copy-start.8
  122.6 9.8 %collective-permute-start.30 = (bf16[2,32,2048]{2,1,0:T(8,128)(2,1)}, bf16[2,32,2048]{2,1,0:T(8,128)(2,1)}, u32[]{:S(2)}, u32[]{:S(2)}) collective-permute-start(bf16[2,32,2048]{2,1,0:T(8,128)(2,1)} %bitcast.19), channel_id=1, source_target_pairs={{0,1},{1,0},{2,3},{3,2},{4,5},{5,4},{6,7},{7,6},{8,9},{9,8},{10,11... | collective-permute-start | bytes 786440 | tf_op jit(solution)/shard_map/ppermute | solution.py:33
  124.1 10.9 %collective-permute-start.28 = (bf16[1,2,32,2048]{3,2,1,0:T(8,128)(2,1)}, bf16[1,2,32,2048]{3,2,1,0:T(8,128)(2,1)S(1)}, u32[]{:S(2)}, u32[]{:S(2)}) collective-permute-start(bf16[1,2,32,2048]{3,2,1,0:T(8,128)(2,1)} %copy-done.14), channel_id=1, source_target_pairs={{0,2},{2,0},{1,3},{3,1},{4,6},{6,4},{5,7},{7,5},{8,10},{10,8},{9,1... | collective-permute-start | bytes 786440 | tf_op jit(solution)/shard_map/ppermute | solution.py:33
  125.6 2.2 %copy-start.3 = (f32[2,256,2048]{2,1,0:T(8,128)S(1)}, f32[2,256,2048]{2,1,0:T(8,128)}, u32[]{:S(2)}) copy-start(f32[2,256,2048]{2,1,0:T(8,128)} %copy-done.2) | copy-start | bytes 12582916
  127.8 0.9 copy-start.5
  128.8 3.7 %copy-start.9 = (f32[2,32,2048]{2,1,0:T(8,128)S(1)}, f32[2,32,2048]{2,1,0:T(8,128)}, u32[]{:S(2)}) copy-start(f32[2,32,2048]{2,1,0:T(8,128)} %copy-done.8) | copy-start | bytes 1572868
  128.8 6.2 %copy-start.7 = (f32[1,2,32,2048]{3,2,1,0:T(8,128)S(1)}, f32[1,2,32,2048]{3,2,1,0:T(8,128)}, u32[]{:S(2)}) copy-start(f32[1,2,32,2048]{3,2,1,0:T(8,128)} %copy-done.6) | copy-start | bytes 1572868
  131.3 9.3 %collective-permute-start.23 = (bf16[2,32,2048]{2,1,0:T(8,128)(2,1)S(1)}, bf16[2,32,2048]{2,1,0:T(8,128)(2,1)S(1)}, u32[]{:S(2)}, u32[]{:S(2)}) collective-permute-start(bf16[2,32,2048]{2,1,0:T(8,128)(2,1)S(1)} %bitcast.30), channel_id=1, source_target_pairs={{0,1},{1,0},{2,3},{3,2},{4,5},{5,4},{6,7},{7,6},{8,9},{9,8},{10,11... | collective-permute-start | bytes 786440 | tf_op jit(solution)/shard_map/ppermute | solution.py:33
  131.9 9.4 %collective-permute-start.21 = (bf16[1,2,32,2048]{3,2,1,0:T(8,128)(2,1)S(1)}, bf16[1,2,32,2048]{3,2,1,0:T(8,128)(2,1)S(1)}, u32[]{:S(2)}, u32[]{:S(2)}) collective-permute-start(bf16[1,2,32,2048]{3,2,1,0:T(8,128)(2,1)S(1)} %get-tuple-element.28), channel_id=1, source_target_pairs={{0,2},{2,0},{1,3},{3,1},{4,6},{6,4},{5,7},{7,5},{8,10},{10,8},{9,1... | collective-permute-start | bytes 786440 | tf_op jit(solution)/shard_map/ppermute | solution.py:33
  133.5 10.1 %collective-permute-start.31 = (bf16[1,32,2048]{2,1,0:T(8,128)(2,1)S(1)}, bf16[1,32,2048]{2,1,0:T(8,128)(2,1)S(1)}, u32[]{:S(2)}, u32[]{:S(2)}) collective-permute-start(bf16[1,32,2048]{2,1,0:T(8,128)(2,1)S(1)} %slice.26), channel_id=1, source_target_pairs={{0,2},{2,0},{1,3},{3,1},{4,6},{6,4},{5,7},{7,5},{8,10},{10,8},{9,1... | collective-permute-start | bytes 393224 | tf_op jit(solution)/shard_map/ppermute | solution.py:33
  135.1 8.5 %collective-permute-start.29 = (bf16[1,32,2048]{2,1,0:T(8,128)(2,1)S(1)}, bf16[1,32,2048]{2,1,0:T(8,128)(2,1)S(1)}, u32[]{:S(2)}, u32[]{:S(2)}) collective-permute-start(bf16[1,32,2048]{2,1,0:T(8,128)(2,1)S(1)} %fusion.1), channel_id=1, source_target_pairs={{0,1},{1,0},{2,3},{3,2},{4,5},{5,4},{6,7},{7,6},{8,9},{9,8},{10,11... | collective-permute-start | bytes 393224 | tf_op jit(solution)/shard_map/ppermute | solution.py:33
  140.7 7.6 %collective-permute-start.24 = (bf16[1,32,2048]{2,1,0:T(8,128)(2,1)S(1)}, bf16[1,32,2048]{2,1,0:T(8,128)(2,1)S(1)}, u32[]{:S(2)}, u32[]{:S(2)}) collective-permute-start(bf16[1,32,2048]{2,1,0:T(8,128)(2,1)S(1)} %slice.27), channel_id=1, source_target_pairs={{0,2},{2,0},{1,3},{3,1},{4,6},{6,4},{5,7},{7,5},{8,10},{10,8},{9,1... | collective-permute-start | bytes 393224 | tf_op jit(solution)/shard_map/ppermute | solution.py:33
  141.3 6.9 %collective-permute-start.22 = (bf16[1,32,2048]{2,1,0:T(8,128)(2,1)S(1)}, bf16[1,32,2048]{2,1,0:T(8,128)(2,1)S(1)}, u32[]{:S(2)}, u32[]{:S(2)}) collective-permute-start(bf16[1,32,2048]{2,1,0:T(8,128)(2,1)S(1)} %fusion), channel_id=1, source_target_pairs={{0,1},{1,0},{2,3},{3,2},{4,5},{5,4},{6,7},{7,6},{8,9},{9,8},{10,11... | collective-permute-start | bytes 393224 | tf_op jit(solution)/shard_map/ppermute | solution.py:33
  143.8 6.9 %collective-permute-start.32 = (bf16[1,64,512]{2,1,0:T(8,128)(2,1)S(1)}, bf16[1,64,512]{2,1,0:T(8,128)(2,1)S(1)}, u32[]{:S(2)}, u32[]{:S(2)}) collective-permute-start(bf16[1,64,512]{2,1,0:T(8,128)(2,1)S(1)} %get-tuple-element.35), channel_id=1, source_target_pairs={{0,8},{4,12},{8,16},{12,20},{16,24},{20,28},{24,0},{28,4},{1,9},{5... | collective-permute-start | bytes 196616 | tf_op jit(solution)/shard_map/ppermute | solution.py:33
  143.9 9.0 %collective-permute-start.33 = (bf16[1,64,512]{2,1,0:T(8,128)(2,1)S(1)}, bf16[1,64,512]{2,1,0:T(8,128)(2,1)S(1)}, u32[]{:S(2)}, u32[]{:S(2)}) collective-permute-start(bf16[1,64,512]{2,1,0:T(8,128)(2,1)S(1)} %get-tuple-element.36), channel_id=1, source_target_pairs={{0,16},{4,20},{8,24},{12,28},{16,0},{20,4},{24,8},{28,12},{1,17},{... | collective-permute-start | bytes 196616 | tf_op jit(solution)/shard_map/ppermute | solution.py:33
  146.8 6.2 %collective-permute-start.34 = (bf16[1,64,512]{2,1,0:T(8,128)(2,1)S(1)}, bf16[1,64,512]{2,1,0:T(8,128)(2,1)S(1)}, u32[]{:S(2)}, u32[]{:S(2)}) collective-permute-start(bf16[1,64,512]{2,1,0:T(8,128)(2,1)S(1)} %get-tuple-element.37), channel_id=1, source_target_pairs={{0,24},{4,28},{8,0},{12,4},{16,8},{20,12},{24,16},{28,20},{1,25},{... | collective-permute-start | bytes 196616 | tf_op jit(solution)/shard_map/ppermute | solution.py:33
  148.5 6.2 %collective-permute-start.25 = (bf16[1,64,512]{2,1,0:T(8,128)(2,1)S(1)}, bf16[1,64,512]{2,1,0:T(8,128)(2,1)S(1)}, u32[]{:S(2)}, u32[]{:S(2)}) collective-permute-start(bf16[1,64,512]{2,1,0:T(8,128)(2,1)S(1)} %get-tuple-element.38), channel_id=1, source_target_pairs={{0,8},{4,12},{8,16},{12,20},{16,24},{20,28},{24,0},{28,4},{1,9},{5... | collective-permute-start | bytes 196616 | tf_op jit(solution)/shard_map/ppermute | solution.py:33
  149.1 7.1 %collective-permute-start.26 = (bf16[1,64,512]{2,1,0:T(8,128)(2,1)S(1)}, bf16[1,64,512]{2,1,0:T(8,128)(2,1)S(1)}, u32[]{:S(2)}, u32[]{:S(2)}) collective-permute-start(bf16[1,64,512]{2,1,0:T(8,128)(2,1)S(1)} %get-tuple-element.39), channel_id=1, source_target_pairs={{0,16},{4,20},{8,24},{12,28},{16,0},{20,4},{24,8},{28,12},{1,17},{... | collective-permute-start | bytes 196616 | tf_op jit(solution)/shard_map/ppermute | solution.py:33
  150.7 5.4 %collective-permute-start.27 = (bf16[1,64,512]{2,1,0:T(8,128)(2,1)S(1)}, bf16[1,64,512]{2,1,0:T(8,128)(2,1)S(1)}, u32[]{:S(2)}, u32[]{:S(2)}) collective-permute-start(bf16[1,64,512]{2,1,0:T(8,128)(2,1)S(1)} %get-tuple-element.40), channel_id=1, source_target_pairs={{0,24},{4,28},{8,0},{12,4},{16,8},{20,12},{24,16},{28,20},{1,25},{... | collective-permute-start | bytes 196616 | tf_op jit(solution)/shard_map/ppermute | solution.py:33
  156.3 1.4 collective-permute-start.35
  (3 other events, 2.1 us)

commit v4 on v3

--- a/solution.py
+++ b/solution.py
@@ -7,9 +7,10 @@
 
 CORES = 2
 PIECES = 2
-VMEM_LIMIT = 8 * 2**20
+VMEM_LIMIT = 28 * 2**20
 F32, BF16 = jnp.float32, jnp.bfloat16
 VMEM = pl.BlockSpec(memory_space=pltpu.VMEM)
+ANY = pl.BlockSpec(memory_space=pl.ANY)
 SMEM = pl.BlockSpec(memory_space=pltpu.SMEM)
 
 
@@ -58,32 +59,38 @@
     shape = jax.ShapeDtypeStruct((groups, rows, total), BF16)
 
     def body(at, *refs):
-        out = refs[-1]
-        for ref, (_, first, row_slot, col_slot) in zip(refs, blocks):
-            many, share, block = ref.shape
+        out, sems = refs[-2:]
+        copies = []
+        for i, (_, first, row_slot, col_slot) in enumerate(blocks):
+            many, share, block = refs[i].shape
             row = pl.multiple_of(at[row_slot], share)
             col = pl.multiple_of(at[col_slot], block)
-            for g in range(many):
-                out[first + g, pl.ds(row, share), pl.ds(col, block)] = ref[g]
+            to = out.at[pl.ds(first, many), pl.ds(row, share), pl.ds(col, block)]
+            copies.append(pltpu.make_async_copy(refs[i], to, sems.at[i]))
+        for copy in copies:
+            copy.start()
+        for copy in copies:
+            copy.wait()
 
     return pl.pallas_call(
         body,
         out_shape=shape,
-        in_specs=[SMEM] + [VMEM] * len(blocks),
-        out_specs=VMEM,
-        cost_estimate=cost(0, shape, shape),
+        in_specs=[SMEM] + [ANY] * len(blocks),
+        out_specs=ANY,
+        scratch_shapes=[pltpu.SemaphoreType.DMA((len(blocks),))],
+        cost_estimate=cost(0, shape),
         compiler_params=params(),
         name="assemble",
     )(where, *[b[0] for b in blocks])
 
 
-def pairs_of(refs, firsts, count, vec, store):
+def pairs_of(refs, vec, store):
     groups, rows, _ = vec.shape
+    count, _, width = refs[0].shape
     for g in range(groups):
         acc = None
-        for r, (ref, first) in enumerate(zip(refs, firsts)):
-            width = ref.shape[2]
-            left = ref[first : first + count].reshape(count * rows, width)
+        for r, ref in enumerate(refs):
+            left = ref[...].reshape(count * rows, width)
             term = dot_nt(left, vec[g, :, r * width : (r + 1) * width])
             acc = term if acc is None else acc + term
         acc = acc.astype(BF16)
@@ -96,135 +103,228 @@
     nr = len(sides[0])
     width = total // nr
     flat = [p for side in sides for p in side]
+    n = len(flat)
     shape = jax.ShapeDtypeStruct((groups, rows, total), F32)
     tile = min(width, 512)
+    tiles = total // tile
 
     def body(*refs):
-        vec, out, held = refs[len(flat) :]
+        vec_in, out = refs[n : n + 2]
+        vec, held, done, sems, out_sems = refs[-5:]
+        ins = refs[n + 2 : 2 * n + 2]
+        first = pltpu.make_async_copy(vec_in, vec, sems.at[n])
+        first.start()
+        copies = [
+            pltpu.make_async_copy(refs[i].at[pl.ds(0, steps)], ins[i], sems.at[i]) for i in range(n)
+        ]
+        for copy in copies:
+            copy.start()
+        first.wait()
         for s in range(len(sides)):
 
             def store(g, k, pair, s=s):
                 held[s, g * rows : (g + 1) * rows, k * rows : (k + 1) * rows] = pair
 
-            pairs_of(refs[s * nr : (s + 1) * nr], [0] * nr, steps, vec, store)
-        for r in range(nr):
-            for at in range(0, width, tile):
-                acc = None
-                for s in range(len(sides)):
-                    right = refs[s * nr + r][0:steps, :, at : at + tile]
-                    term = jnp.dot(
-                        held[s], right.reshape(steps * rows, tile), preferred_element_type=F32
-                    )
-                    acc = term if acc is None else acc + term
-                col = r * width + at
-                out[:, :, col : col + tile] = acc.reshape(groups, rows, tile)
-
-    work = 4 * len(sides) * steps * groups * rows * rows * total
+            for copy in copies[s * nr : (s + 1) * nr]:
+                copy.wait()
+            pairs_of(ins[s * nr : (s + 1) * nr], vec, store)
+        sent = []
+        for i in range(tiles):
+            r, at = i * tile // width, i * tile % width
+            acc = None
+            for s in range(len(sides)):
+                right = ins[s * nr + r][:, :, at : at + tile].reshape(steps * rows, tile)
+                term = jnp.dot(held[s], right, preferred_element_type=F32)
+                acc = term if acc is None else acc + term
+            cols = pl.ds(i * tile, tile)
+            done[:, :, cols] = acc.reshape(groups, rows, tile)
+            sent.append(
+                pltpu.make_async_copy(done.at[:, :, cols], out.at[:, :, cols], out_sems.at[i])
+            )
+            sent[-1].start()
+        for copy in sent:
+            copy.wait()
+
     return pl.pallas_call(
         body,
         out_shape=shape,
-        in_specs=[VMEM] * (len(flat) + 1),
-        out_specs=VMEM,
-        scratch_shapes=[pltpu.VMEM((len(sides), groups * rows, steps * rows), BF16)],
-        cost_estimate=cost(work, *flat, vectors, shape),
+        in_specs=[ANY] * (n + 1),
+        out_specs=ANY,
+        scratch_shapes=[pltpu.VMEM((steps, rows, width), BF16)] * n
+        + [
+            pltpu.VMEM(vectors.shape, BF16),
+            pltpu.VMEM((len(sides), groups * rows, steps * rows), BF16),
+            pltpu.VMEM(shape.shape, F32),
+            pltpu.SemaphoreType.DMA((n + 1,)),
+            pltpu.SemaphoreType.DMA((tiles,)),
+        ],
+        cost_estimate=cost(0, vectors),
         compiler_params=params(),
         name="early_sums",
     )(*flat, vectors)
 
 
-def own_pairs(side, firsts, vectors):
+def step_pairs(side, firsts, vectors):
     groups, rows, total = vectors.shape
     shape = jax.ShapeDtypeStruct((groups, rows, rows), BF16)
+    n = len(side)
+    width = total // n
 
     def body(*refs):
-        vec, out = refs[-2:]
+        vec_in, out = refs[n : n + 2]
+        ins = refs[n + 2 : 2 * n + 2]
+        vec, sems = refs[-2:]
+        copies = [pltpu.make_async_copy(vec_in, vec, sems.at[n])] + [
+            pltpu.make_async_copy(refs[i].at[pl.ds(firsts[i], 1)], ins[i], sems.at[i])
+            for i in range(n)
+        ]
+        for copy in copies:
+            copy.start()
+        for copy in copies:
+            copy.wait()
 
         def store(g, _, pair):
             out[g] = pair
 
-        pairs_of(refs[:-2], firsts, 1, vec, store)
+        pairs_of(ins, vec, store)
 
     return pl.pallas_call(
         body,
         out_shape=shape,
-        in_specs=[VMEM] * (len(side) + 1),
+        in_specs=[ANY] * (n + 1),
         out_specs=VMEM,
-        cost_estimate=cost(2 * groups * rows * rows * total, *side, vectors),
+        scratch_shapes=[pltpu.VMEM((1, rows, width), BF16)] * n
+        + [pltpu.VMEM(vectors.shape, BF16), pltpu.SemaphoreType.DMA((n + 1,))],
+        cost_estimate=cost(0, vectors),
         compiler_params=params(),
-        name="own_pairs",
+        name="step_pairs",
     )(*side, vectors)
 
 
-def last_sums(piece, o, sides, firsts, pairs, early, no, nv):
-    groups, rows, _ = pairs[0].shape
+def last_sums(o, sides, firsts, pair_own, vectors, early, no, nv):
+    groups, rows, total = vectors.shape
     nr = len(sides[0])
-    width = sides[0][0].shape[2]
-    total = nr * width
+    width = total // nr
     flat = [p for side in sides for p in side]
+    n = len(flat)
     per = groups // nv
     own = rows // no
     small = own // (PIECES * 2)
     more = [] if early is None else [early]
     tile = min(width, 512)
+    tiles = total // tile
 
     def body(*refs):
         me = refs[0][0]
-        ins = refs[1 : 1 + len(flat)]
-        pair_refs = refs[1 + len(flat) : 1 + len(flat) + len(pairs)]
-        before = refs[1 + len(flat) + len(pairs)]
-        send_x, keep_x, send_y, keep_y, acc = refs[-5:]
-        places = [oo * own + piece * 2 * small for oo in range(no)]
-        left = [
-            jnp.concatenate(
-                [ref[g, at : at + 2 * small, :] for g in range(groups) for at in places], axis=0
+        refs = refs[1:]
+        pair_in, vec_in = refs[n : n + 2]
+        results = refs[n + 2 + len(more) : n + 2 + len(more) + 4 * PIECES]
+        outs = refs[n + 2 + len(more) + 4 * PIECES : n + 2 + len(more) + 8 * PIECES]
+        ins = refs[-n - 7 : -7]
+        vec, own_pair, their_pair, before, sems, early_sems, out_sems = refs[-7:]
+        copies = [
+            pltpu.make_async_copy(refs[i].at[pl.ds(firsts[i % nr], 1)], ins[i], sems.at[i])
+            for i in range(n)
+        ]
+        vec_copy = pltpu.make_async_copy(vec_in, vec, sems.at[n])
+        pair_copy = pltpu.make_async_copy(pair_in, own_pair, sems.at[n + 1])
+        vec_copy.start()
+        for copy in copies[nr:] + copies[:nr]:
+            copy.start()
+        pair_copy.start()
+        early_copies = []
+        for i in range(tiles if more else 0):
+            cols = pl.ds(i * tile, tile)
+            early_copies.append(
+                pltpu.make_async_copy(
+                    refs[n + 2].at[:, :, cols], before.at[:, :, cols], early_sems.at[i]
+                )
             )
-            for ref in pair_refs
+            early_copies[-1].start()
+        vec_copy.wait()
+        for copy in copies[nr:]:
+            copy.wait()
+
+        def store(g, _, pair):
+            their_pair[g] = pair
+
+        pairs_of(ins[nr:], vec, store)
+        for copy in copies[:nr]:
+            copy.wait()
+        pair_copy.wait()
+        left = [p[...].reshape(groups * rows, rows) for p in (own_pair, their_pair)]
+        for i in range(tiles):
+            r, at = i * tile // width, i * tile % width
+            got = None
+            for s in range(len(sides)):
+                right = ins[s * nr + r][0, :, at : at + tile]
+                term = jnp.dot(left[s], right, preferred_element_type=F32)
+                got = term if got is None else got + term
+            got = got.reshape(groups, rows, tile)
+            if more:
+                early_copies[i].wait()
+                got = got + before[:, :, i * tile : (i + 1) * tile]
+            got = got.reshape(groups, no, PIECES, 2, small, tile)
+            for g in range(groups):
+                v = g // per
+                to = (r - v) % nr * width + at
+                cols = slice(to, to + tile)
+                for p in range(PIECES):
+                    send_x, keep_x, send_y, keep_y = outs[4 * p : 4 * p + 4]
+                    for oo in range(no):
+                        if v == 0:
+                            keep_x[g, oo, :, cols] = got[g, oo, p, 0]
+                        else:
+                            send_x[g - per, oo, :, cols] = got[g, oo, p, 0].astype(BF16)
+            for s in range(no):
+                for oo in range(no):
+
+                    @pl.when(lax.rem(me + s, no) == oo)
+                    def _(s=s, oo=oo, got=got, r=r, at=at):
+                        for g in range(groups):
+                            to = (r - g // per) % nr * width + at
+                            cols = slice(to, to + tile)
+                            for p in range(PIECES):
+                                if s == 0:
+                                    outs[4 * p + 3][g, :, cols] = got[g, oo, p, 1]
+                                else:
+                                    outs[4 * p + 2][s - 1, g, :, cols] = got[g, oo, p, 1].astype(BF16)
+        sent = [
+            pltpu.make_async_copy(out, result, out_sems.at[i])
+            for i, (out, result) in enumerate(zip(outs, results))
         ]
-        for r in range(nr):
-            for at in range(0, width, tile):
-                got = None
-                for s in range(len(sides)):
-                    right = ins[s * nr + r][firsts[r], :, at : at + tile]
-                    term = jnp.dot(left[s], right, preferred_element_type=F32)
-                    got = term if got is None else got + term
-                got = got.reshape(groups, no, 2, small, tile)
-                for g in range(groups):
-                    v = g // per
-                    to = (r - v) % nr * width + at
-                    cols = slice(to, to + tile)
-                    for oo in range(no):
-                        half = [got[g, oo, 0], got[g, oo, 1]]
-                        if more:
-                            col = r * width + at
-                            for h in range(2):
-                                row = places[oo] + h * small
-                                half[h] += before[g, row : row + small, col : col + tile]
-                        if v == 0:
-                            keep_x[g, oo, :, cols] = half[0]
-                        else:
-                            send_x[g - per, oo, :, cols] = half[0].astype(BF16)
-                        acc[oo, g, :, cols] = half[1]
-        keep_y[...] = acc[me]
-        for s in range(1, no):
-            send_y[s - 1] = acc[lax.rem(me + s, no)].astype(BF16)
-
-    work = 2 * len(sides) * groups * rows * rows * total // PIECES
+        for copy in sent:
+            copy.start()
+        for copy in sent:
+            copy.wait()
+
     shapes = [
         jax.ShapeDtypeStruct((groups - per, no, small, total), BF16),
         jax.ShapeDtypeStruct((per, no, small, total), F32),
         jax.ShapeDtypeStruct((no - 1, groups, small, total), BF16),
         jax.ShapeDtypeStruct((groups, small, total), F32),
-    ]
-    return pl.pallas_call(
+    ] * PIECES
+    outs = pl.pallas_call(
         body,
         out_shape=shapes,
-        in_specs=[SMEM] + [VMEM] * (len(flat) + len(pairs) + len(more)),
-        out_specs=[VMEM] * len(shapes),
-        scratch_shapes=[pltpu.VMEM((no, groups, small, total), F32)],
-        cost_estimate=cost(work, *flat, *pairs, *shapes, *shapes),
+        in_specs=[SMEM] + [ANY] * (n + 2 + len(more)),
+        out_specs=[ANY] * len(shapes),
+        scratch_shapes=[pltpu.VMEM(x.shape, x.dtype) for x in shapes]
+        + [pltpu.VMEM((1, rows, width), BF16)] * n
+        + [
+            pltpu.VMEM(vectors.shape, BF16),
+            pltpu.VMEM((groups, rows, rows), BF16),
+            pltpu.VMEM((groups, rows, rows), BF16),
+            pltpu.VMEM(vectors.shape if more else (8, 128), F32),
+            pltpu.SemaphoreType.DMA((n + 2,)),
+            pltpu.SemaphoreType.DMA((tiles,)),
+            pltpu.SemaphoreType.DMA((len(shapes),)),
+        ],
+        cost_estimate=cost(0, *shapes),
         compiler_params=params(),
         name="last_sums",
-    )(o.reshape(1), *flat, *pairs, *more)
+    )(o.reshape(1), *flat, pair_own, vectors, *more)
+    return [outs[4 * p : 4 * p + 4] for p in range(PIECES)]
 
 
 def per_device(na, nv, no, factors, trials):
@@ -257,16 +357,18 @@
     own_whole = over_cores(trial_b)
     own_part = part(own_whole, o, own, 1)
 
-    held, own_part = lax.optimization_barrier((factors, own_part))
     sizes = [early_steps, 1] if early_steps else [1]
-    come, first = [], 0
+    sends, first = [], 0
     for size in sizes:
-        got = []
-        for r in range(1, nv):
-            sent = lax.dynamic_slice_in_dim(held, (v - r) % nv * take + first, size, 0)
-            got.append(shift(sent, "vir", nv, -r))
-        come.append(got)
+        sends.append(
+            [
+                lax.dynamic_slice_in_dim(factors, (v - r) % nv * take + first, size, 0)
+                for r in range(1, nv)
+            ]
+        )
         first += size
+    sends, others = lax.optimization_barrier((sends, others))
+    come = [[shift(x, "vir", nv, -r - 1) for r, x in enumerate(group)] for group in sends]
 
     their = over_cores(jnp.concatenate(others, axis=0)) if others else None
     blocks = []
@@ -300,11 +402,11 @@
     got, early = lax.optimization_barrier((come[-1], early))
     sides = [[kept] + got, [shown] + [sibling(g, na) for g in got]]
     firsts = [early_steps] + [0] * (nv - 1)
-    pairs = [own_pairs(side, firsts, vectors) for side in sides]
+    pair_own = step_pairs(sides[0], firsts, vectors)
 
     out = []
-    for p in range(PIECES):
-        send_x, keep_x, send_y, keep_y = last_sums(p, o, sides, firsts, pairs, early, no, nv)
+    for p in last_sums(o, sides, firsts, pair_own, vectors, early, no, nv):
+        send_x, keep_x, send_y, keep_y = p
         one = keep_x
         for r in range(1, nv):
             sent = send_x[(r - 1) * half_m : r * half_m]

time: 159 us -> 119 us (0.75)
  waiting for transfers between devices: 76 us -> 40.2 us
  local copies, waits for them, and re-layouts: 17.4 us -> 12.7 us
  starting transfers between devices: 41.7 us -> 43.3 us
    ppermute x30, waiting for transfers between devices: 70.1 us -> 35.1 us  [shift(): return lax.ppermute(array, axis, pairs)]
    unnamed x30 -> x20, local copies, waits for them, and re-layouts: 11.5 us -> 6.12 us
    pallas_call x6 -> x4, Pallas kernels: 19.2 us -> 18.5 us  [the longest x1 10.1 us: early_sums(): pl.pallas_call(body, out_shape=shape, in_specs=[ANY] * (n + 1), out_specs...]
  transfers between devices with their start and end apart: 36 -> 36, of which waited for: 23 -> 23; matrix products, arithmetic and copies ran while one was open for 3% -> 7% of each run, Pallas kernels for 9% -> 11%
where the time goes in v4:
time: 119 us
  starting transfers between devices  43.3 us (36%)
  waiting for transfers between devices  40.2 us (34%)
  Pallas kernels  18.5 us (16%)
  local copies, waits for them, and re-layouts  12.7 us (11%)
  other arithmetic  3.83 us (3%)
    ppermute x30, starting transfers between devices, shift(): return lax.ppermute(array, axis, pairs)  42.4 us
    ppermute x30, waiting for transfers between devices, shift(): return lax.ppermute(array, axis, pairs)  35.1 us
    pallas_call x1, Pallas kernels, early_sums(): pl.pallas_call(body, out_shape=shape, in_specs=[ANY] * (n + 1), out_specs...  10.1 us
    unnamed x20, local copies, waits for them, and re-layouts  6.12 us
    pallas_call x1, Pallas kernels, last_sums(): pl.pallas_call(body, out_shape=shapes, in_specs=[SMEM] + [ANY] * (n + 2 +...  5.47 us
    ppermute x6, waiting for transfers between devices, sibling(): return lax.ppermute(array, 'aux', [(i, i ^ 1) for i in range(size)])  5.09 us
    dynamic_slice x2, local copies, waits for them, and re-layouts, per_device(): lax.dynamic_slice_in_dim(factors, (v - r) % nv * take + first, size, 0)  4.56 us
  transfers between devices with their start and end apart: 36, of which 23 were waited for; matrix products, arithmetic and copies ran while one was open for 7% of the time, Pallas kernels for 11%

profile of v4, /device:TPU:0, one launch (start us, length us, event | category | flops | bytes accessed | tf_op | source)
XLA Modules:
  0.0 118.8 jit_solution(3663338897219755070)
XLA Ops:
  0.0 1.1 convert_element_type.93
  1.1 3.0 %collective-permute-start = (bf16[2,128,256]{2,1,0:T(8,128)(2,1)S(1)}, bf16[2,128,256]{2,1,0:T(8,128)(2,1)S(1)}, u32[]{:S(2)}, u32[]{:S(2)}) collective-permute-start(bf16[2,128,256]{2,1,0:T(8,128)(2,1)S(1)} %constant_dynamic-slice_fusion.2), channel_id=1, source_target_pairs={{0,2},{2,0},{1,3},{3,1},{4,6},{6,4},{5,7},{7,5},{8,10},{10,8},{9,1... | collective-permute-start | bytes 393224 | tf_op jit(solution)/shard_map/ppermute | solution.py:34
  4.1 2.7 %constant_dynamic-slice_fusion.4 = bf16[3,256,1024]{2,1,0:T(8,128)(2,1)} fusion(bf16[8,256,1024]{2,1,0:T(8,128)(2,1)} %param.2, s32[]{:T(128)S(6)} %select_n.212), kind=kLoop, calls=%fused_computation.69 | loop fusion | bytes 3145732 | tf_op jit(solution)/shard_map/dynamic_slice | solution.py:365
  6.8 1.9 %constant_dynamic-slice_fusion.3 = bf16[1,256,1024]{2,1,0:T(8,128)(2,1)} fusion(bf16[8,256,1024]{2,1,0:T(8,128)(2,1)} %param.2, s32[]{:T(128)S(6)} %select_n.213), kind=kLoop, calls=%fused_computation.68 | loop fusion | bytes 1048580 | tf_op jit(solution)/shard_map/dynamic_slice | solution.py:365
  10.7 3.7 %collective-permute-start.2 = (bf16[1,128,512]{2,1,0:T(8,128)(2,1)S(1)}, bf16[1,128,512]{2,1,0:T(8,128)(2,1)S(1)}, u32[]{:S(2)}, u32[]{:S(2)}) collective-permute-start(bf16[1,128,512]{2,1,0:T(8,128)(2,1)S(1)} %maximum_select_fusion.2.refs_8_), channel_id=1, source_target_pairs={{0,24},{4,28},{8,0},{12,4},{16,8},{20,12},{24,16},{28,20},{1,25},{... | collective-permute-start | bytes 393224 | tf_op jit(solution)/shard_map/ppermute | solution.py:34
  15.0 1.6 %collective-permute-start.6 = (bf16[1,128,512]{2,1,0:T(8,128)(2,1)S(1)}, bf16[1,128,512]{2,1,0:T(8,128)(2,1)S(1)}, u32[]{:S(2)}, u32[]{:S(2)}) collective-permute-start(bf16[1,128,512]{2,1,0:T(8,128)(2,1)S(1)} %get-tuple-element.45), channel_id=1, source_target_pairs={{0,8},{4,12},{8,16},{12,20},{16,24},{20,28},{24,0},{28,4},{1,9},{5... | collective-permute-start | bytes 393224 | tf_op jit(solution)/shard_map/ppermute | solution.py:34
  16.6 1.7 %collective-permute-done.2.refs_14_ = bf16[1,128,512]{2,1,0:T(8,128)(2,1)S(1)} collective-permute-done((bf16[1,128,512]{2,1,0:T(8,128)(2,1)S(1)}, bf16[1,128,512]{2,1,0:T(8,128)(2,1)S(1)}, u32[]{:S(2)}, u32[]{:S(2)}) %collective-permute-start.2) | collective-permute-done | bytes 131104 | tf_op jit(solution)/shard_map/ppermute | solution.py:34
  18.3 1.8 %constant_dynamic-slice_fusion.refs_0_.refs_1_ = bf16[4,256,1024]{2,1,0:T(8,128)(2,1)S(1)} fusion(bf16[8,256,1024]{2,1,0:T(8,128)(2,1)} %param.2, s32[]{:T(128)S(6)} %select_n.218), kind=kLoop, calls=%fused_computation.65 | loop fusion | bytes 4194308 | tf_op jit(solution)/shard_map/dynamic_slice | solution.py:394
  20.1 1.0 collective-permute-done.10.refs_6_
  21.8 3.1 %collective-permute-done.6.refs_2_ = bf16[1,128,512]{2,1,0:T(8,128)(2,1)S(1)} collective-permute-done((bf16[1,128,512]{2,1,0:T(8,128)(2,1)S(1)}, bf16[1,128,512]{2,1,0:T(8,128)(2,1)S(1)}, u32[]{:S(2)}, u32[]{:S(2)}) %collective-permute-start.6) | collective-permute-done | bytes 131104 | tf_op jit(solution)/shard_map/ppermute | solution.py:34
  24.8 2.5 %collective-permute-start.15 = (bf16[1,128,512]{2,1,0:T(8,128)(2,1)S(1)}, bf16[1,128,512]{2,1,0:T(8,128)(2,1)S(1)}, u32[]{:S(2)}, u32[]{:S(2)}) collective-permute-start(bf16[1,128,512]{2,1,0:T(8,128)(2,1)S(1)} %maximum_select_fusion.2.refs_8_), channel_id=1, source_target_pairs={{0,16},{4,20},{8,24},{12,28},{16,0},{20,4},{24,8},{28,12},{1,17},{... | collective-permute-start | bytes 393224 | tf_op jit(solution)/shard_map/ppermute | solution.py:34
  27.3 7.5 %collective-permute-done.8.refs_4_ = bf16[1,128,512]{2,1,0:T(8,128)(2,1)S(1)} collective-permute-done((bf16[1,128,512]{2,1,0:T(8,128)(2,1)S(1)}, bf16[1,128,512]{2,1,0:T(8,128)(2,1)S(1)}, u32[]{:S(2)}, u32[]{:S(2)}) %collective-permute-start.8) | collective-permute-done | bytes 131104 | tf_op jit(solution)/shard_map/ppermute | solution.py:34
  34.8 1.5 %collective-permute-start.12 = (bf16[1,128,512]{2,1,0:T(8,128)(2,1)S(1)}, bf16[1,128,512]{2,1,0:T(8,128)(2,1)S(1)}, u32[]{:S(2)}, u32[]{:S(2)}) collective-permute-start(bf16[1,128,512]{2,1,0:T(8,128)(2,1)S(1)} %maximum_select_fusion.2.refs_8_), channel_id=1, source_target_pairs={{0,1},{1,0},{2,3},{3,2},{4,5},{5,4},{6,7},{7,6},{8,9},{9,8},{10,11... | collective-permute-start | bytes 393224 | tf_op jit(solution)/shard_map/ppermute | solution.py:34
  37.0 1.5 %collective-permute-start.7 = (bf16[1,128,512]{2,1,0:T(8,128)(2,1)S(1)}, bf16[1,128,512]{2,1,0:T(8,128)(2,1)S(1)}, u32[]{:S(2)}, u32[]{:S(2)}) collective-permute-start(bf16[1,128,512]{2,1,0:T(8,128)(2,1)S(1)} %collective-permute-done.6.refs_2_), channel_id=1, source_target_pairs={{0,1},{1,0},{2,3},{3,2},{4,5},{5,4},{6,7},{7,6},{8,9},{9,8},{10,11... | collective-permute-start | bytes 393224 | tf_op jit(solution)/shard_map/ppermute | solution.py:34
  38.5 2.8 %collective-permute-done.12.refs_9_ = bf16[1,128,512]{2,1,0:T(8,128)(2,1)S(1)} collective-permute-done((bf16[1,128,512]{2,1,0:T(8,128)(2,1)S(1)}, bf16[1,128,512]{2,1,0:T(8,128)(2,1)S(1)}, u32[]{:S(2)}, u32[]{:S(2)}) %collective-permute-start.12) | collective-permute-done | bytes 131104 | tf_op jit(solution)/shard_map/ppermute | solution.py:34
  41.3 1.5 %collective-permute-start.9 = (bf16[1,128,512]{2,1,0:T(8,128)(2,1)S(1)}, bf16[1,128,512]{2,1,0:T(8,128)(2,1)S(1)}, u32[]{:S(2)}, u32[]{:S(2)}) collective-permute-start(bf16[1,128,512]{2,1,0:T(8,128)(2,1)S(1)} %collective-permute-done.8.refs_4_), channel_id=1, source_target_pairs={{0,1},{1,0},{2,3},{3,2},{4,5},{5,4},{6,7},{7,6},{8,9},{9,8},{10,11... | collective-permute-start | bytes 393224 | tf_op jit(solution)/shard_map/ppermute | solution.py:34
  42.8 1.3 %collective-permute-done.11.refs_7_ = bf16[1,128,512]{2,1,0:T(8,128)(2,1)S(1)} collective-permute-done((bf16[1,128,512]{2,1,0:T(8,128)(2,1)S(1)}, bf16[1,128,512]{2,1,0:T(8,128)(2,1)S(1)}, u32[]{:S(2)}, u32[]{:S(2)}) %collective-permute-start.11) | collective-permute-done | bytes 131104 | tf_op jit(solution)/shard_map/ppermute | solution.py:34
  44.1 1.5 %collective-permute-start.14 = (bf16[1,128,512]{2,1,0:T(8,128)(2,1)S(1)}, bf16[1,128,512]{2,1,0:T(8,128)(2,1)}, u32[]{:S(2)}, u32[]{:S(2)}) collective-permute-start(bf16[1,128,512]{2,1,0:T(8,128)(2,1)S(1)} %collective-permute-done.13.refs_10_), channel_id=1, source_target_pairs={{0,1},{1,0},{2,3},{3,2},{4,5},{5,4},{6,7},{7,6},{8,9},{9,8},{10,11... | collective-permute-start | bytes 393224 | tf_op jit(solution)/shard_map/ppermute | solution.py:34
  45.6 1.3 %collective-permute-done.7.refs_3_ = bf16[1,128,512]{2,1,0:T(8,128)(2,1)S(1)} collective-permute-done((bf16[1,128,512]{2,1,0:T(8,128)(2,1)S(1)}, bf16[1,128,512]{2,1,0:T(8,128)(2,1)S(1)}, u32[]{:S(2)}, u32[]{:S(2)}) %collective-permute-start.7) | collective-permute-done | bytes 131104 | tf_op jit(solution)/shard_map/ppermute | solution.py:34
  47.5 1.5 %collective-permute-start.16 = (bf16[1,128,512]{2,1,0:T(8,128)(2,1)S(1)}, bf16[1,128,512]{2,1,0:T(8,128)(2,1)}, u32[]{:S(2)}, u32[]{:S(2)}) collective-permute-start(bf16[1,128,512]{2,1,0:T(8,128)(2,1)S(1)} %collective-permute-done.15.refs_12_), channel_id=1, source_target_pairs={{0,1},{1,0},{2,3},{3,2},{4,5},{5,4},{6,7},{7,6},{8,9},{9,8},{10,11... | collective-permute-start | bytes 393224 | tf_op jit(solution)/shard_map/ppermute | solution.py:34
  50.3 1.5 %collective-permute-start.17 = (bf16[1,128,512]{2,1,0:T(8,128)(2,1)S(1)}, bf16[1,128,512]{2,1,0:T(8,128)(2,1)}, u32[]{:S(2)}, u32[]{:S(2)}) collective-permute-start(bf16[1,128,512]{2,1,0:T(8,128)(2,1)S(1)} %collective-permute-done.2.refs_14_), channel_id=1, source_target_pairs={{0,1},{1,0},{2,3},{3,2},{4,5},{5,4},{6,7},{7,6},{8,9},{9,8},{10,11... | collective-permute-start | bytes 393224 | tf_op jit(solution)/shard_map/ppermute | solution.py:34
  52.6 2.0 %collective-permute-done.16.refs_13_ = bf16[1,128,512]{2,1,0:T(8,128)(2,1)} collective-permute-done((bf16[1,128,512]{2,1,0:T(8,128)(2,1)S(1)}, bf16[1,128,512]{2,1,0:T(8,128)(2,1)}, u32[]{:S(2)}, u32[]{:S(2)}) %collective-permute-start.16) | collective-permute-done | bytes 131104 | tf_op jit(solution)/shard_map/ppermute | solution.py:34
  54.6 1.4 %collective-permute-done.17.refs_15_ = bf16[1,128,512]{2,1,0:T(8,128)(2,1)} collective-permute-done((bf16[1,128,512]{2,1,0:T(8,128)(2,1)S(1)}, bf16[1,128,512]{2,1,0:T(8,128)(2,1)}, u32[]{:S(2)}, u32[]{:S(2)}) %collective-permute-start.17) | collective-permute-done | bytes 131104 | tf_op jit(solution)/shard_map/ppermute | solution.py:34
  56.0 0.9 copy-done.4
  57.8 1.9 %assemble.1.refs_4_.refs_2_.refs_6_ = bf16[2,256,2048]{2,1,0:T(8,128)(2,1)S(1)} custom-call(s32[6]{0:T(128)S(1)} %stack.27.at, bf16[1,128,512]{2,1,0:T(8,128)(2,1)S(1)} %get-tuple-element.47.refs_0_, bf16[1,128,512]{2,1,0:T(8,128)(2,1)S(1)} %get-tuple-element.46.refs_1_, bf16[1,128,512]{2,1,0:T(8,128)(2,1)S(1)} %collective-permute-done.6.refs_2_, ...), custom_call_target="tpu_custom_call" | custom-call | bytes 2097152 | tf_op jit(solution)/shard_map/assemble/pallas_call | solution.py:75
  59.8 1.4 %collective-permute-start.3 = (bf16[1,256,1024]{2,1,0:T(8,128)(2,1)S(1)}, bf16[1,256,1024]{2,1,0:T(8,128)(2,1)S(1)}, u32[]{:S(2)}, u32[]{:S(2)}) collective-permute-start(bf16[1,256,1024]{2,1,0:T(8,128)(2,1)S(1)} %copy-done.9), channel_id=1, source_target_pairs={{0,2},{2,0},{1,3},{3,1},{4,6},{6,4},{5,7},{7,5},{8,10},{10,8},{9,1... | collective-permute-start | bytes 1572872 | tf_op jit(solution)/shard_map/ppermute | solution.py:34
  61.2 2.2 %collective-permute-done.19.refs_3_ = bf16[3,256,1024]{2,1,0:T(8,128)(2,1)S(1)} collective-permute-done((bf16[3,256,1024]{2,1,0:T(8,128)(2,1)}, bf16[3,256,1024]{2,1,0:T(8,128)(2,1)S(1)}, u32[]{:S(2)}, u32[]{:S(2)}) %collective-permute-start.19) | collective-permute-done | bytes 1572896 | tf_op jit(solution)/shard_map/ppermute | solution.py:38
  63.4 10.1 %early_sums.1.refs_7_ = f32[2,256,2048]{2,1,0:T(8,128)S(1)} custom-call(bf16[4,256,1024]{2,1,0:T(8,128)(2,1)S(1)} %constant_dynamic-slice_fusion.refs_0_.refs_1_, bf16[3,256,1024]{2,1,0:T(8,128)(2,1)} %collective-permute-done.4.refs_1_, bf16[4,256,1024]{2,1,0:T(8,128)(2,1)} %collective-permute-done.18.refs_2_.refs_3_, ...), custom_call_target="tpu_custom_call" | custom-call | bytes 2097152 | tf_op jit(solution)/shard_map/early_sums/pallas_call | solution.py:148
  74.2 1.0 step_pairs.1.refs_5_
  75.1 0.9 collective-permute-done.20.refs_4_
  76.1 5.5 %last_sums.1 = (bf16[1,2,32,2048]{3,2,1,0:T(8,128)(2,1)S(1)}, f32[1,2,32,2048]{3,2,1,0:T(8,128)S(1)}, bf16[1,2,32,2048]{3,2,1,0:T(8,128)(2,1)S(1)}, f32[2,32,204...) custom-call(s32[1]{0:T(128)} %bitcast.refs_0_, ...), custom_call_target="tpu_custom_call" | custom-call | bytes 3145728 | tf_op jit(solution)/shard_map/last_sums/pallas_call | solution.py:307
  84.6 1.5 %collective-permute-start.30 = (bf16[2,32,2048]{2,1,0:T(8,128)(2,1)}, bf16[2,32,2048]{2,1,0:T(8,128)(2,1)S(1)}, u32[]{:S(2)}, u32[]{:S(2)}) collective-permute-start(bf16[2,32,2048]{2,1,0:T(8,128)(2,1)} %bitcast.19), channel_id=1, source_target_pairs={{0,1},{1,0},{2,3},{3,2},{4,5},{5,4},{6,7},{7,6},{8,9},{9,8},{10,11... | collective-permute-start | bytes 786440 | tf_op jit(solution)/shard_map/ppermute | solution.py:34
  86.1 1.3 %collective-permute-start.28 = (bf16[1,2,32,2048]{3,2,1,0:T(8,128)(2,1)}, bf16[1,2,32,2048]{3,2,1,0:T(8,128)(2,1)S(1)}, u32[]{:S(2)}, u32[]{:S(2)}) collective-permute-start(bf16[1,2,32,2048]{3,2,1,0:T(8,128)(2,1)} %copy-done.8), channel_id=1, source_target_pairs={{0,2},{2,0},{1,3},{3,1},{4,6},{6,4},{5,7},{7,5},{8,10},{10,8},{9,1... | collective-permute-start | bytes 786440 | tf_op jit(solution)/shard_map/ppermute | solution.py:34
  88.6 5.3 %collective-permute-done.30 = bf16[2,32,2048]{2,1,0:T(8,128)(2,1)S(1)} collective-permute-done((bf16[2,32,2048]{2,1,0:T(8,128)(2,1)}, bf16[2,32,2048]{2,1,0:T(8,128)(2,1)S(1)}, u32[]{:S(2)}, u32[]{:S(2)}) %collective-permute-start.30) | collective-permute-done | bytes 262176 | tf_op jit(solution)/shard_map/ppermute | solution.py:34
  93.9 1.1 convert_add_fusion
  95.0 1.4 %collective-permute-start.31 = (bf16[1,32,2048]{2,1,0:T(8,128)(2,1)S(1)}, bf16[1,32,2048]{2,1,0:T(8,128)(2,1)S(1)}, u32[]{:S(2)}, u32[]{:S(2)}) collective-permute-start(bf16[1,32,2048]{2,1,0:T(8,128)(2,1)S(1)} %slice.26), channel_id=1, source_target_pairs={{0,2},{2,0},{1,3},{3,1},{4,6},{6,4},{5,7},{7,5},{8,10},{10,8},{9,1... | collective-permute-start | bytes 393224 | tf_op jit(solution)/shard_map/ppermute | solution.py:34
  96.5 1.6 %collective-permute-start.29 = (bf16[1,32,2048]{2,1,0:T(8,128)(2,1)S(1)}, bf16[1,32,2048]{2,1,0:T(8,128)(2,1)S(1)}, u32[]{:S(2)}, u32[]{:S(2)}) collective-permute-start(bf16[1,32,2048]{2,1,0:T(8,128)(2,1)S(1)} %fusion.1), channel_id=1, source_target_pairs={{0,1},{1,0},{2,3},{3,2},{4,5},{5,4},{6,7},{7,6},{8,9},{9,8},{10,11... | collective-permute-start | bytes 393224 | tf_op jit(solution)/shard_map/ppermute | solution.py:34
  98.1 1.4 %collective-permute-done.23 = bf16[2,32,2048]{2,1,0:T(8,128)(2,1)S(1)} collective-permute-done((bf16[2,32,2048]{2,1,0:T(8,128)(2,1)}, bf16[2,32,2048]{2,1,0:T(8,128)(2,1)S(1)}, u32[]{:S(2)}, u32[]{:S(2)}) %collective-permute-start.23) | collective-permute-done | bytes 262176 | tf_op jit(solution)/shard_map/ppermute | solution.py:34
  99.6 1.4 %collective-permute-start.24 = (bf16[1,32,2048]{2,1,0:T(8,128)(2,1)S(1)}, bf16[1,32,2048]{2,1,0:T(8,128)(2,1)S(1)}, u32[]{:S(2)}, u32[]{:S(2)}) collective-permute-start(bf16[1,32,2048]{2,1,0:T(8,128)(2,1)S(1)} %slice.27), channel_id=1, source_target_pairs={{0,2},{2,0},{1,3},{3,1},{4,6},{6,4},{5,7},{7,5},{8,10},{10,8},{9,1... | collective-permute-start | bytes 393224 | tf_op jit(solution)/shard_map/ppermute | solution.py:34
  101.2 1.5 %collective-permute-start.22 = (bf16[1,32,2048]{2,1,0:T(8,128)(2,1)S(1)}, bf16[1,32,2048]{2,1,0:T(8,128)(2,1)S(1)}, u32[]{:S(2)}, u32[]{:S(2)}) collective-permute-start(bf16[1,32,2048]{2,1,0:T(8,128)(2,1)S(1)} %fusion), channel_id=1, source_target_pairs={{0,1},{1,0},{2,3},{3,2},{4,5},{5,4},{6,7},{7,6},{8,9},{9,8},{10,11... | collective-permute-start | bytes 393224 | tf_op jit(solution)/shard_map/ppermute | solution.py:34
  102.7 1.2 %collective-permute-done.31 = bf16[1,32,2048]{2,1,0:T(8,128)(2,1)S(1)} collective-permute-done((bf16[1,32,2048]{2,1,0:T(8,128)(2,1)S(1)}, bf16[1,32,2048]{2,1,0:T(8,128)(2,1)S(1)}, u32[]{:S(2)}, u32[]{:S(2)}) %collective-permute-start.31) | collective-permute-done | bytes 131104 | tf_op jit(solution)/shard_map/ppermute | solution.py:34
  104.2 2.7 %collective-permute-start.33 = (bf16[1,64,512]{2,1,0:T(8,128)(2,1)S(1)}, bf16[1,64,512]{2,1,0:T(8,128)(2,1)S(1)}, u32[]{:S(2)}, u32[]{:S(2)}) collective-permute-start(bf16[1,64,512]{2,1,0:T(8,128)(2,1)S(1)} %get-tuple-element.38), channel_id=1, source_target_pairs={{0,16},{4,20},{8,24},{12,28},{16,0},{20,4},{24,8},{28,12},{1,17},{... | collective-permute-start | bytes 196616 | tf_op jit(solution)/shard_map/ppermute | solution.py:34
  106.9 1.6 %collective-permute-start.34 = (bf16[1,64,512]{2,1,0:T(8,128)(2,1)S(1)}, bf16[1,64,512]{2,1,0:T(8,128)(2,1)S(1)}, u32[]{:S(2)}, u32[]{:S(2)}) collective-permute-start(bf16[1,64,512]{2,1,0:T(8,128)(2,1)S(1)} %get-tuple-element.39), channel_id=1, source_target_pairs={{0,24},{4,28},{8,0},{12,4},{16,8},{20,12},{24,16},{28,20},{1,25},{... | collective-permute-start | bytes 196616 | tf_op jit(solution)/shard_map/ppermute | solution.py:34
  109.3 1.2 collective-permute-start.26
  110.5 2.8 %collective-permute-start.27 = (bf16[1,64,512]{2,1,0:T(8,128)(2,1)S(1)}, bf16[1,64,512]{2,1,0:T(8,128)(2,1)S(1)}, u32[]{:S(2)}, u32[]{:S(2)}) collective-permute-start(bf16[1,64,512]{2,1,0:T(8,128)(2,1)S(1)} %get-tuple-element.42), channel_id=1, source_target_pairs={{0,24},{4,28},{8,0},{12,4},{16,8},{20,12},{24,16},{28,20},{1,25},{... | collective-permute-start | bytes 196616 | tf_op jit(solution)/shard_map/ppermute | solution.py:34
  113.4 1.6 %collective-permute-done.25 = bf16[1,64,512]{2,1,0:T(8,128)(2,1)S(1)} collective-permute-done((bf16[1,64,512]{2,1,0:T(8,128)(2,1)S(1)}, bf16[1,64,512]{2,1,0:T(8,128)(2,1)S(1)}, u32[]{:S(2)}, u32[]{:S(2)}) %collective-permute-start.25) | collective-permute-done | bytes 65568 | tf_op jit(solution)/shard_map/ppermute | solution.py:34
  115.0 1.5 %collective-permute-done.26 = bf16[1,64,512]{2,1,0:T(8,128)(2,1)S(1)} collective-permute-done((bf16[1,64,512]{2,1,0:T(8,128)(2,1)S(1)}, bf16[1,64,512]{2,1,0:T(8,128)(2,1)S(1)}, u32[]{:S(2)}, u32[]{:S(2)}) %collective-permute-start.26) | collective-permute-done | bytes 65568 | tf_op jit(solution)/shard_map/ppermute | solution.py:34
  116.8 1.3 %collective-permute-done.35 = f32[1,128,256]{2,1,0:T(8,128)S(1)} collective-permute-done((f32[1,128,256]{2,1,0:T(8,128)S(1)}, f32[1,128,256]{2,1,0:T(8,128)S(1)}, u32[]{:S(2)}, u32[]{:S(2)}) %collective-permute-start.35) | collective-permute-done | bytes 131104 | tf_op jit(solution)/shard_map/ppermute | solution.py:38
  (77 shorter events, 14.9 us)
Async XLA Ops:
  1.1 7.6 %collective-permute-start = (bf16[2,128,256]{2,1,0:T(8,128)(2,1)S(1)}, bf16[2,128,256]{2,1,0:T(8,128)(2,1)S(1)}, u32[]{:S(2)}, u32[]{:S(2)}) collective-permute-start(bf16[2,128,256]{2,1,0:T(8,128)(2,1)S(1)} %constant_dynamic-slice_fusion.2), channel_id=1, source_target_pairs={{0,2},{2,0},{1,3},{3,1},{4,6},{6,4},{5,7},{7,5},{8,10},{10,8},{9,1... | collective-permute-start | bytes 393224 | tf_op jit(solution)/shard_map/ppermute | solution.py:34
  8.7 51.1 %collective-permute-start.4 = (bf16[3,256,1024]{2,1,0:T(8,128)(2,1)}, bf16[3,256,1024]{2,1,0:T(8,128)(2,1)}, u32[]{:S(2)}, u32[]{:S(2)}) collective-permute-start(bf16[3,256,1024]{2,1,0:T(8,128)(2,1)} %constant_dynamic-slice_fusion.4), channel_id=1, source_target_pairs={{0,2},{2,0},{1,3},{3,1},{4,6},{6,4},{5,7},{7,5},{8,10},{10,8},{9,1... | collective-permute-start | bytes 4718600 | tf_op jit(solution)/shard_map/ppermute | solution.py:34
  9.4 1.3 %collective-permute-start.1 = (bf16[1,1,128,256]{3,2,1,0:T(8,128)(2,1)S(1)}, bf16[1,1,128,256]{3,2,1,0:T(8,128)(2,1)S(1)}, u32[]{:S(2)}, u32[]{:S(2)}) collective-permute-start(bf16[1,1,128,256]{3,2,1,0:T(8,128)(2,1)S(1)} %get-tuple-element.51), channel_id=1, source_target_pairs={{0,4},{4,0},{8,12},{12,8},{16,20},{20,16},{24,28},{28,24},{1,5},{5... | collective-permute-start | bytes 196616 | tf_op jit(solution)/shard_map/ppermute | solution.py:38
  9.5 4.9 %collective-permute-start.5 = (bf16[1,1,256,256]{3,2,1,0:T(8,128)(2,1)S(1)}, bf16[1,1,256,256]{3,2,1,0:T(8,128)(2,1)S(1)}, u32[]{:S(2)}, u32[]{:S(2)}) collective-permute-start(bf16[1,1,256,256]{3,2,1,0:T(8,128)(2,1)S(1)} %get-tuple-element.49), channel_id=1, source_target_pairs={{0,4},{4,0},{8,12},{12,8},{16,20},{20,16},{24,28},{28,24},{1,5},{5... | collective-permute-start | bytes 393224 | tf_op jit(solution)/shard_map/ppermute | solution.py:38
  10.7 7.6 %collective-permute-start.2 = (bf16[1,128,512]{2,1,0:T(8,128)(2,1)S(1)}, bf16[1,128,512]{2,1,0:T(8,128)(2,1)S(1)}, u32[]{:S(2)}, u32[]{:S(2)}) collective-permute-start(bf16[1,128,512]{2,1,0:T(8,128)(2,1)S(1)} %maximum_select_fusion.2.refs_8_), channel_id=1, source_target_pairs={{0,24},{4,28},{8,0},{12,4},{16,8},{20,12},{24,16},{28,20},{1,25},{... | collective-permute-start | bytes 393224 | tf_op jit(solution)/shard_map/ppermute | solution.py:34
  14.5 6.5 %collective-permute-start.10 = (bf16[1,128,512]{2,1,0:T(8,128)(2,1)S(1)}, bf16[1,128,512]{2,1,0:T(8,128)(2,1)S(1)}, u32[]{:S(2)}, u32[]{:S(2)}) collective-permute-start(bf16[1,128,512]{2,1,0:T(8,128)(2,1)S(1)} %get-tuple-element.45), channel_id=1, source_target_pairs={{0,24},{4,28},{8,0},{12,4},{16,8},{20,12},{24,16},{28,20},{1,25},{... | collective-permute-start | bytes 393224 | tf_op jit(solution)/shard_map/ppermute | solution.py:34
  15.0 9.8 %collective-permute-start.6 = (bf16[1,128,512]{2,1,0:T(8,128)(2,1)S(1)}, bf16[1,128,512]{2,1,0:T(8,128)(2,1)S(1)}, u32[]{:S(2)}, u32[]{:S(2)}) collective-permute-start(bf16[1,128,512]{2,1,0:T(8,128)(2,1)S(1)} %get-tuple-element.45), channel_id=1, source_target_pairs={{0,8},{4,12},{8,16},{12,20},{16,24},{20,28},{24,0},{28,4},{1,9},{5... | collective-permute-start | bytes 393224 | tf_op jit(solution)/shard_map/ppermute | solution.py:34
  16.6 18.2 %collective-permute-start.8 = (bf16[1,128,512]{2,1,0:T(8,128)(2,1)S(1)}, bf16[1,128,512]{2,1,0:T(8,128)(2,1)S(1)}, u32[]{:S(2)}, u32[]{:S(2)}) collective-permute-start(bf16[1,128,512]{2,1,0:T(8,128)(2,1)S(1)} %get-tuple-element.45), channel_id=1, source_target_pairs={{0,16},{4,20},{8,24},{12,28},{16,0},{20,4},{24,8},{28,12},{1,17},{... | collective-permute-start | bytes 393224 | tf_op jit(solution)/shard_map/ppermute | solution.py:34
  20.0 41.2 %collective-permute-start.18 = (bf16[4,256,1024]{2,1,0:T(8,128)(2,1)S(1)}, bf16[4,256,1024]{2,1,0:T(8,128)(2,1)}, u32[]{:S(2)}, u32[]{:S(2)}) collective-permute-start(bf16[4,256,1024]{2,1,0:T(8,128)(2,1)S(1)} %constant_dynamic-slice_fusion.refs_0_.refs_1_), channel_id=1, source_target_pairs={{0,4},{4,0},{8,12},{12,8},{16,20},{20,16},{24,28},{28,24},{1,5},{5... | collective-permute-start | bytes 6291464 | tf_op jit(solution)/shard_map/ppermute | solution.py:38
  21.1 15.3 %collective-permute-start.13 = (bf16[1,128,512]{2,1,0:T(8,128)(2,1)S(1)}, bf16[1,128,512]{2,1,0:T(8,128)(2,1)S(1)}, u32[]{:S(2)}, u32[]{:S(2)}) collective-permute-start(bf16[1,128,512]{2,1,0:T(8,128)(2,1)S(1)} %maximum_select_fusion.2.refs_8_), channel_id=1, source_target_pairs={{0,8},{4,12},{8,16},{12,20},{16,24},{20,28},{24,0},{28,4},{1,9},{5... | collective-permute-start | bytes 393224 | tf_op jit(solution)/shard_map/ppermute | solution.py:34
  24.8 12.1 %collective-permute-start.15 = (bf16[1,128,512]{2,1,0:T(8,128)(2,1)S(1)}, bf16[1,128,512]{2,1,0:T(8,128)(2,1)S(1)}, u32[]{:S(2)}, u32[]{:S(2)}) collective-permute-start(bf16[1,128,512]{2,1,0:T(8,128)(2,1)S(1)} %maximum_select_fusion.2.refs_8_), channel_id=1, source_target_pairs={{0,16},{4,20},{8,24},{12,28},{16,0},{20,4},{24,8},{28,12},{1,17},{... | collective-permute-start | bytes 393224 | tf_op jit(solution)/shard_map/ppermute | solution.py:34
  34.8 6.4 %collective-permute-start.12 = (bf16[1,128,512]{2,1,0:T(8,128)(2,1)S(1)}, bf16[1,128,512]{2,1,0:T(8,128)(2,1)S(1)}, u32[]{:S(2)}, u32[]{:S(2)}) collective-permute-start(bf16[1,128,512]{2,1,0:T(8,128)(2,1)S(1)} %maximum_select_fusion.2.refs_8_), channel_id=1, source_target_pairs={{0,1},{1,0},{2,3},{3,2},{4,5},{5,4},{6,7},{7,6},{8,9},{9,8},{10,11... | collective-permute-start | bytes 393224 | tf_op jit(solution)/shard_map/ppermute | solution.py:34
  36.4 7.7 %collective-permute-start.11 = (bf16[1,128,512]{2,1,0:T(8,128)(2,1)S(1)}, bf16[1,128,512]{2,1,0:T(8,128)(2,1)S(1)}, u32[]{:S(2)}, u32[]{:S(2)}) collective-permute-start(bf16[1,128,512]{2,1,0:T(8,128)(2,1)S(1)} %collective-permute-done.10.refs_6_), channel_id=1, source_target_pairs={{0,1},{1,0},{2,3},{3,2},{4,5},{5,4},{6,7},{7,6},{8,9},{9,8},{10,11... | collective-permute-start | bytes 393224 | tf_op jit(solution)/shard_map/ppermute | solution.py:34
  37.0 9.9 %collective-permute-start.7 = (bf16[1,128,512]{2,1,0:T(8,128)(2,1)S(1)}, bf16[1,128,512]{2,1,0:T(8,128)(2,1)S(1)}, u32[]{:S(2)}, u32[]{:S(2)}) collective-permute-start(bf16[1,128,512]{2,1,0:T(8,128)(2,1)S(1)} %collective-permute-done.6.refs_2_), channel_id=1, source_target_pairs={{0,1},{1,0},{2,3},{3,2},{4,5},{5,4},{6,7},{7,6},{8,9},{9,8},{10,11... | collective-permute-start | bytes 393224 | tf_op jit(solution)/shard_map/ppermute | solution.py:34
  41.3 8.4 %collective-permute-start.9 = (bf16[1,128,512]{2,1,0:T(8,128)(2,1)S(1)}, bf16[1,128,512]{2,1,0:T(8,128)(2,1)S(1)}, u32[]{:S(2)}, u32[]{:S(2)}) collective-permute-start(bf16[1,128,512]{2,1,0:T(8,128)(2,1)S(1)} %collective-permute-done.8.refs_4_), channel_id=1, source_target_pairs={{0,1},{1,0},{2,3},{3,2},{4,5},{5,4},{6,7},{7,6},{8,9},{9,8},{10,11... | collective-permute-start | bytes 393224 | tf_op jit(solution)/shard_map/ppermute | solution.py:34
  44.1 8.5 %collective-permute-start.14 = (bf16[1,128,512]{2,1,0:T(8,128)(2,1)S(1)}, bf16[1,128,512]{2,1,0:T(8,128)(2,1)}, u32[]{:S(2)}, u32[]{:S(2)}) collective-permute-start(bf16[1,128,512]{2,1,0:T(8,128)(2,1)S(1)} %collective-permute-done.13.refs_10_), channel_id=1, source_target_pairs={{0,1},{1,0},{2,3},{3,2},{4,5},{5,4},{6,7},{7,6},{8,9},{9,8},{10,11... | collective-permute-start | bytes 393224 | tf_op jit(solution)/shard_map/ppermute | solution.py:34
  46.9 0.7 copy-start.3
  47.5 7.1 %collective-permute-start.16 = (bf16[1,128,512]{2,1,0:T(8,128)(2,1)S(1)}, bf16[1,128,512]{2,1,0:T(8,128)(2,1)}, u32[]{:S(2)}, u32[]{:S(2)}) collective-permute-start(bf16[1,128,512]{2,1,0:T(8,128)(2,1)S(1)} %collective-permute-done.15.refs_12_), channel_id=1, source_target_pairs={{0,1},{1,0},{2,3},{3,2},{4,5},{5,4},{6,7},{7,6},{8,9},{9,8},{10,11... | collective-permute-start | bytes 393224 | tf_op jit(solution)/shard_map/ppermute | solution.py:34
  49.7 0.6 copy-start.5
  50.3 5.7 %collective-permute-start.17 = (bf16[1,128,512]{2,1,0:T(8,128)(2,1)S(1)}, bf16[1,128,512]{2,1,0:T(8,128)(2,1)}, u32[]{:S(2)}, u32[]{:S(2)}) collective-permute-start(bf16[1,128,512]{2,1,0:T(8,128)(2,1)S(1)} %collective-permute-done.2.refs_14_), channel_id=1, source_target_pairs={{0,1},{1,0},{2,3},{3,2},{4,5},{5,4},{6,7},{7,6},{8,9},{9,8},{10,11... | collective-permute-start | bytes 393224 | tf_op jit(solution)/shard_map/ppermute | solution.py:34
  56.0 0.9 copy-start.4
  56.9 0.9 copy-start.6
  57.8 2.0 %copy-start.9 = (bf16[1,256,1024]{2,1,0:T(8,128)(2,1)S(1)}, bf16[1,256,1024]{2,1,0:T(8,128)(2,1)}, u32[]{:S(2)}) copy-start(bf16[1,256,1024]{2,1,0:T(8,128)(2,1)} %constant_dynamic-slice_fusion.3) | copy-start | bytes 1572868
  59.7 3.7 %collective-permute-start.19 = (bf16[3,256,1024]{2,1,0:T(8,128)(2,1)}, bf16[3,256,1024]{2,1,0:T(8,128)(2,1)S(1)}, u32[]{:S(2)}, u32[]{:S(2)}) collective-permute-start(bf16[3,256,1024]{2,1,0:T(8,128)(2,1)} %collective-permute-done.4.refs_1_), channel_id=1, source_target_pairs={{0,4},{4,0},{8,12},{12,8},{16,20},{20,16},{24,28},{28,24},{1,5},{5... | collective-permute-start | bytes 4718600 | tf_op jit(solution)/shard_map/ppermute | solution.py:38
  59.8 14.3 %collective-permute-start.3 = (bf16[1,256,1024]{2,1,0:T(8,128)(2,1)S(1)}, bf16[1,256,1024]{2,1,0:T(8,128)(2,1)S(1)}, u32[]{:S(2)}, u32[]{:S(2)}) collective-permute-start(bf16[1,256,1024]{2,1,0:T(8,128)(2,1)S(1)} %copy-done.9), channel_id=1, source_target_pairs={{0,2},{2,0},{1,3},{3,1},{4,6},{6,4},{5,7},{7,5},{8,10},{10,8},{9,1... | collective-permute-start | bytes 1572872 | tf_op jit(solution)/shard_map/ppermute | solution.py:34
  74.1 1.9 %collective-permute-start.20 = (bf16[1,256,1024]{2,1,0:T(8,128)(2,1)S(1)}, bf16[1,256,1024]{2,1,0:T(8,128)(2,1)S(1)}, u32[]{:S(2)}, u32[]{:S(2)}) collective-permute-start(bf16[1,256,1024]{2,1,0:T(8,128)(2,1)S(1)} %collective-permute-done.3.refs_1_.refs_2_), channel_id=1, source_target_pairs={{0,4},{4,0},{8,12},{12,8},{16,20},{20,16},{24,28},{28,24},{1,5},{5... | collective-permute-start | bytes 1572872 | tf_op jit(solution)/shard_map/ppermute | solution.py:38
  81.5 0.8 copy-start
  82.3 0.8 copy-start.2
  83.2 0.7 copy-start.7
  83.9 0.7 copy-start.8
  84.6 11.9 %copy-start.1 = (f32[1,2,32,2048]{3,2,1,0:T(8,128)S(1)}, f32[1,2,32,2048]{3,2,1,0:T(8,128)}, u32[]{:S(2)}) copy-start(f32[1,2,32,2048]{3,2,1,0:T(8,128)} %copy-done) | copy-start | bytes 1572868
  84.6 9.4 %collective-permute-start.30 = (bf16[2,32,2048]{2,1,0:T(8,128)(2,1)}, bf16[2,32,2048]{2,1,0:T(8,128)(2,1)S(1)}, u32[]{:S(2)}, u32[]{:S(2)}) collective-permute-start(bf16[2,32,2048]{2,1,0:T(8,128)(2,1)} %bitcast.19), channel_id=1, source_target_pairs={{0,1},{1,0},{2,3},{3,2},{4,5},{5,4},{6,7},{7,6},{8,9},{9,8},{10,11... | collective-permute-start | bytes 786440 | tf_op jit(solution)/shard_map/ppermute | solution.py:34
  86.1 10.4 %collective-permute-start.28 = (bf16[1,2,32,2048]{3,2,1,0:T(8,128)(2,1)}, bf16[1,2,32,2048]{3,2,1,0:T(8,128)(2,1)S(1)}, u32[]{:S(2)}, u32[]{:S(2)}) collective-permute-start(bf16[1,2,32,2048]{3,2,1,0:T(8,128)(2,1)} %copy-done.8), channel_id=1, source_target_pairs={{0,2},{2,0},{1,3},{3,1},{4,6},{6,4},{5,7},{7,5},{8,10},{10,8},{9,1... | collective-permute-start | bytes 786440 | tf_op jit(solution)/shard_map/ppermute | solution.py:34
  87.4 12.1 %collective-permute-start.23 = (bf16[2,32,2048]{2,1,0:T(8,128)(2,1)}, bf16[2,32,2048]{2,1,0:T(8,128)(2,1)S(1)}, u32[]{:S(2)}, u32[]{:S(2)}) collective-permute-start(bf16[2,32,2048]{2,1,0:T(8,128)(2,1)} %bitcast.30), channel_id=1, source_target_pairs={{0,1},{1,0},{2,3},{3,2},{4,5},{5,4},{6,7},{7,6},{8,9},{9,8},{10,11... | collective-permute-start | bytes 786440 | tf_op jit(solution)/shard_map/ppermute | solution.py:34
  87.9 13.2 %collective-permute-start.21 = (bf16[1,2,32,2048]{3,2,1,0:T(8,128)(2,1)S(1)}, bf16[1,2,32,2048]{3,2,1,0:T(8,128)(2,1)S(1)}, u32[]{:S(2)}, u32[]{:S(2)}) collective-permute-start(bf16[1,2,32,2048]{3,2,1,0:T(8,128)(2,1)S(1)} %get-tuple-element.30), channel_id=1, source_target_pairs={{0,2},{2,0},{1,3},{3,1},{4,6},{6,4},{5,7},{7,5},{8,10},{10,8},{9,1... | collective-permute-start | bytes 786440 | tf_op jit(solution)/shard_map/ppermute | solution.py:34
  95.0 8.9 %collective-permute-start.31 = (bf16[1,32,2048]{2,1,0:T(8,128)(2,1)S(1)}, bf16[1,32,2048]{2,1,0:T(8,128)(2,1)S(1)}, u32[]{:S(2)}, u32[]{:S(2)}) collective-permute-start(bf16[1,32,2048]{2,1,0:T(8,128)(2,1)S(1)} %slice.26), channel_id=1, source_target_pairs={{0,2},{2,0},{1,3},{3,1},{4,6},{6,4},{5,7},{7,5},{8,10},{10,8},{9,1... | collective-permute-start | bytes 393224 | tf_op jit(solution)/shard_map/ppermute | solution.py:34
  96.5 7.4 %collective-permute-start.29 = (bf16[1,32,2048]{2,1,0:T(8,128)(2,1)S(1)}, bf16[1,32,2048]{2,1,0:T(8,128)(2,1)S(1)}, u32[]{:S(2)}, u32[]{:S(2)}) collective-permute-start(bf16[1,32,2048]{2,1,0:T(8,128)(2,1)S(1)} %fusion.1), channel_id=1, source_target_pairs={{0,1},{1,0},{2,3},{3,2},{4,5},{5,4},{6,7},{7,6},{8,9},{9,8},{10,11... | collective-permute-start | bytes 393224 | tf_op jit(solution)/shard_map/ppermute | solution.py:34
  99.6 8.9 %collective-permute-start.24 = (bf16[1,32,2048]{2,1,0:T(8,128)(2,1)S(1)}, bf16[1,32,2048]{2,1,0:T(8,128)(2,1)S(1)}, u32[]{:S(2)}, u32[]{:S(2)}) collective-permute-start(bf16[1,32,2048]{2,1,0:T(8,128)(2,1)S(1)} %slice.27), channel_id=1, source_target_pairs={{0,2},{2,0},{1,3},{3,1},{4,6},{6,4},{5,7},{7,5},{8,10},{10,8},{9,1... | collective-permute-start | bytes 393224 | tf_op jit(solution)/shard_map/ppermute | solution.py:34
  101.2 7.3 %collective-permute-start.22 = (bf16[1,32,2048]{2,1,0:T(8,128)(2,1)S(1)}, bf16[1,32,2048]{2,1,0:T(8,128)(2,1)S(1)}, u32[]{:S(2)}, u32[]{:S(2)}) collective-permute-start(bf16[1,32,2048]{2,1,0:T(8,128)(2,1)S(1)} %fusion), channel_id=1, source_target_pairs={{0,1},{1,0},{2,3},{3,2},{4,5},{5,4},{6,7},{7,6},{8,9},{9,8},{10,11... | collective-permute-start | bytes 393224 | tf_op jit(solution)/shard_map/ppermute | solution.py:34
  104.2 6.3 %collective-permute-start.32 = (bf16[1,64,512]{2,1,0:T(8,128)(2,1)S(1)}, bf16[1,64,512]{2,1,0:T(8,128)(2,1)S(1)}, u32[]{:S(2)}, u32[]{:S(2)}) collective-permute-start(bf16[1,64,512]{2,1,0:T(8,128)(2,1)S(1)} %get-tuple-element.37), channel_id=1, source_target_pairs={{0,8},{4,12},{8,16},{12,20},{16,24},{20,28},{24,0},{28,4},{1,9},{5... | collective-permute-start | bytes 196616 | tf_op jit(solution)/shard_map/ppermute | solution.py:34
  104.2 9.1 %collective-permute-start.33 = (bf16[1,64,512]{2,1,0:T(8,128)(2,1)S(1)}, bf16[1,64,512]{2,1,0:T(8,128)(2,1)S(1)}, u32[]{:S(2)}, u32[]{:S(2)}) collective-permute-start(bf16[1,64,512]{2,1,0:T(8,128)(2,1)S(1)} %get-tuple-element.38), channel_id=1, source_target_pairs={{0,16},{4,20},{8,24},{12,28},{16,0},{20,4},{24,8},{28,12},{1,17},{... | collective-permute-start | bytes 196616 | tf_op jit(solution)/shard_map/ppermute | solution.py:34
  106.9 6.3 %collective-permute-start.34 = (bf16[1,64,512]{2,1,0:T(8,128)(2,1)S(1)}, bf16[1,64,512]{2,1,0:T(8,128)(2,1)S(1)}, u32[]{:S(2)}, u32[]{:S(2)}) collective-permute-start(bf16[1,64,512]{2,1,0:T(8,128)(2,1)S(1)} %get-tuple-element.39), channel_id=1, source_target_pairs={{0,24},{4,28},{8,0},{12,4},{16,8},{20,12},{24,16},{28,20},{1,25},{... | collective-permute-start | bytes 196616 | tf_op jit(solution)/shard_map/ppermute | solution.py:34
  108.7 6.2 %collective-permute-start.25 = (bf16[1,64,512]{2,1,0:T(8,128)(2,1)S(1)}, bf16[1,64,512]{2,1,0:T(8,128)(2,1)S(1)}, u32[]{:S(2)}, u32[]{:S(2)}) collective-permute-start(bf16[1,64,512]{2,1,0:T(8,128)(2,1)S(1)} %get-tuple-element.40), channel_id=1, source_target_pairs={{0,8},{4,12},{8,16},{12,20},{16,24},{20,28},{24,0},{28,4},{1,9},{5... | collective-permute-start | bytes 196616 | tf_op jit(solution)/shard_map/ppermute | solution.py:34
  109.3 7.3 %collective-permute-start.26 = (bf16[1,64,512]{2,1,0:T(8,128)(2,1)S(1)}, bf16[1,64,512]{2,1,0:T(8,128)(2,1)S(1)}, u32[]{:S(2)}, u32[]{:S(2)}) collective-permute-start(bf16[1,64,512]{2,1,0:T(8,128)(2,1)S(1)} %get-tuple-element.41), channel_id=1, source_target_pairs={{0,16},{4,20},{8,24},{12,28},{16,0},{20,4},{24,8},{28,12},{1,17},{... | collective-permute-start | bytes 196616 | tf_op jit(solution)/shard_map/ppermute | solution.py:34
  110.5 6.1 %collective-permute-start.27 = (bf16[1,64,512]{2,1,0:T(8,128)(2,1)S(1)}, bf16[1,64,512]{2,1,0:T(8,128)(2,1)S(1)}, u32[]{:S(2)}, u32[]{:S(2)}) collective-permute-start(bf16[1,64,512]{2,1,0:T(8,128)(2,1)S(1)} %get-tuple-element.42), channel_id=1, source_target_pairs={{0,24},{4,28},{8,0},{12,4},{16,8},{20,12},{24,16},{28,20},{1,25},{... | collective-permute-start | bytes 196616 | tf_op jit(solution)/shard_map/ppermute | solution.py:34
  116.7 1.4 %collective-permute-start.35 = (f32[1,128,256]{2,1,0:T(8,128)S(1)}, f32[1,128,256]{2,1,0:T(8,128)S(1)}, u32[]{:S(2)}, u32[]{:S(2)}) collective-permute-start(f32[1,128,256]{2,1,0:T(8,128)S(1)} %get-tuple-element.44), channel_id=1, source_target_pairs={{0,4},{4,0},{8,12},{12,8},{16,20},{20,16},{24,28},{28,24},{1,5},{5... | collective-permute-start | bytes 393224 | tf_op jit(solution)/shard_map/ppermute | solution.py:38

commit v5 on v4

--- a/solution.py
+++ b/solution.py
@@ -11,6 +11,7 @@
 F32, BF16 = jnp.float32, jnp.bfloat16
 VMEM = pl.BlockSpec(memory_space=pltpu.VMEM)
 ANY = pl.BlockSpec(memory_space=pl.ANY)
+HBM = pl.BlockSpec(memory_space=pltpu.HBM)
 SMEM = pl.BlockSpec(memory_space=pltpu.SMEM)
 
 
@@ -102,8 +103,9 @@
     groups, rows, total = vectors.shape
     nr = len(sides[0])
     width = total // nr
-    flat = [p for side in sides for p in side]
-    n = len(flat)
+    slots = [pieces for side in sides for pieces in side]
+    flat = [p for pieces in slots for p in pieces]
+    n, ns = len(flat), len(slots)
     shape = jax.ShapeDtypeStruct((groups, rows, total), F32)
     tile = min(width, 512)
     tiles = total // tile
@@ -111,22 +113,28 @@
     def body(*refs):
         vec_in, out = refs[n : n + 2]
         vec, held, done, sems, out_sems = refs[-5:]
-        ins = refs[n + 2 : 2 * n + 2]
+        ins = refs[n + 2 : n + 2 + ns]
         first = pltpu.make_async_copy(vec_in, vec, sems.at[n])
         first.start()
-        copies = [
-            pltpu.make_async_copy(refs[i].at[pl.ds(0, steps)], ins[i], sems.at[i]) for i in range(n)
-        ]
-        for copy in copies:
-            copy.start()
+        copies, i = [], 0
+        for slot, pieces in zip(ins, slots):
+            group, at = [], 0
+            for piece in pieces:
+                size = min(piece.shape[0], steps)
+                to = slot.at[pl.ds(at, size)]
+                group.append(pltpu.make_async_copy(refs[i].at[pl.ds(0, size)], to, sems.at[i]))
+                group[-1].start()
+                i, at = i + 1, at + size
+            copies.append(group)
         first.wait()
         for s in range(len(sides)):
 
             def store(g, k, pair, s=s):
                 held[s, g * rows : (g + 1) * rows, k * rows : (k + 1) * rows] = pair
 
-            for copy in copies[s * nr : (s + 1) * nr]:
-                copy.wait()
+            for group in copies[s * nr : (s + 1) * nr]:
+                for copy in group:
+                    copy.wait()
             pairs_of(ins[s * nr : (s + 1) * nr], vec, store)
         sent = []
         for i in range(tiles):
@@ -150,7 +158,7 @@
         out_shape=shape,
         in_specs=[ANY] * (n + 1),
         out_specs=ANY,
-        scratch_shapes=[pltpu.VMEM((steps, rows, width), BF16)] * n
+        scratch_shapes=[pltpu.VMEM((steps, rows, width), BF16)] * ns
         + [
             pltpu.VMEM(vectors.shape, BF16),
             pltpu.VMEM((len(sides), groups * rows, steps * rows), BF16),
@@ -253,6 +261,7 @@
             copy.wait()
         pair_copy.wait()
         left = [p[...].reshape(groups * rows, rows) for p in (own_pair, their_pair)]
+        sent = []
         for i in range(tiles):
             r, at = i * tile // width, i * tile % width
             got = None
@@ -289,12 +298,23 @@
                                     outs[4 * p + 3][g, :, cols] = got[g, oo, p, 1]
                                 else:
                                     outs[4 * p + 2][s - 1, g, :, cols] = got[g, oo, p, 1].astype(BF16)
-        sent = [
-            pltpu.make_async_copy(out, result, out_sems.at[i])
-            for i, (out, result) in enumerate(zip(outs, results))
-        ]
-        for copy in sent:
-            copy.start()
+            for v in range(nv):
+                cols = pl.ds((r - v) % nr * width + at, tile)
+                for p in range(PIECES):
+                    at_x = (pl.ds(0, per) if v == 0 else pl.ds((v - 1) * per, per), slice(None), slice(None), cols)
+                    at_y = (pl.ds(v * per, per), slice(None), cols)
+                    for k, where in (
+                        (1 if v == 0 else 0, at_x),
+                        (2, (slice(None), *at_y)),
+                        (3, at_y),
+                    ):
+                        out, result = outs[4 * p + k], results[4 * p + k]
+                        sent.append(
+                            pltpu.make_async_copy(
+                                out.at[where], result.at[where], out_sems.at[len(sent)]
+                            )
+                        )
+                        sent[-1].start()
         for copy in sent:
             copy.wait()
 
@@ -308,7 +328,7 @@
         body,
         out_shape=shapes,
         in_specs=[SMEM] + [ANY] * (n + 2 + len(more)),
-        out_specs=[ANY] * len(shapes),
+        out_specs=[HBM] * len(shapes),
         scratch_shapes=[pltpu.VMEM(x.shape, x.dtype) for x in shapes]
         + [pltpu.VMEM((1, rows, width), BF16)] * n
         + [
@@ -318,7 +338,7 @@
             pltpu.VMEM(vectors.shape if more else (8, 128), F32),
             pltpu.SemaphoreType.DMA((n + 2,)),
             pltpu.SemaphoreType.DMA((tiles,)),
-            pltpu.SemaphoreType.DMA((len(shapes),)),
+            pltpu.SemaphoreType.DMA((tiles * nv * PIECES * 3,)),
         ],
         cost_estimate=cost(0, *shapes),
         compiler_params=params(),
@@ -339,67 +359,57 @@
     groups = nv * half_m
     early_steps = take - 1
 
-    trial_b = trials.astype(BF16)
-    mine = part(trial_b, o, own, 1)
+    mine = part(trials, o, own, 1).astype(BF16)
     others = [shift(mine, "vir", nv, -r) for r in range(1, nv)]
 
-    def over_cores(x):
-        x = x.reshape(x.shape[0] // nm, CORES, half_m, *x.shape[1:])
-        given = sibling(lax.dynamic_index_in_dim(x, 1 - c, 1, False), na)
-        kept = lax.dynamic_index_in_dim(x, c, 1, False)
-        both = jnp.where(
-            c == 0,
-            jnp.concatenate([kept, given], axis=-1),
-            jnp.concatenate([given, kept], axis=-1),
-        )
-        return both.reshape(-1, *both.shape[2:])
-
-    own_whole = over_cores(trial_b)
-    own_part = part(own_whole, o, own, 1)
-
-    sizes = [early_steps, 1] if early_steps else [1]
-    sends, first = [], 0
-    for size in sizes:
-        sends.append(
-            [
-                lax.dynamic_slice_in_dim(factors, (v - r) % nv * take + first, size, 0)
-                for r in range(1, nv)
-            ]
-        )
-        first += size
-    sends, others = lax.optimization_barrier((sends, others))
-    come = [[shift(x, "vir", nv, -r - 1) for r, x in enumerate(group)] for group in sends]
-
-    their = over_cores(jnp.concatenate(others, axis=0)) if others else None
+    def sends(source, first, size):
+        return [
+            lax.dynamic_slice_in_dim(source, (v - r) % nv * take + first, size, 0)
+            for r in range(1, nv)
+        ]
+
+    def along_vir(group):
+        return [shift(x, "vir", nv, -r - 1) for r, x in enumerate(group)]
+
+    come = None
+    if early_steps:
+        group, others = lax.optimization_barrier((sends(factors, 0, early_steps), others))
+        come = along_vir(group)
+
+    both = jnp.concatenate([mine] + others, axis=0).reshape(nv, CORES, half_m, own, cols)
+    given = sibling(lax.dynamic_index_in_dim(both, 1 - c, 1, False), na)
+    kept = lax.dynamic_index_in_dim(both, c, 1, False)
+    whole = jnp.where(
+        c == 0,
+        jnp.concatenate([kept, given], axis=-1),
+        jnp.concatenate([given, kept], axis=-1),
+    ).reshape(groups, own, block)
+    later, whole = lax.optimization_barrier((factors, whole))
+    come_last = along_vir(sends(later, early_steps, 1))
+
     blocks = []
-    for first, x in ((0, own_part), (half_m, their)):
-        for t in range(nz):
-            if x is None:
-                continue
-            if t == 0 and first == 0:
-                for s in range(no):
-                    blocks.append((part(own_whole, (o + s) % no, own, 1), 0, nz + s, 0))
-                continue
-            got = x if t == 0 else shift(x, "aux", na, t, CORES)
-            blocks.append((got, first, nz, t))
-            for s in range(1, no):
-                blocks.append((shift(got, "outer", no, -s), first, nz + s, t))
+    for t in range(nz):
+        got = whole if t == 0 else shift(whole, "aux", na, t, CORES)
+        blocks.append((got, 0, nz, t))
+        for s in range(1, no):
+            blocks.append((shift(got, "outer", no, -s), 0, nz + s, t))
     where = jnp.stack(
         [((z - t) % nz * block - v * width) % total for t in range(nz)]
         + [(o + s) % no * own for s in range(no)]
     ).astype(jnp.int32)
     vectors = assemble(where, blocks, groups, rows, total)
 
-    later, _ = lax.optimization_barrier((factors, blocks[-no][0]))
+    later, _ = lax.optimization_barrier((factors, blocks[no][0]))
     kept = lax.dynamic_slice_in_dim(later, v * take, take, 0)
     shown = sibling(kept, na)
     early = None
     if early_steps:
-        got, vectors = lax.optimization_barrier((come[0], vectors))
+        got, vectors = lax.optimization_barrier((come, vectors))
+        their = [[sibling(g[k : k + 1], na) for k in range(early_steps)] for g in got]
         early = early_sums(
-            [[kept] + got, [shown] + [sibling(g, na) for g in got]], early_steps, vectors
+            [[[kept]] + [[g] for g in got], [[shown]] + their], early_steps, vectors
         )
-    got, early = lax.optimization_barrier((come[-1], early))
+    got, early = lax.optimization_barrier((come_last, early))
     sides = [[kept] + got, [shown] + [sibling(g, na) for g in got]]
     firsts = [early_steps] + [0] * (nv - 1)
     pair_own = step_pairs(sides[0], firsts, vectors)

time: 119 us -> 122 us (1.025)
  waiting for transfers between devices: 40.2 us -> 50.8 us
  starting transfers between devices: 43.3 us -> 34.9 us
    ppermute x30 -> x24, waiting for transfers between devices: 35.1 us -> 47 us  [shift(): return lax.ppermute(array, axis, pairs)]
    ppermute x30 -> x24, starting transfers between devices: 42.4 us -> 34 us  [shift(): return lax.ppermute(array, axis, pairs)]
    slice x0 -> x1, local copies, waits for them, and re-layouts: none -> 1.48 us  [per_device(): their = [[sibling(g[k:k + 1], na) for k in range(early_steps)] for g in got]]
    ppermute x6 -> x7, waiting for transfers between devices: 5.09 us -> 3.77 us  [sibling(): return lax.ppermute(array, 'aux', [(i, i ^ 1) for i in range(size)])]
    dynamic_slice x5 -> x2, local copies, waits for them, and re-layouts: 4.62 us -> 3.77 us  [sends(): lax.dynamic_slice_in_dim(source, (v - r) % nv * take + first, size, 0)]
  transfers between devices with their start and end apart: 36 -> 31, of which waited for: 23 -> 19; matrix products, arithmetic and copies ran while one was open for 7% -> 7% of each run, Pallas kernels for 11% -> 11%
where the time goes in v5:
time: 122 us
  waiting for transfers between devices  50.8 us (42%)
  starting transfers between devices  34.9 us (29%)
  Pallas kernels  19.3 us (16%)
  local copies, waits for them, and re-layouts  13.8 us (11%)
  other arithmetic  2.76 us (2%)
    ppermute x24, waiting for transfers between devices, shift(): return lax.ppermute(array, axis, pairs)  47 us
    ppermute x24, starting transfers between devices, shift(): return lax.ppermute(array, axis, pairs)  34 us
    pallas_call x1, Pallas kernels, early_sums(): pl.pallas_call(body, out_shape=shape, in_specs=[ANY] * (n + 1), out_specs...  10.2 us
    unnamed x20, local copies, waits for them, and re-layouts  6.54 us
    pallas_call x1, Pallas kernels, last_sums(): pl.pallas_call(body, out_shape=shapes, in_specs=[SMEM] + [ANY] * (n + 2 +...  6.26 us
    ppermute x7, waiting for transfers between devices, sibling(): return lax.ppermute(array, 'aux', [(i, i ^ 1) for i in range(size)])  3.77 us
    dynamic_slice x2, local copies, waits for them, and re-layouts, sends(): lax.dynamic_slice_in_dim(source, (v - r) % nv * take + first, size, 0)  3.77 us
  transfers between devices with their start and end apart: 31, of which 19 were waited for; matrix products, arithmetic and copies ran while one was open for 7% of the time, Pallas kernels for 11%

profile of v5, /device:TPU:0, one launch (start us, length us, event | category | flops | bytes accessed | tf_op | source)
XLA Modules:
  0.0 121.8 jit_solution(4417936090211115179)
XLA Ops:
  0.0 1.0 copy-done
  1.1 3.0 %collective-permute-start = (bf16[2,128,256]{2,1,0:T(8,128)(2,1)S(1)}, bf16[2,128,256]{2,1,0:T(8,128)(2,1)S(1)}, u32[]{:S(2)}, u32[]{:S(2)}) collective-permute-start(bf16[2,128,256]{2,1,0:T(8,128)(2,1)S(1)} %dynamic-slice_convert_fusion.2), channel_id=1, source_target_pairs={{0,2},{2,0},{1,3},{3,1},{4,6},{6,4},{5,7},{7,5},{8,10},{10,8},{9,1... | collective-permute-start | bytes 393224 | tf_op jit(solution)/shard_map/ppermute | solution.py:35
  4.1 2.7 %constant_dynamic-slice_fusion.2 = bf16[3,256,1024]{2,1,0:T(8,128)(2,1)} fusion(bf16[8,256,1024]{2,1,0:T(8,128)(2,1)} %param.2, s32[]{:T(128)S(6)} %select_n.177), kind=kLoop, calls=%fused_computation.64 | loop fusion | bytes 3145732 | tf_op jit(solution)/shard_map/dynamic_slice | solution.py:367
  6.8 0.8 collective-permute-done
  7.7 1.3 %collective-permute-done.1 = bf16[2,1,128,256]{3,2,0,1:T(8,128)(2,1)S(1)} collective-permute-done((bf16[2,1,128,256]{3,2,0,1:T(8,128)(2,1)S(1)}, bf16[2,1,128,256]{3,2,0,1:T(8,128)(2,1)S(1)}, u32[]{:S(2)}, u32[]{:S(2)}) %collective-permute-start.1) | collective-permute-done | bytes 131104 | tf_op jit(solution)/shard_map/ppermute | solution.py:39
  9.2 1.9 %collective-permute-start.2 = (bf16[2,128,512]{2,1,0:T(8,128)(2,1)S(1)}, bf16[2,128,512]{2,1,0:T(8,128)(2,1)S(1)}, u32[]{:S(2)}, u32[]{:S(2)}) collective-permute-start(bf16[2,128,512]{2,1,0:T(8,128)(2,1)S(1)} %maximum_select_fusion.refs_0_), channel_id=1, source_target_pairs={{0,8},{4,12},{8,16},{12,20},{16,24},{20,28},{24,0},{28,4},{1,9},{5... | collective-permute-start | bytes 786440 | tf_op jit(solution)/shard_map/ppermute | solution.py:35
  11.0 1.5 %collective-permute-start.4 = (bf16[3,256,1024]{2,1,0:T(8,128)(2,1)}, bf16[3,256,1024]{2,1,0:T(8,128)(2,1)}, u32[]{:S(2)}, u32[]{:S(2)}) collective-permute-start(bf16[3,256,1024]{2,1,0:T(8,128)(2,1)} %constant_dynamic-slice_fusion.2), channel_id=1, source_target_pairs={{0,2},{2,0},{1,3},{3,1},{4,6},{6,4},{5,7},{7,5},{8,10},{10,8},{9,1... | collective-permute-start | bytes 4718600 | tf_op jit(solution)/shard_map/ppermute | solution.py:35
  12.5 7.2 %collective-permute-done.2.refs_2_ = bf16[2,128,512]{2,1,0:T(8,128)(2,1)S(1)} collective-permute-done((bf16[2,128,512]{2,1,0:T(8,128)(2,1)S(1)}, bf16[2,128,512]{2,1,0:T(8,128)(2,1)S(1)}, u32[]{:S(2)}, u32[]{:S(2)}) %collective-permute-start.2) | collective-permute-done | bytes 262176 | tf_op jit(solution)/shard_map/ppermute | solution.py:35
  19.7 1.8 %constant_dynamic-slice_fusion.1.refs_0_.refs_1_ = bf16[4,256,1024]{2,1,0:T(8,128)(2,1)S(1)} fusion(bf16[8,256,1024]{2,1,0:T(8,128)(2,1)} %param.2, s32[]{:T(128)S(6)} %select_n.181), kind=kLoop, calls=%fused_computation.63 | loop fusion | bytes 4194308 | tf_op jit(solution)/shard_map/dynamic_slice | solution.py:403
  21.5 1.8 %collective-permute-start.9 = (bf16[2,128,512]{2,1,0:T(8,128)(2,1)S(1)}, bf16[2,128,512]{2,1,0:T(8,128)(2,1)S(1)}, u32[]{:S(2)}, u32[]{:S(2)}) collective-permute-start(bf16[2,128,512]{2,1,0:T(8,128)(2,1)S(1)} %maximum_select_fusion.refs_0_), channel_id=1, source_target_pairs={{0,24},{4,28},{8,0},{12,4},{16,8},{20,12},{24,16},{28,20},{1,25},{... | collective-permute-start | bytes 786440 | tf_op jit(solution)/shard_map/ppermute | solution.py:35
  23.3 1.5 %collective-permute-start.5 = (bf16[2,128,512]{2,1,0:T(8,128)(2,1)S(1)}, bf16[2,128,512]{2,1,0:T(8,128)(2,1)S(1)}, u32[]{:S(2)}, u32[]{:S(2)}) collective-permute-start(bf16[2,128,512]{2,1,0:T(8,128)(2,1)S(1)} %maximum_select_fusion.refs_0_), channel_id=1, source_target_pairs={{0,1},{1,0},{2,3},{3,2},{4,5},{5,4},{6,7},{7,6},{8,9},{9,8},{10,11... | collective-permute-start | bytes 786440 | tf_op jit(solution)/shard_map/ppermute | solution.py:35
  24.8 6.5 %collective-permute-done.9.refs_6_ = bf16[2,128,512]{2,1,0:T(8,128)(2,1)S(1)} collective-permute-done((bf16[2,128,512]{2,1,0:T(8,128)(2,1)S(1)}, bf16[2,128,512]{2,1,0:T(8,128)(2,1)S(1)}, u32[]{:S(2)}, u32[]{:S(2)}) %collective-permute-start.9) | collective-permute-done | bytes 262176 | tf_op jit(solution)/shard_map/ppermute | solution.py:35
  31.3 1.5 %collective-permute-start.6 = (bf16[2,128,512]{2,1,0:T(8,128)(2,1)S(1)}, bf16[2,128,512]{2,1,0:T(8,128)(2,1)}, u32[]{:S(2)}, u32[]{:S(2)}) collective-permute-start(bf16[2,128,512]{2,1,0:T(8,128)(2,1)S(1)} %collective-permute-done.2.refs_2_), channel_id=1, source_target_pairs={{0,1},{1,0},{2,3},{3,2},{4,5},{5,4},{6,7},{7,6},{8,9},{9,8},{10,11... | collective-permute-start | bytes 786440 | tf_op jit(solution)/shard_map/ppermute | solution.py:35
  32.9 7.9 %collective-permute-done.7.refs_4_ = bf16[2,128,512]{2,1,0:T(8,128)(2,1)} collective-permute-done((bf16[2,128,512]{2,1,0:T(8,128)(2,1)S(1)}, bf16[2,128,512]{2,1,0:T(8,128)(2,1)}, u32[]{:S(2)}, u32[]{:S(2)}) %collective-permute-start.7) | collective-permute-done | bytes 262176 | tf_op jit(solution)/shard_map/ppermute | solution.py:35
  40.7 1.5 %collective-permute-start.10 = (bf16[2,128,512]{2,1,0:T(8,128)(2,1)S(1)}, bf16[2,128,512]{2,1,0:T(8,128)(2,1)}, u32[]{:S(2)}, u32[]{:S(2)}) collective-permute-start(bf16[2,128,512]{2,1,0:T(8,128)(2,1)S(1)} %collective-permute-done.9.refs_6_), channel_id=1, source_target_pairs={{0,1},{1,0},{2,3},{3,2},{4,5},{5,4},{6,7},{7,6},{8,9},{9,8},{10,11... | collective-permute-start | bytes 786440 | tf_op jit(solution)/shard_map/ppermute | solution.py:35
  43.5 6.5 %collective-permute-done.10.refs_7_ = bf16[2,128,512]{2,1,0:T(8,128)(2,1)} collective-permute-done((bf16[2,128,512]{2,1,0:T(8,128)(2,1)S(1)}, bf16[2,128,512]{2,1,0:T(8,128)(2,1)}, u32[]{:S(2)}, u32[]{:S(2)}) %collective-permute-start.10) | collective-permute-done | bytes 262176 | tf_op jit(solution)/shard_map/ppermute | solution.py:35
  50.1 4.3 %collective-permute-done.8.refs_5_ = bf16[2,128,512]{2,1,0:T(8,128)(2,1)} collective-permute-done((bf16[2,128,512]{2,1,0:T(8,128)(2,1)}, bf16[2,128,512]{2,1,0:T(8,128)(2,1)}, u32[]{:S(2)}, u32[]{:S(2)}) %collective-permute-start.8) | collective-permute-done | bytes 262176 | tf_op jit(solution)/shard_map/ppermute | solution.py:35
  54.3 0.9 copy-done.7
  55.3 1.9 %assemble.1.refs_6_.refs_2_ = bf16[2,256,2048]{2,1,0:T(8,128)(2,1)S(1)} custom-call(s32[6]{0:T(128)S(1)} %stack.27.at, bf16[2,128,512]{2,1,0:T(8,128)(2,1)S(1)} %maximum_select_fusion.refs_0_, bf16[2,128,512]{2,1,0:T(8,128)(2,1)S(1)} %copy-done.7, bf16[2,128,512]{2,1,0:T(8,128)(2,1)S(1)} %collective-permute-done.2.refs_2_, ...), custom_call_target="tpu_custom_call" | custom-call | bytes 2097152 | tf_op jit(solution)/shard_map/assemble/pallas_call | solution.py:76
  57.2 1.5 %fusion.24 = (bf16[1,256,1024]{2,1,0:T(8,128)(2,1)S(1)}, bf16[1,256,1024]{2,1,0:T(8,128)(2,1)S(1)}, bf16[1,256,1024]{2,1,0:T(8,128)(2,1)S(1)}) fusion(bf16[3,256,1024]{2,1,0:T(8,128)(2,1)} %collective-permute-done.4.refs_1_), kind=kLoop, calls=%fused_computation.65 | loop fusion | bytes 3145728 | tf_op jit(solution)/shard_map/slice | solution.py:408
  59.3 1.1 constant_dynamic-slice_fusion
  60.4 1.6 %collective-permute-start.3 = (bf16[1,256,1024]{2,1,0:T(8,128)(2,1)S(1)}, bf16[1,256,1024]{2,1,0:T(8,128)(2,1)S(1)}, u32[]{:S(2)}, u32[]{:S(2)}) collective-permute-start(bf16[1,256,1024]{2,1,0:T(8,128)(2,1)S(1)} %constant_dynamic-slice_fusion), channel_id=1, source_target_pairs={{0,2},{2,0},{1,3},{3,1},{4,6},{6,4},{5,7},{7,5},{8,10},{10,8},{9,1... | collective-permute-start | bytes 1572872 | tf_op jit(solution)/shard_map/ppermute | solution.py:35
  62.1 10.2 %early_sums.1.refs_7_ = f32[2,256,2048]{2,1,0:T(8,128)S(1)} custom-call(bf16[4,256,1024]{2,1,0:T(8,128)(2,1)S(1)} %constant_dynamic-slice_fusion.1.refs_0_.refs_1_, bf16[3,256,1024]{2,1,0:T(8,128)(2,1)} %collective-permute-done.4.refs_1_, bf16[4,256,1024]{2,1,0:T(8,128)(2,1)} %collective-permute-done.11.refs_2_.refs_3_, ...), custom_call_target="tpu_custom_call" | custom-call | bytes 2097152 | tf_op jit(solution)/shard_map/early_sums/pallas_call | solution.py:156
  72.3 2.4 %collective-permute-done.3.refs_1_.refs_2_ = bf16[1,256,1024]{2,1,0:T(8,128)(2,1)S(1)} collective-permute-done((bf16[1,256,1024]{2,1,0:T(8,128)(2,1)S(1)}, bf16[1,256,1024]{2,1,0:T(8,128)(2,1)S(1)}, u32[]{:S(2)}, u32[]{:S(2)}) %collective-permute-start.3) | collective-permute-done | bytes 524320 | tf_op jit(solution)/shard_map/ppermute | solution.py:35
  74.7 1.0 step_pairs.1.refs_5_
  75.7 0.9 collective-permute-done.15.refs_4_
  76.6 6.3 %last_sums.1 = (bf16[1,2,32,2048]{3,2,1,0:T(8,128)(2,1)S(1)}, f32[1,2,32,2048]{3,2,1,0:T(8,128)S(1)}, bf16[1,2,32,2048]{3,2,1,0:T(8,128)(2,1)S(1)}, f32[2,32,204...) custom-call(s32[1]{0:T(128)} %bitcast.refs_0_, ...), custom_call_target="tpu_custom_call" | custom-call | bytes 3145728 | tf_op jit(solution)/shard_map/last_sums/pallas_call | solution.py:327
  82.9 0.8 copy-done.1
  83.7 0.8 copy-done.3
  84.5 0.8 copy-done.5
  85.3 0.7 copy-done.8
  86.0 0.7 copy-done.9
  86.7 1.5 %collective-permute-start.25 = (bf16[2,32,2048]{2,1,0:T(8,128)(2,1)}, bf16[2,32,2048]{2,1,0:T(8,128)(2,1)S(1)}, u32[]{:S(2)}, u32[]{:S(2)}) collective-permute-start(bf16[2,32,2048]{2,1,0:T(8,128)(2,1)} %bitcast.16), channel_id=1, source_target_pairs={{0,1},{1,0},{2,3},{3,2},{4,5},{5,4},{6,7},{7,6},{8,9},{9,8},{10,11... | collective-permute-start | bytes 786440 | tf_op jit(solution)/shard_map/ppermute | solution.py:35
  88.3 1.5 %collective-permute-start.23 = (bf16[1,2,32,2048]{3,2,1,0:T(8,128)(2,1)}, bf16[1,2,32,2048]{3,2,1,0:T(8,128)(2,1)S(1)}, u32[]{:S(2)}, u32[]{:S(2)}) collective-permute-start(bf16[1,2,32,2048]{3,2,1,0:T(8,128)(2,1)} %copy-done.9), channel_id=1, source_target_pairs={{0,2},{2,0},{1,3},{3,1},{4,6},{6,4},{5,7},{7,5},{8,10},{10,8},{9,1... | collective-permute-start | bytes 786440 | tf_op jit(solution)/shard_map/ppermute | solution.py:35
  90.8 5.3 %collective-permute-done.25 = bf16[2,32,2048]{2,1,0:T(8,128)(2,1)S(1)} collective-permute-done((bf16[2,32,2048]{2,1,0:T(8,128)(2,1)}, bf16[2,32,2048]{2,1,0:T(8,128)(2,1)S(1)}, u32[]{:S(2)}, u32[]{:S(2)}) %collective-permute-start.25) | collective-permute-done | bytes 262176 | tf_op jit(solution)/shard_map/ppermute | solution.py:35
  96.1 1.1 convert_add_fusion
  97.2 1.6 %collective-permute-start.26 = (bf16[1,32,2048]{2,1,0:T(8,128)(2,1)S(1)}, bf16[1,32,2048]{2,1,0:T(8,128)(2,1)S(1)}, u32[]{:S(2)}, u32[]{:S(2)}) collective-permute-start(bf16[1,32,2048]{2,1,0:T(8,128)(2,1)S(1)} %slice.38), channel_id=1, source_target_pairs={{0,2},{2,0},{1,3},{3,1},{4,6},{6,4},{5,7},{7,5},{8,10},{10,8},{9,1... | collective-permute-start | bytes 393224 | tf_op jit(solution)/shard_map/ppermute | solution.py:35
  98.9 1.6 %collective-permute-start.24 = (bf16[1,32,2048]{2,1,0:T(8,128)(2,1)S(1)}, bf16[1,32,2048]{2,1,0:T(8,128)(2,1)S(1)}, u32[]{:S(2)}, u32[]{:S(2)}) collective-permute-start(bf16[1,32,2048]{2,1,0:T(8,128)(2,1)S(1)} %fusion.1), channel_id=1, source_target_pairs={{0,1},{1,0},{2,3},{3,2},{4,5},{5,4},{6,7},{7,6},{8,9},{9,8},{10,11... | collective-permute-start | bytes 393224 | tf_op jit(solution)/shard_map/ppermute | solution.py:35
  100.5 1.3 %collective-permute-done.18 = bf16[2,32,2048]{2,1,0:T(8,128)(2,1)S(1)} collective-permute-done((bf16[2,32,2048]{2,1,0:T(8,128)(2,1)}, bf16[2,32,2048]{2,1,0:T(8,128)(2,1)S(1)}, u32[]{:S(2)}, u32[]{:S(2)}) %collective-permute-start.18) | collective-permute-done | bytes 262176 | tf_op jit(solution)/shard_map/ppermute | solution.py:35
  101.8 1.6 %collective-permute-start.19 = (bf16[1,32,2048]{2,1,0:T(8,128)(2,1)S(1)}, bf16[1,32,2048]{2,1,0:T(8,128)(2,1)S(1)}, u32[]{:S(2)}, u32[]{:S(2)}) collective-permute-start(bf16[1,32,2048]{2,1,0:T(8,128)(2,1)S(1)} %slice.39), channel_id=1, source_target_pairs={{0,2},{2,0},{1,3},{3,1},{4,6},{6,4},{5,7},{7,5},{8,10},{10,8},{9,1... | collective-permute-start | bytes 393224 | tf_op jit(solution)/shard_map/ppermute | solution.py:35
  103.5 1.6 %collective-permute-start.17 = (bf16[1,32,2048]{2,1,0:T(8,128)(2,1)S(1)}, bf16[1,32,2048]{2,1,0:T(8,128)(2,1)S(1)}, u32[]{:S(2)}, u32[]{:S(2)}) collective-permute-start(bf16[1,32,2048]{2,1,0:T(8,128)(2,1)S(1)} %fusion), channel_id=1, source_target_pairs={{0,1},{1,0},{2,3},{3,2},{4,5},{5,4},{6,7},{7,6},{8,9},{9,8},{10,11... | collective-permute-start | bytes 393224 | tf_op jit(solution)/shard_map/ppermute | solution.py:35
  105.1 1.0 collective-permute-done.26
  106.8 3.5 %collective-permute-start.28 = (bf16[1,64,512]{2,1,0:T(8,128)(2,1)S(1)}, bf16[1,64,512]{2,1,0:T(8,128)(2,1)S(1)}, u32[]{:S(2)}, u32[]{:S(2)}) collective-permute-start(bf16[1,64,512]{2,1,0:T(8,128)(2,1)S(1)} %get-tuple-element.43), channel_id=1, source_target_pairs={{0,16},{4,20},{8,24},{12,28},{16,0},{20,4},{24,8},{28,12},{1,17},{... | collective-permute-start | bytes 196616 | tf_op jit(solution)/shard_map/ppermute | solution.py:35
  110.5 2.1 %collective-permute-start.20 = (bf16[1,64,512]{2,1,0:T(8,128)(2,1)S(1)}, bf16[1,64,512]{2,1,0:T(8,128)(2,1)S(1)}, u32[]{:S(2)}, u32[]{:S(2)}) collective-permute-start(bf16[1,64,512]{2,1,0:T(8,128)(2,1)S(1)} %get-tuple-element.45), channel_id=1, source_target_pairs={{0,8},{4,12},{8,16},{12,20},{16,24},{20,28},{24,0},{28,4},{1,9},{5... | collective-permute-start | bytes 196616 | tf_op jit(solution)/shard_map/ppermute | solution.py:35
  112.8 2.8 %collective-permute-start.22 = (bf16[1,64,512]{2,1,0:T(8,128)(2,1)S(1)}, bf16[1,64,512]{2,1,0:T(8,128)(2,1)S(1)}, u32[]{:S(2)}, u32[]{:S(2)}) collective-permute-start(bf16[1,64,512]{2,1,0:T(8,128)(2,1)S(1)} %get-tuple-element.47), channel_id=1, source_target_pairs={{0,24},{4,28},{8,0},{12,4},{16,8},{20,12},{24,16},{28,20},{1,25},{... | collective-permute-start | bytes 196616 | tf_op jit(solution)/shard_map/ppermute | solution.py:35
  116.8 2.6 %collective-permute-done.21 = bf16[1,64,512]{2,1,0:T(8,128)(2,1)S(1)} collective-permute-done((bf16[1,64,512]{2,1,0:T(8,128)(2,1)S(1)}, bf16[1,64,512]{2,1,0:T(8,128)(2,1)S(1)}, u32[]{:S(2)}, u32[]{:S(2)}) %collective-permute-start.21) | collective-permute-done | bytes 65568 | tf_op jit(solution)/shard_map/ppermute | solution.py:35
  119.7 1.3 %collective-permute-done.30 = f32[1,128,256]{2,1,0:T(8,128)S(1)} collective-permute-done((f32[1,128,256]{2,1,0:T(8,128)S(1)}, f32[1,128,256]{2,1,0:T(8,128)S(1)}, u32[]{:S(2)}, u32[]{:S(2)}) %collective-permute-start.30) | collective-permute-done | bytes 131104 | tf_op jit(solution)/shard_map/ppermute | solution.py:39
  121.0 0.7 maximum_select_fusion.1
  (65 shorter events, 6.3 us)
Async XLA Ops:
  0.0 1.0 copy-start
  1.1 6.5 %collective-permute-start = (bf16[2,128,256]{2,1,0:T(8,128)(2,1)S(1)}, bf16[2,128,256]{2,1,0:T(8,128)(2,1)S(1)}, u32[]{:S(2)}, u32[]{:S(2)}) collective-permute-start(bf16[2,128,256]{2,1,0:T(8,128)(2,1)S(1)} %dynamic-slice_convert_fusion.2), channel_id=1, source_target_pairs={{0,2},{2,0},{1,3},{3,1},{4,6},{6,4},{5,7},{7,5},{8,10},{10,8},{9,1... | collective-permute-start | bytes 393224 | tf_op jit(solution)/shard_map/ppermute | solution.py:35
  7.6 1.4 %collective-permute-start.1 = (bf16[2,1,128,256]{3,2,0,1:T(8,128)(2,1)S(1)}, bf16[2,1,128,256]{3,2,0,1:T(8,128)(2,1)S(1)}, u32[]{:S(2)}, u32[]{:S(2)}) collective-permute-start(bf16[2,1,128,256]{3,2,0,1:T(8,128)(2,1)S(1)} %get-tuple-element.51), channel_id=1, source_target_pairs={{0,4},{4,0},{8,12},{12,8},{16,20},{20,16},{24,28},{28,24},{1,5},{5... | collective-permute-start | bytes 393224 | tf_op jit(solution)/shard_map/ppermute | solution.py:39
  9.2 10.5 %collective-permute-start.2 = (bf16[2,128,512]{2,1,0:T(8,128)(2,1)S(1)}, bf16[2,128,512]{2,1,0:T(8,128)(2,1)S(1)}, u32[]{:S(2)}, u32[]{:S(2)}) collective-permute-start(bf16[2,128,512]{2,1,0:T(8,128)(2,1)S(1)} %maximum_select_fusion.refs_0_), channel_id=1, source_target_pairs={{0,8},{4,12},{8,16},{12,20},{16,24},{20,28},{24,0},{28,4},{1,9},{5... | collective-permute-start | bytes 786440 | tf_op jit(solution)/shard_map/ppermute | solution.py:35
  11.0 46.1 %collective-permute-start.4 = (bf16[3,256,1024]{2,1,0:T(8,128)(2,1)}, bf16[3,256,1024]{2,1,0:T(8,128)(2,1)}, u32[]{:S(2)}, u32[]{:S(2)}) collective-permute-start(bf16[3,256,1024]{2,1,0:T(8,128)(2,1)} %constant_dynamic-slice_fusion.2), channel_id=1, source_target_pairs={{0,2},{2,0},{1,3},{3,1},{4,6},{6,4},{5,7},{7,5},{8,10},{10,8},{9,1... | collective-permute-start | bytes 4718600 | tf_op jit(solution)/shard_map/ppermute | solution.py:35
  21.4 40.7 %collective-permute-start.11 = (bf16[4,256,1024]{2,1,0:T(8,128)(2,1)S(1)}, bf16[4,256,1024]{2,1,0:T(8,128)(2,1)}, u32[]{:S(2)}, u32[]{:S(2)}) collective-permute-start(bf16[4,256,1024]{2,1,0:T(8,128)(2,1)S(1)} %constant_dynamic-slice_fusion.1.refs_0_.refs_1_), channel_id=1, source_target_pairs={{0,4},{4,0},{8,12},{12,8},{16,20},{20,16},{24,28},{28,24},{1,5},{5... | collective-permute-start | bytes 6291464 | tf_op jit(solution)/shard_map/ppermute | solution.py:39
  21.5 9.8 %collective-permute-start.9 = (bf16[2,128,512]{2,1,0:T(8,128)(2,1)S(1)}, bf16[2,128,512]{2,1,0:T(8,128)(2,1)S(1)}, u32[]{:S(2)}, u32[]{:S(2)}) collective-permute-start(bf16[2,128,512]{2,1,0:T(8,128)(2,1)S(1)} %maximum_select_fusion.refs_0_), channel_id=1, source_target_pairs={{0,24},{4,28},{8,0},{12,4},{16,8},{20,12},{24,16},{28,20},{1,25},{... | collective-permute-start | bytes 786440 | tf_op jit(solution)/shard_map/ppermute | solution.py:35
  23.3 17.4 %collective-permute-start.7 = (bf16[2,128,512]{2,1,0:T(8,128)(2,1)S(1)}, bf16[2,128,512]{2,1,0:T(8,128)(2,1)}, u32[]{:S(2)}, u32[]{:S(2)}) collective-permute-start(bf16[2,128,512]{2,1,0:T(8,128)(2,1)S(1)} %maximum_select_fusion.refs_0_), channel_id=1, source_target_pairs={{0,16},{4,20},{8,24},{12,28},{16,0},{20,4},{24,8},{28,12},{1,17},{... | collective-permute-start | bytes 786440 | tf_op jit(solution)/shard_map/ppermute | solution.py:35
  23.3 18.9 %collective-permute-start.5 = (bf16[2,128,512]{2,1,0:T(8,128)(2,1)S(1)}, bf16[2,128,512]{2,1,0:T(8,128)(2,1)S(1)}, u32[]{:S(2)}, u32[]{:S(2)}) collective-permute-start(bf16[2,128,512]{2,1,0:T(8,128)(2,1)S(1)} %maximum_select_fusion.refs_0_), channel_id=1, source_target_pairs={{0,1},{1,0},{2,3},{3,2},{4,5},{5,4},{6,7},{7,6},{8,9},{9,8},{10,11... | collective-permute-start | bytes 786440 | tf_op jit(solution)/shard_map/ppermute | solution.py:35
  31.3 18.7 %collective-permute-start.6 = (bf16[2,128,512]{2,1,0:T(8,128)(2,1)S(1)}, bf16[2,128,512]{2,1,0:T(8,128)(2,1)}, u32[]{:S(2)}, u32[]{:S(2)}) collective-permute-start(bf16[2,128,512]{2,1,0:T(8,128)(2,1)S(1)} %collective-permute-done.2.refs_2_), channel_id=1, source_target_pairs={{0,1},{1,0},{2,3},{3,2},{4,5},{5,4},{6,7},{7,6},{8,9},{9,8},{10,11... | collective-permute-start | bytes 786440 | tf_op jit(solution)/shard_map/ppermute | solution.py:35
  40.7 9.3 %collective-permute-start.10 = (bf16[2,128,512]{2,1,0:T(8,128)(2,1)S(1)}, bf16[2,128,512]{2,1,0:T(8,128)(2,1)}, u32[]{:S(2)}, u32[]{:S(2)}) collective-permute-start(bf16[2,128,512]{2,1,0:T(8,128)(2,1)S(1)} %collective-permute-done.9.refs_6_), channel_id=1, source_target_pairs={{0,1},{1,0},{2,3},{3,2},{4,5},{5,4},{6,7},{7,6},{8,9},{9,8},{10,11... | collective-permute-start | bytes 786440 | tf_op jit(solution)/shard_map/ppermute | solution.py:35
  42.2 0.7 copy-start.6
  43.0 11.4 %collective-permute-start.8 = (bf16[2,128,512]{2,1,0:T(8,128)(2,1)}, bf16[2,128,512]{2,1,0:T(8,128)(2,1)}, u32[]{:S(2)}, u32[]{:S(2)}) collective-permute-start(bf16[2,128,512]{2,1,0:T(8,128)(2,1)} %collective-permute-done.7.refs_4_), channel_id=1, source_target_pairs={{0,1},{1,0},{2,3},{3,2},{4,5},{5,4},{6,7},{7,6},{8,9},{9,8},{10,11... | collective-permute-start | bytes 786440 | tf_op jit(solution)/shard_map/ppermute | solution.py:35
  54.3 1.0 copy-start.7
  58.6 3.3 %collective-permute-start.12 = (bf16[1,256,1024]{2,1,0:T(8,128)(2,1)S(1)}, bf16[1,256,1024]{2,1,0:T(8,128)(2,1)S(1)}, u32[]{:S(2)}, u32[]{:S(2)}) collective-permute-start(bf16[1,256,1024]{2,1,0:T(8,128)(2,1)S(1)} %get-tuple-element.41), channel_id=1, source_target_pairs={{0,4},{4,0},{8,12},{12,8},{16,20},{20,16},{24,28},{28,24},{1,5},{5... | collective-permute-start | bytes 1572872 | tf_op jit(solution)/shard_map/ppermute | solution.py:39
  58.7 3.2 %collective-permute-start.13 = (bf16[1,256,1024]{2,1,0:T(8,128)(2,1)S(1)}, bf16[1,256,1024]{2,1,0:T(8,128)(2,1)S(1)}, u32[]{:S(2)}, u32[]{:S(2)}) collective-permute-start(bf16[1,256,1024]{2,1,0:T(8,128)(2,1)S(1)} %get-tuple-element.40), channel_id=1, source_target_pairs={{0,4},{4,0},{8,12},{12,8},{16,20},{20,16},{24,28},{28,24},{1,5},{5... | collective-permute-start | bytes 1572872 | tf_op jit(solution)/shard_map/ppermute | solution.py:39
  59.2 2.9 %collective-permute-start.14 = (bf16[1,256,1024]{2,1,0:T(8,128)(2,1)S(1)}, bf16[1,256,1024]{2,1,0:T(8,128)(2,1)S(1)}, u32[]{:S(2)}, u32[]{:S(2)}) collective-permute-start(bf16[1,256,1024]{2,1,0:T(8,128)(2,1)S(1)} %get-tuple-element.39), channel_id=1, source_target_pairs={{0,4},{4,0},{8,12},{12,8},{16,20},{20,16},{24,28},{28,24},{1,5},{5... | collective-permute-start | bytes 1572872 | tf_op jit(solution)/shard_map/ppermute | solution.py:39
  60.4 14.3 %collective-permute-start.3 = (bf16[1,256,1024]{2,1,0:T(8,128)(2,1)S(1)}, bf16[1,256,1024]{2,1,0:T(8,128)(2,1)S(1)}, u32[]{:S(2)}, u32[]{:S(2)}) collective-permute-start(bf16[1,256,1024]{2,1,0:T(8,128)(2,1)S(1)} %constant_dynamic-slice_fusion), channel_id=1, source_target_pairs={{0,2},{2,0},{1,3},{3,1},{4,6},{6,4},{5,7},{7,5},{8,10},{10,8},{9,1... | collective-permute-start | bytes 1572872 | tf_op jit(solution)/shard_map/ppermute | solution.py:35
  74.7 1.9 %collective-permute-start.15 = (bf16[1,256,1024]{2,1,0:T(8,128)(2,1)S(1)}, bf16[1,256,1024]{2,1,0:T(8,128)(2,1)S(1)}, u32[]{:S(2)}, u32[]{:S(2)}) collective-permute-start(bf16[1,256,1024]{2,1,0:T(8,128)(2,1)S(1)} %collective-permute-done.3.refs_1_.refs_2_), channel_id=1, source_target_pairs={{0,4},{4,0},{8,12},{12,8},{16,20},{20,16},{24,28},{28,24},{1,5},{5... | collective-permute-start | bytes 1572872 | tf_op jit(solution)/shard_map/ppermute | solution.py:39
  82.9 0.8 copy-start.1
  83.7 0.8 copy-start.3
  84.5 0.8 copy-start.5
  85.3 0.7 copy-start.8
  86.0 0.7 copy-start.9
  86.7 12.0 %copy-start.4 = (f32[1,2,32,2048]{3,2,1,0:T(8,128)S(1)}, f32[1,2,32,2048]{3,2,1,0:T(8,128)}, u32[]{:S(2)}) copy-start(f32[1,2,32,2048]{3,2,1,0:T(8,128)} %copy-done.3) | copy-start | bytes 1572868
  86.7 15.0 %copy-start.2 = (f32[2,32,2048]{2,1,0:T(8,128)S(1)}, f32[2,32,2048]{2,1,0:T(8,128)}, u32[]{:S(2)}) copy-start(f32[2,32,2048]{2,1,0:T(8,128)} %copy-done.1) | copy-start | bytes 1572868
  86.7 9.4 %collective-permute-start.25 = (bf16[2,32,2048]{2,1,0:T(8,128)(2,1)}, bf16[2,32,2048]{2,1,0:T(8,128)(2,1)S(1)}, u32[]{:S(2)}, u32[]{:S(2)}) collective-permute-start(bf16[2,32,2048]{2,1,0:T(8,128)(2,1)} %bitcast.16), channel_id=1, source_target_pairs={{0,1},{1,0},{2,3},{3,2},{4,5},{5,4},{6,7},{7,6},{8,9},{9,8},{10,11... | collective-permute-start | bytes 786440 | tf_op jit(solution)/shard_map/ppermute | solution.py:35
  88.3 10.5 %collective-permute-start.23 = (bf16[1,2,32,2048]{3,2,1,0:T(8,128)(2,1)}, bf16[1,2,32,2048]{3,2,1,0:T(8,128)(2,1)S(1)}, u32[]{:S(2)}, u32[]{:S(2)}) collective-permute-start(bf16[1,2,32,2048]{3,2,1,0:T(8,128)(2,1)} %copy-done.9), channel_id=1, source_target_pairs={{0,2},{2,0},{1,3},{3,1},{4,6},{6,4},{5,7},{7,5},{8,10},{10,8},{9,1... | collective-permute-start | bytes 786440 | tf_op jit(solution)/shard_map/ppermute | solution.py:35
  89.8 12.0 %collective-permute-start.18 = (bf16[2,32,2048]{2,1,0:T(8,128)(2,1)}, bf16[2,32,2048]{2,1,0:T(8,128)(2,1)S(1)}, u32[]{:S(2)}, u32[]{:S(2)}) collective-permute-start(bf16[2,32,2048]{2,1,0:T(8,128)(2,1)} %bitcast.27), channel_id=1, source_target_pairs={{0,1},{1,0},{2,3},{3,2},{4,5},{5,4},{6,7},{7,6},{8,9},{9,8},{10,11... | collective-permute-start | bytes 786440 | tf_op jit(solution)/shard_map/ppermute | solution.py:35
  90.3 13.1 %collective-permute-start.16 = (bf16[1,2,32,2048]{3,2,1,0:T(8,128)(2,1)S(1)}, bf16[1,2,32,2048]{3,2,1,0:T(8,128)(2,1)S(1)}, u32[]{:S(2)}, u32[]{:S(2)}) collective-permute-start(bf16[1,2,32,2048]{3,2,1,0:T(8,128)(2,1)S(1)} %get-tuple-element.32), channel_id=1, source_target_pairs={{0,2},{2,0},{1,3},{3,1},{4,6},{6,4},{5,7},{7,5},{8,10},{10,8},{9,1... | collective-permute-start | bytes 786440 | tf_op jit(solution)/shard_map/ppermute | solution.py:35
  97.2 8.9 %collective-permute-start.26 = (bf16[1,32,2048]{2,1,0:T(8,128)(2,1)S(1)}, bf16[1,32,2048]{2,1,0:T(8,128)(2,1)S(1)}, u32[]{:S(2)}, u32[]{:S(2)}) collective-permute-start(bf16[1,32,2048]{2,1,0:T(8,128)(2,1)S(1)} %slice.38), channel_id=1, source_target_pairs={{0,2},{2,0},{1,3},{3,1},{4,6},{6,4},{5,7},{7,5},{8,10},{10,8},{9,1... | collective-permute-start | bytes 393224 | tf_op jit(solution)/shard_map/ppermute | solution.py:35
  98.9 7.3 %collective-permute-start.24 = (bf16[1,32,2048]{2,1,0:T(8,128)(2,1)S(1)}, bf16[1,32,2048]{2,1,0:T(8,128)(2,1)S(1)}, u32[]{:S(2)}, u32[]{:S(2)}) collective-permute-start(bf16[1,32,2048]{2,1,0:T(8,128)(2,1)S(1)} %fusion.1), channel_id=1, source_target_pairs={{0,1},{1,0},{2,3},{3,2},{4,5},{5,4},{6,7},{7,6},{8,9},{9,8},{10,11... | collective-permute-start | bytes 393224 | tf_op jit(solution)/shard_map/ppermute | solution.py:35
  101.8 8.5 %collective-permute-start.19 = (bf16[1,32,2048]{2,1,0:T(8,128)(2,1)S(1)}, bf16[1,32,2048]{2,1,0:T(8,128)(2,1)S(1)}, u32[]{:S(2)}, u32[]{:S(2)}) collective-permute-start(bf16[1,32,2048]{2,1,0:T(8,128)(2,1)S(1)} %slice.39), channel_id=1, source_target_pairs={{0,2},{2,0},{1,3},{3,1},{4,6},{6,4},{5,7},{7,5},{8,10},{10,8},{9,1... | collective-permute-start | bytes 393224 | tf_op jit(solution)/shard_map/ppermute | solution.py:35
  103.5 6.9 %collective-permute-start.17 = (bf16[1,32,2048]{2,1,0:T(8,128)(2,1)S(1)}, bf16[1,32,2048]{2,1,0:T(8,128)(2,1)S(1)}, u32[]{:S(2)}, u32[]{:S(2)}) collective-permute-start(bf16[1,32,2048]{2,1,0:T(8,128)(2,1)S(1)} %fusion), channel_id=1, source_target_pairs={{0,1},{1,0},{2,3},{3,2},{4,5},{5,4},{6,7},{7,6},{8,9},{9,8},{10,11... | collective-permute-start | bytes 393224 | tf_op jit(solution)/shard_map/ppermute | solution.py:35
  106.3 6.4 %collective-permute-start.27 = (bf16[1,64,512]{2,1,0:T(8,128)(2,1)S(1)}, bf16[1,64,512]{2,1,0:T(8,128)(2,1)S(1)}, u32[]{:S(2)}, u32[]{:S(2)}) collective-permute-start(bf16[1,64,512]{2,1,0:T(8,128)(2,1)S(1)} %get-tuple-element.42), channel_id=1, source_target_pairs={{0,8},{4,12},{8,16},{12,20},{16,24},{20,28},{24,0},{28,4},{1,9},{5... | collective-permute-start | bytes 196616 | tf_op jit(solution)/shard_map/ppermute | solution.py:35
  106.8 9.1 %collective-permute-start.28 = (bf16[1,64,512]{2,1,0:T(8,128)(2,1)S(1)}, bf16[1,64,512]{2,1,0:T(8,128)(2,1)S(1)}, u32[]{:S(2)}, u32[]{:S(2)}) collective-permute-start(bf16[1,64,512]{2,1,0:T(8,128)(2,1)S(1)} %get-tuple-element.43), channel_id=1, source_target_pairs={{0,16},{4,20},{8,24},{12,28},{16,0},{20,4},{24,8},{28,12},{1,17},{... | collective-permute-start | bytes 196616 | tf_op jit(solution)/shard_map/ppermute | solution.py:35
  110.3 5.8 %collective-permute-start.29 = (bf16[1,64,512]{2,1,0:T(8,128)(2,1)S(1)}, bf16[1,64,512]{2,1,0:T(8,128)(2,1)S(1)}, u32[]{:S(2)}, u32[]{:S(2)}) collective-permute-start(bf16[1,64,512]{2,1,0:T(8,128)(2,1)S(1)} %get-tuple-element.44), channel_id=1, source_target_pairs={{0,24},{4,28},{8,0},{12,4},{16,8},{20,12},{24,16},{28,20},{1,25},{... | collective-permute-start | bytes 196616 | tf_op jit(solution)/shard_map/ppermute | solution.py:35
  110.5 6.3 %collective-permute-start.20 = (bf16[1,64,512]{2,1,0:T(8,128)(2,1)S(1)}, bf16[1,64,512]{2,1,0:T(8,128)(2,1)S(1)}, u32[]{:S(2)}, u32[]{:S(2)}) collective-permute-start(bf16[1,64,512]{2,1,0:T(8,128)(2,1)S(1)} %get-tuple-element.45), channel_id=1, source_target_pairs={{0,8},{4,12},{8,16},{12,20},{16,24},{20,28},{24,0},{28,4},{1,9},{5... | collective-permute-start | bytes 196616 | tf_op jit(solution)/shard_map/ppermute | solution.py:35
  112.6 6.9 %collective-permute-start.21 = (bf16[1,64,512]{2,1,0:T(8,128)(2,1)S(1)}, bf16[1,64,512]{2,1,0:T(8,128)(2,1)S(1)}, u32[]{:S(2)}, u32[]{:S(2)}) collective-permute-start(bf16[1,64,512]{2,1,0:T(8,128)(2,1)S(1)} %get-tuple-element.46), channel_id=1, source_target_pairs={{0,16},{4,20},{8,24},{12,28},{16,0},{20,4},{24,8},{28,12},{1,17},{... | collective-permute-start | bytes 196616 | tf_op jit(solution)/shard_map/ppermute | solution.py:35
  112.8 6.7 %collective-permute-start.22 = (bf16[1,64,512]{2,1,0:T(8,128)(2,1)S(1)}, bf16[1,64,512]{2,1,0:T(8,128)(2,1)S(1)}, u32[]{:S(2)}, u32[]{:S(2)}) collective-permute-start(bf16[1,64,512]{2,1,0:T(8,128)(2,1)S(1)} %get-tuple-element.47), channel_id=1, source_target_pairs={{0,24},{4,28},{8,0},{12,4},{16,8},{20,12},{24,16},{28,20},{1,25},{... | collective-permute-start | bytes 196616 | tf_op jit(solution)/shard_map/ppermute | solution.py:35
  119.6 1.4 %collective-permute-start.30 = (f32[1,128,256]{2,1,0:T(8,128)S(1)}, f32[1,128,256]{2,1,0:T(8,128)S(1)}, u32[]{:S(2)}, u32[]{:S(2)}) collective-permute-start(f32[1,128,256]{2,1,0:T(8,128)S(1)} %get-tuple-element.49), channel_id=1, source_target_pairs={{0,4},{4,0},{8,12},{12,8},{16,20},{20,16},{24,28},{28,24},{1,5},{5... | collective-permute-start | bytes 393224 | tf_op jit(solution)/shard_map/ppermute | solution.py:39

commit v6 on v5

--- a/solution.py
+++ b/solution.py
@@ -49,6 +49,10 @@
 
 def params():
     return pltpu.CompilerParams(vmem_limit_bytes=VMEM_LIMIT)
+
+
+def in_hbm(x):
+    return pltpu.with_memory_space_constraint(x, pltpu.HBM)
 
 
 def cost(flops, *arrays):
@@ -82,7 +86,7 @@
         cost_estimate=cost(0, shape),
         compiler_params=params(),
         name="assemble",
-    )(where, *[b[0] for b in blocks])
+    )(where, *[in_hbm(b[0]) for b in blocks])
 
 
 def pairs_of(refs, vec, store):
@@ -326,7 +330,7 @@
     ] * PIECES
     outs = pl.pallas_call(
         body,
-        out_shape=shapes,
+        out_shape=[pltpu.HBM(x.shape, x.dtype) for x in shapes],
         in_specs=[SMEM] + [ANY] * (n + 2 + len(more)),
         out_specs=[HBM] * len(shapes),
         scratch_shapes=[pltpu.VMEM(x.shape, x.dtype) for x in shapes]
@@ -358,6 +362,7 @@
     own = rows // no
     groups = nv * half_m
     early_steps = take - 1
+    last_steps = take - early_steps
 
     mine = part(trials, o, own, 1).astype(BF16)
     others = [shift(mine, "vir", nv, -r) for r in range(1, nv)]
@@ -385,11 +390,10 @@
         jnp.concatenate([given, kept], axis=-1),
     ).reshape(groups, own, block)
     later, whole = lax.optimization_barrier((factors, whole))
-    come_last = along_vir(sends(later, early_steps, 1))
-
+
+    steps = [whole] + [shift(whole, "aux", na, t, CORES) for t in range(1, nz)]
     blocks = []
-    for t in range(nz):
-        got = whole if t == 0 else shift(whole, "aux", na, t, CORES)
+    for t, got in enumerate(steps):
         blocks.append((got, 0, nz, t))
         for s in range(1, no):
             blocks.append((shift(got, "outer", no, -s), 0, nz + s, t))
@@ -397,15 +401,19 @@
         [((z - t) % nz * block - v * width) % total for t in range(nz)]
         + [(o + s) % no * own for s in range(no)]
     ).astype(jnp.int32)
+    later, _ = lax.optimization_barrier((factors, blocks[no - 1][0]))
+    held = (come, sends(later, early_steps, last_steps), [b[0] for b in blocks])
+    come, group, arrays = lax.optimization_barrier(held)
+    come_last = along_vir(group)
+    blocks = [(x, *b[1:]) for x, b in zip(arrays, blocks)]
     vectors = assemble(where, blocks, groups, rows, total)
 
-    later, _ = lax.optimization_barrier((factors, blocks[no][0]))
     kept = lax.dynamic_slice_in_dim(later, v * take, take, 0)
     shown = sibling(kept, na)
     early = None
     if early_steps:
-        got, vectors = lax.optimization_barrier((come, vectors))
-        their = [[sibling(g[k : k + 1], na) for k in range(early_steps)] for g in got]
+        got = come
+        their = [[sibling(g, na)] for g in got]
         early = early_sums(
             [[[kept]] + [[g] for g in got], [[shown]] + their], early_steps, vectors
         )

time: 122 us -> 107 us (0.88)
  waiting for transfers between devices: 50.8 us -> 43 us
  local copies, waits for them, and re-layouts: 13.8 us -> 8.39 us
    ppermute x24, waiting for transfers between devices: 47 us -> 38.4 us  [shift(): return lax.ppermute(array, axis, pairs)]
    unnamed x20 -> x18, local copies, waits for them, and re-layouts: 6.54 us -> 1.76 us
    slice x1 -> x0, local copies, waits for them, and re-layouts: 1.48 us -> none  [per_device(): their = [[sibling(g[k:k + 1], na) for k in range(early_steps)] for g in got]]
    ppermute x7 -> x5, waiting for transfers between devices: 3.77 us -> 4.57 us  [sibling(): return lax.ppermute(array, 'aux', [(i, i ^ 1) for i in range(size)])]
  transfers between devices with their start and end apart: 31 -> 29, of which waited for: 19 -> 17; matrix products, arithmetic and copies ran while one was open for 7% -> 8% of each run, Pallas kernels for 11% -> 12%
where the time goes in v6:
time: 107 us
  waiting for transfers between devices  43 us (40%)
  starting transfers between devices  33.8 us (32%)
  Pallas kernels  18.9 us (18%)
  local copies, waits for them, and re-layouts  8.39 us (8%)
  other arithmetic  2.81 us (3%)
    ppermute x24, waiting for transfers between devices, shift(): return lax.ppermute(array, axis, pairs)  38.4 us
    ppermute x24, starting transfers between devices, shift(): return lax.ppermute(array, axis, pairs)  33.6 us
    pallas_call x1, Pallas kernels, early_sums(): pl.pallas_call(body, out_shape=shape, in_specs=[ANY] * (n + 1), out_specs...  10.1 us
    pallas_call x1, Pallas kernels, last_sums(): pl.pallas_call(body, out_shape=[pltpu.HBM(x.shape, x.dtype) for x in shap...  5.64 us
    dynamic_slice x2, local copies, waits for them, and re-layouts, sends(): lax.dynamic_slice_in_dim(source, (v - r) % nv * take + first, size, 0)  4.57 us
    ppermute x5, waiting for transfers between devices, sibling(): return lax.ppermute(array, 'aux', [(i, i ^ 1) for i in range(size)])  4.57 us
  transfers between devices with their start and end apart: 29, of which 17 were waited for; matrix products, arithmetic and copies ran while one was open for 8% of the time, Pallas kernels for 12%

profile of v6, /device:TPU:0, one launch (start us, length us, event | category | flops | bytes accessed | tf_op | source)
XLA Modules:
  0.0 107.2 jit_solution(7389822151394437569)
XLA Ops:
  0.0 1.0 copy-done
  1.1 3.0 %collective-permute-start = (bf16[2,128,256]{2,1,0:T(8,128)(2,1)S(1)}, bf16[2,128,256]{2,1,0:T(8,128)(2,1)S(1)}, u32[]{:S(2)}, u32[]{:S(2)}) collective-permute-start(bf16[2,128,256]{2,1,0:T(8,128)(2,1)S(1)} %dynamic-slice_convert_fusion.2), channel_id=1, source_target_pairs={{0,2},{2,0},{1,3},{3,1},{4,6},{6,4},{5,7},{7,5},{8,10},{10,8},{9,1... | collective-permute-start | bytes 393224 | tf_op jit(solution)/shard_map/ppermute | solution.py:35
  4.1 2.7 %constant_dynamic-slice_fusion.2 = bf16[3,256,1024]{2,1,0:T(8,128)(2,1)} fusion(bf16[8,256,1024]{2,1,0:T(8,128)(2,1)} %param.2, s32[]{:T(128)S(6)} %select_n.177), kind=kLoop, calls=%fused_computation.64 | loop fusion | bytes 3145732 | tf_op jit(solution)/shard_map/dynamic_slice | solution.py:372
  6.8 0.8 collective-permute-done
  7.6 1.7 %collective-permute-start.3 = (bf16[3,256,1024]{2,1,0:T(8,128)(2,1)}, bf16[3,256,1024]{2,1,0:T(8,128)(2,1)}, u32[]{:S(2)}, u32[]{:S(2)}) collective-permute-start(bf16[3,256,1024]{2,1,0:T(8,128)(2,1)} %constant_dynamic-slice_fusion.2), channel_id=1, source_target_pairs={{0,2},{2,0},{1,3},{3,1},{4,6},{6,4},{5,7},{7,5},{8,10},{10,8},{9,1... | collective-permute-start | bytes 4718600 | tf_op jit(solution)/shard_map/ppermute | solution.py:35
  9.4 1.3 %collective-permute-done.1 = bf16[2,1,128,256]{3,2,0,1:T(8,128)(2,1)S(1)} collective-permute-done((bf16[2,1,128,256]{3,2,0,1:T(8,128)(2,1)S(1)}, bf16[2,1,128,256]{3,2,0,1:T(8,128)(2,1)S(1)}, u32[]{:S(2)}, u32[]{:S(2)}) %collective-permute-start.1) | collective-permute-done | bytes 131104 | tf_op jit(solution)/shard_map/ppermute | solution.py:39
  10.9 1.6 %collective-permute-start.2 = (bf16[2,128,512]{2,1,0:T(8,128)(2,1)S(1)}, bf16[2,128,512]{2,1,0:T(8,128)(2,1)S(1)}, u32[]{:S(2)}, u32[]{:S(2)}) collective-permute-start(bf16[2,128,512]{2,1,0:T(8,128)(2,1)S(1)} %maximum_select_fusion.refs_0_), channel_id=1, source_target_pairs={{0,1},{1,0},{2,3},{3,2},{4,5},{5,4},{6,7},{7,6},{8,9},{9,8},{10,11... | collective-permute-start | bytes 786440 | tf_op jit(solution)/shard_map/ppermute | solution.py:35
  12.5 1.6 %collective-permute-start.4 = (bf16[2,128,512]{2,1,0:T(8,128)(2,1)S(1)}, bf16[2,128,512]{2,1,0:T(8,128)(2,1)S(1)}, u32[]{:S(2)}, u32[]{:S(2)}) collective-permute-start(bf16[2,128,512]{2,1,0:T(8,128)(2,1)S(1)} %maximum_select_fusion.refs_0_), channel_id=1, source_target_pairs={{0,8},{4,12},{8,16},{12,20},{16,24},{20,28},{24,0},{28,4},{1,9},{5... | collective-permute-start | bytes 786440 | tf_op jit(solution)/shard_map/ppermute | solution.py:35
  14.1 2.6 %collective-permute-start.6 = (bf16[2,128,512]{2,1,0:T(8,128)(2,1)S(1)}, bf16[2,128,512]{2,1,0:T(8,128)(2,1)}, u32[]{:S(2)}, u32[]{:S(2)}) collective-permute-start(bf16[2,128,512]{2,1,0:T(8,128)(2,1)S(1)} %maximum_select_fusion.refs_0_), channel_id=1, source_target_pairs={{0,16},{4,20},{8,24},{12,28},{16,0},{20,4},{24,8},{28,12},{1,17},{... | collective-permute-start | bytes 786440 | tf_op jit(solution)/shard_map/ppermute | solution.py:35
  16.7 1.3 %collective-permute-start.8 = (bf16[2,128,512]{2,1,0:T(8,128)(2,1)S(1)}, bf16[2,128,512]{2,1,0:T(8,128)(2,1)}, u32[]{:S(2)}, u32[]{:S(2)}) collective-permute-start(bf16[2,128,512]{2,1,0:T(8,128)(2,1)S(1)} %maximum_select_fusion.refs_0_), channel_id=1, source_target_pairs={{0,24},{4,28},{8,0},{12,4},{16,8},{20,12},{24,16},{28,20},{1,25},{... | collective-permute-start | bytes 786440 | tf_op jit(solution)/shard_map/ppermute | solution.py:35
  18.0 1.3 %collective-permute-done.2.refs_1_ = bf16[2,128,512]{2,1,0:T(8,128)(2,1)S(1)} collective-permute-done((bf16[2,128,512]{2,1,0:T(8,128)(2,1)S(1)}, bf16[2,128,512]{2,1,0:T(8,128)(2,1)S(1)}, u32[]{:S(2)}, u32[]{:S(2)}) %collective-permute-start.2) | collective-permute-done | bytes 262176 | tf_op jit(solution)/shard_map/ppermute | solution.py:35
  19.3 1.9 %constant_dynamic-slice_fusion.1.refs_0_.refs_1_ = bf16[4,256,1024]{2,1,0:T(8,128)(2,1)S(1)} fusion(bf16[8,256,1024]{2,1,0:T(8,128)(2,1)} %param.2, s32[]{:T(128)S(6)} %select_n.181), kind=kLoop, calls=%fused_computation.63 | loop fusion | bytes 4194308 | tf_op jit(solution)/shard_map/dynamic_slice | solution.py:411
  21.3 2.3 %collective-permute-done.4.refs_2_ = bf16[2,128,512]{2,1,0:T(8,128)(2,1)S(1)} collective-permute-done((bf16[2,128,512]{2,1,0:T(8,128)(2,1)S(1)}, bf16[2,128,512]{2,1,0:T(8,128)(2,1)S(1)}, u32[]{:S(2)}, u32[]{:S(2)}) %collective-permute-start.4) | collective-permute-done | bytes 262176 | tf_op jit(solution)/shard_map/ppermute | solution.py:35
  24.1 9.8 %collective-permute-done.6.refs_4_ = bf16[2,128,512]{2,1,0:T(8,128)(2,1)} collective-permute-done((bf16[2,128,512]{2,1,0:T(8,128)(2,1)S(1)}, bf16[2,128,512]{2,1,0:T(8,128)(2,1)}, u32[]{:S(2)}, u32[]{:S(2)}) %collective-permute-start.6) | collective-permute-done | bytes 262176 | tf_op jit(solution)/shard_map/ppermute | solution.py:35
  34.4 1.5 %collective-permute-start.9 = (bf16[2,128,512]{2,1,0:T(8,128)(2,1)}, bf16[2,128,512]{2,1,0:T(8,128)(2,1)S(1)}, u32[]{:S(2)}, u32[]{:S(2)}) collective-permute-start(bf16[2,128,512]{2,1,0:T(8,128)(2,1)} %collective-permute-done.8.refs_6_), channel_id=1, source_target_pairs={{0,1},{1,0},{2,3},{3,2},{4,5},{5,4},{6,7},{7,6},{8,9},{9,8},{10,11... | collective-permute-start | bytes 786440 | tf_op jit(solution)/shard_map/ppermute | solution.py:35
  35.9 1.9 %constant_dynamic-slice_fusion = bf16[1,256,1024]{2,1,0:T(8,128)(2,1)} fusion(bf16[8,256,1024]{2,1,0:T(8,128)(2,1)} %param.2, s32[]{:T(128)S(6)} %select_n.182), kind=kLoop, calls=%fused_computation.62 | loop fusion | bytes 1048580 | tf_op jit(solution)/shard_map/dynamic_slice | solution.py:372
  37.8 5.6 %collective-permute-done.7.refs_5_ = bf16[2,128,512]{2,1,0:T(8,128)(2,1)} collective-permute-done((bf16[2,128,512]{2,1,0:T(8,128)(2,1)}, bf16[2,128,512]{2,1,0:T(8,128)(2,1)}, u32[]{:S(2)}, u32[]{:S(2)}) %collective-permute-start.7) | collective-permute-done | bytes 262176 | tf_op jit(solution)/shard_map/ppermute | solution.py:35
  43.4 4.5 %collective-permute-done.9.refs_7_ = bf16[2,128,512]{2,1,0:T(8,128)(2,1)S(1)} collective-permute-done((bf16[2,128,512]{2,1,0:T(8,128)(2,1)}, bf16[2,128,512]{2,1,0:T(8,128)(2,1)S(1)}, u32[]{:S(2)}, u32[]{:S(2)}) %collective-permute-start.9) | collective-permute-done | bytes 262176 | tf_op jit(solution)/shard_map/ppermute | solution.py:35
  47.9 0.7 copy-done.8
  48.6 0.5 collective-permute-start.10
  49.2 2.1 %assemble.1.refs_4_.refs_2_.refs_6_ = bf16[2,256,2048]{2,1,0:T(8,128)(2,1)S(1)} custom-call(s32[6]{0:T(128)S(1)} %stack.27.at, bf16[2,128,512]{2,1,0:T(8,128)(2,1)} %copy-done.1, bf16[2,128,512]{2,1,0:T(8,128)(2,1)} %copy-done.5, bf16[2,128,512]{2,1,0:T(8,128)(2,1)} %copy-done.6, bf16[2,128,512]{2,1,0:T(8,128)(2,1)} %copy-done.7, ...), custom_call_target="tpu_custom_call" | custom-call | bytes 2097152 | tf_op jit(solution)/shard_map/assemble/pallas_call | solution.py:80
  51.3 1.0 collective-permute-done.12.refs_3_
  52.3 10.1 %early_sums.1.refs_7_ = f32[2,256,2048]{2,1,0:T(8,128)S(1)} custom-call(bf16[4,256,1024]{2,1,0:T(8,128)(2,1)S(1)} %constant_dynamic-slice_fusion.1.refs_0_.refs_1_, bf16[3,256,1024]{2,1,0:T(8,128)(2,1)} %collective-permute-done.3.refs_1_, bf16[4,256,1024]{2,1,0:T(8,128)(2,1)} %collective-permute-done.11.refs_2_.refs_3_, ...), custom_call_target="tpu_custom_call" | custom-call | bytes 2097152 | tf_op jit(solution)/shard_map/early_sums/pallas_call | solution.py:160
  62.5 0.6 collective-permute-done.10.refs_1_.refs_2_
  63.1 1.0 step_pairs.1.refs_5_
  64.1 0.9 collective-permute-done.13.refs_4_
  65.0 5.6 %last_sums.1 = (bf16[1,2,32,2048]{3,2,1,0:T(8,128)(2,1)}, f32[1,2,32,2048]{3,2,1,0:T(8,128)}, bf16[1,2,32,2048]{3,2,1,0:T(8,128)(2,1)}, f32[2,32,2048]{2,1,0:T(8...) custom-call(s32[1]{0:T(128)} %bitcast.refs_0_, ...), custom_call_target="tpu_custom_call" | custom-call | bytes 3145728 | tf_op jit(solution)/shard_map/last_sums/pallas_call | solution.py:331
  70.7 0.6 collective-permute-start.23
  71.3 0.5 collective-permute-start.21
  71.8 1.5 %collective-permute-start.16 = (bf16[2,32,2048]{2,1,0:T(8,128)(2,1)}, bf16[2,32,2048]{2,1,0:T(8,128)(2,1)S(1)}, u32[]{:S(2)}, u32[]{:S(2)}) collective-permute-start(bf16[2,32,2048]{2,1,0:T(8,128)(2,1)} %bitcast.29), channel_id=1, source_target_pairs={{0,1},{1,0},{2,3},{3,2},{4,5},{5,4},{6,7},{7,6},{8,9},{9,8},{10,11... | collective-permute-start | bytes 786440 | tf_op jit(solution)/shard_map/ppermute | solution.py:35
  73.3 1.5 %collective-permute-start.14 = (bf16[1,2,32,2048]{3,2,1,0:T(8,128)(2,1)}, bf16[1,2,32,2048]{3,2,1,0:T(8,128)(2,1)S(1)}, u32[]{:S(2)}, u32[]{:S(2)}) collective-permute-start(bf16[1,2,32,2048]{3,2,1,0:T(8,128)(2,1)} %get-tuple-element.46), channel_id=1, source_target_pairs={{0,2},{2,0},{1,3},{3,1},{4,6},{6,4},{5,7},{7,5},{8,10},{10,8},{9,1... | collective-permute-start | bytes 786440 | tf_op jit(solution)/shard_map/ppermute | solution.py:35
  74.8 5.3 %collective-permute-done.23 = bf16[2,32,2048]{2,1,0:T(8,128)(2,1)S(1)} collective-permute-done((bf16[2,32,2048]{2,1,0:T(8,128)(2,1)}, bf16[2,32,2048]{2,1,0:T(8,128)(2,1)S(1)}, u32[]{:S(2)}, u32[]{:S(2)}) %collective-permute-start.23) | collective-permute-done | bytes 262176 | tf_op jit(solution)/shard_map/ppermute | solution.py:35
  80.1 1.1 %convert_add_fusion = f32[2,32,2048]{2,1,0:T(8,128)S(1)} fusion(f32[2,32,2048]{2,1,0:T(8,128)} %get-tuple-element.51, bf16[2,32,2048]{2,1,0:T(8,128)(2,1)S(1)} %collective-permute-done.23), kind=kLoop, calls=%fused_computation.16 | loop fusion | flops 262144 | bytes 1310720 | tf_op jit(solution)/shard_map/add | solution.py:438
  81.3 0.6 collective-permute-start.24
  82.0 0.6 collective-permute-start.22
  82.6 3.2 %collective-permute-done.16 = bf16[2,32,2048]{2,1,0:T(8,128)(2,1)S(1)} collective-permute-done((bf16[2,32,2048]{2,1,0:T(8,128)(2,1)}, bf16[2,32,2048]{2,1,0:T(8,128)(2,1)S(1)}, u32[]{:S(2)}, u32[]{:S(2)}) %collective-permute-start.16) | collective-permute-done | bytes 262176 | tf_op jit(solution)/shard_map/ppermute | solution.py:35
  85.8 0.6 collective-permute-start.17
  86.5 1.4 %collective-permute-start.15 = (bf16[1,32,2048]{2,1,0:T(8,128)(2,1)S(1)}, bf16[1,32,2048]{2,1,0:T(8,128)(2,1)S(1)}, u32[]{:S(2)}, u32[]{:S(2)}) collective-permute-start(bf16[1,32,2048]{2,1,0:T(8,128)(2,1)S(1)} %fusion), channel_id=1, source_target_pairs={{0,1},{1,0},{2,3},{3,2},{4,5},{5,4},{6,7},{7,6},{8,9},{9,8},{10,11... | collective-permute-start | bytes 393224 | tf_op jit(solution)/shard_map/ppermute | solution.py:35
  88.0 0.9 collective-permute-done.24
  89.1 3.4 %collective-permute-start.25 = (bf16[1,64,512]{2,1,0:T(8,128)(2,1)S(1)}, bf16[1,64,512]{2,1,0:T(8,128)(2,1)S(1)}, u32[]{:S(2)}, u32[]{:S(2)}) collective-permute-start(bf16[1,64,512]{2,1,0:T(8,128)(2,1)S(1)} %get-tuple-element.53), channel_id=1, source_target_pairs={{0,8},{4,12},{8,16},{12,20},{16,24},{20,28},{24,0},{28,4},{1,9},{5... | collective-permute-start | bytes 196616 | tf_op jit(solution)/shard_map/ppermute | solution.py:35
  92.5 3.4 %collective-permute-start.26 = (bf16[1,64,512]{2,1,0:T(8,128)(2,1)S(1)}, bf16[1,64,512]{2,1,0:T(8,128)(2,1)S(1)}, u32[]{:S(2)}, u32[]{:S(2)}) collective-permute-start(bf16[1,64,512]{2,1,0:T(8,128)(2,1)S(1)} %get-tuple-element.54), channel_id=1, source_target_pairs={{0,16},{4,20},{8,24},{12,28},{16,0},{20,4},{24,8},{28,12},{1,17},{... | collective-permute-start | bytes 196616 | tf_op jit(solution)/shard_map/ppermute | solution.py:35
  96.2 2.1 %collective-permute-start.18 = (bf16[1,64,512]{2,1,0:T(8,128)(2,1)S(1)}, bf16[1,64,512]{2,1,0:T(8,128)(2,1)S(1)}, u32[]{:S(2)}, u32[]{:S(2)}) collective-permute-start(bf16[1,64,512]{2,1,0:T(8,128)(2,1)S(1)} %get-tuple-element.56), channel_id=1, source_target_pairs={{0,8},{4,12},{8,16},{12,20},{16,24},{20,28},{24,0},{28,4},{1,9},{5... | collective-permute-start | bytes 196616 | tf_op jit(solution)/shard_map/ppermute | solution.py:35
  98.6 2.1 %collective-permute-start.20 = (bf16[1,64,512]{2,1,0:T(8,128)(2,1)S(1)}, bf16[1,64,512]{2,1,0:T(8,128)(2,1)S(1)}, u32[]{:S(2)}, u32[]{:S(2)}) collective-permute-start(bf16[1,64,512]{2,1,0:T(8,128)(2,1)S(1)} %get-tuple-element.58), channel_id=1, source_target_pairs={{0,24},{4,28},{8,0},{12,4},{16,8},{20,12},{24,16},{28,20},{1,25},{... | collective-permute-start | bytes 196616 | tf_op jit(solution)/shard_map/ppermute | solution.py:35
  100.7 0.7 collective-permute-done.26
  101.3 1.2 %collective-permute-done.27 = bf16[1,64,512]{2,1,0:T(8,128)(2,1)S(1)} collective-permute-done((bf16[1,64,512]{2,1,0:T(8,128)(2,1)S(1)}, bf16[1,64,512]{2,1,0:T(8,128)(2,1)S(1)}, u32[]{:S(2)}, u32[]{:S(2)}) %collective-permute-start.27) | collective-permute-done | bytes 65568 | tf_op jit(solution)/shard_map/ppermute | solution.py:35
  102.7 2.2 %collective-permute-done.19 = bf16[1,64,512]{2,1,0:T(8,128)(2,1)S(1)} collective-permute-done((bf16[1,64,512]{2,1,0:T(8,128)(2,1)S(1)}, bf16[1,64,512]{2,1,0:T(8,128)(2,1)S(1)}, u32[]{:S(2)}, u32[]{:S(2)}) %collective-permute-start.19) | collective-permute-done | bytes 65568 | tf_op jit(solution)/shard_map/ppermute | solution.py:35
  105.1 1.3 %collective-permute-done.28 = f32[1,128,256]{2,1,0:T(8,128)S(1)} collective-permute-done((f32[1,128,256]{2,1,0:T(8,128)S(1)}, f32[1,128,256]{2,1,0:T(8,128)S(1)}, u32[]{:S(2)}, u32[]{:S(2)}) %collective-permute-start.28) | collective-permute-done | bytes 131104 | tf_op jit(solution)/shard_map/ppermute | solution.py:39
  106.4 0.7 maximum_select_fusion.1
  (58 shorter events, 2.8 us)
Async XLA Ops:
  0.0 1.0 copy-start
  1.1 6.5 %collective-permute-start = (bf16[2,128,256]{2,1,0:T(8,128)(2,1)S(1)}, bf16[2,128,256]{2,1,0:T(8,128)(2,1)S(1)}, u32[]{:S(2)}, u32[]{:S(2)}) collective-permute-start(bf16[2,128,256]{2,1,0:T(8,128)(2,1)S(1)} %dynamic-slice_convert_fusion.2), channel_id=1, source_target_pairs={{0,2},{2,0},{1,3},{3,1},{4,6},{6,4},{5,7},{7,5},{8,10},{10,8},{9,1... | collective-permute-start | bytes 393224 | tf_op jit(solution)/shard_map/ppermute | solution.py:35
  7.6 40.3 %collective-permute-start.3 = (bf16[3,256,1024]{2,1,0:T(8,128)(2,1)}, bf16[3,256,1024]{2,1,0:T(8,128)(2,1)}, u32[]{:S(2)}, u32[]{:S(2)}) collective-permute-start(bf16[3,256,1024]{2,1,0:T(8,128)(2,1)} %constant_dynamic-slice_fusion.2), channel_id=1, source_target_pairs={{0,2},{2,0},{1,3},{3,1},{4,6},{6,4},{5,7},{7,5},{8,10},{10,8},{9,1... | collective-permute-start | bytes 4718600 | tf_op jit(solution)/shard_map/ppermute | solution.py:35
  9.4 1.4 %collective-permute-start.1 = (bf16[2,1,128,256]{3,2,0,1:T(8,128)(2,1)S(1)}, bf16[2,1,128,256]{3,2,0,1:T(8,128)(2,1)S(1)}, u32[]{:S(2)}, u32[]{:S(2)}) collective-permute-start(bf16[2,1,128,256]{3,2,0,1:T(8,128)(2,1)S(1)} %get-tuple-element.62), channel_id=1, source_target_pairs={{0,4},{4,0},{8,12},{12,8},{16,20},{20,16},{24,28},{28,24},{1,5},{5... | collective-permute-start | bytes 393224 | tf_op jit(solution)/shard_map/ppermute | solution.py:39
  10.9 10.3 %copy-start.1 = (bf16[2,128,512]{2,1,0:T(8,128)(2,1)}, bf16[2,128,512]{2,1,0:T(8,128)(2,1)S(1)}, u32[]{:S(2)}) copy-start(bf16[2,128,512]{2,1,0:T(8,128)(2,1)S(1)} %maximum_select_fusion.refs_0_) | copy-start | bytes 786436
  10.9 8.4 %collective-permute-start.2 = (bf16[2,128,512]{2,1,0:T(8,128)(2,1)S(1)}, bf16[2,128,512]{2,1,0:T(8,128)(2,1)S(1)}, u32[]{:S(2)}, u32[]{:S(2)}) collective-permute-start(bf16[2,128,512]{2,1,0:T(8,128)(2,1)S(1)} %maximum_select_fusion.refs_0_), channel_id=1, source_target_pairs={{0,1},{1,0},{2,3},{3,2},{4,5},{5,4},{6,7},{7,6},{8,9},{9,8},{10,11... | collective-permute-start | bytes 786440 | tf_op jit(solution)/shard_map/ppermute | solution.py:35
  12.5 11.1 %collective-permute-start.4 = (bf16[2,128,512]{2,1,0:T(8,128)(2,1)S(1)}, bf16[2,128,512]{2,1,0:T(8,128)(2,1)S(1)}, u32[]{:S(2)}, u32[]{:S(2)}) collective-permute-start(bf16[2,128,512]{2,1,0:T(8,128)(2,1)S(1)} %maximum_select_fusion.refs_0_), channel_id=1, source_target_pairs={{0,8},{4,12},{8,16},{12,20},{16,24},{20,28},{24,0},{28,4},{1,9},{5... | collective-permute-start | bytes 786440 | tf_op jit(solution)/shard_map/ppermute | solution.py:35
  14.1 19.8 %collective-permute-start.6 = (bf16[2,128,512]{2,1,0:T(8,128)(2,1)S(1)}, bf16[2,128,512]{2,1,0:T(8,128)(2,1)}, u32[]{:S(2)}, u32[]{:S(2)}) collective-permute-start(bf16[2,128,512]{2,1,0:T(8,128)(2,1)S(1)} %maximum_select_fusion.refs_0_), channel_id=1, source_target_pairs={{0,16},{4,20},{8,24},{12,28},{16,0},{20,4},{24,8},{28,12},{1,17},{... | collective-permute-start | bytes 786440 | tf_op jit(solution)/shard_map/ppermute | solution.py:35
  16.7 17.8 %collective-permute-start.8 = (bf16[2,128,512]{2,1,0:T(8,128)(2,1)S(1)}, bf16[2,128,512]{2,1,0:T(8,128)(2,1)}, u32[]{:S(2)}, u32[]{:S(2)}) collective-permute-start(bf16[2,128,512]{2,1,0:T(8,128)(2,1)S(1)} %maximum_select_fusion.refs_0_), channel_id=1, source_target_pairs={{0,24},{4,28},{8,0},{12,4},{16,8},{20,12},{24,16},{28,20},{1,25},{... | collective-permute-start | bytes 786440 | tf_op jit(solution)/shard_map/ppermute | solution.py:35
  19.3 1.9 %copy-start.5 = (bf16[2,128,512]{2,1,0:T(8,128)(2,1)}, bf16[2,128,512]{2,1,0:T(8,128)(2,1)S(1)}, u32[]{:S(2)}) copy-start(bf16[2,128,512]{2,1,0:T(8,128)(2,1)S(1)} %collective-permute-done.2.refs_1_) | copy-start | bytes 786436
  21.2 30.1 %collective-permute-start.11 = (bf16[4,256,1024]{2,1,0:T(8,128)(2,1)S(1)}, bf16[4,256,1024]{2,1,0:T(8,128)(2,1)}, u32[]{:S(2)}, u32[]{:S(2)}) collective-permute-start(bf16[4,256,1024]{2,1,0:T(8,128)(2,1)S(1)} %constant_dynamic-slice_fusion.1.refs_0_.refs_1_), channel_id=1, source_target_pairs={{0,4},{4,0},{8,12},{12,8},{16,20},{20,16},{24,28},{28,24},{1,5},{5... | collective-permute-start | bytes 6291464 | tf_op jit(solution)/shard_map/ppermute | solution.py:39
  23.6 24.3 %copy-start.6 = (bf16[2,128,512]{2,1,0:T(8,128)(2,1)}, bf16[2,128,512]{2,1,0:T(8,128)(2,1)S(1)}, u32[]{:S(2)}) copy-start(bf16[2,128,512]{2,1,0:T(8,128)(2,1)S(1)} %collective-permute-done.4.refs_2_) | copy-start | bytes 786436
  23.6 14.2 %collective-permute-start.5 = (bf16[2,128,512]{2,1,0:T(8,128)(2,1)S(1)}, bf16[2,128,512]{2,1,0:T(8,128)(2,1)S(1)}, u32[]{:S(2)}, u32[]{:S(2)}) collective-permute-start(bf16[2,128,512]{2,1,0:T(8,128)(2,1)S(1)} %collective-permute-done.4.refs_2_), channel_id=1, source_target_pairs={{0,1},{1,0},{2,3},{3,2},{4,5},{5,4},{6,7},{7,6},{8,9},{9,8},{10,11... | collective-permute-start | bytes 786440 | tf_op jit(solution)/shard_map/ppermute | solution.py:35
  33.9 9.5 %collective-permute-start.7 = (bf16[2,128,512]{2,1,0:T(8,128)(2,1)}, bf16[2,128,512]{2,1,0:T(8,128)(2,1)}, u32[]{:S(2)}, u32[]{:S(2)}) collective-permute-start(bf16[2,128,512]{2,1,0:T(8,128)(2,1)} %collective-permute-done.6.refs_4_), channel_id=1, source_target_pairs={{0,1},{1,0},{2,3},{3,2},{4,5},{5,4},{6,7},{7,6},{8,9},{9,8},{10,11... | collective-permute-start | bytes 786440 | tf_op jit(solution)/shard_map/ppermute | solution.py:35
  34.4 13.5 %collective-permute-start.9 = (bf16[2,128,512]{2,1,0:T(8,128)(2,1)}, bf16[2,128,512]{2,1,0:T(8,128)(2,1)S(1)}, u32[]{:S(2)}, u32[]{:S(2)}) collective-permute-start(bf16[2,128,512]{2,1,0:T(8,128)(2,1)} %collective-permute-done.8.refs_6_), channel_id=1, source_target_pairs={{0,1},{1,0},{2,3},{3,2},{4,5},{5,4},{6,7},{7,6},{8,9},{9,8},{10,11... | collective-permute-start | bytes 786440 | tf_op jit(solution)/shard_map/ppermute | solution.py:35
  37.8 11.4 %copy-start.7 = (bf16[2,128,512]{2,1,0:T(8,128)(2,1)}, bf16[2,128,512]{2,1,0:T(8,128)(2,1)S(1)}, u32[]{:S(2)}) copy-start(bf16[2,128,512]{2,1,0:T(8,128)(2,1)S(1)} %collective-permute-done.5.refs_3_) | copy-start | bytes 786436
  47.9 0.7 copy-start.8
  48.6 3.8 %collective-permute-start.12 = (bf16[3,256,1024]{2,1,0:T(8,128)(2,1)}, bf16[3,256,1024]{2,1,0:T(8,128)(2,1)}, u32[]{:S(2)}, u32[]{:S(2)}) collective-permute-start(bf16[3,256,1024]{2,1,0:T(8,128)(2,1)} %collective-permute-done.3.refs_1_), channel_id=1, source_target_pairs={{0,4},{4,0},{8,12},{12,8},{16,20},{20,16},{24,28},{28,24},{1,5},{5... | collective-permute-start | bytes 4718600 | tf_op jit(solution)/shard_map/ppermute | solution.py:39
  48.6 14.5 %collective-permute-start.10 = (bf16[1,256,1024]{2,1,0:T(8,128)(2,1)}, bf16[1,256,1024]{2,1,0:T(8,128)(2,1)S(1)}, u32[]{:S(2)}, u32[]{:S(2)}) collective-permute-start(bf16[1,256,1024]{2,1,0:T(8,128)(2,1)} %constant_dynamic-slice_fusion), channel_id=1, source_target_pairs={{0,2},{2,0},{1,3},{3,1},{4,6},{6,4},{5,7},{7,5},{8,10},{10,8},{9,1... | collective-permute-start | bytes 1572872 | tf_op jit(solution)/shard_map/ppermute | solution.py:35
  63.1 1.9 %collective-permute-start.13 = (bf16[1,256,1024]{2,1,0:T(8,128)(2,1)S(1)}, bf16[1,256,1024]{2,1,0:T(8,128)(2,1)S(1)}, u32[]{:S(2)}, u32[]{:S(2)}) collective-permute-start(bf16[1,256,1024]{2,1,0:T(8,128)(2,1)S(1)} %collective-permute-done.10.refs_1_.refs_2_), channel_id=1, source_target_pairs={{0,4},{4,0},{8,12},{12,8},{16,20},{20,16},{24,28},{28,24},{1,5},{5... | collective-permute-start | bytes 1572872 | tf_op jit(solution)/shard_map/ppermute | solution.py:39
  70.7 11.2 %copy-start.4 = (f32[1,2,32,2048]{3,2,1,0:T(8,128)S(1)}, f32[1,2,32,2048]{3,2,1,0:T(8,128)}, u32[]{:S(2)}) copy-start(f32[1,2,32,2048]{3,2,1,0:T(8,128)} %get-tuple-element.49) | copy-start | bytes 1572868
  70.7 15.1 %copy-start.3 = (f32[2,32,2048]{2,1,0:T(8,128)S(1)}, f32[2,32,2048]{2,1,0:T(8,128)}, u32[]{:S(2)}) copy-start(f32[2,32,2048]{2,1,0:T(8,128)} %get-tuple-element.47) | copy-start | bytes 1572868
  70.7 9.4 %collective-permute-start.23 = (bf16[2,32,2048]{2,1,0:T(8,128)(2,1)}, bf16[2,32,2048]{2,1,0:T(8,128)(2,1)S(1)}, u32[]{:S(2)}, u32[]{:S(2)}) collective-permute-start(bf16[2,32,2048]{2,1,0:T(8,128)(2,1)} %bitcast.30), channel_id=1, source_target_pairs={{0,1},{1,0},{2,3},{3,2},{4,5},{5,4},{6,7},{7,6},{8,9},{9,8},{10,11... | collective-permute-start | bytes 786440 | tf_op jit(solution)/shard_map/ppermute | solution.py:35
  71.3 10.6 %collective-permute-start.21 = (bf16[1,2,32,2048]{3,2,1,0:T(8,128)(2,1)}, bf16[1,2,32,2048]{3,2,1,0:T(8,128)(2,1)S(1)}, u32[]{:S(2)}, u32[]{:S(2)}) collective-permute-start(bf16[1,2,32,2048]{3,2,1,0:T(8,128)(2,1)} %get-tuple-element.50), channel_id=1, source_target_pairs={{0,2},{2,0},{1,3},{3,1},{4,6},{6,4},{5,7},{7,5},{8,10},{10,8},{9,1... | collective-permute-start | bytes 786440 | tf_op jit(solution)/shard_map/ppermute | solution.py:35
  71.8 13.9 %collective-permute-start.16 = (bf16[2,32,2048]{2,1,0:T(8,128)(2,1)}, bf16[2,32,2048]{2,1,0:T(8,128)(2,1)S(1)}, u32[]{:S(2)}, u32[]{:S(2)}) collective-permute-start(bf16[2,32,2048]{2,1,0:T(8,128)(2,1)} %bitcast.29), channel_id=1, source_target_pairs={{0,1},{1,0},{2,3},{3,2},{4,5},{5,4},{6,7},{7,6},{8,9},{9,8},{10,11... | collective-permute-start | bytes 786440 | tf_op jit(solution)/shard_map/ppermute | solution.py:35
  73.3 13.1 %collective-permute-start.14 = (bf16[1,2,32,2048]{3,2,1,0:T(8,128)(2,1)}, bf16[1,2,32,2048]{3,2,1,0:T(8,128)(2,1)S(1)}, u32[]{:S(2)}, u32[]{:S(2)}) collective-permute-start(bf16[1,2,32,2048]{3,2,1,0:T(8,128)(2,1)} %get-tuple-element.46), channel_id=1, source_target_pairs={{0,2},{2,0},{1,3},{3,1},{4,6},{6,4},{5,7},{7,5},{8,10},{10,8},{9,1... | collective-permute-start | bytes 786440 | tf_op jit(solution)/shard_map/ppermute | solution.py:35
  80.1 6.3 %copy-start.2 = (f32[1,2,32,2048]{3,2,1,0:T(8,128)S(1)}, f32[1,2,32,2048]{3,2,1,0:T(8,128)}, u32[]{:S(2)}) copy-start(f32[1,2,32,2048]{3,2,1,0:T(8,128)} %get-tuple-element.45) | copy-start | bytes 1572868
  81.3 7.6 %collective-permute-start.24 = (bf16[1,32,2048]{2,1,0:T(8,128)(2,1)S(1)}, bf16[1,32,2048]{2,1,0:T(8,128)(2,1)S(1)}, u32[]{:S(2)}, u32[]{:S(2)}) collective-permute-start(bf16[1,32,2048]{2,1,0:T(8,128)(2,1)S(1)} %slice.26), channel_id=1, source_target_pairs={{0,2},{2,0},{1,3},{3,1},{4,6},{6,4},{5,7},{7,5},{8,10},{10,8},{9,1... | collective-permute-start | bytes 393224 | tf_op jit(solution)/shard_map/ppermute | solution.py:35
  82.0 6.9 %collective-permute-start.22 = (bf16[1,32,2048]{2,1,0:T(8,128)(2,1)S(1)}, bf16[1,32,2048]{2,1,0:T(8,128)(2,1)S(1)}, u32[]{:S(2)}, u32[]{:S(2)}) collective-permute-start(bf16[1,32,2048]{2,1,0:T(8,128)(2,1)S(1)} %fusion.1), channel_id=1, source_target_pairs={{0,1},{1,0},{2,3},{3,2},{4,5},{5,4},{6,7},{7,6},{8,9},{9,8},{10,11... | collective-permute-start | bytes 393224 | tf_op jit(solution)/shard_map/ppermute | solution.py:35
  85.8 10.1 %collective-permute-start.17 = (bf16[1,32,2048]{2,1,0:T(8,128)(2,1)S(1)}, bf16[1,32,2048]{2,1,0:T(8,128)(2,1)S(1)}, u32[]{:S(2)}, u32[]{:S(2)}) collective-permute-start(bf16[1,32,2048]{2,1,0:T(8,128)(2,1)S(1)} %slice.27), channel_id=1, source_target_pairs={{0,2},{2,0},{1,3},{3,1},{4,6},{6,4},{5,7},{7,5},{8,10},{10,8},{9,1... | collective-permute-start | bytes 393224 | tf_op jit(solution)/shard_map/ppermute | solution.py:35
  86.5 9.4 %collective-permute-start.15 = (bf16[1,32,2048]{2,1,0:T(8,128)(2,1)S(1)}, bf16[1,32,2048]{2,1,0:T(8,128)(2,1)S(1)}, u32[]{:S(2)}, u32[]{:S(2)}) collective-permute-start(bf16[1,32,2048]{2,1,0:T(8,128)(2,1)S(1)} %fusion), channel_id=1, source_target_pairs={{0,1},{1,0},{2,3},{3,2},{4,5},{5,4},{6,7},{7,6},{8,9},{9,8},{10,11... | collective-permute-start | bytes 393224 | tf_op jit(solution)/shard_map/ppermute | solution.py:35
  89.1 9.4 %collective-permute-start.25 = (bf16[1,64,512]{2,1,0:T(8,128)(2,1)S(1)}, bf16[1,64,512]{2,1,0:T(8,128)(2,1)S(1)}, u32[]{:S(2)}, u32[]{:S(2)}) collective-permute-start(bf16[1,64,512]{2,1,0:T(8,128)(2,1)S(1)} %get-tuple-element.53), channel_id=1, source_target_pairs={{0,8},{4,12},{8,16},{12,20},{16,24},{20,28},{24,0},{28,4},{1,9},{5... | collective-permute-start | bytes 196616 | tf_op jit(solution)/shard_map/ppermute | solution.py:35
  92.5 8.8 %collective-permute-start.26 = (bf16[1,64,512]{2,1,0:T(8,128)(2,1)S(1)}, bf16[1,64,512]{2,1,0:T(8,128)(2,1)S(1)}, u32[]{:S(2)}, u32[]{:S(2)}) collective-permute-start(bf16[1,64,512]{2,1,0:T(8,128)(2,1)S(1)} %get-tuple-element.54), channel_id=1, source_target_pairs={{0,16},{4,20},{8,24},{12,28},{16,0},{20,4},{24,8},{28,12},{1,17},{... | collective-permute-start | bytes 196616 | tf_op jit(solution)/shard_map/ppermute | solution.py:35
  95.9 6.6 %collective-permute-start.27 = (bf16[1,64,512]{2,1,0:T(8,128)(2,1)S(1)}, bf16[1,64,512]{2,1,0:T(8,128)(2,1)S(1)}, u32[]{:S(2)}, u32[]{:S(2)}) collective-permute-start(bf16[1,64,512]{2,1,0:T(8,128)(2,1)S(1)} %get-tuple-element.55), channel_id=1, source_target_pairs={{0,24},{4,28},{8,0},{12,4},{16,8},{20,12},{24,16},{28,20},{1,25},{... | collective-permute-start | bytes 196616 | tf_op jit(solution)/shard_map/ppermute | solution.py:35
  96.2 6.5 %collective-permute-start.18 = (bf16[1,64,512]{2,1,0:T(8,128)(2,1)S(1)}, bf16[1,64,512]{2,1,0:T(8,128)(2,1)S(1)}, u32[]{:S(2)}, u32[]{:S(2)}) collective-permute-start(bf16[1,64,512]{2,1,0:T(8,128)(2,1)S(1)} %get-tuple-element.56), channel_id=1, source_target_pairs={{0,8},{4,12},{8,16},{12,20},{16,24},{20,28},{24,0},{28,4},{1,9},{5... | collective-permute-start | bytes 196616 | tf_op jit(solution)/shard_map/ppermute | solution.py:35
  98.2 6.6 %collective-permute-start.19 = (bf16[1,64,512]{2,1,0:T(8,128)(2,1)S(1)}, bf16[1,64,512]{2,1,0:T(8,128)(2,1)S(1)}, u32[]{:S(2)}, u32[]{:S(2)}) collective-permute-start(bf16[1,64,512]{2,1,0:T(8,128)(2,1)S(1)} %get-tuple-element.57), channel_id=1, source_target_pairs={{0,16},{4,20},{8,24},{12,28},{16,0},{20,4},{24,8},{28,12},{1,17},{... | collective-permute-start | bytes 196616 | tf_op jit(solution)/shard_map/ppermute | solution.py:35
  98.6 6.3 %collective-permute-start.20 = (bf16[1,64,512]{2,1,0:T(8,128)(2,1)S(1)}, bf16[1,64,512]{2,1,0:T(8,128)(2,1)S(1)}, u32[]{:S(2)}, u32[]{:S(2)}) collective-permute-start(bf16[1,64,512]{2,1,0:T(8,128)(2,1)S(1)} %get-tuple-element.58), channel_id=1, source_target_pairs={{0,24},{4,28},{8,0},{12,4},{16,8},{20,12},{24,16},{28,20},{1,25},{... | collective-permute-start | bytes 196616 | tf_op jit(solution)/shard_map/ppermute | solution.py:35
  105.0 1.4 %collective-permute-start.28 = (f32[1,128,256]{2,1,0:T(8,128)S(1)}, f32[1,128,256]{2,1,0:T(8,128)S(1)}, u32[]{:S(2)}, u32[]{:S(2)}) collective-permute-start(f32[1,128,256]{2,1,0:T(8,128)S(1)} %get-tuple-element.60), channel_id=1, source_target_pairs={{0,4},{4,0},{8,12},{12,8},{16,20},{20,16},{24,28},{28,24},{1,5},{5... | collective-permute-start | bytes 393224 | tf_op jit(solution)/shard_map/ppermute | solution.py:39

commit v7 on v6

--- a/solution.py
+++ b/solution.py
@@ -7,7 +7,7 @@
 
 CORES = 2
 PIECES = 2
-VMEM_LIMIT = 28 * 2**20
+VMEM_LIMIT = 20 * 2**20
 F32, BF16 = jnp.float32, jnp.bfloat16
 VMEM = pl.BlockSpec(memory_space=pltpu.VMEM)
 ANY = pl.BlockSpec(memory_space=pl.ANY)
@@ -115,11 +115,9 @@
     tiles = total // tile
 
     def body(*refs):
-        vec_in, out = refs[n : n + 2]
-        vec, held, done, sems, out_sems = refs[-5:]
+        vec, out = refs[n : n + 2]
+        held, sems = refs[-2:]
         ins = refs[n + 2 : n + 2 + ns]
-        first = pltpu.make_async_copy(vec_in, vec, sems.at[n])
-        first.start()
         copies, i = [], 0
         for slot, pieces in zip(ins, slots):
             group, at = [], 0
@@ -130,7 +128,6 @@
                 group[-1].start()
                 i, at = i + 1, at + size
             copies.append(group)
-        first.wait()
         for s in range(len(sides)):
 
             def store(g, k, pair, s=s):
@@ -140,7 +137,6 @@
                 for copy in group:
                     copy.wait()
             pairs_of(ins[s * nr : (s + 1) * nr], vec, store)
-        sent = []
         for i in range(tiles):
             r, at = i * tile // width, i * tile % width
             acc = None
@@ -148,27 +144,17 @@
                 right = ins[s * nr + r][:, :, at : at + tile].reshape(steps * rows, tile)
                 term = jnp.dot(held[s], right, preferred_element_type=F32)
                 acc = term if acc is None else acc + term
-            cols = pl.ds(i * tile, tile)
-            done[:, :, cols] = acc.reshape(groups, rows, tile)
-            sent.append(
-                pltpu.make_async_copy(done.at[:, :, cols], out.at[:, :, cols], out_sems.at[i])
-            )
-            sent[-1].start()
-        for copy in sent:
-            copy.wait()
+            out[:, :, i * tile : (i + 1) * tile] = acc.reshape(groups, rows, tile)
 
     return pl.pallas_call(
         body,
         out_shape=shape,
-        in_specs=[ANY] * (n + 1),
-        out_specs=ANY,
+        in_specs=[ANY] * n + [VMEM],
+        out_specs=VMEM,
         scratch_shapes=[pltpu.VMEM((steps, rows, width), BF16)] * ns
         + [
-            pltpu.VMEM(vectors.shape, BF16),
             pltpu.VMEM((len(sides), groups * rows, steps * rows), BF16),
-            pltpu.VMEM(shape.shape, F32),
-            pltpu.SemaphoreType.DMA((n + 1,)),
-            pltpu.SemaphoreType.DMA((tiles,)),
+            pltpu.SemaphoreType.DMA((n,)),
         ],
         cost_estimate=cost(0, vectors),
         compiler_params=params(),
@@ -183,10 +169,10 @@
     width = total // n
 
     def body(*refs):
-        vec_in, out = refs[n : n + 2]
+        vec, out = refs[n : n + 2]
         ins = refs[n + 2 : 2 * n + 2]
-        vec, sems = refs[-2:]
-        copies = [pltpu.make_async_copy(vec_in, vec, sems.at[n])] + [
+        sems = refs[-1]
+        copies = [
             pltpu.make_async_copy(refs[i].at[pl.ds(firsts[i], 1)], ins[i], sems.at[i])
             for i in range(n)
         ]
@@ -203,10 +189,10 @@
     return pl.pallas_call(
         body,
         out_shape=shape,
-        in_specs=[ANY] * (n + 1),
+        in_specs=[ANY] * n + [VMEM],
         out_specs=VMEM,
         scratch_shapes=[pltpu.VMEM((1, rows, width), BF16)] * n
-        + [pltpu.VMEM(vectors.shape, BF16), pltpu.SemaphoreType.DMA((n + 1,))],
+        + [pltpu.SemaphoreType.DMA((n,))],
         cost_estimate=cost(0, vectors),
         compiler_params=params(),
         name="step_pairs",
@@ -229,31 +215,18 @@
     def body(*refs):
         me = refs[0][0]
         refs = refs[1:]
-        pair_in, vec_in = refs[n : n + 2]
+        own_pair, vec = refs[n : n + 2]
+        before = refs[n + 2] if more else None
         results = refs[n + 2 + len(more) : n + 2 + len(more) + 4 * PIECES]
         outs = refs[n + 2 + len(more) + 4 * PIECES : n + 2 + len(more) + 8 * PIECES]
-        ins = refs[-n - 7 : -7]
-        vec, own_pair, their_pair, before, sems, early_sems, out_sems = refs[-7:]
+        ins = refs[-n - 3 : -3]
+        their_pair, sems, out_sems = refs[-3:]
         copies = [
             pltpu.make_async_copy(refs[i].at[pl.ds(firsts[i % nr], 1)], ins[i], sems.at[i])
             for i in range(n)
         ]
-        vec_copy = pltpu.make_async_copy(vec_in, vec, sems.at[n])
-        pair_copy = pltpu.make_async_copy(pair_in, own_pair, sems.at[n + 1])
-        vec_copy.start()
         for copy in copies[nr:] + copies[:nr]:
             copy.start()
-        pair_copy.start()
-        early_copies = []
-        for i in range(tiles if more else 0):
-            cols = pl.ds(i * tile, tile)
-            early_copies.append(
-                pltpu.make_async_copy(
-                    refs[n + 2].at[:, :, cols], before.at[:, :, cols], early_sems.at[i]
-                )
-            )
-            early_copies[-1].start()
-        vec_copy.wait()
         for copy in copies[nr:]:
             copy.wait()
 
@@ -263,7 +236,6 @@
         pairs_of(ins[nr:], vec, store)
         for copy in copies[:nr]:
             copy.wait()
-        pair_copy.wait()
         left = [p[...].reshape(groups * rows, rows) for p in (own_pair, their_pair)]
         sent = []
         for i in range(tiles):
@@ -275,7 +247,6 @@
                 got = term if got is None else got + term
             got = got.reshape(groups, rows, tile)
             if more:
-                early_copies[i].wait()
                 got = got + before[:, :, i * tile : (i + 1) * tile]
             got = got.reshape(groups, no, PIECES, 2, small, tile)
             for g in range(groups):
@@ -331,17 +302,13 @@
     outs = pl.pallas_call(
         body,
         out_shape=[pltpu.HBM(x.shape, x.dtype) for x in shapes],
-        in_specs=[SMEM] + [ANY] * (n + 2 + len(more)),
+        in_specs=[SMEM] + [ANY] * n + [VMEM] * (2 + len(more)),
         out_specs=[HBM] * len(shapes),
         scratch_shapes=[pltpu.VMEM(x.shape, x.dtype) for x in shapes]
         + [pltpu.VMEM((1, rows, width), BF16)] * n
         + [
-            pltpu.VMEM(vectors.shape, BF16),
             pltpu.VMEM((groups, rows, rows), BF16),
-            pltpu.VMEM((groups, rows, rows), BF16),
-            pltpu.VMEM(vectors.shape if more else (8, 128), F32),
-            pltpu.SemaphoreType.DMA((n + 2,)),
-            pltpu.SemaphoreType.DMA((tiles,)),
+            pltpu.SemaphoreType.DMA((n,)),
             pltpu.SemaphoreType.DMA((tiles * nv * PIECES * 3,)),
         ],
         cost_estimate=cost(0, *shapes),
@@ -391,9 +358,9 @@
     ).reshape(groups, own, block)
     later, whole = lax.optimization_barrier((factors, whole))
 
-    steps = [whole] + [shift(whole, "aux", na, t, CORES) for t in range(1, nz)]
     blocks = []
-    for t, got in enumerate(steps):
+    for t in sorted(range(nz), key=lambda t: min(t, nz - t)):
+        got = whole if t == 0 else shift(whole, "aux", na, t, CORES)
         blocks.append((got, 0, nz, t))
         for s in range(1, no):
             blocks.append((shift(got, "outer", no, -s), 0, nz + s, t))
@@ -403,9 +370,8 @@
     ).astype(jnp.int32)
     later, _ = lax.optimization_barrier((factors, blocks[no - 1][0]))
     held = (come, sends(later, early_steps, last_steps), [b[0] for b in blocks])
-    come, group, arrays = lax.optimization_barrier(held)
+    come, group, _ = lax.optimization_barrier(held)
     come_last = along_vir(group)
-    blocks = [(x, *b[1:]) for x, b in zip(arrays, blocks)]
     vectors = assemble(where, blocks, groups, rows, total)
 
     kept = lax.dynamic_slice_in_dim(later, v * take, take, 0)

time: 107 us -> 104 us (0.972)
  starting transfers between devices: 33.8 us -> 29.9 us
  waiting for transfers between devices: 43 us -> 45.9 us
  Pallas kernels: 18.9 us -> 16.4 us
    ppermute x24, starting transfers between devices: 33.6 us -> 29.7 us  [shift(): return lax.ppermute(array, axis, pairs)]
    ppermute x24, waiting for transfers between devices: 38.4 us -> 41.2 us  [shift(): return lax.ppermute(array, axis, pairs)]
    pallas_call x2, Pallas kernels: 11.1 us -> 9.27 us  [the longest x1 8.44 us: early_sums(): pl.pallas_call(body, out_shape=shape, in_specs=[ANY] * n + [VMEM], out_sp...]
  transfers between devices with their start and end apart: 29 -> 29, of which waited for: 17 -> 16; matrix products, arithmetic and copies ran while one was open for 8% -> 8% of each run, Pallas kernels for 12% -> 11%
where the time goes in v7:
time: 104 us
  waiting for transfers between devices  45.9 us (44%)
  starting transfers between devices  29.9 us (29%)
  Pallas kernels  16.4 us (16%)
  local copies, waits for them, and re-layouts  8.39 us (8%)
  other arithmetic  2.81 us (3%)
    ppermute x24, waiting for transfers between devices, shift(): return lax.ppermute(array, axis, pairs)  41.2 us
    ppermute x24, starting transfers between devices, shift(): return lax.ppermute(array, axis, pairs)  29.7 us
    pallas_call x1, Pallas kernels, early_sums(): pl.pallas_call(body, out_shape=shape, in_specs=[ANY] * n + [VMEM], out_sp...  8.44 us
    pallas_call x1, Pallas kernels, last_sums(): pl.pallas_call(body, out_shape=[pltpu.HBM(x.shape, x.dtype) for x in shap...  4.96 us
    ppermute x5, waiting for transfers between devices, sibling(): return lax.ppermute(array, 'aux', [(i, i ^ 1) for i in range(size)])  4.72 us
    dynamic_slice x2, local copies, waits for them, and re-layouts, sends(): lax.dynamic_slice_in_dim(source, (v - r) % nv * take + first, size, 0)  4.57 us
    pallas_call x1, Pallas kernels, assemble(): pl.pallas_call(body, out_shape=shape, in_specs=[SMEM] + [ANY] * len(block...  2.13 us
  transfers between devices with their start and end apart: 29, of which 16 were waited for; matrix products, arithmetic and copies ran while one was open for 8% of the time, Pallas kernels for 11%

profile of v7, /device:TPU:0, one launch (start us, length us, event | category | flops | bytes accessed | tf_op | source)
XLA Modules:
  0.0 103.7 jit_solution(8548118021415250427)
XLA Ops:
  0.0 1.0 %copy-done = f32[2,256,256]{2,1,0:T(8,128)S(1)} copy-done((f32[2,256,256]{2,1,0:T(8,128)S(1)}, f32[2,256,256]{2,1,0:T(8,128)}, u32[]{:S(2)}) %copy-start) | copy-done | bytes 524312
  1.1 3.0 %collective-permute-start = (bf16[2,128,256]{2,1,0:T(8,128)(2,1)S(1)}, bf16[2,128,256]{2,1,0:T(8,128)(2,1)S(1)}, u32[]{:S(2)}, u32[]{:S(2)}) collective-permute-start(bf16[2,128,256]{2,1,0:T(8,128)(2,1)S(1)} %dynamic-slice_convert_fusion.2), channel_id=1, source_target_pairs={{0,2},{2,0},{1,3},{3,1},{4,6},{6,4},{5,7},{7,5},{8,10},{10,8},{9,1... | collective-permute-start | bytes 393224 | tf_op jit(solution)/shard_map/ppermute | solution.py:35
  4.1 2.7 %constant_dynamic-slice_fusion.2 = bf16[3,256,1024]{2,1,0:T(8,128)(2,1)} fusion(bf16[8,256,1024]{2,1,0:T(8,128)(2,1)} %param.2, s32[]{:T(128)S(6)} %select_n.177), kind=kLoop, calls=%fused_computation.64 | loop fusion | bytes 3145732 | tf_op jit(solution)/shard_map/dynamic_slice | solution.py:339
  6.8 0.8 collective-permute-done
  7.6 1.7 %collective-permute-start.3 = (bf16[3,256,1024]{2,1,0:T(8,128)(2,1)}, bf16[3,256,1024]{2,1,0:T(8,128)(2,1)}, u32[]{:S(2)}, u32[]{:S(2)}) collective-permute-start(bf16[3,256,1024]{2,1,0:T(8,128)(2,1)} %constant_dynamic-slice_fusion.2), channel_id=1, source_target_pairs={{0,2},{2,0},{1,3},{3,1},{4,6},{6,4},{5,7},{7,5},{8,10},{10,8},{9,1... | collective-permute-start | bytes 4718600 | tf_op jit(solution)/shard_map/ppermute | solution.py:35
  9.4 1.3 %collective-permute-done.1 = bf16[2,1,128,256]{3,2,0,1:T(8,128)(2,1)S(1)} collective-permute-done((bf16[2,1,128,256]{3,2,0,1:T(8,128)(2,1)S(1)}, bf16[2,1,128,256]{3,2,0,1:T(8,128)(2,1)S(1)}, u32[]{:S(2)}, u32[]{:S(2)}) %collective-permute-start.1) | collective-permute-done | bytes 131104 | tf_op jit(solution)/shard_map/ppermute | solution.py:39
  10.9 1.6 %collective-permute-start.2 = (bf16[2,128,512]{2,1,0:T(8,128)(2,1)S(1)}, bf16[2,128,512]{2,1,0:T(8,128)(2,1)S(1)}, u32[]{:S(2)}, u32[]{:S(2)}) collective-permute-start(bf16[2,128,512]{2,1,0:T(8,128)(2,1)S(1)} %maximum_select_fusion.refs_0_), channel_id=1, source_target_pairs={{0,1},{1,0},{2,3},{3,2},{4,5},{5,4},{6,7},{7,6},{8,9},{9,8},{10,11... | collective-permute-start | bytes 786440 | tf_op jit(solution)/shard_map/ppermute | solution.py:35
  12.5 1.6 %collective-permute-start.4 = (bf16[2,128,512]{2,1,0:T(8,128)(2,1)S(1)}, bf16[2,128,512]{2,1,0:T(8,128)(2,1)S(1)}, u32[]{:S(2)}, u32[]{:S(2)}) collective-permute-start(bf16[2,128,512]{2,1,0:T(8,128)(2,1)S(1)} %maximum_select_fusion.refs_0_), channel_id=1, source_target_pairs={{0,8},{4,12},{8,16},{12,20},{16,24},{20,28},{24,0},{28,4},{1,9},{5... | collective-permute-start | bytes 786440 | tf_op jit(solution)/shard_map/ppermute | solution.py:35
  14.1 2.2 %collective-permute-start.6 = (bf16[2,128,512]{2,1,0:T(8,128)(2,1)S(1)}, bf16[2,128,512]{2,1,0:T(8,128)(2,1)}, u32[]{:S(2)}, u32[]{:S(2)}) collective-permute-start(bf16[2,128,512]{2,1,0:T(8,128)(2,1)S(1)} %maximum_select_fusion.refs_0_), channel_id=1, source_target_pairs={{0,24},{4,28},{8,0},{12,4},{16,8},{20,12},{24,16},{28,20},{1,25},{... | collective-permute-start | bytes 786440 | tf_op jit(solution)/shard_map/ppermute | solution.py:35
  16.3 0.8 collective-permute-start.8
  17.1 2.2 %collective-permute-done.2.refs_1_ = bf16[2,128,512]{2,1,0:T(8,128)(2,1)S(1)} collective-permute-done((bf16[2,128,512]{2,1,0:T(8,128)(2,1)S(1)}, bf16[2,128,512]{2,1,0:T(8,128)(2,1)S(1)}, u32[]{:S(2)}, u32[]{:S(2)}) %collective-permute-start.2) | collective-permute-done | bytes 262176 | tf_op jit(solution)/shard_map/ppermute | solution.py:35
  19.3 1.9 %constant_dynamic-slice_fusion.1.refs_0_.refs_1_ = bf16[4,256,1024]{2,1,0:T(8,128)(2,1)S(1)} fusion(bf16[8,256,1024]{2,1,0:T(8,128)(2,1)} %param.2, s32[]{:T(128)S(6)} %select_n.181), kind=kLoop, calls=%fused_computation.63 | loop fusion | bytes 4194308 | tf_op jit(solution)/shard_map/dynamic_slice | solution.py:377
  21.3 2.2 %collective-permute-done.4.refs_2_ = bf16[2,128,512]{2,1,0:T(8,128)(2,1)S(1)} collective-permute-done((bf16[2,128,512]{2,1,0:T(8,128)(2,1)S(1)}, bf16[2,128,512]{2,1,0:T(8,128)(2,1)S(1)}, u32[]{:S(2)}, u32[]{:S(2)}) %collective-permute-start.4) | collective-permute-done | bytes 262176 | tf_op jit(solution)/shard_map/ppermute | solution.py:35
  23.5 0.5 collective-permute-start.5
  24.0 3.6 %collective-permute-done.6.refs_4_ = bf16[2,128,512]{2,1,0:T(8,128)(2,1)} collective-permute-done((bf16[2,128,512]{2,1,0:T(8,128)(2,1)S(1)}, bf16[2,128,512]{2,1,0:T(8,128)(2,1)}, u32[]{:S(2)}, u32[]{:S(2)}) %collective-permute-start.6) | collective-permute-done | bytes 262176 | tf_op jit(solution)/shard_map/ppermute | solution.py:35
  28.1 11.3 %collective-permute-done.8.refs_6_ = bf16[2,128,512]{2,1,0:T(8,128)(2,1)} collective-permute-done((bf16[2,128,512]{2,1,0:T(8,128)(2,1)S(1)}, bf16[2,128,512]{2,1,0:T(8,128)(2,1)}, u32[]{:S(2)}, u32[]{:S(2)}) %collective-permute-start.8) | collective-permute-done | bytes 262176 | tf_op jit(solution)/shard_map/ppermute | solution.py:35
  39.9 1.9 %constant_dynamic-slice_fusion = bf16[1,256,1024]{2,1,0:T(8,128)(2,1)} fusion(bf16[8,256,1024]{2,1,0:T(8,128)(2,1)} %param.2, s32[]{:T(128)S(6)} %select_n.182), kind=kLoop, calls=%fused_computation.62 | loop fusion | bytes 1048580 | tf_op jit(solution)/shard_map/dynamic_slice | solution.py:339
  41.8 6.0 %collective-permute-done.9.refs_7_ = bf16[2,128,512]{2,1,0:T(8,128)(2,1)S(1)} collective-permute-done((bf16[2,128,512]{2,1,0:T(8,128)(2,1)}, bf16[2,128,512]{2,1,0:T(8,128)(2,1)S(1)}, u32[]{:S(2)}, u32[]{:S(2)}) %collective-permute-start.9) | collective-permute-done | bytes 262176 | tf_op jit(solution)/shard_map/ppermute | solution.py:35
  47.8 0.7 copy-done.8
  48.5 0.5 collective-permute-start.10
  49.2 2.1 %assemble.1.refs_4_.refs_2_.refs_6_ = bf16[2,256,2048]{2,1,0:T(8,128)(2,1)S(1)} custom-call(s32[6]{0:T(128)S(1)} %stack.27.at, bf16[2,128,512]{2,1,0:T(8,128)(2,1)} %copy-done.1, bf16[2,128,512]{2,1,0:T(8,128)(2,1)} %copy-done.5, bf16[2,128,512]{2,1,0:T(8,128)(2,1)} %copy-done.6, bf16[2,128,512]{2,1,0:T(8,128)(2,1)} %copy-done.7, ...), custom_call_target="tpu_custom_call" | custom-call | bytes 2097152 | tf_op jit(solution)/shard_map/assemble/pallas_call | solution.py:80
  51.3 1.0 collective-permute-done.12.refs_3_
  52.3 8.4 %early_sums.1.refs_7_ = f32[2,256,2048]{2,1,0:T(8,128)S(1)} custom-call(bf16[4,256,1024]{2,1,0:T(8,128)(2,1)S(1)} %constant_dynamic-slice_fusion.1.refs_0_.refs_1_, bf16[3,256,1024]{2,1,0:T(8,128)(2,1)} %collective-permute-done.3.refs_1_, bf16[4,256,1024]{2,1,0:T(8,128)(2,1)} %collective-permute-done.11.refs_2_.refs_3_, ...), custom_call_target="tpu_custom_call" | custom-call | bytes 2097152 | tf_op jit(solution)/shard_map/early_sums/pallas_call | solution.py:149
  60.7 2.4 %collective-permute-done.10.refs_1_.refs_2_ = bf16[1,256,1024]{2,1,0:T(8,128)(2,1)S(1)} collective-permute-done((bf16[1,256,1024]{2,1,0:T(8,128)(2,1)}, bf16[1,256,1024]{2,1,0:T(8,128)(2,1)S(1)}, u32[]{:S(2)}, u32[]{:S(2)}) %collective-permute-start.10) | collective-permute-done | bytes 524320 | tf_op jit(solution)/shard_map/ppermute | solution.py:35
  63.1 0.8 step_pairs.1.refs_5_
  63.9 1.1 %collective-permute-done.13.refs_4_ = bf16[1,256,1024]{2,1,0:T(8,128)(2,1)S(1)} collective-permute-done((bf16[1,256,1024]{2,1,0:T(8,128)(2,1)S(1)}, bf16[1,256,1024]{2,1,0:T(8,128)(2,1)S(1)}, u32[]{:S(2)}, u32[]{:S(2)}) %collective-permute-start.13) | collective-permute-done | bytes 524320 | tf_op jit(solution)/shard_map/ppermute | solution.py:39
  65.0 5.0 %last_sums.1 = (bf16[1,2,32,2048]{3,2,1,0:T(8,128)(2,1)}, f32[1,2,32,2048]{3,2,1,0:T(8,128)}, bf16[1,2,32,2048]{3,2,1,0:T(8,128)(2,1)}, f32[2,32,2048]{2,1,0:T(8...) custom-call(s32[1]{0:T(128)} %bitcast.refs_0_, ...), custom_call_target="tpu_custom_call" | custom-call | bytes 3145728 | tf_op jit(solution)/shard_map/last_sums/pallas_call | solution.py:302
  70.0 0.6 collective-permute-start.23
  70.6 0.5 collective-permute-start.21
  71.1 1.5 %collective-permute-start.16 = (bf16[2,32,2048]{2,1,0:T(8,128)(2,1)}, bf16[2,32,2048]{2,1,0:T(8,128)(2,1)S(1)}, u32[]{:S(2)}, u32[]{:S(2)}) collective-permute-start(bf16[2,32,2048]{2,1,0:T(8,128)(2,1)} %bitcast.29), channel_id=1, source_target_pairs={{0,1},{1,0},{2,3},{3,2},{4,5},{5,4},{6,7},{7,6},{8,9},{9,8},{10,11... | collective-permute-start | bytes 786440 | tf_op jit(solution)/shard_map/ppermute | solution.py:35
  72.6 1.5 %collective-permute-start.14 = (bf16[1,2,32,2048]{3,2,1,0:T(8,128)(2,1)}, bf16[1,2,32,2048]{3,2,1,0:T(8,128)(2,1)S(1)}, u32[]{:S(2)}, u32[]{:S(2)}) collective-permute-start(bf16[1,2,32,2048]{3,2,1,0:T(8,128)(2,1)} %get-tuple-element.30), channel_id=1, source_target_pairs={{0,2},{2,0},{1,3},{3,1},{4,6},{6,4},{5,7},{7,5},{8,10},{10,8},{9,1... | collective-permute-start | bytes 786440 | tf_op jit(solution)/shard_map/ppermute | solution.py:35
  74.1 5.3 %collective-permute-done.23 = bf16[2,32,2048]{2,1,0:T(8,128)(2,1)S(1)} collective-permute-done((bf16[2,32,2048]{2,1,0:T(8,128)(2,1)}, bf16[2,32,2048]{2,1,0:T(8,128)(2,1)S(1)}, u32[]{:S(2)}, u32[]{:S(2)}) %collective-permute-start.23) | collective-permute-done | bytes 262176 | tf_op jit(solution)/shard_map/ppermute | solution.py:35
  79.4 1.1 %convert_add_fusion = f32[2,32,2048]{2,1,0:T(8,128)S(1)} fusion(f32[2,32,2048]{2,1,0:T(8,128)} %get-tuple-element.35, bf16[2,32,2048]{2,1,0:T(8,128)(2,1)S(1)} %collective-permute-done.23), kind=kLoop, calls=%fused_computation.16 | loop fusion | flops 262144 | bytes 1310720 | tf_op jit(solution)/shard_map/add | solution.py:404
  80.6 0.6 collective-permute-start.24
  81.3 0.6 collective-permute-start.22
  81.9 3.1 %collective-permute-done.16 = bf16[2,32,2048]{2,1,0:T(8,128)(2,1)S(1)} collective-permute-done((bf16[2,32,2048]{2,1,0:T(8,128)(2,1)}, bf16[2,32,2048]{2,1,0:T(8,128)(2,1)S(1)}, u32[]{:S(2)}, u32[]{:S(2)}) %collective-permute-start.16) | collective-permute-done | bytes 262176 | tf_op jit(solution)/shard_map/ppermute | solution.py:35
  85.1 0.6 collective-permute-start.17
  85.8 1.5 %collective-permute-start.15 = (bf16[1,32,2048]{2,1,0:T(8,128)(2,1)S(1)}, bf16[1,32,2048]{2,1,0:T(8,128)(2,1)S(1)}, u32[]{:S(2)}, u32[]{:S(2)}) collective-permute-start(bf16[1,32,2048]{2,1,0:T(8,128)(2,1)S(1)} %fusion), channel_id=1, source_target_pairs={{0,1},{1,0},{2,3},{3,2},{4,5},{5,4},{6,7},{7,6},{8,9},{9,8},{10,11... | collective-permute-start | bytes 393224 | tf_op jit(solution)/shard_map/ppermute | solution.py:35
  87.3 1.0 collective-permute-done.24
  88.4 0.6 collective-permute-start.25
  89.0 2.0 %collective-permute-start.26 = (bf16[1,64,512]{2,1,0:T(8,128)(2,1)S(1)}, bf16[1,64,512]{2,1,0:T(8,128)(2,1)S(1)}, u32[]{:S(2)}, u32[]{:S(2)}) collective-permute-start(bf16[1,64,512]{2,1,0:T(8,128)(2,1)S(1)} %get-tuple-element.38), channel_id=1, source_target_pairs={{0,16},{4,20},{8,24},{12,28},{16,0},{20,4},{24,8},{28,12},{1,17},{... | collective-permute-start | bytes 196616 | tf_op jit(solution)/shard_map/ppermute | solution.py:35
  91.0 2.8 %collective-permute-start.27 = (bf16[1,64,512]{2,1,0:T(8,128)(2,1)S(1)}, bf16[1,64,512]{2,1,0:T(8,128)(2,1)S(1)}, u32[]{:S(2)}, u32[]{:S(2)}) collective-permute-start(bf16[1,64,512]{2,1,0:T(8,128)(2,1)S(1)} %get-tuple-element.39), channel_id=1, source_target_pairs={{0,24},{4,28},{8,0},{12,4},{16,8},{20,12},{24,16},{28,20},{1,25},{... | collective-permute-start | bytes 196616 | tf_op jit(solution)/shard_map/ppermute | solution.py:35
  94.2 0.6 collective-permute-start.19
  94.7 3.3 %collective-permute-start.20 = (bf16[1,64,512]{2,1,0:T(8,128)(2,1)S(1)}, bf16[1,64,512]{2,1,0:T(8,128)(2,1)S(1)}, u32[]{:S(2)}, u32[]{:S(2)}) collective-permute-start(bf16[1,64,512]{2,1,0:T(8,128)(2,1)S(1)} %get-tuple-element.42), channel_id=1, source_target_pairs={{0,24},{4,28},{8,0},{12,4},{16,8},{20,12},{24,16},{28,20},{1,25},{... | collective-permute-start | bytes 196616 | tf_op jit(solution)/shard_map/ppermute | solution.py:35
  98.1 2.2 %collective-permute-done.18 = bf16[1,64,512]{2,1,0:T(8,128)(2,1)S(1)} collective-permute-done((bf16[1,64,512]{2,1,0:T(8,128)(2,1)S(1)}, bf16[1,64,512]{2,1,0:T(8,128)(2,1)S(1)}, u32[]{:S(2)}, u32[]{:S(2)}) %collective-permute-start.18) | collective-permute-done | bytes 65568 | tf_op jit(solution)/shard_map/ppermute | solution.py:35
  100.4 1.0 collective-permute-done.19
  101.6 1.3 %collective-permute-done.28 = f32[1,128,256]{2,1,0:T(8,128)S(1)} collective-permute-done((f32[1,128,256]{2,1,0:T(8,128)S(1)}, f32[1,128,256]{2,1,0:T(8,128)S(1)}, u32[]{:S(2)}, u32[]{:S(2)}) %collective-permute-start.28) | collective-permute-done | bytes 131104 | tf_op jit(solution)/shard_map/ppermute | solution.py:39
  103.0 0.7 maximum_select_fusion.1
  (58 shorter events, 2.5 us)
Async XLA Ops:
  0.0 1.0 %copy-start = (f32[2,256,256]{2,1,0:T(8,128)S(1)}, f32[2,256,256]{2,1,0:T(8,128)}, u32[]{:S(2)}) copy-start(f32[2,256,256]{2,1,0:T(8,128)} %param.3) | copy-start | bytes 1572868
  1.1 6.5 %collective-permute-start = (bf16[2,128,256]{2,1,0:T(8,128)(2,1)S(1)}, bf16[2,128,256]{2,1,0:T(8,128)(2,1)S(1)}, u32[]{:S(2)}, u32[]{:S(2)}) collective-permute-start(bf16[2,128,256]{2,1,0:T(8,128)(2,1)S(1)} %dynamic-slice_convert_fusion.2), channel_id=1, source_target_pairs={{0,2},{2,0},{1,3},{3,1},{4,6},{6,4},{5,7},{7,5},{8,10},{10,8},{9,1... | collective-permute-start | bytes 393224 | tf_op jit(solution)/shard_map/ppermute | solution.py:35
  7.6 40.3 %collective-permute-start.3 = (bf16[3,256,1024]{2,1,0:T(8,128)(2,1)}, bf16[3,256,1024]{2,1,0:T(8,128)(2,1)}, u32[]{:S(2)}, u32[]{:S(2)}) collective-permute-start(bf16[3,256,1024]{2,1,0:T(8,128)(2,1)} %constant_dynamic-slice_fusion.2), channel_id=1, source_target_pairs={{0,2},{2,0},{1,3},{3,1},{4,6},{6,4},{5,7},{7,5},{8,10},{10,8},{9,1... | collective-permute-start | bytes 4718600 | tf_op jit(solution)/shard_map/ppermute | solution.py:35
  9.4 1.4 %collective-permute-start.1 = (bf16[2,1,128,256]{3,2,0,1:T(8,128)(2,1)S(1)}, bf16[2,1,128,256]{3,2,0,1:T(8,128)(2,1)S(1)}, u32[]{:S(2)}, u32[]{:S(2)}) collective-permute-start(bf16[2,1,128,256]{3,2,0,1:T(8,128)(2,1)S(1)} %get-tuple-element.46), channel_id=1, source_target_pairs={{0,4},{4,0},{8,12},{12,8},{16,20},{20,16},{24,28},{28,24},{1,5},{5... | collective-permute-start | bytes 393224 | tf_op jit(solution)/shard_map/ppermute | solution.py:39
  10.9 10.3 %copy-start.1 = (bf16[2,128,512]{2,1,0:T(8,128)(2,1)}, bf16[2,128,512]{2,1,0:T(8,128)(2,1)S(1)}, u32[]{:S(2)}) copy-start(bf16[2,128,512]{2,1,0:T(8,128)(2,1)S(1)} %maximum_select_fusion.refs_0_) | copy-start | bytes 786436
  10.9 8.4 %collective-permute-start.2 = (bf16[2,128,512]{2,1,0:T(8,128)(2,1)S(1)}, bf16[2,128,512]{2,1,0:T(8,128)(2,1)S(1)}, u32[]{:S(2)}, u32[]{:S(2)}) collective-permute-start(bf16[2,128,512]{2,1,0:T(8,128)(2,1)S(1)} %maximum_select_fusion.refs_0_), channel_id=1, source_target_pairs={{0,1},{1,0},{2,3},{3,2},{4,5},{5,4},{6,7},{7,6},{8,9},{9,8},{10,11... | collective-permute-start | bytes 786440 | tf_op jit(solution)/shard_map/ppermute | solution.py:35
  12.5 11.0 %collective-permute-start.4 = (bf16[2,128,512]{2,1,0:T(8,128)(2,1)S(1)}, bf16[2,128,512]{2,1,0:T(8,128)(2,1)S(1)}, u32[]{:S(2)}, u32[]{:S(2)}) collective-permute-start(bf16[2,128,512]{2,1,0:T(8,128)(2,1)S(1)} %maximum_select_fusion.refs_0_), channel_id=1, source_target_pairs={{0,8},{4,12},{8,16},{12,20},{16,24},{20,28},{24,0},{28,4},{1,9},{5... | collective-permute-start | bytes 786440 | tf_op jit(solution)/shard_map/ppermute | solution.py:35
  14.1 13.5 %collective-permute-start.6 = (bf16[2,128,512]{2,1,0:T(8,128)(2,1)S(1)}, bf16[2,128,512]{2,1,0:T(8,128)(2,1)}, u32[]{:S(2)}, u32[]{:S(2)}) collective-permute-start(bf16[2,128,512]{2,1,0:T(8,128)(2,1)S(1)} %maximum_select_fusion.refs_0_), channel_id=1, source_target_pairs={{0,24},{4,28},{8,0},{12,4},{16,8},{20,12},{24,16},{28,20},{1,25},{... | collective-permute-start | bytes 786440 | tf_op jit(solution)/shard_map/ppermute | solution.py:35
  16.3 23.1 %collective-permute-start.8 = (bf16[2,128,512]{2,1,0:T(8,128)(2,1)S(1)}, bf16[2,128,512]{2,1,0:T(8,128)(2,1)}, u32[]{:S(2)}, u32[]{:S(2)}) collective-permute-start(bf16[2,128,512]{2,1,0:T(8,128)(2,1)S(1)} %maximum_select_fusion.refs_0_), channel_id=1, source_target_pairs={{0,16},{4,20},{8,24},{12,28},{16,0},{20,4},{24,8},{28,12},{1,17},{... | collective-permute-start | bytes 786440 | tf_op jit(solution)/shard_map/ppermute | solution.py:35
  19.3 1.9 %copy-start.5 = (bf16[2,128,512]{2,1,0:T(8,128)(2,1)}, bf16[2,128,512]{2,1,0:T(8,128)(2,1)S(1)}, u32[]{:S(2)}) copy-start(bf16[2,128,512]{2,1,0:T(8,128)(2,1)S(1)} %collective-permute-done.2.refs_1_) | copy-start | bytes 786436
  21.2 30.1 %collective-permute-start.11 = (bf16[4,256,1024]{2,1,0:T(8,128)(2,1)S(1)}, bf16[4,256,1024]{2,1,0:T(8,128)(2,1)}, u32[]{:S(2)}, u32[]{:S(2)}) collective-permute-start(bf16[4,256,1024]{2,1,0:T(8,128)(2,1)S(1)} %constant_dynamic-slice_fusion.1.refs_0_.refs_1_), channel_id=1, source_target_pairs={{0,4},{4,0},{8,12},{12,8},{16,20},{20,16},{24,28},{28,24},{1,5},{5... | collective-permute-start | bytes 6291464 | tf_op jit(solution)/shard_map/ppermute | solution.py:39
  23.5 24.3 %copy-start.6 = (bf16[2,128,512]{2,1,0:T(8,128)(2,1)}, bf16[2,128,512]{2,1,0:T(8,128)(2,1)S(1)}, u32[]{:S(2)}) copy-start(bf16[2,128,512]{2,1,0:T(8,128)(2,1)S(1)} %collective-permute-done.4.refs_2_) | copy-start | bytes 786436
  23.5 18.2 %collective-permute-start.5 = (bf16[2,128,512]{2,1,0:T(8,128)(2,1)S(1)}, bf16[2,128,512]{2,1,0:T(8,128)(2,1)S(1)}, u32[]{:S(2)}, u32[]{:S(2)}) collective-permute-start(bf16[2,128,512]{2,1,0:T(8,128)(2,1)S(1)} %collective-permute-done.4.refs_2_), channel_id=1, source_target_pairs={{0,1},{1,0},{2,3},{3,2},{4,5},{5,4},{6,7},{7,6},{8,9},{9,8},{10,11... | collective-permute-start | bytes 786440 | tf_op jit(solution)/shard_map/ppermute | solution.py:35
  27.6 14.2 %collective-permute-start.7 = (bf16[2,128,512]{2,1,0:T(8,128)(2,1)}, bf16[2,128,512]{2,1,0:T(8,128)(2,1)}, u32[]{:S(2)}, u32[]{:S(2)}) collective-permute-start(bf16[2,128,512]{2,1,0:T(8,128)(2,1)} %collective-permute-done.6.refs_4_), channel_id=1, source_target_pairs={{0,1},{1,0},{2,3},{3,2},{4,5},{5,4},{6,7},{7,6},{8,9},{9,8},{10,11... | collective-permute-start | bytes 786440 | tf_op jit(solution)/shard_map/ppermute | solution.py:35
  39.4 8.4 %collective-permute-start.9 = (bf16[2,128,512]{2,1,0:T(8,128)(2,1)}, bf16[2,128,512]{2,1,0:T(8,128)(2,1)S(1)}, u32[]{:S(2)}, u32[]{:S(2)}) collective-permute-start(bf16[2,128,512]{2,1,0:T(8,128)(2,1)} %collective-permute-done.8.refs_6_), channel_id=1, source_target_pairs={{0,1},{1,0},{2,3},{3,2},{4,5},{5,4},{6,7},{7,6},{8,9},{9,8},{10,11... | collective-permute-start | bytes 786440 | tf_op jit(solution)/shard_map/ppermute | solution.py:35
  41.8 7.4 %copy-start.7 = (bf16[2,128,512]{2,1,0:T(8,128)(2,1)}, bf16[2,128,512]{2,1,0:T(8,128)(2,1)S(1)}, u32[]{:S(2)}) copy-start(bf16[2,128,512]{2,1,0:T(8,128)(2,1)S(1)} %collective-permute-done.5.refs_3_) | copy-start | bytes 786436
  47.8 0.7 copy-start.8
  48.5 3.8 %collective-permute-start.12 = (bf16[3,256,1024]{2,1,0:T(8,128)(2,1)}, bf16[3,256,1024]{2,1,0:T(8,128)(2,1)}, u32[]{:S(2)}, u32[]{:S(2)}) collective-permute-start(bf16[3,256,1024]{2,1,0:T(8,128)(2,1)} %collective-permute-done.3.refs_1_), channel_id=1, source_target_pairs={{0,4},{4,0},{8,12},{12,8},{16,20},{20,16},{24,28},{28,24},{1,5},{5... | collective-permute-start | bytes 4718600 | tf_op jit(solution)/shard_map/ppermute | solution.py:39
  48.5 14.5 %collective-permute-start.10 = (bf16[1,256,1024]{2,1,0:T(8,128)(2,1)}, bf16[1,256,1024]{2,1,0:T(8,128)(2,1)S(1)}, u32[]{:S(2)}, u32[]{:S(2)}) collective-permute-start(bf16[1,256,1024]{2,1,0:T(8,128)(2,1)} %constant_dynamic-slice_fusion), channel_id=1, source_target_pairs={{0,2},{2,0},{1,3},{3,1},{4,6},{6,4},{5,7},{7,5},{8,10},{10,8},{9,1... | collective-permute-start | bytes 1572872 | tf_op jit(solution)/shard_map/ppermute | solution.py:35
  63.1 1.9 %collective-permute-start.13 = (bf16[1,256,1024]{2,1,0:T(8,128)(2,1)S(1)}, bf16[1,256,1024]{2,1,0:T(8,128)(2,1)S(1)}, u32[]{:S(2)}, u32[]{:S(2)}) collective-permute-start(bf16[1,256,1024]{2,1,0:T(8,128)(2,1)S(1)} %collective-permute-done.10.refs_1_.refs_2_), channel_id=1, source_target_pairs={{0,4},{4,0},{8,12},{12,8},{16,20},{20,16},{24,28},{28,24},{1,5},{5... | collective-permute-start | bytes 1572872 | tf_op jit(solution)/shard_map/ppermute | solution.py:39
  70.0 11.2 %copy-start.4 = (f32[1,2,32,2048]{3,2,1,0:T(8,128)S(1)}, f32[1,2,32,2048]{3,2,1,0:T(8,128)}, u32[]{:S(2)}) copy-start(f32[1,2,32,2048]{3,2,1,0:T(8,128)} %get-tuple-element.33) | copy-start | bytes 1572868
  70.0 15.1 %copy-start.3 = (f32[2,32,2048]{2,1,0:T(8,128)S(1)}, f32[2,32,2048]{2,1,0:T(8,128)}, u32[]{:S(2)}) copy-start(f32[2,32,2048]{2,1,0:T(8,128)} %get-tuple-element.31) | copy-start | bytes 1572868
  70.0 9.4 %collective-permute-start.23 = (bf16[2,32,2048]{2,1,0:T(8,128)(2,1)}, bf16[2,32,2048]{2,1,0:T(8,128)(2,1)S(1)}, u32[]{:S(2)}, u32[]{:S(2)}) collective-permute-start(bf16[2,32,2048]{2,1,0:T(8,128)(2,1)} %bitcast.30), channel_id=1, source_target_pairs={{0,1},{1,0},{2,3},{3,2},{4,5},{5,4},{6,7},{7,6},{8,9},{9,8},{10,11... | collective-permute-start | bytes 786440 | tf_op jit(solution)/shard_map/ppermute | solution.py:35
  70.6 10.6 %collective-permute-start.21 = (bf16[1,2,32,2048]{3,2,1,0:T(8,128)(2,1)}, bf16[1,2,32,2048]{3,2,1,0:T(8,128)(2,1)S(1)}, u32[]{:S(2)}, u32[]{:S(2)}) collective-permute-start(bf16[1,2,32,2048]{3,2,1,0:T(8,128)(2,1)} %get-tuple-element.34), channel_id=1, source_target_pairs={{0,2},{2,0},{1,3},{3,1},{4,6},{6,4},{5,7},{7,5},{8,10},{10,8},{9,1... | collective-permute-start | bytes 786440 | tf_op jit(solution)/shard_map/ppermute | solution.py:35
  71.1 13.9 %collective-permute-start.16 = (bf16[2,32,2048]{2,1,0:T(8,128)(2,1)}, bf16[2,32,2048]{2,1,0:T(8,128)(2,1)S(1)}, u32[]{:S(2)}, u32[]{:S(2)}) collective-permute-start(bf16[2,32,2048]{2,1,0:T(8,128)(2,1)} %bitcast.29), channel_id=1, source_target_pairs={{0,1},{1,0},{2,3},{3,2},{4,5},{5,4},{6,7},{7,6},{8,9},{9,8},{10,11... | collective-permute-start | bytes 786440 | tf_op jit(solution)/shard_map/ppermute | solution.py:35
  72.6 13.1 %collective-permute-start.14 = (bf16[1,2,32,2048]{3,2,1,0:T(8,128)(2,1)}, bf16[1,2,32,2048]{3,2,1,0:T(8,128)(2,1)S(1)}, u32[]{:S(2)}, u32[]{:S(2)}) collective-permute-start(bf16[1,2,32,2048]{3,2,1,0:T(8,128)(2,1)} %get-tuple-element.30), channel_id=1, source_target_pairs={{0,2},{2,0},{1,3},{3,1},{4,6},{6,4},{5,7},{7,5},{8,10},{10,8},{9,1... | collective-permute-start | bytes 786440 | tf_op jit(solution)/shard_map/ppermute | solution.py:35
  79.4 6.3 %copy-start.2 = (f32[1,2,32,2048]{3,2,1,0:T(8,128)S(1)}, f32[1,2,32,2048]{3,2,1,0:T(8,128)}, u32[]{:S(2)}) copy-start(f32[1,2,32,2048]{3,2,1,0:T(8,128)} %get-tuple-element.29) | copy-start | bytes 1572868
  80.6 7.6 %collective-permute-start.24 = (bf16[1,32,2048]{2,1,0:T(8,128)(2,1)S(1)}, bf16[1,32,2048]{2,1,0:T(8,128)(2,1)S(1)}, u32[]{:S(2)}, u32[]{:S(2)}) collective-permute-start(bf16[1,32,2048]{2,1,0:T(8,128)(2,1)S(1)} %slice.26), channel_id=1, source_target_pairs={{0,2},{2,0},{1,3},{3,1},{4,6},{6,4},{5,7},{7,5},{8,10},{10,8},{9,1... | collective-permute-start | bytes 393224 | tf_op jit(solution)/shard_map/ppermute | solution.py:35
  81.3 7.0 %collective-permute-start.22 = (bf16[1,32,2048]{2,1,0:T(8,128)(2,1)S(1)}, bf16[1,32,2048]{2,1,0:T(8,128)(2,1)S(1)}, u32[]{:S(2)}, u32[]{:S(2)}) collective-permute-start(bf16[1,32,2048]{2,1,0:T(8,128)(2,1)S(1)} %fusion.1), channel_id=1, source_target_pairs={{0,1},{1,0},{2,3},{3,2},{4,5},{5,4},{6,7},{7,6},{8,9},{9,8},{10,11... | collective-permute-start | bytes 393224 | tf_op jit(solution)/shard_map/ppermute | solution.py:35
  85.1 8.8 %collective-permute-start.17 = (bf16[1,32,2048]{2,1,0:T(8,128)(2,1)S(1)}, bf16[1,32,2048]{2,1,0:T(8,128)(2,1)S(1)}, u32[]{:S(2)}, u32[]{:S(2)}) collective-permute-start(bf16[1,32,2048]{2,1,0:T(8,128)(2,1)S(1)} %slice.27), channel_id=1, source_target_pairs={{0,2},{2,0},{1,3},{3,1},{4,6},{6,4},{5,7},{7,5},{8,10},{10,8},{9,1... | collective-permute-start | bytes 393224 | tf_op jit(solution)/shard_map/ppermute | solution.py:35
  85.8 8.1 %collective-permute-start.15 = (bf16[1,32,2048]{2,1,0:T(8,128)(2,1)S(1)}, bf16[1,32,2048]{2,1,0:T(8,128)(2,1)S(1)}, u32[]{:S(2)}, u32[]{:S(2)}) collective-permute-start(bf16[1,32,2048]{2,1,0:T(8,128)(2,1)S(1)} %fusion), channel_id=1, source_target_pairs={{0,1},{1,0},{2,3},{3,2},{4,5},{5,4},{6,7},{7,6},{8,9},{9,8},{10,11... | collective-permute-start | bytes 393224 | tf_op jit(solution)/shard_map/ppermute | solution.py:35
  88.4 6.3 %collective-permute-start.25 = (bf16[1,64,512]{2,1,0:T(8,128)(2,1)S(1)}, bf16[1,64,512]{2,1,0:T(8,128)(2,1)S(1)}, u32[]{:S(2)}, u32[]{:S(2)}) collective-permute-start(bf16[1,64,512]{2,1,0:T(8,128)(2,1)S(1)} %get-tuple-element.37), channel_id=1, source_target_pairs={{0,8},{4,12},{8,16},{12,20},{16,24},{20,28},{24,0},{28,4},{1,9},{5... | collective-permute-start | bytes 196616 | tf_op jit(solution)/shard_map/ppermute | solution.py:35
  89.0 9.0 %collective-permute-start.26 = (bf16[1,64,512]{2,1,0:T(8,128)(2,1)S(1)}, bf16[1,64,512]{2,1,0:T(8,128)(2,1)S(1)}, u32[]{:S(2)}, u32[]{:S(2)}) collective-permute-start(bf16[1,64,512]{2,1,0:T(8,128)(2,1)S(1)} %get-tuple-element.38), channel_id=1, source_target_pairs={{0,16},{4,20},{8,24},{12,28},{16,0},{20,4},{24,8},{28,12},{1,17},{... | collective-permute-start | bytes 196616 | tf_op jit(solution)/shard_map/ppermute | solution.py:35
  91.0 7.0 %collective-permute-start.27 = (bf16[1,64,512]{2,1,0:T(8,128)(2,1)S(1)}, bf16[1,64,512]{2,1,0:T(8,128)(2,1)S(1)}, u32[]{:S(2)}, u32[]{:S(2)}) collective-permute-start(bf16[1,64,512]{2,1,0:T(8,128)(2,1)S(1)} %get-tuple-element.39), channel_id=1, source_target_pairs={{0,24},{4,28},{8,0},{12,4},{16,8},{20,12},{24,16},{28,20},{1,25},{... | collective-permute-start | bytes 196616 | tf_op jit(solution)/shard_map/ppermute | solution.py:35
  94.1 6.2 %collective-permute-start.18 = (bf16[1,64,512]{2,1,0:T(8,128)(2,1)S(1)}, bf16[1,64,512]{2,1,0:T(8,128)(2,1)S(1)}, u32[]{:S(2)}, u32[]{:S(2)}) collective-permute-start(bf16[1,64,512]{2,1,0:T(8,128)(2,1)S(1)} %get-tuple-element.40), channel_id=1, source_target_pairs={{0,8},{4,12},{8,16},{12,20},{16,24},{20,28},{24,0},{28,4},{1,9},{5... | collective-permute-start | bytes 196616 | tf_op jit(solution)/shard_map/ppermute | solution.py:35
  94.2 7.2 %collective-permute-start.19 = (bf16[1,64,512]{2,1,0:T(8,128)(2,1)S(1)}, bf16[1,64,512]{2,1,0:T(8,128)(2,1)S(1)}, u32[]{:S(2)}, u32[]{:S(2)}) collective-permute-start(bf16[1,64,512]{2,1,0:T(8,128)(2,1)S(1)} %get-tuple-element.41), channel_id=1, source_target_pairs={{0,16},{4,20},{8,24},{12,28},{16,0},{20,4},{24,8},{28,12},{1,17},{... | collective-permute-start | bytes 196616 | tf_op jit(solution)/shard_map/ppermute | solution.py:35
  94.7 6.7 %collective-permute-start.20 = (bf16[1,64,512]{2,1,0:T(8,128)(2,1)S(1)}, bf16[1,64,512]{2,1,0:T(8,128)(2,1)S(1)}, u32[]{:S(2)}, u32[]{:S(2)}) collective-permute-start(bf16[1,64,512]{2,1,0:T(8,128)(2,1)S(1)} %get-tuple-element.42), channel_id=1, source_target_pairs={{0,24},{4,28},{8,0},{12,4},{16,8},{20,12},{24,16},{28,20},{1,25},{... | collective-permute-start | bytes 196616 | tf_op jit(solution)/shard_map/ppermute | solution.py:35
  101.5 1.4 %collective-permute-start.28 = (f32[1,128,256]{2,1,0:T(8,128)S(1)}, f32[1,128,256]{2,1,0:T(8,128)S(1)}, u32[]{:S(2)}, u32[]{:S(2)}) collective-permute-start(f32[1,128,256]{2,1,0:T(8,128)S(1)} %get-tuple-element.44), channel_id=1, source_target_pairs={{0,4},{4,0},{8,12},{12,8},{16,20},{20,16},{24,28},{28,24},{1,5},{5... | collective-permute-start | bytes 393224 | tf_op jit(solution)/shard_map/ppermute | solution.py:39

commit v8 on v7

--- a/solution.py
+++ b/solution.py
@@ -7,7 +7,7 @@
 
 CORES = 2
 PIECES = 2
-VMEM_LIMIT = 20 * 2**20
+VMEM_LIMIT = 30 * 2**20
 F32, BF16 = jnp.float32, jnp.bfloat16
 VMEM = pl.BlockSpec(memory_space=pltpu.VMEM)
 ANY = pl.BlockSpec(memory_space=pl.ANY)
@@ -209,7 +209,7 @@
     own = rows // no
     small = own // (PIECES * 2)
     more = [] if early is None else [early]
-    tile = min(width, 512)
+    tile = min(width, 1024)
     tiles = total // tile
 
     def body(*refs):
@@ -260,33 +260,28 @@
                             keep_x[g, oo, :, cols] = got[g, oo, p, 0]
                         else:
                             send_x[g - per, oo, :, cols] = got[g, oo, p, 0].astype(BF16)
-            for s in range(no):
-                for oo in range(no):
-
-                    @pl.when(lax.rem(me + s, no) == oo)
-                    def _(s=s, oo=oo, got=got, r=r, at=at):
-                        for g in range(groups):
-                            to = (r - g // per) % nr * width + at
-                            cols = slice(to, to + tile)
-                            for p in range(PIECES):
-                                if s == 0:
-                                    outs[4 * p + 3][g, :, cols] = got[g, oo, p, 1]
-                                else:
-                                    outs[4 * p + 2][s - 1, g, :, cols] = got[g, oo, p, 1].astype(BF16)
+            for oo in range(no):
+                slot = lax.rem(oo - me + no, no)
+                for g in range(groups):
+                    to = (r - g // per) % nr * width + at
+                    cols = slice(to, to + tile)
+                    for p in range(PIECES):
+                        outs[4 * p + 2][slot, g, :, cols] = got[g, oo, p, 1].astype(BF16)
+                        outs[4 * p + 3][slot, g, :, cols] = got[g, oo, p, 1]
             for v in range(nv):
                 cols = pl.ds((r - v) % nr * width + at, tile)
                 for p in range(PIECES):
                     at_x = (pl.ds(0, per) if v == 0 else pl.ds((v - 1) * per, per), slice(None), slice(None), cols)
                     at_y = (pl.ds(v * per, per), slice(None), cols)
-                    for k, where in (
-                        (1 if v == 0 else 0, at_x),
-                        (2, (slice(None), *at_y)),
-                        (3, at_y),
+                    for k, source, where in (
+                        (1 if v == 0 else 0, at_x, at_x),
+                        (2, (pl.ds(1, no - 1), *at_y), (slice(None), *at_y)),
+                        (3, (0, *at_y), at_y),
                     ):
                         out, result = outs[4 * p + k], results[4 * p + k]
                         sent.append(
                             pltpu.make_async_copy(
-                                out.at[where], result.at[where], out_sems.at[len(sent)]
+                                out.at[source], result.at[where], out_sems.at[len(sent)]
                             )
                         )
                         sent[-1].start()
@@ -299,12 +294,14 @@
         jax.ShapeDtypeStruct((no - 1, groups, small, total), BF16),
         jax.ShapeDtypeStruct((groups, small, total), F32),
     ] * PIECES
+    every = (no, groups, small, total)
+    held = [(shapes[0].shape, BF16), (shapes[1].shape, F32), (every, BF16), (every, F32)] * PIECES
     outs = pl.pallas_call(
         body,
         out_shape=[pltpu.HBM(x.shape, x.dtype) for x in shapes],
         in_specs=[SMEM] + [ANY] * n + [VMEM] * (2 + len(more)),
         out_specs=[HBM] * len(shapes),
-        scratch_shapes=[pltpu.VMEM(x.shape, x.dtype) for x in shapes]
+        scratch_shapes=[pltpu.VMEM(x, d) for x, d in held]
         + [pltpu.VMEM((1, rows, width), BF16)] * n
         + [
             pltpu.VMEM((groups, rows, rows), BF16),
@@ -369,9 +366,9 @@
         + [(o + s) % no * own for s in range(no)]
     ).astype(jnp.int32)
     later, _ = lax.optimization_barrier((factors, blocks[no - 1][0]))
-    held = (come, sends(later, early_steps, last_steps), [b[0] for b in blocks])
-    come, group, _ = lax.optimization_barrier(held)
+    group = sends(later, early_steps, last_steps)
     come_last = along_vir(group)
+    come, _ = lax.optimization_barrier((come, (group, [b[0] for b in blocks])))
     vectors = assemble(where, blocks, groups, rows, total)
 
     kept = lax.dynamic_slice_in_dim(later, v * take, take, 0)

time: 104 us -> 108 us (1.038)
  starting transfers between devices: 29.9 us -> 34.2 us
    ppermute x24, starting transfers between devices: 29.7 us -> 34 us  [shift(): return lax.ppermute(array, axis, pairs)]
where the time goes in v8:
time: 108 us; the launch traced here: 107 us
  waiting for transfers between devices  45.9 us (42%)
  starting transfers between devices  34.2 us (32%)
  Pallas kernels  15.7 us (15%)
  local copies, waits for them, and re-layouts  8.4 us (8%)
  other arithmetic  2.81 us (3%)
    ppermute x24, waiting for transfers between devices, shift(): return lax.ppermute(array, axis, pairs)  41.2 us
    ppermute x24, starting transfers between devices, shift(): return lax.ppermute(array, axis, pairs)  34 us
    pallas_call x1, Pallas kernels, early_sums(): pl.pallas_call(body, out_shape=shape, in_specs=[ANY] * n + [VMEM], out_sp...  8.44 us
    ppermute x5, waiting for transfers between devices, sibling(): return lax.ppermute(array, 'aux', [(i, i ^ 1) for i in range(size)])  4.72 us
    dynamic_slice x2, local copies, waits for them, and re-layouts, sends(): lax.dynamic_slice_in_dim(source, (v - r) % nv * take + first, size, 0)  4.57 us
    pallas_call x1, Pallas kernels, last_sums(): pl.pallas_call(body, out_shape=[pltpu.HBM(x.shape, x.dtype) for x in shap...  4.34 us
  transfers between devices with their start and end apart: 29, of which 16 were waited for; matrix products, arithmetic and copies ran while one was open for 8% of the time, Pallas kernels for 11%

profile of v8, /device:TPU:0, one launch (start us, length us, event | category | flops | bytes accessed | tf_op | source)
XLA Modules:
  0.0 107.4 jit_solution(12101562046477305631)
XLA Ops:
  0.0 1.0 copy-done
  1.1 3.0 %collective-permute-start = (bf16[2,128,256]{2,1,0:T(8,128)(2,1)S(1)}, bf16[2,128,256]{2,1,0:T(8,128)(2,1)S(1)}, u32[]{:S(2)}, u32[]{:S(2)}) collective-permute-start(bf16[2,128,256]{2,1,0:T(8,128)(2,1)S(1)} %dynamic-slice_convert_fusion.2), channel_id=1, source_target_pairs={{0,2},{2,0},{1,3},{3,1},{4,6},{6,4},{5,7},{7,5},{8,10},{10,8},{9,1... | collective-permute-start | bytes 393224 | tf_op jit(solution)/shard_map/ppermute | solution.py:35
  4.1 2.7 %constant_dynamic-slice_fusion.2 = bf16[3,256,1024]{2,1,0:T(8,128)(2,1)} fusion(bf16[8,256,1024]{2,1,0:T(8,128)(2,1)} %param.2, s32[]{:T(128)S(6)} %select_n.177), kind=kLoop, calls=%fused_computation.64 | loop fusion | bytes 3145732 | tf_op jit(solution)/shard_map/dynamic_slice | solution.py:336
  6.8 0.8 collective-permute-done
  7.6 1.7 %collective-permute-start.4 = (bf16[3,256,1024]{2,1,0:T(8,128)(2,1)}, bf16[3,256,1024]{2,1,0:T(8,128)(2,1)}, u32[]{:S(2)}, u32[]{:S(2)}) collective-permute-start(bf16[3,256,1024]{2,1,0:T(8,128)(2,1)} %constant_dynamic-slice_fusion.2), channel_id=1, source_target_pairs={{0,2},{2,0},{1,3},{3,1},{4,6},{6,4},{5,7},{7,5},{8,10},{10,8},{9,1... | collective-permute-start | bytes 4718600 | tf_op jit(solution)/shard_map/ppermute | solution.py:35
  9.4 1.3 %collective-permute-done.1 = bf16[2,1,128,256]{3,2,0,1:T(8,128)(2,1)S(1)} collective-permute-done((bf16[2,1,128,256]{3,2,0,1:T(8,128)(2,1)S(1)}, bf16[2,1,128,256]{3,2,0,1:T(8,128)(2,1)S(1)}, u32[]{:S(2)}, u32[]{:S(2)}) %collective-permute-start.1) | collective-permute-done | bytes 131104 | tf_op jit(solution)/shard_map/ppermute | solution.py:39
  10.9 1.6 %collective-permute-start.2 = (bf16[2,128,512]{2,1,0:T(8,128)(2,1)S(1)}, bf16[2,128,512]{2,1,0:T(8,128)(2,1)S(1)}, u32[]{:S(2)}, u32[]{:S(2)}) collective-permute-start(bf16[2,128,512]{2,1,0:T(8,128)(2,1)S(1)} %maximum_select_fusion.refs_0_), channel_id=1, source_target_pairs={{0,1},{1,0},{2,3},{3,2},{4,5},{5,4},{6,7},{7,6},{8,9},{9,8},{10,11... | collective-permute-start | bytes 786440 | tf_op jit(solution)/shard_map/ppermute | solution.py:35
  12.5 2.6 %collective-permute-start.9 = (bf16[2,128,512]{2,1,0:T(8,128)(2,1)S(1)}, bf16[2,128,512]{2,1,0:T(8,128)(2,1)S(1)}, u32[]{:S(2)}, u32[]{:S(2)}) collective-permute-start(bf16[2,128,512]{2,1,0:T(8,128)(2,1)S(1)} %maximum_select_fusion.refs_0_), channel_id=1, source_target_pairs={{0,16},{4,20},{8,24},{12,28},{16,0},{20,4},{24,8},{28,12},{1,17},{... | collective-permute-start | bytes 786440 | tf_op jit(solution)/shard_map/ppermute | solution.py:35
  15.1 1.6 %collective-permute-start.5 = (bf16[2,128,512]{2,1,0:T(8,128)(2,1)S(1)}, bf16[2,128,512]{2,1,0:T(8,128)(2,1)}, u32[]{:S(2)}, u32[]{:S(2)}) collective-permute-start(bf16[2,128,512]{2,1,0:T(8,128)(2,1)S(1)} %maximum_select_fusion.refs_0_), channel_id=1, source_target_pairs={{0,8},{4,12},{8,16},{12,20},{16,24},{20,28},{24,0},{28,4},{1,9},{5... | collective-permute-start | bytes 786440 | tf_op jit(solution)/shard_map/ppermute | solution.py:35
  16.7 2.2 %collective-permute-start.7 = (bf16[2,128,512]{2,1,0:T(8,128)(2,1)S(1)}, bf16[2,128,512]{2,1,0:T(8,128)(2,1)}, u32[]{:S(2)}, u32[]{:S(2)}) collective-permute-start(bf16[2,128,512]{2,1,0:T(8,128)(2,1)S(1)} %maximum_select_fusion.refs_0_), channel_id=1, source_target_pairs={{0,24},{4,28},{8,0},{12,4},{16,8},{20,12},{24,16},{28,20},{1,25},{... | collective-permute-start | bytes 786440 | tf_op jit(solution)/shard_map/ppermute | solution.py:35
  19.3 1.9 %constant_dynamic-slice_fusion.1.refs_0_.refs_1_ = bf16[4,256,1024]{2,1,0:T(8,128)(2,1)S(1)} fusion(bf16[8,256,1024]{2,1,0:T(8,128)(2,1)} %param.2, s32[]{:T(128)S(6)} %select_n.181), kind=kLoop, calls=%fused_computation.63 | loop fusion | bytes 4194308 | tf_op jit(solution)/shard_map/dynamic_slice | solution.py:374
  21.3 12.6 %collective-permute-done.9.refs_6_ = bf16[2,128,512]{2,1,0:T(8,128)(2,1)S(1)} collective-permute-done((bf16[2,128,512]{2,1,0:T(8,128)(2,1)S(1)}, bf16[2,128,512]{2,1,0:T(8,128)(2,1)S(1)}, u32[]{:S(2)}, u32[]{:S(2)}) %collective-permute-start.9) | collective-permute-done | bytes 262176 | tf_op jit(solution)/shard_map/ppermute | solution.py:35
  34.4 1.5 %collective-permute-start.6 = (bf16[2,128,512]{2,1,0:T(8,128)(2,1)}, bf16[2,128,512]{2,1,0:T(8,128)(2,1)}, u32[]{:S(2)}, u32[]{:S(2)}) collective-permute-start(bf16[2,128,512]{2,1,0:T(8,128)(2,1)} %collective-permute-done.5.refs_2_), channel_id=1, source_target_pairs={{0,1},{1,0},{2,3},{3,2},{4,5},{5,4},{6,7},{7,6},{8,9},{9,8},{10,11... | collective-permute-start | bytes 786440 | tf_op jit(solution)/shard_map/ppermute | solution.py:35
  35.9 0.5 collective-permute-start.8
  36.4 1.9 %constant_dynamic-slice_fusion = bf16[1,256,1024]{2,1,0:T(8,128)(2,1)} fusion(bf16[8,256,1024]{2,1,0:T(8,128)(2,1)} %param.2, s32[]{:T(128)S(6)} %select_n.182), kind=kLoop, calls=%fused_computation.62 | loop fusion | bytes 1048580 | tf_op jit(solution)/shard_map/dynamic_slice | solution.py:336
  38.3 4.8 %collective-permute-done.10.refs_7_ = bf16[2,128,512]{2,1,0:T(8,128)(2,1)S(1)} collective-permute-done((bf16[2,128,512]{2,1,0:T(8,128)(2,1)S(1)}, bf16[2,128,512]{2,1,0:T(8,128)(2,1)S(1)}, u32[]{:S(2)}, u32[]{:S(2)}) %collective-permute-start.10) | collective-permute-done | bytes 262176 | tf_op jit(solution)/shard_map/ppermute | solution.py:35
  43.1 5.4 %collective-permute-done.6.refs_3_ = bf16[2,128,512]{2,1,0:T(8,128)(2,1)} collective-permute-done((bf16[2,128,512]{2,1,0:T(8,128)(2,1)}, bf16[2,128,512]{2,1,0:T(8,128)(2,1)}, u32[]{:S(2)}, u32[]{:S(2)}) %collective-permute-start.6) | collective-permute-done | bytes 262176 | tf_op jit(solution)/shard_map/ppermute | solution.py:35
  48.5 2.7 %collective-permute-done.8.refs_5_ = bf16[2,128,512]{2,1,0:T(8,128)(2,1)S(1)} collective-permute-done((bf16[2,128,512]{2,1,0:T(8,128)(2,1)}, bf16[2,128,512]{2,1,0:T(8,128)(2,1)S(1)}, u32[]{:S(2)}, u32[]{:S(2)}) %collective-permute-start.8) | collective-permute-done | bytes 262176 | tf_op jit(solution)/shard_map/ppermute | solution.py:35
  51.2 0.7 copy-done.8
  51.9 0.5 collective-permute-start.3
  52.6 2.1 %assemble.1.refs_4_.refs_2_.refs_6_ = bf16[2,256,2048]{2,1,0:T(8,128)(2,1)S(1)} custom-call(s32[6]{0:T(128)S(1)} %stack.27.at, bf16[2,128,512]{2,1,0:T(8,128)(2,1)} %copy-done.1, bf16[2,128,512]{2,1,0:T(8,128)(2,1)} %copy-done.5, bf16[2,128,512]{2,1,0:T(8,128)(2,1)} %collective-permute-done.5.refs_2_, bf16[2,128,512]{2,1,0:T(8,128)(2,1)} %collective-permute-done.6.refs_3_, ...), custom_call_target="tpu_custom_call" | custom-call | bytes 2097152 | tf_op jit(solution)/shard_map/assemble/pallas_call | solution.py:80
  54.7 1.0 collective-permute-done.12.refs_3_
  55.7 8.4 %early_sums.1.refs_7_ = f32[2,256,2048]{2,1,0:T(8,128)S(1)} custom-call(bf16[4,256,1024]{2,1,0:T(8,128)(2,1)S(1)} %constant_dynamic-slice_fusion.1.refs_0_.refs_1_, bf16[3,256,1024]{2,1,0:T(8,128)(2,1)} %collective-permute-done.4.refs_1_, bf16[4,256,1024]{2,1,0:T(8,128)(2,1)} %collective-permute-done.11.refs_2_.refs_3_, ...), custom_call_target="tpu_custom_call" | custom-call | bytes 2097152 | tf_op jit(solution)/shard_map/early_sums/pallas_call | solution.py:149
  64.1 2.4 %collective-permute-done.3.refs_1_.refs_2_ = bf16[1,256,1024]{2,1,0:T(8,128)(2,1)S(1)} collective-permute-done((bf16[1,256,1024]{2,1,0:T(8,128)(2,1)}, bf16[1,256,1024]{2,1,0:T(8,128)(2,1)S(1)}, u32[]{:S(2)}, u32[]{:S(2)}) %collective-permute-start.3) | collective-permute-done | bytes 524320 | tf_op jit(solution)/shard_map/ppermute | solution.py:35
  66.5 0.8 step_pairs.1.refs_5_
  67.3 1.1 collective-permute-done.13.refs_4_
  68.4 4.3 %last_sums.1 = (bf16[1,2,32,2048]{3,2,1,0:T(8,128)(2,1)}, f32[1,2,32,2048]{3,2,1,0:T(8,128)}, bf16[1,2,32,2048]{3,2,1,0:T(8,128)(2,1)}, f32[2,32,2048]{2,1,0:T(8...) custom-call(s32[1]{0:T(128)} %bitcast.refs_0_, ...), custom_call_target="tpu_custom_call" | custom-call | bytes 3145728 | tf_op jit(solution)/shard_map/last_sums/pallas_call | solution.py:299
  72.8 0.6 collective-permute-start.23
  73.3 0.7 collective-permute-start.21
  74.0 1.4 %collective-permute-start.16 = (bf16[2,32,2048]{2,1,0:T(8,128)(2,1)}, bf16[2,32,2048]{2,1,0:T(8,128)(2,1)S(1)}, u32[]{:S(2)}, u32[]{:S(2)}) collective-permute-start(bf16[2,32,2048]{2,1,0:T(8,128)(2,1)} %bitcast.29), channel_id=1, source_target_pairs={{0,1},{1,0},{2,3},{3,2},{4,5},{5,4},{6,7},{7,6},{8,9},{9,8},{10,11... | collective-permute-start | bytes 786440 | tf_op jit(solution)/shard_map/ppermute | solution.py:35
  75.4 1.5 %collective-permute-start.14 = (bf16[1,2,32,2048]{3,2,1,0:T(8,128)(2,1)}, bf16[1,2,32,2048]{3,2,1,0:T(8,128)(2,1)S(1)}, u32[]{:S(2)}, u32[]{:S(2)}) collective-permute-start(bf16[1,2,32,2048]{3,2,1,0:T(8,128)(2,1)} %get-tuple-element.28), channel_id=1, source_target_pairs={{0,2},{2,0},{1,3},{3,1},{4,6},{6,4},{5,7},{7,5},{8,10},{10,8},{9,1... | collective-permute-start | bytes 786440 | tf_op jit(solution)/shard_map/ppermute | solution.py:35
  76.9 5.3 %collective-permute-done.23 = bf16[2,32,2048]{2,1,0:T(8,128)(2,1)S(1)} collective-permute-done((bf16[2,32,2048]{2,1,0:T(8,128)(2,1)}, bf16[2,32,2048]{2,1,0:T(8,128)(2,1)S(1)}, u32[]{:S(2)}, u32[]{:S(2)}) %collective-permute-start.23) | collective-permute-done | bytes 262176 | tf_op jit(solution)/shard_map/ppermute | solution.py:35
  82.2 1.1 %convert_add_fusion = f32[2,32,2048]{2,1,0:T(8,128)S(1)} fusion(f32[2,32,2048]{2,1,0:T(8,128)} %get-tuple-element.33, bf16[2,32,2048]{2,1,0:T(8,128)(2,1)S(1)} %collective-permute-done.23), kind=kLoop, calls=%fused_computation.16 | loop fusion | flops 262144 | bytes 1310720 | tf_op jit(solution)/shard_map/add | solution.py:401
  83.4 0.6 collective-permute-start.24
  84.1 0.7 collective-permute-start.22
  84.8 3.0 %collective-permute-done.16 = bf16[2,32,2048]{2,1,0:T(8,128)(2,1)S(1)} collective-permute-done((bf16[2,32,2048]{2,1,0:T(8,128)(2,1)}, bf16[2,32,2048]{2,1,0:T(8,128)(2,1)S(1)}, u32[]{:S(2)}, u32[]{:S(2)}) %collective-permute-start.16) | collective-permute-done | bytes 262176 | tf_op jit(solution)/shard_map/ppermute | solution.py:35
  87.9 0.6 collective-permute-start.17
  88.6 1.4 %collective-permute-start.15 = (bf16[1,32,2048]{2,1,0:T(8,128)(2,1)S(1)}, bf16[1,32,2048]{2,1,0:T(8,128)(2,1)S(1)}, u32[]{:S(2)}, u32[]{:S(2)}) collective-permute-start(bf16[1,32,2048]{2,1,0:T(8,128)(2,1)S(1)} %fusion), channel_id=1, source_target_pairs={{0,1},{1,0},{2,3},{3,2},{4,5},{5,4},{6,7},{7,6},{8,9},{9,8},{10,11... | collective-permute-start | bytes 393224 | tf_op jit(solution)/shard_map/ppermute | solution.py:35
  90.0 0.9 collective-permute-done.24
  91.2 1.9 %collective-permute-start.25 = (bf16[1,64,512]{2,1,0:T(8,128)(2,1)S(1)}, bf16[1,64,512]{2,1,0:T(8,128)(2,1)S(1)}, u32[]{:S(2)}, u32[]{:S(2)}) collective-permute-start(bf16[1,64,512]{2,1,0:T(8,128)(2,1)S(1)} %get-tuple-element.35), channel_id=1, source_target_pairs={{0,8},{4,12},{8,16},{12,20},{16,24},{20,28},{24,0},{28,4},{1,9},{5... | collective-permute-start | bytes 196616 | tf_op jit(solution)/shard_map/ppermute | solution.py:35
  93.1 2.1 %collective-permute-start.26 = (bf16[1,64,512]{2,1,0:T(8,128)(2,1)S(1)}, bf16[1,64,512]{2,1,0:T(8,128)(2,1)S(1)}, u32[]{:S(2)}, u32[]{:S(2)}) collective-permute-start(bf16[1,64,512]{2,1,0:T(8,128)(2,1)S(1)} %get-tuple-element.36), channel_id=1, source_target_pairs={{0,16},{4,20},{8,24},{12,28},{16,0},{20,4},{24,8},{28,12},{1,17},{... | collective-permute-start | bytes 196616 | tf_op jit(solution)/shard_map/ppermute | solution.py:35
  95.2 2.8 %collective-permute-start.27 = (bf16[1,64,512]{2,1,0:T(8,128)(2,1)S(1)}, bf16[1,64,512]{2,1,0:T(8,128)(2,1)S(1)}, u32[]{:S(2)}, u32[]{:S(2)}) collective-permute-start(bf16[1,64,512]{2,1,0:T(8,128)(2,1)S(1)} %get-tuple-element.37), channel_id=1, source_target_pairs={{0,24},{4,28},{8,0},{12,4},{16,8},{20,12},{24,16},{28,20},{1,25},{... | collective-permute-start | bytes 196616 | tf_op jit(solution)/shard_map/ppermute | solution.py:35
  98.3 0.6 collective-permute-start.19
  98.9 3.3 %collective-permute-start.20 = (bf16[1,64,512]{2,1,0:T(8,128)(2,1)S(1)}, bf16[1,64,512]{2,1,0:T(8,128)(2,1)S(1)}, u32[]{:S(2)}, u32[]{:S(2)}) collective-permute-start(bf16[1,64,512]{2,1,0:T(8,128)(2,1)S(1)} %get-tuple-element.40), channel_id=1, source_target_pairs={{0,24},{4,28},{8,0},{12,4},{16,8},{20,12},{24,16},{28,20},{1,25},{... | collective-permute-start | bytes 196616 | tf_op jit(solution)/shard_map/ppermute | solution.py:35
  102.3 2.1 %collective-permute-done.18 = bf16[1,64,512]{2,1,0:T(8,128)(2,1)S(1)} collective-permute-done((bf16[1,64,512]{2,1,0:T(8,128)(2,1)S(1)}, bf16[1,64,512]{2,1,0:T(8,128)(2,1)S(1)}, u32[]{:S(2)}, u32[]{:S(2)}) %collective-permute-start.18) | collective-permute-done | bytes 65568 | tf_op jit(solution)/shard_map/ppermute | solution.py:35
  104.4 0.7 collective-permute-done.20
  105.3 1.3 %collective-permute-done.28 = f32[1,128,256]{2,1,0:T(8,128)S(1)} collective-permute-done((f32[1,128,256]{2,1,0:T(8,128)S(1)}, f32[1,128,256]{2,1,0:T(8,128)S(1)}, u32[]{:S(2)}, u32[]{:S(2)}) %collective-permute-start.28) | collective-permute-done | bytes 131104 | tf_op jit(solution)/shard_map/ppermute | solution.py:39
  106.6 0.7 maximum_select_fusion.1
  (58 shorter events, 2.4 us)
Async XLA Ops:
  0.0 1.0 copy-start
  1.1 6.5 %collective-permute-start = (bf16[2,128,256]{2,1,0:T(8,128)(2,1)S(1)}, bf16[2,128,256]{2,1,0:T(8,128)(2,1)S(1)}, u32[]{:S(2)}, u32[]{:S(2)}) collective-permute-start(bf16[2,128,256]{2,1,0:T(8,128)(2,1)S(1)} %dynamic-slice_convert_fusion.2), channel_id=1, source_target_pairs={{0,2},{2,0},{1,3},{3,1},{4,6},{6,4},{5,7},{7,5},{8,10},{10,8},{9,1... | collective-permute-start | bytes 393224 | tf_op jit(solution)/shard_map/ppermute | solution.py:35
  7.6 43.7 %collective-permute-start.4 = (bf16[3,256,1024]{2,1,0:T(8,128)(2,1)}, bf16[3,256,1024]{2,1,0:T(8,128)(2,1)}, u32[]{:S(2)}, u32[]{:S(2)}) collective-permute-start(bf16[3,256,1024]{2,1,0:T(8,128)(2,1)} %constant_dynamic-slice_fusion.2), channel_id=1, source_target_pairs={{0,2},{2,0},{1,3},{3,1},{4,6},{6,4},{5,7},{7,5},{8,10},{10,8},{9,1... | collective-permute-start | bytes 4718600 | tf_op jit(solution)/shard_map/ppermute | solution.py:35
  9.4 1.4 %collective-permute-start.1 = (bf16[2,1,128,256]{3,2,0,1:T(8,128)(2,1)S(1)}, bf16[2,1,128,256]{3,2,0,1:T(8,128)(2,1)S(1)}, u32[]{:S(2)}, u32[]{:S(2)}) collective-permute-start(bf16[2,1,128,256]{3,2,0,1:T(8,128)(2,1)S(1)} %get-tuple-element.44), channel_id=1, source_target_pairs={{0,4},{4,0},{8,12},{12,8},{16,20},{20,16},{24,28},{28,24},{1,5},{5... | collective-permute-start | bytes 393224 | tf_op jit(solution)/shard_map/ppermute | solution.py:39
  10.9 10.3 %copy-start.1 = (bf16[2,128,512]{2,1,0:T(8,128)(2,1)}, bf16[2,128,512]{2,1,0:T(8,128)(2,1)S(1)}, u32[]{:S(2)}) copy-start(bf16[2,128,512]{2,1,0:T(8,128)(2,1)S(1)} %maximum_select_fusion.refs_0_) | copy-start | bytes 786436
  10.9 8.4 %collective-permute-start.2 = (bf16[2,128,512]{2,1,0:T(8,128)(2,1)S(1)}, bf16[2,128,512]{2,1,0:T(8,128)(2,1)S(1)}, u32[]{:S(2)}, u32[]{:S(2)}) collective-permute-start(bf16[2,128,512]{2,1,0:T(8,128)(2,1)S(1)} %maximum_select_fusion.refs_0_), channel_id=1, source_target_pairs={{0,1},{1,0},{2,3},{3,2},{4,5},{5,4},{6,7},{7,6},{8,9},{9,8},{10,11... | collective-permute-start | bytes 786440 | tf_op jit(solution)/shard_map/ppermute | solution.py:35
  12.5 21.4 %collective-permute-start.9 = (bf16[2,128,512]{2,1,0:T(8,128)(2,1)S(1)}, bf16[2,128,512]{2,1,0:T(8,128)(2,1)S(1)}, u32[]{:S(2)}, u32[]{:S(2)}) collective-permute-start(bf16[2,128,512]{2,1,0:T(8,128)(2,1)S(1)} %maximum_select_fusion.refs_0_), channel_id=1, source_target_pairs={{0,16},{4,20},{8,24},{12,28},{16,0},{20,4},{24,8},{28,12},{1,17},{... | collective-permute-start | bytes 786440 | tf_op jit(solution)/shard_map/ppermute | solution.py:35
  15.1 19.3 %collective-permute-start.5 = (bf16[2,128,512]{2,1,0:T(8,128)(2,1)S(1)}, bf16[2,128,512]{2,1,0:T(8,128)(2,1)}, u32[]{:S(2)}, u32[]{:S(2)}) collective-permute-start(bf16[2,128,512]{2,1,0:T(8,128)(2,1)S(1)} %maximum_select_fusion.refs_0_), channel_id=1, source_target_pairs={{0,8},{4,12},{8,16},{12,20},{16,24},{20,28},{24,0},{28,4},{1,9},{5... | collective-permute-start | bytes 786440 | tf_op jit(solution)/shard_map/ppermute | solution.py:35
  16.7 19.2 %collective-permute-start.7 = (bf16[2,128,512]{2,1,0:T(8,128)(2,1)S(1)}, bf16[2,128,512]{2,1,0:T(8,128)(2,1)}, u32[]{:S(2)}, u32[]{:S(2)}) collective-permute-start(bf16[2,128,512]{2,1,0:T(8,128)(2,1)S(1)} %maximum_select_fusion.refs_0_), channel_id=1, source_target_pairs={{0,24},{4,28},{8,0},{12,4},{16,8},{20,12},{24,16},{28,20},{1,25},{... | collective-permute-start | bytes 786440 | tf_op jit(solution)/shard_map/ppermute | solution.py:35
  19.3 1.9 %copy-start.5 = (bf16[2,128,512]{2,1,0:T(8,128)(2,1)}, bf16[2,128,512]{2,1,0:T(8,128)(2,1)S(1)}, u32[]{:S(2)}) copy-start(bf16[2,128,512]{2,1,0:T(8,128)(2,1)S(1)} %collective-permute-done.2.refs_1_) | copy-start | bytes 786436
  21.2 33.5 %collective-permute-start.11 = (bf16[4,256,1024]{2,1,0:T(8,128)(2,1)S(1)}, bf16[4,256,1024]{2,1,0:T(8,128)(2,1)}, u32[]{:S(2)}, u32[]{:S(2)}) collective-permute-start(bf16[4,256,1024]{2,1,0:T(8,128)(2,1)S(1)} %constant_dynamic-slice_fusion.1.refs_0_.refs_1_), channel_id=1, source_target_pairs={{0,4},{4,0},{8,12},{12,8},{16,20},{20,16},{24,28},{28,24},{1,5},{5... | collective-permute-start | bytes 6291464 | tf_op jit(solution)/shard_map/ppermute | solution.py:39
  33.9 17.4 %copy-start.6 = (bf16[2,128,512]{2,1,0:T(8,128)(2,1)}, bf16[2,128,512]{2,1,0:T(8,128)(2,1)S(1)}, u32[]{:S(2)}) copy-start(bf16[2,128,512]{2,1,0:T(8,128)(2,1)S(1)} %collective-permute-done.9.refs_6_) | copy-start | bytes 786436
  33.9 9.2 %collective-permute-start.10 = (bf16[2,128,512]{2,1,0:T(8,128)(2,1)S(1)}, bf16[2,128,512]{2,1,0:T(8,128)(2,1)S(1)}, u32[]{:S(2)}, u32[]{:S(2)}) collective-permute-start(bf16[2,128,512]{2,1,0:T(8,128)(2,1)S(1)} %collective-permute-done.9.refs_6_), channel_id=1, source_target_pairs={{0,1},{1,0},{2,3},{3,2},{4,5},{5,4},{6,7},{7,6},{8,9},{9,8},{10,11... | collective-permute-start | bytes 786440 | tf_op jit(solution)/shard_map/ppermute | solution.py:35
  34.4 14.1 %collective-permute-start.6 = (bf16[2,128,512]{2,1,0:T(8,128)(2,1)}, bf16[2,128,512]{2,1,0:T(8,128)(2,1)}, u32[]{:S(2)}, u32[]{:S(2)}) collective-permute-start(bf16[2,128,512]{2,1,0:T(8,128)(2,1)} %collective-permute-done.5.refs_2_), channel_id=1, source_target_pairs={{0,1},{1,0},{2,3},{3,2},{4,5},{5,4},{6,7},{7,6},{8,9},{9,8},{10,11... | collective-permute-start | bytes 786440 | tf_op jit(solution)/shard_map/ppermute | solution.py:35
  35.9 15.3 %collective-permute-start.8 = (bf16[2,128,512]{2,1,0:T(8,128)(2,1)}, bf16[2,128,512]{2,1,0:T(8,128)(2,1)S(1)}, u32[]{:S(2)}, u32[]{:S(2)}) collective-permute-start(bf16[2,128,512]{2,1,0:T(8,128)(2,1)} %collective-permute-done.7.refs_4_), channel_id=1, source_target_pairs={{0,1},{1,0},{2,3},{3,2},{4,5},{5,4},{6,7},{7,6},{8,9},{9,8},{10,11... | collective-permute-start | bytes 786440 | tf_op jit(solution)/shard_map/ppermute | solution.py:35
  43.1 9.4 %copy-start.7 = (bf16[2,128,512]{2,1,0:T(8,128)(2,1)}, bf16[2,128,512]{2,1,0:T(8,128)(2,1)S(1)}, u32[]{:S(2)}) copy-start(bf16[2,128,512]{2,1,0:T(8,128)(2,1)S(1)} %collective-permute-done.10.refs_7_) | copy-start | bytes 786436
  51.2 0.7 copy-start.8
  51.9 3.8 %collective-permute-start.12 = (bf16[3,256,1024]{2,1,0:T(8,128)(2,1)}, bf16[3,256,1024]{2,1,0:T(8,128)(2,1)}, u32[]{:S(2)}, u32[]{:S(2)}) collective-permute-start(bf16[3,256,1024]{2,1,0:T(8,128)(2,1)} %collective-permute-done.4.refs_1_), channel_id=1, source_target_pairs={{0,4},{4,0},{8,12},{12,8},{16,20},{20,16},{24,28},{28,24},{1,5},{5... | collective-permute-start | bytes 4718600 | tf_op jit(solution)/shard_map/ppermute | solution.py:39
  51.9 14.5 %collective-permute-start.3 = (bf16[1,256,1024]{2,1,0:T(8,128)(2,1)}, bf16[1,256,1024]{2,1,0:T(8,128)(2,1)S(1)}, u32[]{:S(2)}, u32[]{:S(2)}) collective-permute-start(bf16[1,256,1024]{2,1,0:T(8,128)(2,1)} %constant_dynamic-slice_fusion), channel_id=1, source_target_pairs={{0,2},{2,0},{1,3},{3,1},{4,6},{6,4},{5,7},{7,5},{8,10},{10,8},{9,1... | collective-permute-start | bytes 1572872 | tf_op jit(solution)/shard_map/ppermute | solution.py:35
  66.5 1.9 %collective-permute-start.13 = (bf16[1,256,1024]{2,1,0:T(8,128)(2,1)S(1)}, bf16[1,256,1024]{2,1,0:T(8,128)(2,1)S(1)}, u32[]{:S(2)}, u32[]{:S(2)}) collective-permute-start(bf16[1,256,1024]{2,1,0:T(8,128)(2,1)S(1)} %collective-permute-done.3.refs_1_.refs_2_), channel_id=1, source_target_pairs={{0,4},{4,0},{8,12},{12,8},{16,20},{20,16},{24,28},{28,24},{1,5},{5... | collective-permute-start | bytes 1572872 | tf_op jit(solution)/shard_map/ppermute | solution.py:39
  72.7 11.2 %copy-start.4 = (f32[1,2,32,2048]{3,2,1,0:T(8,128)S(1)}, f32[1,2,32,2048]{3,2,1,0:T(8,128)}, u32[]{:S(2)}) copy-start(f32[1,2,32,2048]{3,2,1,0:T(8,128)} %get-tuple-element.31) | copy-start | bytes 1572868
  72.7 15.1 %copy-start.3 = (f32[2,32,2048]{2,1,0:T(8,128)S(1)}, f32[2,32,2048]{2,1,0:T(8,128)}, u32[]{:S(2)}) copy-start(f32[2,32,2048]{2,1,0:T(8,128)} %get-tuple-element.29) | copy-start | bytes 1572868
  72.8 9.4 %collective-permute-start.23 = (bf16[2,32,2048]{2,1,0:T(8,128)(2,1)}, bf16[2,32,2048]{2,1,0:T(8,128)(2,1)S(1)}, u32[]{:S(2)}, u32[]{:S(2)}) collective-permute-start(bf16[2,32,2048]{2,1,0:T(8,128)(2,1)} %bitcast.30), channel_id=1, source_target_pairs={{0,1},{1,0},{2,3},{3,2},{4,5},{5,4},{6,7},{7,6},{8,9},{9,8},{10,11... | collective-permute-start | bytes 786440 | tf_op jit(solution)/shard_map/ppermute | solution.py:35
  73.3 10.6 %collective-permute-start.21 = (bf16[1,2,32,2048]{3,2,1,0:T(8,128)(2,1)}, bf16[1,2,32,2048]{3,2,1,0:T(8,128)(2,1)S(1)}, u32[]{:S(2)}, u32[]{:S(2)}) collective-permute-start(bf16[1,2,32,2048]{3,2,1,0:T(8,128)(2,1)} %get-tuple-element.32), channel_id=1, source_target_pairs={{0,2},{2,0},{1,3},{3,1},{4,6},{6,4},{5,7},{7,5},{8,10},{10,8},{9,1... | collective-permute-start | bytes 786440 | tf_op jit(solution)/shard_map/ppermute | solution.py:35
  74.0 13.8 %collective-permute-start.16 = (bf16[2,32,2048]{2,1,0:T(8,128)(2,1)}, bf16[2,32,2048]{2,1,0:T(8,128)(2,1)S(1)}, u32[]{:S(2)}, u32[]{:S(2)}) collective-permute-start(bf16[2,32,2048]{2,1,0:T(8,128)(2,1)} %bitcast.29), channel_id=1, source_target_pairs={{0,1},{1,0},{2,3},{3,2},{4,5},{5,4},{6,7},{7,6},{8,9},{9,8},{10,11... | collective-permute-start | bytes 786440 | tf_op jit(solution)/shard_map/ppermute | solution.py:35
  75.4 13.1 %collective-permute-start.14 = (bf16[1,2,32,2048]{3,2,1,0:T(8,128)(2,1)}, bf16[1,2,32,2048]{3,2,1,0:T(8,128)(2,1)S(1)}, u32[]{:S(2)}, u32[]{:S(2)}) collective-permute-start(bf16[1,2,32,2048]{3,2,1,0:T(8,128)(2,1)} %get-tuple-element.28), channel_id=1, source_target_pairs={{0,2},{2,0},{1,3},{3,1},{4,6},{6,4},{5,7},{7,5},{8,10},{10,8},{9,1... | collective-permute-start | bytes 786440 | tf_op jit(solution)/shard_map/ppermute | solution.py:35
  82.2 6.3 %copy-start.2 = (f32[1,2,32,2048]{3,2,1,0:T(8,128)S(1)}, f32[1,2,32,2048]{3,2,1,0:T(8,128)}, u32[]{:S(2)}) copy-start(f32[1,2,32,2048]{3,2,1,0:T(8,128)} %get-tuple-element.27) | copy-start | bytes 1572868
  83.4 7.6 %collective-permute-start.24 = (bf16[1,32,2048]{2,1,0:T(8,128)(2,1)S(1)}, bf16[1,32,2048]{2,1,0:T(8,128)(2,1)S(1)}, u32[]{:S(2)}, u32[]{:S(2)}) collective-permute-start(bf16[1,32,2048]{2,1,0:T(8,128)(2,1)S(1)} %slice.26), channel_id=1, source_target_pairs={{0,2},{2,0},{1,3},{3,1},{4,6},{6,4},{5,7},{7,5},{8,10},{10,8},{9,1... | collective-permute-start | bytes 393224 | tf_op jit(solution)/shard_map/ppermute | solution.py:35
  84.1 6.9 %collective-permute-start.22 = (bf16[1,32,2048]{2,1,0:T(8,128)(2,1)S(1)}, bf16[1,32,2048]{2,1,0:T(8,128)(2,1)S(1)}, u32[]{:S(2)}, u32[]{:S(2)}) collective-permute-start(bf16[1,32,2048]{2,1,0:T(8,128)(2,1)S(1)} %fusion.1), channel_id=1, source_target_pairs={{0,1},{1,0},{2,3},{3,2},{4,5},{5,4},{6,7},{7,6},{8,9},{9,8},{10,11... | collective-permute-start | bytes 393224 | tf_op jit(solution)/shard_map/ppermute | solution.py:35
  87.9 10.1 %collective-permute-start.17 = (bf16[1,32,2048]{2,1,0:T(8,128)(2,1)S(1)}, bf16[1,32,2048]{2,1,0:T(8,128)(2,1)S(1)}, u32[]{:S(2)}, u32[]{:S(2)}) collective-permute-start(bf16[1,32,2048]{2,1,0:T(8,128)(2,1)S(1)} %slice.27), channel_id=1, source_target_pairs={{0,2},{2,0},{1,3},{3,1},{4,6},{6,4},{5,7},{7,5},{8,10},{10,8},{9,1... | collective-permute-start | bytes 393224 | tf_op jit(solution)/shard_map/ppermute | solution.py:35
  88.6 9.5 %collective-permute-start.15 = (bf16[1,32,2048]{2,1,0:T(8,128)(2,1)S(1)}, bf16[1,32,2048]{2,1,0:T(8,128)(2,1)S(1)}, u32[]{:S(2)}, u32[]{:S(2)}) collective-permute-start(bf16[1,32,2048]{2,1,0:T(8,128)(2,1)S(1)} %fusion), channel_id=1, source_target_pairs={{0,1},{1,0},{2,3},{3,2},{4,5},{5,4},{6,7},{7,6},{8,9},{9,8},{10,11... | collective-permute-start | bytes 393224 | tf_op jit(solution)/shard_map/ppermute | solution.py:35
  91.2 7.7 %collective-permute-start.25 = (bf16[1,64,512]{2,1,0:T(8,128)(2,1)S(1)}, bf16[1,64,512]{2,1,0:T(8,128)(2,1)S(1)}, u32[]{:S(2)}, u32[]{:S(2)}) collective-permute-start(bf16[1,64,512]{2,1,0:T(8,128)(2,1)S(1)} %get-tuple-element.35), channel_id=1, source_target_pairs={{0,8},{4,12},{8,16},{12,20},{16,24},{20,28},{24,0},{28,4},{1,9},{5... | collective-permute-start | bytes 196616 | tf_op jit(solution)/shard_map/ppermute | solution.py:35
  93.1 9.1 %collective-permute-start.26 = (bf16[1,64,512]{2,1,0:T(8,128)(2,1)S(1)}, bf16[1,64,512]{2,1,0:T(8,128)(2,1)S(1)}, u32[]{:S(2)}, u32[]{:S(2)}) collective-permute-start(bf16[1,64,512]{2,1,0:T(8,128)(2,1)S(1)} %get-tuple-element.36), channel_id=1, source_target_pairs={{0,16},{4,20},{8,24},{12,28},{16,0},{20,4},{24,8},{28,12},{1,17},{... | collective-permute-start | bytes 196616 | tf_op jit(solution)/shard_map/ppermute | solution.py:35
  95.2 7.0 %collective-permute-start.27 = (bf16[1,64,512]{2,1,0:T(8,128)(2,1)S(1)}, bf16[1,64,512]{2,1,0:T(8,128)(2,1)S(1)}, u32[]{:S(2)}, u32[]{:S(2)}) collective-permute-start(bf16[1,64,512]{2,1,0:T(8,128)(2,1)S(1)} %get-tuple-element.37), channel_id=1, source_target_pairs={{0,24},{4,28},{8,0},{12,4},{16,8},{20,12},{24,16},{28,20},{1,25},{... | collective-permute-start | bytes 196616 | tf_op jit(solution)/shard_map/ppermute | solution.py:35
  98.2 6.1 %collective-permute-start.18 = (bf16[1,64,512]{2,1,0:T(8,128)(2,1)S(1)}, bf16[1,64,512]{2,1,0:T(8,128)(2,1)S(1)}, u32[]{:S(2)}, u32[]{:S(2)}) collective-permute-start(bf16[1,64,512]{2,1,0:T(8,128)(2,1)S(1)} %get-tuple-element.38), channel_id=1, source_target_pairs={{0,8},{4,12},{8,16},{12,20},{16,24},{20,28},{24,0},{28,4},{1,9},{5... | collective-permute-start | bytes 196616 | tf_op jit(solution)/shard_map/ppermute | solution.py:35
  98.3 6.1 %collective-permute-start.19 = (bf16[1,64,512]{2,1,0:T(8,128)(2,1)S(1)}, bf16[1,64,512]{2,1,0:T(8,128)(2,1)S(1)}, u32[]{:S(2)}, u32[]{:S(2)}) collective-permute-start(bf16[1,64,512]{2,1,0:T(8,128)(2,1)S(1)} %get-tuple-element.39), channel_id=1, source_target_pairs={{0,16},{4,20},{8,24},{12,28},{16,0},{20,4},{24,8},{28,12},{1,17},{... | collective-permute-start | bytes 196616 | tf_op jit(solution)/shard_map/ppermute | solution.py:35
  98.9 6.2 %collective-permute-start.20 = (bf16[1,64,512]{2,1,0:T(8,128)(2,1)S(1)}, bf16[1,64,512]{2,1,0:T(8,128)(2,1)S(1)}, u32[]{:S(2)}, u32[]{:S(2)}) collective-permute-start(bf16[1,64,512]{2,1,0:T(8,128)(2,1)S(1)} %get-tuple-element.40), channel_id=1, source_target_pairs={{0,24},{4,28},{8,0},{12,4},{16,8},{20,12},{24,16},{28,20},{1,25},{... | collective-permute-start | bytes 196616 | tf_op jit(solution)/shard_map/ppermute | solution.py:35
  105.2 1.4 %collective-permute-start.28 = (f32[1,128,256]{2,1,0:T(8,128)S(1)}, f32[1,128,256]{2,1,0:T(8,128)S(1)}, u32[]{:S(2)}, u32[]{:S(2)}) collective-permute-start(f32[1,128,256]{2,1,0:T(8,128)S(1)} %get-tuple-element.42), channel_id=1, source_target_pairs={{0,4},{4,0},{8,12},{12,8},{16,20},{20,16},{24,28},{28,24},{1,5},{5... | collective-permute-start | bytes 393224 | tf_op jit(solution)/shard_map/ppermute | solution.py:39

commit v9 on v8

--- a/solution.py
+++ b/solution.py
@@ -366,9 +366,9 @@
         + [(o + s) % no * own for s in range(no)]
     ).astype(jnp.int32)
     later, _ = lax.optimization_barrier((factors, blocks[no - 1][0]))
-    group = sends(later, early_steps, last_steps)
+    held = (come, sends(later, early_steps, last_steps), [b[0] for b in blocks])
+    come, group, _ = lax.optimization_barrier(held)
     come_last = along_vir(group)
-    come, _ = lax.optimization_barrier((come, (group, [b[0] for b in blocks])))
     vectors = assemble(where, blocks, groups, rows, total)
 
     kept = lax.dynamic_slice_in_dim(later, v * take, take, 0)

time: 108 us -> 103 us (0.954)
  starting transfers between devices: 34.2 us -> 29.9 us
    ppermute x24, starting transfers between devices: 34 us -> 29.6 us  [shift(): return lax.ppermute(array, axis, pairs)]
where the time goes in v9:
time: 103 us
  waiting for transfers between devices  46 us (45%)
  starting transfers between devices  29.9 us (29%)
  Pallas kernels  15.7 us (15%)
  local copies, waits for them, and re-layouts  8.39 us (8%)
  other arithmetic  2.81 us (3%)
    ppermute x24, waiting for transfers between devices, shift(): return lax.ppermute(array, axis, pairs)  41.2 us
    ppermute x24, starting transfers between devices, shift(): return lax.ppermute(array, axis, pairs)  29.6 us
    pallas_call x1, Pallas kernels, early_sums(): pl.pallas_call(body, out_shape=shape, in_specs=[ANY] * n + [VMEM], out_sp...  8.44 us
    ppermute x5, waiting for transfers between devices, sibling(): return lax.ppermute(array, 'aux', [(i, i ^ 1) for i in range(size)])  4.72 us
    dynamic_slice x2, local copies, waits for them, and re-layouts, sends(): lax.dynamic_slice_in_dim(source, (v - r) % nv * take + first, size, 0)  4.57 us
    pallas_call x1, Pallas kernels, last_sums(): pl.pallas_call(body, out_shape=[pltpu.HBM(x.shape, x.dtype) for x in shap...  4.34 us
    pallas_call x1, Pallas kernels, assemble(): pl.pallas_call(body, out_shape=shape, in_specs=[SMEM] + [ANY] * len(block...  2.13 us
  transfers between devices with their start and end apart: 29, of which 16 were waited for; matrix products, arithmetic and copies ran while one was open for 8% of the time, Pallas kernels for 11%

profile of v9, /device:TPU:0, one launch (start us, length us, event | category | flops | bytes accessed | tf_op | source)
XLA Modules:
  0.0 103.1 jit_solution(2722311858908471663)
XLA Ops:
  0.0 1.0 %copy-done = f32[2,256,256]{2,1,0:T(8,128)S(1)} copy-done((f32[2,256,256]{2,1,0:T(8,128)S(1)}, f32[2,256,256]{2,1,0:T(8,128)}, u32[]{:S(2)}) %copy-start) | copy-done | bytes 524312
  1.1 3.0 %collective-permute-start = (bf16[2,128,256]{2,1,0:T(8,128)(2,1)S(1)}, bf16[2,128,256]{2,1,0:T(8,128)(2,1)S(1)}, u32[]{:S(2)}, u32[]{:S(2)}) collective-permute-start(bf16[2,128,256]{2,1,0:T(8,128)(2,1)S(1)} %dynamic-slice_convert_fusion.2), channel_id=1, source_target_pairs={{0,2},{2,0},{1,3},{3,1},{4,6},{6,4},{5,7},{7,5},{8,10},{10,8},{9,1... | collective-permute-start | bytes 393224 | tf_op jit(solution)/shard_map/ppermute | solution.py:35
  4.1 2.7 %constant_dynamic-slice_fusion.2 = bf16[3,256,1024]{2,1,0:T(8,128)(2,1)} fusion(bf16[8,256,1024]{2,1,0:T(8,128)(2,1)} %param.2, s32[]{:T(128)S(6)} %select_n.177), kind=kLoop, calls=%fused_computation.64 | loop fusion | bytes 3145732 | tf_op jit(solution)/shard_map/dynamic_slice | solution.py:336
  6.8 0.8 collective-permute-done
  7.6 1.7 %collective-permute-start.3 = (bf16[3,256,1024]{2,1,0:T(8,128)(2,1)}, bf16[3,256,1024]{2,1,0:T(8,128)(2,1)}, u32[]{:S(2)}, u32[]{:S(2)}) collective-permute-start(bf16[3,256,1024]{2,1,0:T(8,128)(2,1)} %constant_dynamic-slice_fusion.2), channel_id=1, source_target_pairs={{0,2},{2,0},{1,3},{3,1},{4,6},{6,4},{5,7},{7,5},{8,10},{10,8},{9,1... | collective-permute-start | bytes 4718600 | tf_op jit(solution)/shard_map/ppermute | solution.py:35
  9.4 1.3 %collective-permute-done.1 = bf16[2,1,128,256]{3,2,0,1:T(8,128)(2,1)S(1)} collective-permute-done((bf16[2,1,128,256]{3,2,0,1:T(8,128)(2,1)S(1)}, bf16[2,1,128,256]{3,2,0,1:T(8,128)(2,1)S(1)}, u32[]{:S(2)}, u32[]{:S(2)}) %collective-permute-start.1) | collective-permute-done | bytes 131104 | tf_op jit(solution)/shard_map/ppermute | solution.py:39
  10.9 1.6 %collective-permute-start.2 = (bf16[2,128,512]{2,1,0:T(8,128)(2,1)S(1)}, bf16[2,128,512]{2,1,0:T(8,128)(2,1)S(1)}, u32[]{:S(2)}, u32[]{:S(2)}) collective-permute-start(bf16[2,128,512]{2,1,0:T(8,128)(2,1)S(1)} %maximum_select_fusion.refs_0_), channel_id=1, source_target_pairs={{0,1},{1,0},{2,3},{3,2},{4,5},{5,4},{6,7},{7,6},{8,9},{9,8},{10,11... | collective-permute-start | bytes 786440 | tf_op jit(solution)/shard_map/ppermute | solution.py:35
  12.5 1.6 %collective-permute-start.4 = (bf16[2,128,512]{2,1,0:T(8,128)(2,1)S(1)}, bf16[2,128,512]{2,1,0:T(8,128)(2,1)S(1)}, u32[]{:S(2)}, u32[]{:S(2)}) collective-permute-start(bf16[2,128,512]{2,1,0:T(8,128)(2,1)S(1)} %maximum_select_fusion.refs_0_), channel_id=1, source_target_pairs={{0,8},{4,12},{8,16},{12,20},{16,24},{20,28},{24,0},{28,4},{1,9},{5... | collective-permute-start | bytes 786440 | tf_op jit(solution)/shard_map/ppermute | solution.py:35
  14.1 2.2 %collective-permute-start.6 = (bf16[2,128,512]{2,1,0:T(8,128)(2,1)S(1)}, bf16[2,128,512]{2,1,0:T(8,128)(2,1)}, u32[]{:S(2)}, u32[]{:S(2)}) collective-permute-start(bf16[2,128,512]{2,1,0:T(8,128)(2,1)S(1)} %maximum_select_fusion.refs_0_), channel_id=1, source_target_pairs={{0,24},{4,28},{8,0},{12,4},{16,8},{20,12},{24,16},{28,20},{1,25},{... | collective-permute-start | bytes 786440 | tf_op jit(solution)/shard_map/ppermute | solution.py:35
  16.3 0.8 collective-permute-start.8
  17.1 2.2 %collective-permute-done.2.refs_1_ = bf16[2,128,512]{2,1,0:T(8,128)(2,1)S(1)} collective-permute-done((bf16[2,128,512]{2,1,0:T(8,128)(2,1)S(1)}, bf16[2,128,512]{2,1,0:T(8,128)(2,1)S(1)}, u32[]{:S(2)}, u32[]{:S(2)}) %collective-permute-start.2) | collective-permute-done | bytes 262176 | tf_op jit(solution)/shard_map/ppermute | solution.py:35
  19.3 1.9 %constant_dynamic-slice_fusion.1.refs_0_.refs_1_ = bf16[4,256,1024]{2,1,0:T(8,128)(2,1)S(1)} fusion(bf16[8,256,1024]{2,1,0:T(8,128)(2,1)} %param.2, s32[]{:T(128)S(6)} %select_n.181), kind=kLoop, calls=%fused_computation.63 | loop fusion | bytes 4194308 | tf_op jit(solution)/shard_map/dynamic_slice | solution.py:374
  21.3 2.2 %collective-permute-done.4.refs_2_ = bf16[2,128,512]{2,1,0:T(8,128)(2,1)S(1)} collective-permute-done((bf16[2,128,512]{2,1,0:T(8,128)(2,1)S(1)}, bf16[2,128,512]{2,1,0:T(8,128)(2,1)S(1)}, u32[]{:S(2)}, u32[]{:S(2)}) %collective-permute-start.4) | collective-permute-done | bytes 262176 | tf_op jit(solution)/shard_map/ppermute | solution.py:35
  23.5 0.5 collective-permute-start.5
  24.0 3.6 %collective-permute-done.6.refs_4_ = bf16[2,128,512]{2,1,0:T(8,128)(2,1)} collective-permute-done((bf16[2,128,512]{2,1,0:T(8,128)(2,1)S(1)}, bf16[2,128,512]{2,1,0:T(8,128)(2,1)}, u32[]{:S(2)}, u32[]{:S(2)}) %collective-permute-start.6) | collective-permute-done | bytes 262176 | tf_op jit(solution)/shard_map/ppermute | solution.py:35
  28.1 11.3 %collective-permute-done.8.refs_6_ = bf16[2,128,512]{2,1,0:T(8,128)(2,1)} collective-permute-done((bf16[2,128,512]{2,1,0:T(8,128)(2,1)S(1)}, bf16[2,128,512]{2,1,0:T(8,128)(2,1)}, u32[]{:S(2)}, u32[]{:S(2)}) %collective-permute-start.8) | collective-permute-done | bytes 262176 | tf_op jit(solution)/shard_map/ppermute | solution.py:35
  39.9 1.9 %constant_dynamic-slice_fusion = bf16[1,256,1024]{2,1,0:T(8,128)(2,1)} fusion(bf16[8,256,1024]{2,1,0:T(8,128)(2,1)} %param.2, s32[]{:T(128)S(6)} %select_n.182), kind=kLoop, calls=%fused_computation.62 | loop fusion | bytes 1048580 | tf_op jit(solution)/shard_map/dynamic_slice | solution.py:336
  41.8 6.0 %collective-permute-done.9.refs_7_ = bf16[2,128,512]{2,1,0:T(8,128)(2,1)S(1)} collective-permute-done((bf16[2,128,512]{2,1,0:T(8,128)(2,1)}, bf16[2,128,512]{2,1,0:T(8,128)(2,1)S(1)}, u32[]{:S(2)}, u32[]{:S(2)}) %collective-permute-start.9) | collective-permute-done | bytes 262176 | tf_op jit(solution)/shard_map/ppermute | solution.py:35
  47.8 0.7 copy-done.8
  48.5 0.5 collective-permute-start.10
  49.2 2.1 %assemble.1.refs_4_.refs_2_.refs_6_ = bf16[2,256,2048]{2,1,0:T(8,128)(2,1)S(1)} custom-call(s32[6]{0:T(128)S(1)} %stack.27.at, bf16[2,128,512]{2,1,0:T(8,128)(2,1)} %copy-done.1, bf16[2,128,512]{2,1,0:T(8,128)(2,1)} %copy-done.5, bf16[2,128,512]{2,1,0:T(8,128)(2,1)} %copy-done.6, bf16[2,128,512]{2,1,0:T(8,128)(2,1)} %copy-done.7, ...), custom_call_target="tpu_custom_call" | custom-call | bytes 2097152 | tf_op jit(solution)/shard_map/assemble/pallas_call | solution.py:80
  51.3 1.0 collective-permute-done.12.refs_3_
  52.3 8.4 %early_sums.1.refs_7_ = f32[2,256,2048]{2,1,0:T(8,128)S(1)} custom-call(bf16[4,256,1024]{2,1,0:T(8,128)(2,1)S(1)} %constant_dynamic-slice_fusion.1.refs_0_.refs_1_, bf16[3,256,1024]{2,1,0:T(8,128)(2,1)} %collective-permute-done.3.refs_1_, bf16[4,256,1024]{2,1,0:T(8,128)(2,1)} %collective-permute-done.11.refs_2_.refs_3_, ...), custom_call_target="tpu_custom_call" | custom-call | bytes 2097152 | tf_op jit(solution)/shard_map/early_sums/pallas_call | solution.py:149
  60.7 2.4 %collective-permute-done.10.refs_1_.refs_2_ = bf16[1,256,1024]{2,1,0:T(8,128)(2,1)S(1)} collective-permute-done((bf16[1,256,1024]{2,1,0:T(8,128)(2,1)}, bf16[1,256,1024]{2,1,0:T(8,128)(2,1)S(1)}, u32[]{:S(2)}, u32[]{:S(2)}) %collective-permute-start.10) | collective-permute-done | bytes 524320 | tf_op jit(solution)/shard_map/ppermute | solution.py:35
  63.1 0.8 step_pairs.1.refs_5_
  63.9 1.1 %collective-permute-done.13.refs_4_ = bf16[1,256,1024]{2,1,0:T(8,128)(2,1)S(1)} collective-permute-done((bf16[1,256,1024]{2,1,0:T(8,128)(2,1)S(1)}, bf16[1,256,1024]{2,1,0:T(8,128)(2,1)S(1)}, u32[]{:S(2)}, u32[]{:S(2)}) %collective-permute-start.13) | collective-permute-done | bytes 524320 | tf_op jit(solution)/shard_map/ppermute | solution.py:39
  65.0 4.3 %last_sums.1 = (bf16[1,2,32,2048]{3,2,1,0:T(8,128)(2,1)}, f32[1,2,32,2048]{3,2,1,0:T(8,128)}, bf16[1,2,32,2048]{3,2,1,0:T(8,128)(2,1)}, f32[2,32,2048]{2,1,0:T(8...) custom-call(s32[1]{0:T(128)} %bitcast.refs_0_, ...), custom_call_target="tpu_custom_call" | custom-call | bytes 3145728 | tf_op jit(solution)/shard_map/last_sums/pallas_call | solution.py:299
  69.4 0.6 collective-permute-start.23
  69.9 0.5 collective-permute-start.21
  70.5 1.5 %collective-permute-start.16 = (bf16[2,32,2048]{2,1,0:T(8,128)(2,1)}, bf16[2,32,2048]{2,1,0:T(8,128)(2,1)S(1)}, u32[]{:S(2)}, u32[]{:S(2)}) collective-permute-start(bf16[2,32,2048]{2,1,0:T(8,128)(2,1)} %bitcast.29), channel_id=1, source_target_pairs={{0,1},{1,0},{2,3},{3,2},{4,5},{5,4},{6,7},{7,6},{8,9},{9,8},{10,11... | collective-permute-start | bytes 786440 | tf_op jit(solution)/shard_map/ppermute | solution.py:35
  72.0 1.5 %collective-permute-start.14 = (bf16[1,2,32,2048]{3,2,1,0:T(8,128)(2,1)}, bf16[1,2,32,2048]{3,2,1,0:T(8,128)(2,1)S(1)}, u32[]{:S(2)}, u32[]{:S(2)}) collective-permute-start(bf16[1,2,32,2048]{3,2,1,0:T(8,128)(2,1)} %get-tuple-element.30), channel_id=1, source_target_pairs={{0,2},{2,0},{1,3},{3,1},{4,6},{6,4},{5,7},{7,5},{8,10},{10,8},{9,1... | collective-permute-start | bytes 786440 | tf_op jit(solution)/shard_map/ppermute | solution.py:35
  73.5 5.3 %collective-permute-done.23 = bf16[2,32,2048]{2,1,0:T(8,128)(2,1)S(1)} collective-permute-done((bf16[2,32,2048]{2,1,0:T(8,128)(2,1)}, bf16[2,32,2048]{2,1,0:T(8,128)(2,1)S(1)}, u32[]{:S(2)}, u32[]{:S(2)}) %collective-permute-start.23) | collective-permute-done | bytes 262176 | tf_op jit(solution)/shard_map/ppermute | solution.py:35
  78.8 1.1 %convert_add_fusion = f32[2,32,2048]{2,1,0:T(8,128)S(1)} fusion(f32[2,32,2048]{2,1,0:T(8,128)} %get-tuple-element.35, bf16[2,32,2048]{2,1,0:T(8,128)(2,1)S(1)} %collective-permute-done.23), kind=kLoop, calls=%fused_computation.16 | loop fusion | flops 262144 | bytes 1310720 | tf_op jit(solution)/shard_map/add | solution.py:401
  80.0 0.6 collective-permute-start.24
  80.7 0.6 collective-permute-start.22
  81.2 3.2 %collective-permute-done.16 = bf16[2,32,2048]{2,1,0:T(8,128)(2,1)S(1)} collective-permute-done((bf16[2,32,2048]{2,1,0:T(8,128)(2,1)}, bf16[2,32,2048]{2,1,0:T(8,128)(2,1)S(1)}, u32[]{:S(2)}, u32[]{:S(2)}) %collective-permute-start.16) | collective-permute-done | bytes 262176 | tf_op jit(solution)/shard_map/ppermute | solution.py:35
  84.5 0.6 collective-permute-start.17
  85.2 1.4 %collective-permute-start.15 = (bf16[1,32,2048]{2,1,0:T(8,128)(2,1)S(1)}, bf16[1,32,2048]{2,1,0:T(8,128)(2,1)S(1)}, u32[]{:S(2)}, u32[]{:S(2)}) collective-permute-start(bf16[1,32,2048]{2,1,0:T(8,128)(2,1)S(1)} %fusion), channel_id=1, source_target_pairs={{0,1},{1,0},{2,3},{3,2},{4,5},{5,4},{6,7},{7,6},{8,9},{9,8},{10,11... | collective-permute-start | bytes 393224 | tf_op jit(solution)/shard_map/ppermute | solution.py:35
  86.6 0.9 collective-permute-done.24
  87.8 0.6 collective-permute-start.25
  88.4 2.0 %collective-permute-start.26 = (bf16[1,64,512]{2,1,0:T(8,128)(2,1)S(1)}, bf16[1,64,512]{2,1,0:T(8,128)(2,1)S(1)}, u32[]{:S(2)}, u32[]{:S(2)}) collective-permute-start(bf16[1,64,512]{2,1,0:T(8,128)(2,1)S(1)} %get-tuple-element.38), channel_id=1, source_target_pairs={{0,16},{4,20},{8,24},{12,28},{16,0},{20,4},{24,8},{28,12},{1,17},{... | collective-permute-start | bytes 196616 | tf_op jit(solution)/shard_map/ppermute | solution.py:35
  90.4 2.8 %collective-permute-start.27 = (bf16[1,64,512]{2,1,0:T(8,128)(2,1)S(1)}, bf16[1,64,512]{2,1,0:T(8,128)(2,1)S(1)}, u32[]{:S(2)}, u32[]{:S(2)}) collective-permute-start(bf16[1,64,512]{2,1,0:T(8,128)(2,1)S(1)} %get-tuple-element.39), channel_id=1, source_target_pairs={{0,24},{4,28},{8,0},{12,4},{16,8},{20,12},{24,16},{28,20},{1,25},{... | collective-permute-start | bytes 196616 | tf_op jit(solution)/shard_map/ppermute | solution.py:35
  93.5 0.6 collective-permute-start.19
  94.1 3.3 %collective-permute-start.20 = (bf16[1,64,512]{2,1,0:T(8,128)(2,1)S(1)}, bf16[1,64,512]{2,1,0:T(8,128)(2,1)S(1)}, u32[]{:S(2)}, u32[]{:S(2)}) collective-permute-start(bf16[1,64,512]{2,1,0:T(8,128)(2,1)S(1)} %get-tuple-element.42), channel_id=1, source_target_pairs={{0,24},{4,28},{8,0},{12,4},{16,8},{20,12},{24,16},{28,20},{1,25},{... | collective-permute-start | bytes 196616 | tf_op jit(solution)/shard_map/ppermute | solution.py:35
  97.5 2.2 %collective-permute-done.18 = bf16[1,64,512]{2,1,0:T(8,128)(2,1)S(1)} collective-permute-done((bf16[1,64,512]{2,1,0:T(8,128)(2,1)S(1)}, bf16[1,64,512]{2,1,0:T(8,128)(2,1)S(1)}, u32[]{:S(2)}, u32[]{:S(2)}) %collective-permute-start.18) | collective-permute-done | bytes 65568 | tf_op jit(solution)/shard_map/ppermute | solution.py:35
  99.7 1.1 %collective-permute-done.19 = bf16[1,64,512]{2,1,0:T(8,128)(2,1)S(1)} collective-permute-done((bf16[1,64,512]{2,1,0:T(8,128)(2,1)S(1)}, bf16[1,64,512]{2,1,0:T(8,128)(2,1)S(1)}, u32[]{:S(2)}, u32[]{:S(2)}) %collective-permute-start.19) | collective-permute-done | bytes 65568 | tf_op jit(solution)/shard_map/ppermute | solution.py:35
  101.0 1.3 %collective-permute-done.28 = f32[1,128,256]{2,1,0:T(8,128)S(1)} collective-permute-done((f32[1,128,256]{2,1,0:T(8,128)S(1)}, f32[1,128,256]{2,1,0:T(8,128)S(1)}, u32[]{:S(2)}, u32[]{:S(2)}) %collective-permute-start.28) | collective-permute-done | bytes 131104 | tf_op jit(solution)/shard_map/ppermute | solution.py:39
  102.3 0.7 maximum_select_fusion.1
  (58 shorter events, 2.5 us)
Async XLA Ops:
  0.0 1.0 %copy-start = (f32[2,256,256]{2,1,0:T(8,128)S(1)}, f32[2,256,256]{2,1,0:T(8,128)}, u32[]{:S(2)}) copy-start(f32[2,256,256]{2,1,0:T(8,128)} %param.3) | copy-start | bytes 1572868
  1.1 6.5 %collective-permute-start = (bf16[2,128,256]{2,1,0:T(8,128)(2,1)S(1)}, bf16[2,128,256]{2,1,0:T(8,128)(2,1)S(1)}, u32[]{:S(2)}, u32[]{:S(2)}) collective-permute-start(bf16[2,128,256]{2,1,0:T(8,128)(2,1)S(1)} %dynamic-slice_convert_fusion.2), channel_id=1, source_target_pairs={{0,2},{2,0},{1,3},{3,1},{4,6},{6,4},{5,7},{7,5},{8,10},{10,8},{9,1... | collective-permute-start | bytes 393224 | tf_op jit(solution)/shard_map/ppermute | solution.py:35
  7.6 40.3 %collective-permute-start.3 = (bf16[3,256,1024]{2,1,0:T(8,128)(2,1)}, bf16[3,256,1024]{2,1,0:T(8,128)(2,1)}, u32[]{:S(2)}, u32[]{:S(2)}) collective-permute-start(bf16[3,256,1024]{2,1,0:T(8,128)(2,1)} %constant_dynamic-slice_fusion.2), channel_id=1, source_target_pairs={{0,2},{2,0},{1,3},{3,1},{4,6},{6,4},{5,7},{7,5},{8,10},{10,8},{9,1... | collective-permute-start | bytes 4718600 | tf_op jit(solution)/shard_map/ppermute | solution.py:35
  9.4 1.4 %collective-permute-start.1 = (bf16[2,1,128,256]{3,2,0,1:T(8,128)(2,1)S(1)}, bf16[2,1,128,256]{3,2,0,1:T(8,128)(2,1)S(1)}, u32[]{:S(2)}, u32[]{:S(2)}) collective-permute-start(bf16[2,1,128,256]{3,2,0,1:T(8,128)(2,1)S(1)} %get-tuple-element.46), channel_id=1, source_target_pairs={{0,4},{4,0},{8,12},{12,8},{16,20},{20,16},{24,28},{28,24},{1,5},{5... | collective-permute-start | bytes 393224 | tf_op jit(solution)/shard_map/ppermute | solution.py:39
  10.9 10.3 %copy-start.1 = (bf16[2,128,512]{2,1,0:T(8,128)(2,1)}, bf16[2,128,512]{2,1,0:T(8,128)(2,1)S(1)}, u32[]{:S(2)}) copy-start(bf16[2,128,512]{2,1,0:T(8,128)(2,1)S(1)} %maximum_select_fusion.refs_0_) | copy-start | bytes 786436
  10.9 8.4 %collective-permute-start.2 = (bf16[2,128,512]{2,1,0:T(8,128)(2,1)S(1)}, bf16[2,128,512]{2,1,0:T(8,128)(2,1)S(1)}, u32[]{:S(2)}, u32[]{:S(2)}) collective-permute-start(bf16[2,128,512]{2,1,0:T(8,128)(2,1)S(1)} %maximum_select_fusion.refs_0_), channel_id=1, source_target_pairs={{0,1},{1,0},{2,3},{3,2},{4,5},{5,4},{6,7},{7,6},{8,9},{9,8},{10,11... | collective-permute-start | bytes 786440 | tf_op jit(solution)/shard_map/ppermute | solution.py:35
  12.5 11.0 %collective-permute-start.4 = (bf16[2,128,512]{2,1,0:T(8,128)(2,1)S(1)}, bf16[2,128,512]{2,1,0:T(8,128)(2,1)S(1)}, u32[]{:S(2)}, u32[]{:S(2)}) collective-permute-start(bf16[2,128,512]{2,1,0:T(8,128)(2,1)S(1)} %maximum_select_fusion.refs_0_), channel_id=1, source_target_pairs={{0,8},{4,12},{8,16},{12,20},{16,24},{20,28},{24,0},{28,4},{1,9},{5... | collective-permute-start | bytes 786440 | tf_op jit(solution)/shard_map/ppermute | solution.py:35
  14.1 13.5 %collective-permute-start.6 = (bf16[2,128,512]{2,1,0:T(8,128)(2,1)S(1)}, bf16[2,128,512]{2,1,0:T(8,128)(2,1)}, u32[]{:S(2)}, u32[]{:S(2)}) collective-permute-start(bf16[2,128,512]{2,1,0:T(8,128)(2,1)S(1)} %maximum_select_fusion.refs_0_), channel_id=1, source_target_pairs={{0,24},{4,28},{8,0},{12,4},{16,8},{20,12},{24,16},{28,20},{1,25},{... | collective-permute-start | bytes 786440 | tf_op jit(solution)/shard_map/ppermute | solution.py:35
  16.3 23.1 %collective-permute-start.8 = (bf16[2,128,512]{2,1,0:T(8,128)(2,1)S(1)}, bf16[2,128,512]{2,1,0:T(8,128)(2,1)}, u32[]{:S(2)}, u32[]{:S(2)}) collective-permute-start(bf16[2,128,512]{2,1,0:T(8,128)(2,1)S(1)} %maximum_select_fusion.refs_0_), channel_id=1, source_target_pairs={{0,16},{4,20},{8,24},{12,28},{16,0},{20,4},{24,8},{28,12},{1,17},{... | collective-permute-start | bytes 786440 | tf_op jit(solution)/shard_map/ppermute | solution.py:35
  19.3 1.9 %copy-start.5 = (bf16[2,128,512]{2,1,0:T(8,128)(2,1)}, bf16[2,128,512]{2,1,0:T(8,128)(2,1)S(1)}, u32[]{:S(2)}) copy-start(bf16[2,128,512]{2,1,0:T(8,128)(2,1)S(1)} %collective-permute-done.2.refs_1_) | copy-start | bytes 786436
  21.2 30.1 %collective-permute-start.11 = (bf16[4,256,1024]{2,1,0:T(8,128)(2,1)S(1)}, bf16[4,256,1024]{2,1,0:T(8,128)(2,1)}, u32[]{:S(2)}, u32[]{:S(2)}) collective-permute-start(bf16[4,256,1024]{2,1,0:T(8,128)(2,1)S(1)} %constant_dynamic-slice_fusion.1.refs_0_.refs_1_), channel_id=1, source_target_pairs={{0,4},{4,0},{8,12},{12,8},{16,20},{20,16},{24,28},{28,24},{1,5},{5... | collective-permute-start | bytes 6291464 | tf_op jit(solution)/shard_map/ppermute | solution.py:39
  23.5 24.3 %copy-start.6 = (bf16[2,128,512]{2,1,0:T(8,128)(2,1)}, bf16[2,128,512]{2,1,0:T(8,128)(2,1)S(1)}, u32[]{:S(2)}) copy-start(bf16[2,128,512]{2,1,0:T(8,128)(2,1)S(1)} %collective-permute-done.4.refs_2_) | copy-start | bytes 786436
  23.5 18.2 %collective-permute-start.5 = (bf16[2,128,512]{2,1,0:T(8,128)(2,1)S(1)}, bf16[2,128,512]{2,1,0:T(8,128)(2,1)S(1)}, u32[]{:S(2)}, u32[]{:S(2)}) collective-permute-start(bf16[2,128,512]{2,1,0:T(8,128)(2,1)S(1)} %collective-permute-done.4.refs_2_), channel_id=1, source_target_pairs={{0,1},{1,0},{2,3},{3,2},{4,5},{5,4},{6,7},{7,6},{8,9},{9,8},{10,11... | collective-permute-start | bytes 786440 | tf_op jit(solution)/shard_map/ppermute | solution.py:35
  27.6 14.2 %collective-permute-start.7 = (bf16[2,128,512]{2,1,0:T(8,128)(2,1)}, bf16[2,128,512]{2,1,0:T(8,128)(2,1)}, u32[]{:S(2)}, u32[]{:S(2)}) collective-permute-start(bf16[2,128,512]{2,1,0:T(8,128)(2,1)} %collective-permute-done.6.refs_4_), channel_id=1, source_target_pairs={{0,1},{1,0},{2,3},{3,2},{4,5},{5,4},{6,7},{7,6},{8,9},{9,8},{10,11... | collective-permute-start | bytes 786440 | tf_op jit(solution)/shard_map/ppermute | solution.py:35
  39.4 8.4 %collective-permute-start.9 = (bf16[2,128,512]{2,1,0:T(8,128)(2,1)}, bf16[2,128,512]{2,1,0:T(8,128)(2,1)S(1)}, u32[]{:S(2)}, u32[]{:S(2)}) collective-permute-start(bf16[2,128,512]{2,1,0:T(8,128)(2,1)} %collective-permute-done.8.refs_6_), channel_id=1, source_target_pairs={{0,1},{1,0},{2,3},{3,2},{4,5},{5,4},{6,7},{7,6},{8,9},{9,8},{10,11... | collective-permute-start | bytes 786440 | tf_op jit(solution)/shard_map/ppermute | solution.py:35
  41.8 7.4 %copy-start.7 = (bf16[2,128,512]{2,1,0:T(8,128)(2,1)}, bf16[2,128,512]{2,1,0:T(8,128)(2,1)S(1)}, u32[]{:S(2)}) copy-start(bf16[2,128,512]{2,1,0:T(8,128)(2,1)S(1)} %collective-permute-done.5.refs_3_) | copy-start | bytes 786436
  47.8 0.7 copy-start.8
  48.5 3.8 %collective-permute-start.12 = (bf16[3,256,1024]{2,1,0:T(8,128)(2,1)}, bf16[3,256,1024]{2,1,0:T(8,128)(2,1)}, u32[]{:S(2)}, u32[]{:S(2)}) collective-permute-start(bf16[3,256,1024]{2,1,0:T(8,128)(2,1)} %collective-permute-done.3.refs_1_), channel_id=1, source_target_pairs={{0,4},{4,0},{8,12},{12,8},{16,20},{20,16},{24,28},{28,24},{1,5},{5... | collective-permute-start | bytes 4718600 | tf_op jit(solution)/shard_map/ppermute | solution.py:39
  48.5 14.5 %collective-permute-start.10 = (bf16[1,256,1024]{2,1,0:T(8,128)(2,1)}, bf16[1,256,1024]{2,1,0:T(8,128)(2,1)S(1)}, u32[]{:S(2)}, u32[]{:S(2)}) collective-permute-start(bf16[1,256,1024]{2,1,0:T(8,128)(2,1)} %constant_dynamic-slice_fusion), channel_id=1, source_target_pairs={{0,2},{2,0},{1,3},{3,1},{4,6},{6,4},{5,7},{7,5},{8,10},{10,8},{9,1... | collective-permute-start | bytes 1572872 | tf_op jit(solution)/shard_map/ppermute | solution.py:35
  63.1 1.9 %collective-permute-start.13 = (bf16[1,256,1024]{2,1,0:T(8,128)(2,1)S(1)}, bf16[1,256,1024]{2,1,0:T(8,128)(2,1)S(1)}, u32[]{:S(2)}, u32[]{:S(2)}) collective-permute-start(bf16[1,256,1024]{2,1,0:T(8,128)(2,1)S(1)} %collective-permute-done.10.refs_1_.refs_2_), channel_id=1, source_target_pairs={{0,4},{4,0},{8,12},{12,8},{16,20},{20,16},{24,28},{28,24},{1,5},{5... | collective-permute-start | bytes 1572872 | tf_op jit(solution)/shard_map/ppermute | solution.py:39
  69.3 11.2 %copy-start.4 = (f32[1,2,32,2048]{3,2,1,0:T(8,128)S(1)}, f32[1,2,32,2048]{3,2,1,0:T(8,128)}, u32[]{:S(2)}) copy-start(f32[1,2,32,2048]{3,2,1,0:T(8,128)} %get-tuple-element.33) | copy-start | bytes 1572868
  69.3 15.1 %copy-start.3 = (f32[2,32,2048]{2,1,0:T(8,128)S(1)}, f32[2,32,2048]{2,1,0:T(8,128)}, u32[]{:S(2)}) copy-start(f32[2,32,2048]{2,1,0:T(8,128)} %get-tuple-element.31) | copy-start | bytes 1572868
  69.4 9.4 %collective-permute-start.23 = (bf16[2,32,2048]{2,1,0:T(8,128)(2,1)}, bf16[2,32,2048]{2,1,0:T(8,128)(2,1)S(1)}, u32[]{:S(2)}, u32[]{:S(2)}) collective-permute-start(bf16[2,32,2048]{2,1,0:T(8,128)(2,1)} %bitcast.30), channel_id=1, source_target_pairs={{0,1},{1,0},{2,3},{3,2},{4,5},{5,4},{6,7},{7,6},{8,9},{9,8},{10,11... | collective-permute-start | bytes 786440 | tf_op jit(solution)/shard_map/ppermute | solution.py:35
  69.9 10.6 %collective-permute-start.21 = (bf16[1,2,32,2048]{3,2,1,0:T(8,128)(2,1)}, bf16[1,2,32,2048]{3,2,1,0:T(8,128)(2,1)S(1)}, u32[]{:S(2)}, u32[]{:S(2)}) collective-permute-start(bf16[1,2,32,2048]{3,2,1,0:T(8,128)(2,1)} %get-tuple-element.34), channel_id=1, source_target_pairs={{0,2},{2,0},{1,3},{3,1},{4,6},{6,4},{5,7},{7,5},{8,10},{10,8},{9,1... | collective-permute-start | bytes 786440 | tf_op jit(solution)/shard_map/ppermute | solution.py:35
  70.5 13.9 %collective-permute-start.16 = (bf16[2,32,2048]{2,1,0:T(8,128)(2,1)}, bf16[2,32,2048]{2,1,0:T(8,128)(2,1)S(1)}, u32[]{:S(2)}, u32[]{:S(2)}) collective-permute-start(bf16[2,32,2048]{2,1,0:T(8,128)(2,1)} %bitcast.29), channel_id=1, source_target_pairs={{0,1},{1,0},{2,3},{3,2},{4,5},{5,4},{6,7},{7,6},{8,9},{9,8},{10,11... | collective-permute-start | bytes 786440 | tf_op jit(solution)/shard_map/ppermute | solution.py:35
  72.0 13.1 %collective-permute-start.14 = (bf16[1,2,32,2048]{3,2,1,0:T(8,128)(2,1)}, bf16[1,2,32,2048]{3,2,1,0:T(8,128)(2,1)S(1)}, u32[]{:S(2)}, u32[]{:S(2)}) collective-permute-start(bf16[1,2,32,2048]{3,2,1,0:T(8,128)(2,1)} %get-tuple-element.30), channel_id=1, source_target_pairs={{0,2},{2,0},{1,3},{3,1},{4,6},{6,4},{5,7},{7,5},{8,10},{10,8},{9,1... | collective-permute-start | bytes 786440 | tf_op jit(solution)/shard_map/ppermute | solution.py:35
  78.8 6.3 %copy-start.2 = (f32[1,2,32,2048]{3,2,1,0:T(8,128)S(1)}, f32[1,2,32,2048]{3,2,1,0:T(8,128)}, u32[]{:S(2)}) copy-start(f32[1,2,32,2048]{3,2,1,0:T(8,128)} %get-tuple-element.29) | copy-start | bytes 1572868
  80.0 7.6 %collective-permute-start.24 = (bf16[1,32,2048]{2,1,0:T(8,128)(2,1)S(1)}, bf16[1,32,2048]{2,1,0:T(8,128)(2,1)S(1)}, u32[]{:S(2)}, u32[]{:S(2)}) collective-permute-start(bf16[1,32,2048]{2,1,0:T(8,128)(2,1)S(1)} %slice.26), channel_id=1, source_target_pairs={{0,2},{2,0},{1,3},{3,1},{4,6},{6,4},{5,7},{7,5},{8,10},{10,8},{9,1... | collective-permute-start | bytes 393224 | tf_op jit(solution)/shard_map/ppermute | solution.py:35
  80.7 6.9 %collective-permute-start.22 = (bf16[1,32,2048]{2,1,0:T(8,128)(2,1)S(1)}, bf16[1,32,2048]{2,1,0:T(8,128)(2,1)S(1)}, u32[]{:S(2)}, u32[]{:S(2)}) collective-permute-start(bf16[1,32,2048]{2,1,0:T(8,128)(2,1)S(1)} %fusion.1), channel_id=1, source_target_pairs={{0,1},{1,0},{2,3},{3,2},{4,5},{5,4},{6,7},{7,6},{8,9},{9,8},{10,11... | collective-permute-start | bytes 393224 | tf_op jit(solution)/shard_map/ppermute | solution.py:35
  84.5 8.7 %collective-permute-start.17 = (bf16[1,32,2048]{2,1,0:T(8,128)(2,1)S(1)}, bf16[1,32,2048]{2,1,0:T(8,128)(2,1)S(1)}, u32[]{:S(2)}, u32[]{:S(2)}) collective-permute-start(bf16[1,32,2048]{2,1,0:T(8,128)(2,1)S(1)} %slice.27), channel_id=1, source_target_pairs={{0,2},{2,0},{1,3},{3,1},{4,6},{6,4},{5,7},{7,5},{8,10},{10,8},{9,1... | collective-permute-start | bytes 393224 | tf_op jit(solution)/shard_map/ppermute | solution.py:35
  85.2 8.1 %collective-permute-start.15 = (bf16[1,32,2048]{2,1,0:T(8,128)(2,1)S(1)}, bf16[1,32,2048]{2,1,0:T(8,128)(2,1)S(1)}, u32[]{:S(2)}, u32[]{:S(2)}) collective-permute-start(bf16[1,32,2048]{2,1,0:T(8,128)(2,1)S(1)} %fusion), channel_id=1, source_target_pairs={{0,1},{1,0},{2,3},{3,2},{4,5},{5,4},{6,7},{7,6},{8,9},{9,8},{10,11... | collective-permute-start | bytes 393224 | tf_op jit(solution)/shard_map/ppermute | solution.py:35
  87.8 6.3 %collective-permute-start.25 = (bf16[1,64,512]{2,1,0:T(8,128)(2,1)S(1)}, bf16[1,64,512]{2,1,0:T(8,128)(2,1)S(1)}, u32[]{:S(2)}, u32[]{:S(2)}) collective-permute-start(bf16[1,64,512]{2,1,0:T(8,128)(2,1)S(1)} %get-tuple-element.37), channel_id=1, source_target_pairs={{0,8},{4,12},{8,16},{12,20},{16,24},{20,28},{24,0},{28,4},{1,9},{5... | collective-permute-start | bytes 196616 | tf_op jit(solution)/shard_map/ppermute | solution.py:35
  88.4 9.0 %collective-permute-start.26 = (bf16[1,64,512]{2,1,0:T(8,128)(2,1)S(1)}, bf16[1,64,512]{2,1,0:T(8,128)(2,1)S(1)}, u32[]{:S(2)}, u32[]{:S(2)}) collective-permute-start(bf16[1,64,512]{2,1,0:T(8,128)(2,1)S(1)} %get-tuple-element.38), channel_id=1, source_target_pairs={{0,16},{4,20},{8,24},{12,28},{16,0},{20,4},{24,8},{28,12},{1,17},{... | collective-permute-start | bytes 196616 | tf_op jit(solution)/shard_map/ppermute | solution.py:35
  90.4 7.0 %collective-permute-start.27 = (bf16[1,64,512]{2,1,0:T(8,128)(2,1)S(1)}, bf16[1,64,512]{2,1,0:T(8,128)(2,1)S(1)}, u32[]{:S(2)}, u32[]{:S(2)}) collective-permute-start(bf16[1,64,512]{2,1,0:T(8,128)(2,1)S(1)} %get-tuple-element.39), channel_id=1, source_target_pairs={{0,24},{4,28},{8,0},{12,4},{16,8},{20,12},{24,16},{28,20},{1,25},{... | collective-permute-start | bytes 196616 | tf_op jit(solution)/shard_map/ppermute | solution.py:35
  93.5 6.2 %collective-permute-start.18 = (bf16[1,64,512]{2,1,0:T(8,128)(2,1)S(1)}, bf16[1,64,512]{2,1,0:T(8,128)(2,1)S(1)}, u32[]{:S(2)}, u32[]{:S(2)}) collective-permute-start(bf16[1,64,512]{2,1,0:T(8,128)(2,1)S(1)} %get-tuple-element.40), channel_id=1, source_target_pairs={{0,8},{4,12},{8,16},{12,20},{16,24},{20,28},{24,0},{28,4},{1,9},{5... | collective-permute-start | bytes 196616 | tf_op jit(solution)/shard_map/ppermute | solution.py:35
  93.5 7.2 %collective-permute-start.19 = (bf16[1,64,512]{2,1,0:T(8,128)(2,1)S(1)}, bf16[1,64,512]{2,1,0:T(8,128)(2,1)S(1)}, u32[]{:S(2)}, u32[]{:S(2)}) collective-permute-start(bf16[1,64,512]{2,1,0:T(8,128)(2,1)S(1)} %get-tuple-element.41), channel_id=1, source_target_pairs={{0,16},{4,20},{8,24},{12,28},{16,0},{20,4},{24,8},{28,12},{1,17},{... | collective-permute-start | bytes 196616 | tf_op jit(solution)/shard_map/ppermute | solution.py:35
  94.1 6.7 %collective-permute-start.20 = (bf16[1,64,512]{2,1,0:T(8,128)(2,1)S(1)}, bf16[1,64,512]{2,1,0:T(8,128)(2,1)S(1)}, u32[]{:S(2)}, u32[]{:S(2)}) collective-permute-start(bf16[1,64,512]{2,1,0:T(8,128)(2,1)S(1)} %get-tuple-element.42), channel_id=1, source_target_pairs={{0,24},{4,28},{8,0},{12,4},{16,8},{20,12},{24,16},{28,20},{1,25},{... | collective-permute-start | bytes 196616 | tf_op jit(solution)/shard_map/ppermute | solution.py:35
  100.9 1.4 %collective-permute-start.28 = (f32[1,128,256]{2,1,0:T(8,128)S(1)}, f32[1,128,256]{2,1,0:T(8,128)S(1)}, u32[]{:S(2)}, u32[]{:S(2)}) collective-permute-start(f32[1,128,256]{2,1,0:T(8,128)S(1)} %get-tuple-element.44), channel_id=1, source_target_pairs={{0,4},{4,0},{8,12},{12,8},{16,20},{20,16},{24,28},{28,24},{1,5},{5... | collective-permute-start | bytes 393224 | tf_op jit(solution)/shard_map/ppermute | solution.py:39

commit v10 on v9

--- a/solution.py
+++ b/solution.py
@@ -86,7 +86,7 @@
         cost_estimate=cost(0, shape),
         compiler_params=params(),
         name="assemble",
-    )(where, *[in_hbm(b[0]) for b in blocks])
+    )(where, *[in_hbm(b[0]) for b in blocks[:-1]], blocks[-1][0])
 
 
 def pairs_of(refs, vec, store):
@@ -388,21 +388,34 @@
     out = []
     for p in last_sums(o, sides, firsts, pair_own, vectors, early, no, nv):
         send_x, keep_x, send_y, keep_y = p
-        one = keep_x
-        for r in range(1, nv):
-            sent = send_x[(r - 1) * half_m : r * half_m]
-            one += shift(sent, "vir", nv, r).astype(F32)
-        u_one = lax.dynamic_index_in_dim(one, o, 1, False)
-        for s in range(1, no):
-            sent = lax.dynamic_index_in_dim(one, (o + s) % no, 1, False).astype(BF16)
-            u_one += shift(sent, "outer", no, s).astype(F32)
-        two = keep_y
-        for s in range(1, no):
-            two += shift(send_y[s - 1], "outer", no, s).astype(F32)
-        u_two = two[:half_m]
-        for r in range(1, nv):
-            sent = two[r * half_m : (r + 1) * half_m].astype(BF16)
-            u_two += shift(sent, "vir", nv, r).astype(F32)
+        come_x = [
+            shift(send_x[(r - 1) * half_m : r * half_m], "vir", nv, r) for r in range(1, nv)
+        ]
+
+        def one(oo):
+            got = lax.dynamic_index_in_dim(keep_x, oo, 1, False)
+            for x in come_x:
+                got += lax.dynamic_index_in_dim(x, oo, 1, False).astype(F32)
+            return got
+
+        come_x2 = [shift(one((o + s) % no).astype(BF16), "outer", no, s) for s in range(1, no)]
+        u_one = one(o)
+        for x in come_x2:
+            u_one += x.astype(F32)
+
+        come_y = [shift(send_y[s - 1], "outer", no, s) for s in range(1, no)]
+
+        def two(r):
+            rows_r = slice(r * half_m, (r + 1) * half_m)
+            got = keep_y[rows_r]
+            for x in come_y:
+                got += x[rows_r].astype(F32)
+            return got
+
+        come_y2 = [shift(two(r).astype(BF16), "vir", nv, r) for r in range(1, nv)]
+        u_two = two(0)
+        for x in come_y2:
+            u_two += x.astype(F32)
         u = jnp.concatenate([u_one, u_two], axis=1)
 
         def to(zz):

time: 103 us -> 103 us (level)
  other arithmetic: 2.81 us -> 5.54 us
  waiting for transfers between devices: 46 us -> 44.4 us
    convert_element_type x0 -> x4, other arithmetic: none -> 3.98 us  [the longest x2 2.01 us: per_device(): come_y2 = [shift(two(r).astype(BF16), 'vir', nv, r) for r in range(1, nv)]]
    ppermute x24, waiting for transfers between devices: 41.2 us -> 39.6 us  [shift(): return lax.ppermute(array, axis, pairs)]
    add x8 -> x4, other arithmetic: 1.42 us -> 0.18 us  [the longest x2 0.1 us: per_device(): u_one += x.astype(F32)]
  transfers between devices with their start and end apart: 29 -> 29, of which waited for: 16 -> 15; matrix products, arithmetic and copies ran while one was open for 8% -> 11% of each run, Pallas kernels for 11% -> 11%
where the time goes in v10:
time: 103 us; the launch traced here: 102 us
  waiting for transfers between devices  44.4 us (43%)
  starting transfers between devices  29.1 us (28%)
  Pallas kernels  15.6 us (15%)
  local copies, waits for them, and re-layouts  7.52 us (7%)
  other arithmetic  5.54 us (5%)
    ppermute x24, waiting for transfers between devices, shift(): return lax.ppermute(array, axis, pairs)  39.6 us
    ppermute x24, starting transfers between devices, shift(): return lax.ppermute(array, axis, pairs)  28.8 us
    pallas_call x1, Pallas kernels, early_sums(): pl.pallas_call(body, out_shape=shape, in_specs=[ANY] * n + [VMEM], out_sp...  8.44 us
    ppermute x5, waiting for transfers between devices, sibling(): return lax.ppermute(array, 'aux', [(i, i ^ 1) for i in range(size)])  4.72 us
    dynamic_slice x2, local copies, waits for them, and re-layouts, sends(): lax.dynamic_slice_in_dim(source, (v - r) % nv * take + first, size, 0)  4.56 us
    pallas_call x1, Pallas kernels, last_sums(): pl.pallas_call(body, out_shape=[pltpu.HBM(x.shape, x.dtype) for x in shap...  4.32 us
  transfers between devices with their start and end apart: 29, of which 15 were waited for; matrix products, arithmetic and copies ran while one was open for 11% of the time, Pallas kernels for 11%

profile of v10, /device:TPU:0, one launch (start us, length us, event | category | flops | bytes accessed | tf_op | source)
XLA Modules:
  0.0 102.5 jit_solution(14651407733246172742)
XLA Ops:
  0.0 1.0 %copy-done = f32[2,256,256]{2,1,0:T(8,128)S(1)} copy-done((f32[2,256,256]{2,1,0:T(8,128)S(1)}, f32[2,256,256]{2,1,0:T(8,128)}, u32[]{:S(2)}) %copy-start) | copy-done | bytes 524312
  1.1 3.0 %collective-permute-start = (bf16[2,128,256]{2,1,0:T(8,128)(2,1)S(1)}, bf16[2,128,256]{2,1,0:T(8,128)(2,1)S(1)}, u32[]{:S(2)}, u32[]{:S(2)}) collective-permute-start(bf16[2,128,256]{2,1,0:T(8,128)(2,1)S(1)} %dynamic-slice_convert_fusion), channel_id=1, source_target_pairs={{0,2},{2,0},{1,3},{3,1},{4,6},{6,4},{5,7},{7,5},{8,10},{10,8},{9,1... | collective-permute-start | bytes 393224 | tf_op jit(solution)/shard_map/ppermute | solution.py:35
  4.1 2.7 %constant_dynamic-slice_fusion.2 = bf16[3,256,1024]{2,1,0:T(8,128)(2,1)} fusion(bf16[8,256,1024]{2,1,0:T(8,128)(2,1)} %param.2, s32[]{:T(128)S(6)} %select_n.182), kind=kLoop, calls=%fused_computation.60 | loop fusion | bytes 3145732 | tf_op jit(solution)/shard_map/dynamic_slice | solution.py:336
  6.8 0.8 collective-permute-done
  7.6 1.7 %collective-permute-start.3 = (bf16[3,256,1024]{2,1,0:T(8,128)(2,1)}, bf16[3,256,1024]{2,1,0:T(8,128)(2,1)}, u32[]{:S(2)}, u32[]{:S(2)}) collective-permute-start(bf16[3,256,1024]{2,1,0:T(8,128)(2,1)} %constant_dynamic-slice_fusion.2), channel_id=1, source_target_pairs={{0,2},{2,0},{1,3},{3,1},{4,6},{6,4},{5,7},{7,5},{8,10},{10,8},{9,1... | collective-permute-start | bytes 4718600 | tf_op jit(solution)/shard_map/ppermute | solution.py:35
  9.4 1.3 %collective-permute-done.1 = bf16[2,1,128,256]{3,2,0,1:T(8,128)(2,1)S(1)} collective-permute-done((bf16[2,1,128,256]{3,2,0,1:T(8,128)(2,1)S(1)}, bf16[2,1,128,256]{3,2,0,1:T(8,128)(2,1)S(1)}, u32[]{:S(2)}, u32[]{:S(2)}) %collective-permute-start.1) | collective-permute-done | bytes 131104 | tf_op jit(solution)/shard_map/ppermute | solution.py:39
  10.9 1.6 %collective-permute-start.2 = (bf16[2,128,512]{2,1,0:T(8,128)(2,1)S(1)}, bf16[2,128,512]{2,1,0:T(8,128)(2,1)}, u32[]{:S(2)}, u32[]{:S(2)}) collective-permute-start(bf16[2,128,512]{2,1,0:T(8,128)(2,1)S(1)} %maximum_select_fusion.refs_0_), channel_id=1, source_target_pairs={{0,1},{1,0},{2,3},{3,2},{4,5},{5,4},{6,7},{7,6},{8,9},{9,8},{10,11... | collective-permute-start | bytes 786440 | tf_op jit(solution)/shard_map/ppermute | solution.py:35
  12.5 1.6 %collective-permute-start.4 = (bf16[2,128,512]{2,1,0:T(8,128)(2,1)S(1)}, bf16[2,128,512]{2,1,0:T(8,128)(2,1)S(1)}, u32[]{:S(2)}, u32[]{:S(2)}) collective-permute-start(bf16[2,128,512]{2,1,0:T(8,128)(2,1)S(1)} %maximum_select_fusion.refs_0_), channel_id=1, source_target_pairs={{0,8},{4,12},{8,16},{12,20},{16,24},{20,28},{24,0},{28,4},{1,9},{5... | collective-permute-start | bytes 786440 | tf_op jit(solution)/shard_map/ppermute | solution.py:35
  14.1 2.2 %collective-permute-start.6 = (bf16[2,128,512]{2,1,0:T(8,128)(2,1)S(1)}, bf16[2,128,512]{2,1,0:T(8,128)(2,1)S(1)}, u32[]{:S(2)}, u32[]{:S(2)}) collective-permute-start(bf16[2,128,512]{2,1,0:T(8,128)(2,1)S(1)} %maximum_select_fusion.refs_0_), channel_id=1, source_target_pairs={{0,24},{4,28},{8,0},{12,4},{16,8},{20,12},{24,16},{28,20},{1,25},{... | collective-permute-start | bytes 786440 | tf_op jit(solution)/shard_map/ppermute | solution.py:35
  16.3 0.8 collective-permute-start.8
  17.1 2.3 %collective-permute-done.2.refs_1_ = bf16[2,128,512]{2,1,0:T(8,128)(2,1)} collective-permute-done((bf16[2,128,512]{2,1,0:T(8,128)(2,1)S(1)}, bf16[2,128,512]{2,1,0:T(8,128)(2,1)}, u32[]{:S(2)}, u32[]{:S(2)}) %collective-permute-start.2) | collective-permute-done | bytes 262176 | tf_op jit(solution)/shard_map/ppermute | solution.py:35
  19.4 1.8 %constant_dynamic-slice_fusion.1.refs_0_.refs_1_ = bf16[4,256,1024]{2,1,0:T(8,128)(2,1)S(1)} fusion(bf16[8,256,1024]{2,1,0:T(8,128)(2,1)} %param.2, s32[]{:T(128)S(6)} %select_n.186), kind=kLoop, calls=%fused_computation.59 | loop fusion | bytes 4194308 | tf_op jit(solution)/shard_map/dynamic_slice | solution.py:374
  21.3 2.2 %collective-permute-done.4.refs_2_ = bf16[2,128,512]{2,1,0:T(8,128)(2,1)S(1)} collective-permute-done((bf16[2,128,512]{2,1,0:T(8,128)(2,1)S(1)}, bf16[2,128,512]{2,1,0:T(8,128)(2,1)S(1)}, u32[]{:S(2)}, u32[]{:S(2)}) %collective-permute-start.4) | collective-permute-done | bytes 262176 | tf_op jit(solution)/shard_map/ppermute | solution.py:35
  23.5 0.5 collective-permute-start.5
  24.0 3.5 %collective-permute-done.6.refs_4_ = bf16[2,128,512]{2,1,0:T(8,128)(2,1)S(1)} collective-permute-done((bf16[2,128,512]{2,1,0:T(8,128)(2,1)S(1)}, bf16[2,128,512]{2,1,0:T(8,128)(2,1)S(1)}, u32[]{:S(2)}, u32[]{:S(2)}) %collective-permute-start.6) | collective-permute-done | bytes 262176 | tf_op jit(solution)/shard_map/ppermute | solution.py:35
  28.0 11.4 %collective-permute-done.8.refs_6_ = bf16[2,128,512]{2,1,0:T(8,128)(2,1)} collective-permute-done((bf16[2,128,512]{2,1,0:T(8,128)(2,1)S(1)}, bf16[2,128,512]{2,1,0:T(8,128)(2,1)}, u32[]{:S(2)}, u32[]{:S(2)}) %collective-permute-start.8) | collective-permute-done | bytes 262176 | tf_op jit(solution)/shard_map/ppermute | solution.py:35
  39.9 1.9 %constant_dynamic-slice_fusion = bf16[1,256,1024]{2,1,0:T(8,128)(2,1)} fusion(bf16[8,256,1024]{2,1,0:T(8,128)(2,1)} %param.2, s32[]{:T(128)S(6)} %select_n.187), kind=kLoop, calls=%fused_computation.58 | loop fusion | bytes 1048580 | tf_op jit(solution)/shard_map/dynamic_slice | solution.py:336
  41.8 6.1 %collective-permute-done.9.refs_7_ = bf16[2,128,512]{2,1,0:T(8,128)(2,1)S(1)} collective-permute-done((bf16[2,128,512]{2,1,0:T(8,128)(2,1)}, bf16[2,128,512]{2,1,0:T(8,128)(2,1)S(1)}, u32[]{:S(2)}, u32[]{:S(2)}) %collective-permute-start.9) | collective-permute-done | bytes 262176 | tf_op jit(solution)/shard_map/ppermute | solution.py:35
  47.9 0.6 collective-permute-start.10
  48.6 2.0 %assemble.1.refs_4_.refs_2_.refs_6_ = bf16[2,256,2048]{2,1,0:T(8,128)(2,1)S(1)} custom-call(s32[6]{0:T(128)S(1)} %stack.27.at, bf16[2,128,512]{2,1,0:T(8,128)(2,1)} %copy-done.1, bf16[2,128,512]{2,1,0:T(8,128)(2,1)} %collective-permute-done.2.refs_1_, bf16[2,128,512]{2,1,0:T(8,128)(2,1)} %copy-done.6, bf16[2,128,512]{2,1,0:T(8,128)(2,1)} %collective-permute-done.5.refs_3_, ...), custom_call_target="tpu_custom_call" | custom-call | bytes 2097152 | tf_op jit(solution)/shard_map/assemble/pallas_call | solution.py:80
  50.7 1.0 collective-permute-done.12.refs_3_
  51.7 8.4 %early_sums.1.refs_7_ = f32[2,256,2048]{2,1,0:T(8,128)S(1)} custom-call(bf16[4,256,1024]{2,1,0:T(8,128)(2,1)S(1)} %constant_dynamic-slice_fusion.1.refs_0_.refs_1_, bf16[3,256,1024]{2,1,0:T(8,128)(2,1)} %collective-permute-done.3.refs_1_, bf16[4,256,1024]{2,1,0:T(8,128)(2,1)} %collective-permute-done.11.refs_2_.refs_3_, ...), custom_call_target="tpu_custom_call" | custom-call | bytes 2097152 | tf_op jit(solution)/shard_map/early_sums/pallas_call | solution.py:149
  60.1 2.4 %collective-permute-done.10.refs_1_.refs_2_ = bf16[1,256,1024]{2,1,0:T(8,128)(2,1)S(1)} collective-permute-done((bf16[1,256,1024]{2,1,0:T(8,128)(2,1)}, bf16[1,256,1024]{2,1,0:T(8,128)(2,1)S(1)}, u32[]{:S(2)}, u32[]{:S(2)}) %collective-permute-start.10) | collective-permute-done | bytes 524320 | tf_op jit(solution)/shard_map/ppermute | solution.py:35
  62.5 0.8 step_pairs.1.refs_5_
  63.3 1.1 %collective-permute-done.13.refs_4_ = bf16[1,256,1024]{2,1,0:T(8,128)(2,1)S(1)} collective-permute-done((bf16[1,256,1024]{2,1,0:T(8,128)(2,1)S(1)}, bf16[1,256,1024]{2,1,0:T(8,128)(2,1)S(1)}, u32[]{:S(2)}, u32[]{:S(2)}) %collective-permute-start.13) | collective-permute-done | bytes 524320 | tf_op jit(solution)/shard_map/ppermute | solution.py:39
  64.4 4.3 %last_sums.1 = (bf16[1,2,32,2048]{3,2,1,0:T(8,128)(2,1)}, f32[1,2,32,2048]{3,2,1,0:T(8,128)}, bf16[1,2,32,2048]{3,2,1,0:T(8,128)(2,1)}, f32[2,32,2048]{2,1,0:T(8...) custom-call(s32[1]{0:T(128)} %bitcast.refs_0_, ...), custom_call_target="tpu_custom_call" | custom-call | bytes 3145728 | tf_op jit(solution)/shard_map/last_sums/pallas_call | solution.py:299
  68.7 0.6 collective-permute-start.23
  69.3 0.5 collective-permute-start.21
  69.8 1.5 %collective-permute-start.16 = (bf16[2,32,2048]{2,1,0:T(8,128)(2,1)}, bf16[2,32,2048]{2,1,0:T(8,128)(2,1)S(1)}, u32[]{:S(2)}, u32[]{:S(2)}) collective-permute-start(bf16[2,32,2048]{2,1,0:T(8,128)(2,1)} %bitcast.29), channel_id=1, source_target_pairs={{0,1},{1,0},{2,3},{3,2},{4,5},{5,4},{6,7},{7,6},{8,9},{9,8},{10,11... | collective-permute-start | bytes 786440 | tf_op jit(solution)/shard_map/ppermute | solution.py:35
  71.4 1.5 %collective-permute-start.14 = (bf16[1,2,32,2048]{3,2,1,0:T(8,128)(2,1)}, bf16[1,2,32,2048]{3,2,1,0:T(8,128)(2,1)S(1)}, u32[]{:S(2)}, u32[]{:S(2)}) collective-permute-start(bf16[1,2,32,2048]{3,2,1,0:T(8,128)(2,1)} %get-tuple-element.30), channel_id=1, source_target_pairs={{0,2},{2,0},{1,3},{3,1},{4,6},{6,4},{5,7},{7,5},{8,10},{10,8},{9,1... | collective-permute-start | bytes 786440 | tf_op jit(solution)/shard_map/ppermute | solution.py:35
  72.8 5.3 %collective-permute-done.23 = bf16[2,32,2048]{2,1,0:T(8,128)(2,1)S(1)} collective-permute-done((bf16[2,32,2048]{2,1,0:T(8,128)(2,1)}, bf16[2,32,2048]{2,1,0:T(8,128)(2,1)S(1)}, u32[]{:S(2)}, u32[]{:S(2)}) %collective-permute-start.23) | collective-permute-done | bytes 262176 | tf_op jit(solution)/shard_map/ppermute | solution.py:35
  78.2 1.0 %add_convert_fusion = bf16[1,32,2048]{2,1,0:T(8,128)(2,1)S(1)} fusion(f32[2,32,2048]{2,1,0:T(8,128)} %get-tuple-element.35, bf16[2,32,2048]{2,1,0:T(8,128)(2,1)S(1)} %collective-permute-done.23), kind=kLoop, calls=%fused_computation.26 | loop fusion | flops 196608 | bytes 524288 | tf_op jit(solution)/shard_map/convert_element_type | solution.py:415
  79.2 0.6 collective-permute-start.24
  79.8 1.0 fusion.1
  80.8 0.6 collective-permute-start.22
  81.4 2.4 %collective-permute-done.16 = bf16[2,32,2048]{2,1,0:T(8,128)(2,1)S(1)} collective-permute-done((bf16[2,32,2048]{2,1,0:T(8,128)(2,1)}, bf16[2,32,2048]{2,1,0:T(8,128)(2,1)S(1)}, u32[]{:S(2)}, u32[]{:S(2)}) %collective-permute-start.16) | collective-permute-done | bytes 262176 | tf_op jit(solution)/shard_map/ppermute | solution.py:35
  83.8 1.0 add_convert_fusion.2
  84.8 1.0 fusion
  85.8 1.0 %collective-permute-start.15 = (bf16[1,32,2048]{2,1,0:T(8,128)(2,1)S(1)}, bf16[1,32,2048]{2,1,0:T(8,128)(2,1)S(1)}, u32[]{:S(2)}, u32[]{:S(2)}) collective-permute-start(bf16[1,32,2048]{2,1,0:T(8,128)(2,1)S(1)} %fusion), channel_id=1, source_target_pairs={{0,1},{1,0},{2,3},{3,2},{4,5},{5,4},{6,7},{7,6},{8,9},{9,8},{10,11... | collective-permute-start | bytes 393224 | tf_op jit(solution)/shard_map/ppermute | solution.py:35
  87.2 0.6 collective-permute-start.25
  87.8 2.0 %collective-permute-start.26 = (bf16[1,64,512]{2,1,0:T(8,128)(2,1)S(1)}, bf16[1,64,512]{2,1,0:T(8,128)(2,1)S(1)}, u32[]{:S(2)}, u32[]{:S(2)}) collective-permute-start(bf16[1,64,512]{2,1,0:T(8,128)(2,1)S(1)} %get-tuple-element.38), channel_id=1, source_target_pairs={{0,16},{4,20},{8,24},{12,28},{16,0},{20,4},{24,8},{28,12},{1,17},{... | collective-permute-start | bytes 196616 | tf_op jit(solution)/shard_map/ppermute | solution.py:35
  89.8 2.8 %collective-permute-start.27 = (bf16[1,64,512]{2,1,0:T(8,128)(2,1)S(1)}, bf16[1,64,512]{2,1,0:T(8,128)(2,1)S(1)}, u32[]{:S(2)}, u32[]{:S(2)}) collective-permute-start(bf16[1,64,512]{2,1,0:T(8,128)(2,1)S(1)} %get-tuple-element.39), channel_id=1, source_target_pairs={{0,24},{4,28},{8,0},{12,4},{16,8},{20,12},{24,16},{28,20},{1,25},{... | collective-permute-start | bytes 196616 | tf_op jit(solution)/shard_map/ppermute | solution.py:35
  93.0 0.7 collective-permute-start.19
  93.7 3.1 %collective-permute-start.20 = (bf16[1,64,512]{2,1,0:T(8,128)(2,1)S(1)}, bf16[1,64,512]{2,1,0:T(8,128)(2,1)S(1)}, u32[]{:S(2)}, u32[]{:S(2)}) collective-permute-start(bf16[1,64,512]{2,1,0:T(8,128)(2,1)S(1)} %get-tuple-element.42), channel_id=1, source_target_pairs={{0,24},{4,28},{8,0},{12,4},{16,8},{20,12},{24,16},{28,20},{1,25},{... | collective-permute-start | bytes 196616 | tf_op jit(solution)/shard_map/ppermute | solution.py:35
  96.9 2.2 %collective-permute-done.18 = bf16[1,64,512]{2,1,0:T(8,128)(2,1)S(1)} collective-permute-done((bf16[1,64,512]{2,1,0:T(8,128)(2,1)S(1)}, bf16[1,64,512]{2,1,0:T(8,128)(2,1)S(1)}, u32[]{:S(2)}, u32[]{:S(2)}) %collective-permute-start.18) | collective-permute-done | bytes 65568 | tf_op jit(solution)/shard_map/ppermute | solution.py:35
  99.1 1.0 %collective-permute-done.19 = bf16[1,64,512]{2,1,0:T(8,128)(2,1)S(1)} collective-permute-done((bf16[1,64,512]{2,1,0:T(8,128)(2,1)S(1)}, bf16[1,64,512]{2,1,0:T(8,128)(2,1)S(1)}, u32[]{:S(2)}, u32[]{:S(2)}) %collective-permute-start.19) | collective-permute-done | bytes 65568 | tf_op jit(solution)/shard_map/ppermute | solution.py:35
  100.4 1.3 %collective-permute-done.28 = f32[1,128,256]{2,1,0:T(8,128)S(1)} collective-permute-done((f32[1,128,256]{2,1,0:T(8,128)S(1)}, f32[1,128,256]{2,1,0:T(8,128)S(1)}, u32[]{:S(2)}, u32[]{:S(2)}) %collective-permute-start.28) | collective-permute-done | bytes 131104 | tf_op jit(solution)/shard_map/ppermute | solution.py:39
  101.7 0.7 maximum_select_fusion.1
  (52 shorter events, 2.5 us)
Async XLA Ops:
  0.0 1.0 %copy-start = (f32[2,256,256]{2,1,0:T(8,128)S(1)}, f32[2,256,256]{2,1,0:T(8,128)}, u32[]{:S(2)}) copy-start(f32[2,256,256]{2,1,0:T(8,128)} %param.3) | copy-start | bytes 1572868
  1.1 6.5 %collective-permute-start = (bf16[2,128,256]{2,1,0:T(8,128)(2,1)S(1)}, bf16[2,128,256]{2,1,0:T(8,128)(2,1)S(1)}, u32[]{:S(2)}, u32[]{:S(2)}) collective-permute-start(bf16[2,128,256]{2,1,0:T(8,128)(2,1)S(1)} %dynamic-slice_convert_fusion), channel_id=1, source_target_pairs={{0,2},{2,0},{1,3},{3,1},{4,6},{6,4},{5,7},{7,5},{8,10},{10,8},{9,1... | collective-permute-start | bytes 393224 | tf_op jit(solution)/shard_map/ppermute | solution.py:35
  7.6 40.3 %collective-permute-start.3 = (bf16[3,256,1024]{2,1,0:T(8,128)(2,1)}, bf16[3,256,1024]{2,1,0:T(8,128)(2,1)}, u32[]{:S(2)}, u32[]{:S(2)}) collective-permute-start(bf16[3,256,1024]{2,1,0:T(8,128)(2,1)} %constant_dynamic-slice_fusion.2), channel_id=1, source_target_pairs={{0,2},{2,0},{1,3},{3,1},{4,6},{6,4},{5,7},{7,5},{8,10},{10,8},{9,1... | collective-permute-start | bytes 4718600 | tf_op jit(solution)/shard_map/ppermute | solution.py:35
  9.4 1.4 %collective-permute-start.1 = (bf16[2,1,128,256]{3,2,0,1:T(8,128)(2,1)S(1)}, bf16[2,1,128,256]{3,2,0,1:T(8,128)(2,1)S(1)}, u32[]{:S(2)}, u32[]{:S(2)}) collective-permute-start(bf16[2,1,128,256]{3,2,0,1:T(8,128)(2,1)S(1)} %get-tuple-element.46), channel_id=1, source_target_pairs={{0,4},{4,0},{8,12},{12,8},{16,20},{20,16},{24,28},{28,24},{1,5},{5... | collective-permute-start | bytes 393224 | tf_op jit(solution)/shard_map/ppermute | solution.py:39
  10.9 10.3 %copy-start.1 = (bf16[2,128,512]{2,1,0:T(8,128)(2,1)}, bf16[2,128,512]{2,1,0:T(8,128)(2,1)S(1)}, u32[]{:S(2)}) copy-start(bf16[2,128,512]{2,1,0:T(8,128)(2,1)S(1)} %maximum_select_fusion.refs_0_) | copy-start | bytes 786436
  10.9 8.5 %collective-permute-start.2 = (bf16[2,128,512]{2,1,0:T(8,128)(2,1)S(1)}, bf16[2,128,512]{2,1,0:T(8,128)(2,1)}, u32[]{:S(2)}, u32[]{:S(2)}) collective-permute-start(bf16[2,128,512]{2,1,0:T(8,128)(2,1)S(1)} %maximum_select_fusion.refs_0_), channel_id=1, source_target_pairs={{0,1},{1,0},{2,3},{3,2},{4,5},{5,4},{6,7},{7,6},{8,9},{9,8},{10,11... | collective-permute-start | bytes 786440 | tf_op jit(solution)/shard_map/ppermute | solution.py:35
  12.5 11.0 %collective-permute-start.4 = (bf16[2,128,512]{2,1,0:T(8,128)(2,1)S(1)}, bf16[2,128,512]{2,1,0:T(8,128)(2,1)S(1)}, u32[]{:S(2)}, u32[]{:S(2)}) collective-permute-start(bf16[2,128,512]{2,1,0:T(8,128)(2,1)S(1)} %maximum_select_fusion.refs_0_), channel_id=1, source_target_pairs={{0,8},{4,12},{8,16},{12,20},{16,24},{20,28},{24,0},{28,4},{1,9},{5... | collective-permute-start | bytes 786440 | tf_op jit(solution)/shard_map/ppermute | solution.py:35
  14.1 13.4 %collective-permute-start.6 = (bf16[2,128,512]{2,1,0:T(8,128)(2,1)S(1)}, bf16[2,128,512]{2,1,0:T(8,128)(2,1)S(1)}, u32[]{:S(2)}, u32[]{:S(2)}) collective-permute-start(bf16[2,128,512]{2,1,0:T(8,128)(2,1)S(1)} %maximum_select_fusion.refs_0_), channel_id=1, source_target_pairs={{0,24},{4,28},{8,0},{12,4},{16,8},{20,12},{24,16},{28,20},{1,25},{... | collective-permute-start | bytes 786440 | tf_op jit(solution)/shard_map/ppermute | solution.py:35
  16.3 23.1 %collective-permute-start.8 = (bf16[2,128,512]{2,1,0:T(8,128)(2,1)S(1)}, bf16[2,128,512]{2,1,0:T(8,128)(2,1)}, u32[]{:S(2)}, u32[]{:S(2)}) collective-permute-start(bf16[2,128,512]{2,1,0:T(8,128)(2,1)S(1)} %maximum_select_fusion.refs_0_), channel_id=1, source_target_pairs={{0,16},{4,20},{8,24},{12,28},{16,0},{20,4},{24,8},{28,12},{1,17},{... | collective-permute-start | bytes 786440 | tf_op jit(solution)/shard_map/ppermute | solution.py:35
  21.2 29.4 %collective-permute-start.11 = (bf16[4,256,1024]{2,1,0:T(8,128)(2,1)S(1)}, bf16[4,256,1024]{2,1,0:T(8,128)(2,1)}, u32[]{:S(2)}, u32[]{:S(2)}) collective-permute-start(bf16[4,256,1024]{2,1,0:T(8,128)(2,1)S(1)} %constant_dynamic-slice_fusion.1.refs_0_.refs_1_), channel_id=1, source_target_pairs={{0,4},{4,0},{8,12},{12,8},{16,20},{20,16},{24,28},{28,24},{1,5},{5... | collective-permute-start | bytes 6291464 | tf_op jit(solution)/shard_map/ppermute | solution.py:39
  23.5 24.3 %copy-start.6 = (bf16[2,128,512]{2,1,0:T(8,128)(2,1)}, bf16[2,128,512]{2,1,0:T(8,128)(2,1)S(1)}, u32[]{:S(2)}) copy-start(bf16[2,128,512]{2,1,0:T(8,128)(2,1)S(1)} %collective-permute-done.4.refs_2_) | copy-start | bytes 786436
  23.5 18.2 %collective-permute-start.5 = (bf16[2,128,512]{2,1,0:T(8,128)(2,1)S(1)}, bf16[2,128,512]{2,1,0:T(8,128)(2,1)}, u32[]{:S(2)}, u32[]{:S(2)}) collective-permute-start(bf16[2,128,512]{2,1,0:T(8,128)(2,1)S(1)} %collective-permute-done.4.refs_2_), channel_id=1, source_target_pairs={{0,1},{1,0},{2,3},{3,2},{4,5},{5,4},{6,7},{7,6},{8,9},{9,8},{10,11... | collective-permute-start | bytes 786440 | tf_op jit(solution)/shard_map/ppermute | solution.py:35
  27.5 20.3 %copy-start.7 = (bf16[2,128,512]{2,1,0:T(8,128)(2,1)}, bf16[2,128,512]{2,1,0:T(8,128)(2,1)S(1)}, u32[]{:S(2)}) copy-start(bf16[2,128,512]{2,1,0:T(8,128)(2,1)S(1)} %collective-permute-done.6.refs_4_) | copy-start | bytes 786436
  27.5 14.3 %collective-permute-start.7 = (bf16[2,128,512]{2,1,0:T(8,128)(2,1)S(1)}, bf16[2,128,512]{2,1,0:T(8,128)(2,1)}, u32[]{:S(2)}, u32[]{:S(2)}) collective-permute-start(bf16[2,128,512]{2,1,0:T(8,128)(2,1)S(1)} %collective-permute-done.6.refs_4_), channel_id=1, source_target_pairs={{0,1},{1,0},{2,3},{3,2},{4,5},{5,4},{6,7},{7,6},{8,9},{9,8},{10,11... | collective-permute-start | bytes 786440 | tf_op jit(solution)/shard_map/ppermute | solution.py:35
  39.4 8.4 %collective-permute-start.9 = (bf16[2,128,512]{2,1,0:T(8,128)(2,1)}, bf16[2,128,512]{2,1,0:T(8,128)(2,1)S(1)}, u32[]{:S(2)}, u32[]{:S(2)}) collective-permute-start(bf16[2,128,512]{2,1,0:T(8,128)(2,1)} %collective-permute-done.8.refs_6_), channel_id=1, source_target_pairs={{0,1},{1,0},{2,3},{3,2},{4,5},{5,4},{6,7},{7,6},{8,9},{9,8},{10,11... | collective-permute-start | bytes 786440 | tf_op jit(solution)/shard_map/ppermute | solution.py:35
  47.8 3.8 %collective-permute-start.12 = (bf16[3,256,1024]{2,1,0:T(8,128)(2,1)}, bf16[3,256,1024]{2,1,0:T(8,128)(2,1)}, u32[]{:S(2)}, u32[]{:S(2)}) collective-permute-start(bf16[3,256,1024]{2,1,0:T(8,128)(2,1)} %collective-permute-done.3.refs_1_), channel_id=1, source_target_pairs={{0,4},{4,0},{8,12},{12,8},{16,20},{20,16},{24,28},{28,24},{1,5},{5... | collective-permute-start | bytes 4718600 | tf_op jit(solution)/shard_map/ppermute | solution.py:39
  47.9 14.5 %collective-permute-start.10 = (bf16[1,256,1024]{2,1,0:T(8,128)(2,1)}, bf16[1,256,1024]{2,1,0:T(8,128)(2,1)S(1)}, u32[]{:S(2)}, u32[]{:S(2)}) collective-permute-start(bf16[1,256,1024]{2,1,0:T(8,128)(2,1)} %constant_dynamic-slice_fusion), channel_id=1, source_target_pairs={{0,2},{2,0},{1,3},{3,1},{4,6},{6,4},{5,7},{7,5},{8,10},{10,8},{9,1... | collective-permute-start | bytes 1572872 | tf_op jit(solution)/shard_map/ppermute | solution.py:35
  62.5 1.9 %collective-permute-start.13 = (bf16[1,256,1024]{2,1,0:T(8,128)(2,1)S(1)}, bf16[1,256,1024]{2,1,0:T(8,128)(2,1)S(1)}, u32[]{:S(2)}, u32[]{:S(2)}) collective-permute-start(bf16[1,256,1024]{2,1,0:T(8,128)(2,1)S(1)} %collective-permute-done.10.refs_1_.refs_2_), channel_id=1, source_target_pairs={{0,4},{4,0},{8,12},{12,8},{16,20},{20,16},{24,28},{28,24},{1,5},{5... | collective-permute-start | bytes 1572872 | tf_op jit(solution)/shard_map/ppermute | solution.py:39
  68.7 18.2 %copy-start.3 = (f32[2,32,2048]{2,1,0:T(8,128)S(1)}, f32[2,32,2048]{2,1,0:T(8,128)}, u32[]{:S(2)}) copy-start(f32[2,32,2048]{2,1,0:T(8,128)} %get-tuple-element.35) | copy-start | bytes 1572868
  68.7 18.2 %copy-start.5 = (f32[1,2,32,2048]{3,2,1,0:T(8,128)S(1)}, f32[1,2,32,2048]{3,2,1,0:T(8,128)}, u32[]{:S(2)}) copy-start(f32[1,2,32,2048]{3,2,1,0:T(8,128)} %get-tuple-element.33) | copy-start | bytes 1572868
  68.7 9.4 %collective-permute-start.23 = (bf16[2,32,2048]{2,1,0:T(8,128)(2,1)}, bf16[2,32,2048]{2,1,0:T(8,128)(2,1)S(1)}, u32[]{:S(2)}, u32[]{:S(2)}) collective-permute-start(bf16[2,32,2048]{2,1,0:T(8,128)(2,1)} %bitcast.30), channel_id=1, source_target_pairs={{0,1},{1,0},{2,3},{3,2},{4,5},{5,4},{6,7},{7,6},{8,9},{9,8},{10,11... | collective-permute-start | bytes 786440 | tf_op jit(solution)/shard_map/ppermute | solution.py:35
  69.3 10.5 %collective-permute-start.21 = (bf16[1,2,32,2048]{3,2,1,0:T(8,128)(2,1)}, bf16[1,2,32,2048]{3,2,1,0:T(8,128)(2,1)S(1)}, u32[]{:S(2)}, u32[]{:S(2)}) collective-permute-start(bf16[1,2,32,2048]{3,2,1,0:T(8,128)(2,1)} %get-tuple-element.34), channel_id=1, source_target_pairs={{0,2},{2,0},{1,3},{3,1},{4,6},{6,4},{5,7},{7,5},{8,10},{10,8},{9,1... | collective-permute-start | bytes 786440 | tf_op jit(solution)/shard_map/ppermute | solution.py:35
  69.8 13.9 %collective-permute-start.16 = (bf16[2,32,2048]{2,1,0:T(8,128)(2,1)}, bf16[2,32,2048]{2,1,0:T(8,128)(2,1)S(1)}, u32[]{:S(2)}, u32[]{:S(2)}) collective-permute-start(bf16[2,32,2048]{2,1,0:T(8,128)(2,1)} %bitcast.29), channel_id=1, source_target_pairs={{0,1},{1,0},{2,3},{3,2},{4,5},{5,4},{6,7},{7,6},{8,9},{9,8},{10,11... | collective-permute-start | bytes 786440 | tf_op jit(solution)/shard_map/ppermute | solution.py:35
  71.4 13.5 %collective-permute-start.14 = (bf16[1,2,32,2048]{3,2,1,0:T(8,128)(2,1)}, bf16[1,2,32,2048]{3,2,1,0:T(8,128)(2,1)S(1)}, u32[]{:S(2)}, u32[]{:S(2)}) collective-permute-start(bf16[1,2,32,2048]{3,2,1,0:T(8,128)(2,1)} %get-tuple-element.30), channel_id=1, source_target_pairs={{0,2},{2,0},{1,3},{3,1},{4,6},{6,4},{5,7},{7,5},{8,10},{10,8},{9,1... | collective-permute-start | bytes 786440 | tf_op jit(solution)/shard_map/ppermute | solution.py:35
  78.2 14.5 %copy-start.2 = (f32[2,32,2048]{2,1,0:T(8,128)S(1)}, f32[2,32,2048]{2,1,0:T(8,128)}, u32[]{:S(2)}) copy-start(f32[2,32,2048]{2,1,0:T(8,128)} %get-tuple-element.31) | copy-start | bytes 1572868
  79.2 7.7 %collective-permute-start.24 = (bf16[1,32,2048]{2,1,0:T(8,128)(2,1)S(1)}, bf16[1,32,2048]{2,1,0:T(8,128)(2,1)S(1)}, u32[]{:S(2)}, u32[]{:S(2)}) collective-permute-start(bf16[1,32,2048]{2,1,0:T(8,128)(2,1)S(1)} %add_convert_fusion), channel_id=1, source_target_pairs={{0,2},{2,0},{1,3},{3,1},{4,6},{6,4},{5,7},{7,5},{8,10},{10,8},{9,1... | collective-permute-start | bytes 393224 | tf_op jit(solution)/shard_map/ppermute | solution.py:35
  80.8 11.9 %copy-start.4 = (f32[1,2,32,2048]{3,2,1,0:T(8,128)S(1)}, f32[1,2,32,2048]{3,2,1,0:T(8,128)}, u32[]{:S(2)}) copy-start(f32[1,2,32,2048]{3,2,1,0:T(8,128)} %get-tuple-element.29) | copy-start | bytes 1572868
  80.8 6.1 %collective-permute-start.22 = (bf16[1,32,2048]{2,1,0:T(8,128)(2,1)S(1)}, bf16[1,32,2048]{2,1,0:T(8,128)(2,1)S(1)}, u32[]{:S(2)}, u32[]{:S(2)}) collective-permute-start(bf16[1,32,2048]{2,1,0:T(8,128)(2,1)S(1)} %fusion.1), channel_id=1, source_target_pairs={{0,1},{1,0},{2,3},{3,2},{4,5},{5,4},{6,7},{7,6},{8,9},{9,8},{10,11... | collective-permute-start | bytes 393224 | tf_op jit(solution)/shard_map/ppermute | solution.py:35
  84.8 7.9 %collective-permute-start.17 = (bf16[1,32,2048]{2,1,0:T(8,128)(2,1)S(1)}, bf16[1,32,2048]{2,1,0:T(8,128)(2,1)S(1)}, u32[]{:S(2)}, u32[]{:S(2)}) collective-permute-start(bf16[1,32,2048]{2,1,0:T(8,128)(2,1)S(1)} %add_convert_fusion.2), channel_id=1, source_target_pairs={{0,2},{2,0},{1,3},{3,1},{4,6},{6,4},{5,7},{7,5},{8,10},{10,8},{9,1... | collective-permute-start | bytes 393224 | tf_op jit(solution)/shard_map/ppermute | solution.py:35
  85.8 6.8 %collective-permute-start.15 = (bf16[1,32,2048]{2,1,0:T(8,128)(2,1)S(1)}, bf16[1,32,2048]{2,1,0:T(8,128)(2,1)S(1)}, u32[]{:S(2)}, u32[]{:S(2)}) collective-permute-start(bf16[1,32,2048]{2,1,0:T(8,128)(2,1)S(1)} %fusion), channel_id=1, source_target_pairs={{0,1},{1,0},{2,3},{3,2},{4,5},{5,4},{6,7},{7,6},{8,9},{9,8},{10,11... | collective-permute-start | bytes 393224 | tf_op jit(solution)/shard_map/ppermute | solution.py:35
  87.2 6.5 %collective-permute-start.25 = (bf16[1,64,512]{2,1,0:T(8,128)(2,1)S(1)}, bf16[1,64,512]{2,1,0:T(8,128)(2,1)S(1)}, u32[]{:S(2)}, u32[]{:S(2)}) collective-permute-start(bf16[1,64,512]{2,1,0:T(8,128)(2,1)S(1)} %get-tuple-element.37), channel_id=1, source_target_pairs={{0,8},{4,12},{8,16},{12,20},{16,24},{20,28},{24,0},{28,4},{1,9},{5... | collective-permute-start | bytes 196616 | tf_op jit(solution)/shard_map/ppermute | solution.py:35
  87.8 9.0 %collective-permute-start.26 = (bf16[1,64,512]{2,1,0:T(8,128)(2,1)S(1)}, bf16[1,64,512]{2,1,0:T(8,128)(2,1)S(1)}, u32[]{:S(2)}, u32[]{:S(2)}) collective-permute-start(bf16[1,64,512]{2,1,0:T(8,128)(2,1)S(1)} %get-tuple-element.38), channel_id=1, source_target_pairs={{0,16},{4,20},{8,24},{12,28},{16,0},{20,4},{24,8},{28,12},{1,17},{... | collective-permute-start | bytes 196616 | tf_op jit(solution)/shard_map/ppermute | solution.py:35
  89.8 7.0 %collective-permute-start.27 = (bf16[1,64,512]{2,1,0:T(8,128)(2,1)S(1)}, bf16[1,64,512]{2,1,0:T(8,128)(2,1)S(1)}, u32[]{:S(2)}, u32[]{:S(2)}) collective-permute-start(bf16[1,64,512]{2,1,0:T(8,128)(2,1)S(1)} %get-tuple-element.39), channel_id=1, source_target_pairs={{0,24},{4,28},{8,0},{12,4},{16,8},{20,12},{24,16},{28,20},{1,25},{... | collective-permute-start | bytes 196616 | tf_op jit(solution)/shard_map/ppermute | solution.py:35
  92.9 6.2 %collective-permute-start.18 = (bf16[1,64,512]{2,1,0:T(8,128)(2,1)S(1)}, bf16[1,64,512]{2,1,0:T(8,128)(2,1)S(1)}, u32[]{:S(2)}, u32[]{:S(2)}) collective-permute-start(bf16[1,64,512]{2,1,0:T(8,128)(2,1)S(1)} %get-tuple-element.40), channel_id=1, source_target_pairs={{0,8},{4,12},{8,16},{12,20},{16,24},{20,28},{24,0},{28,4},{1,9},{5... | collective-permute-start | bytes 196616 | tf_op jit(solution)/shard_map/ppermute | solution.py:35
  93.0 7.2 %collective-permute-start.19 = (bf16[1,64,512]{2,1,0:T(8,128)(2,1)S(1)}, bf16[1,64,512]{2,1,0:T(8,128)(2,1)S(1)}, u32[]{:S(2)}, u32[]{:S(2)}) collective-permute-start(bf16[1,64,512]{2,1,0:T(8,128)(2,1)S(1)} %get-tuple-element.41), channel_id=1, source_target_pairs={{0,16},{4,20},{8,24},{12,28},{16,0},{20,4},{24,8},{28,12},{1,17},{... | collective-permute-start | bytes 196616 | tf_op jit(solution)/shard_map/ppermute | solution.py:35
  93.7 6.5 %collective-permute-start.20 = (bf16[1,64,512]{2,1,0:T(8,128)(2,1)S(1)}, bf16[1,64,512]{2,1,0:T(8,128)(2,1)S(1)}, u32[]{:S(2)}, u32[]{:S(2)}) collective-permute-start(bf16[1,64,512]{2,1,0:T(8,128)(2,1)S(1)} %get-tuple-element.42), channel_id=1, source_target_pairs={{0,24},{4,28},{8,0},{12,4},{16,8},{20,12},{24,16},{28,20},{1,25},{... | collective-permute-start | bytes 196616 | tf_op jit(solution)/shard_map/ppermute | solution.py:35
  100.3 1.4 %collective-permute-start.28 = (f32[1,128,256]{2,1,0:T(8,128)S(1)}, f32[1,128,256]{2,1,0:T(8,128)S(1)}, u32[]{:S(2)}, u32[]{:S(2)}) collective-permute-start(f32[1,128,256]{2,1,0:T(8,128)S(1)} %get-tuple-element.44), channel_id=1, source_target_pairs={{0,4},{4,0},{8,12},{12,8},{16,20},{20,16},{24,28},{28,24},{1,5},{5... | collective-permute-start | bytes 393224 | tf_op jit(solution)/shard_map/ppermute | solution.py:39

commit v11 on v9

--- a/solution.py
+++ b/solution.py
@@ -86,7 +86,7 @@
         cost_estimate=cost(0, shape),
         compiler_params=params(),
         name="assemble",
-    )(where, *[in_hbm(b[0]) for b in blocks])
+    )(where, *[in_hbm(b[0]) for b in blocks[:-1]], blocks[-1][0])
 
 
 def pairs_of(refs, vec, store):

time: 103 us -> 103 us (level)
  no operation moved by 1% of the time
where the time goes in v11:
time: 103 us; the launch traced here: 102 us
  waiting for transfers between devices  46.1 us (45%)
  starting transfers between devices  30 us (29%)
  Pallas kernels  15.7 us (15%)
  local copies, waits for them, and re-layouts  7.58 us (7%)
  other arithmetic  2.81 us (3%)
    ppermute x24, waiting for transfers between devices, shift(): return lax.ppermute(array, axis, pairs)  41.4 us
    ppermute x24, starting transfers between devices, shift(): return lax.ppermute(array, axis, pairs)  29.7 us
    pallas_call x1, Pallas kernels, early_sums(): pl.pallas_call(body, out_shape=shape, in_specs=[ANY] * n + [VMEM], out_sp...  8.44 us
    ppermute x5, waiting for transfers between devices, sibling(): return lax.ppermute(array, 'aux', [(i, i ^ 1) for i in range(size)])  4.72 us
    dynamic_slice x2, local copies, waits for them, and re-layouts, sends(): lax.dynamic_slice_in_dim(source, (v - r) % nv * take + first, size, 0)  4.55 us
    pallas_call x1, Pallas kernels, last_sums(): pl.pallas_call(body, out_shape=[pltpu.HBM(x.shape, x.dtype) for x in shap...  4.33 us
  transfers between devices with their start and end apart: 29, of which 16 were waited for; matrix products, arithmetic and copies ran while one was open for 8% of the time, Pallas kernels for 11%

profile of v11, /device:TPU:0, one launch (start us, length us, event | category | flops | bytes accessed | tf_op | source)
XLA Modules:
  0.0 102.4 jit_solution(14818998123224116694)
XLA Ops:
  0.0 1.0 %copy-done = f32[2,256,256]{2,1,0:T(8,128)S(1)} copy-done((f32[2,256,256]{2,1,0:T(8,128)S(1)}, f32[2,256,256]{2,1,0:T(8,128)}, u32[]{:S(2)}) %copy-start) | copy-done | bytes 524312
  1.1 3.0 %collective-permute-start = (bf16[2,128,256]{2,1,0:T(8,128)(2,1)S(1)}, bf16[2,128,256]{2,1,0:T(8,128)(2,1)S(1)}, u32[]{:S(2)}, u32[]{:S(2)}) collective-permute-start(bf16[2,128,256]{2,1,0:T(8,128)(2,1)S(1)} %dynamic-slice_convert_fusion.2), channel_id=1, source_target_pairs={{0,2},{2,0},{1,3},{3,1},{4,6},{6,4},{5,7},{7,5},{8,10},{10,8},{9,1... | collective-permute-start | bytes 393224 | tf_op jit(solution)/shard_map/ppermute | solution.py:35
  4.1 2.7 %constant_dynamic-slice_fusion.2 = bf16[3,256,1024]{2,1,0:T(8,128)(2,1)} fusion(bf16[8,256,1024]{2,1,0:T(8,128)(2,1)} %param.2, s32[]{:T(128)S(6)} %select_n.177), kind=kLoop, calls=%fused_computation.64 | loop fusion | bytes 3145732 | tf_op jit(solution)/shard_map/dynamic_slice | solution.py:336
  6.8 0.8 collective-permute-done
  7.6 1.7 %collective-permute-start.3 = (bf16[3,256,1024]{2,1,0:T(8,128)(2,1)}, bf16[3,256,1024]{2,1,0:T(8,128)(2,1)}, u32[]{:S(2)}, u32[]{:S(2)}) collective-permute-start(bf16[3,256,1024]{2,1,0:T(8,128)(2,1)} %constant_dynamic-slice_fusion.2), channel_id=1, source_target_pairs={{0,2},{2,0},{1,3},{3,1},{4,6},{6,4},{5,7},{7,5},{8,10},{10,8},{9,1... | collective-permute-start | bytes 4718600 | tf_op jit(solution)/shard_map/ppermute | solution.py:35
  9.4 1.3 %collective-permute-done.1 = bf16[2,1,128,256]{3,2,0,1:T(8,128)(2,1)S(1)} collective-permute-done((bf16[2,1,128,256]{3,2,0,1:T(8,128)(2,1)S(1)}, bf16[2,1,128,256]{3,2,0,1:T(8,128)(2,1)S(1)}, u32[]{:S(2)}, u32[]{:S(2)}) %collective-permute-start.1) | collective-permute-done | bytes 131104 | tf_op jit(solution)/shard_map/ppermute | solution.py:39
  10.9 1.6 %collective-permute-start.2 = (bf16[2,128,512]{2,1,0:T(8,128)(2,1)S(1)}, bf16[2,128,512]{2,1,0:T(8,128)(2,1)}, u32[]{:S(2)}, u32[]{:S(2)}) collective-permute-start(bf16[2,128,512]{2,1,0:T(8,128)(2,1)S(1)} %maximum_select_fusion.refs_0_), channel_id=1, source_target_pairs={{0,1},{1,0},{2,3},{3,2},{4,5},{5,4},{6,7},{7,6},{8,9},{9,8},{10,11... | collective-permute-start | bytes 786440 | tf_op jit(solution)/shard_map/ppermute | solution.py:35
  12.5 1.6 %collective-permute-start.4 = (bf16[2,128,512]{2,1,0:T(8,128)(2,1)S(1)}, bf16[2,128,512]{2,1,0:T(8,128)(2,1)S(1)}, u32[]{:S(2)}, u32[]{:S(2)}) collective-permute-start(bf16[2,128,512]{2,1,0:T(8,128)(2,1)S(1)} %maximum_select_fusion.refs_0_), channel_id=1, source_target_pairs={{0,8},{4,12},{8,16},{12,20},{16,24},{20,28},{24,0},{28,4},{1,9},{5... | collective-permute-start | bytes 786440 | tf_op jit(solution)/shard_map/ppermute | solution.py:35
  14.1 2.2 %collective-permute-start.6 = (bf16[2,128,512]{2,1,0:T(8,128)(2,1)S(1)}, bf16[2,128,512]{2,1,0:T(8,128)(2,1)S(1)}, u32[]{:S(2)}, u32[]{:S(2)}) collective-permute-start(bf16[2,128,512]{2,1,0:T(8,128)(2,1)S(1)} %maximum_select_fusion.refs_0_), channel_id=1, source_target_pairs={{0,24},{4,28},{8,0},{12,4},{16,8},{20,12},{24,16},{28,20},{1,25},{... | collective-permute-start | bytes 786440 | tf_op jit(solution)/shard_map/ppermute | solution.py:35
  16.3 0.8 collective-permute-start.8
  17.1 2.3 %collective-permute-done.2.refs_1_ = bf16[2,128,512]{2,1,0:T(8,128)(2,1)} collective-permute-done((bf16[2,128,512]{2,1,0:T(8,128)(2,1)S(1)}, bf16[2,128,512]{2,1,0:T(8,128)(2,1)}, u32[]{:S(2)}, u32[]{:S(2)}) %collective-permute-start.2) | collective-permute-done | bytes 262176 | tf_op jit(solution)/shard_map/ppermute | solution.py:35
  19.4 1.8 %constant_dynamic-slice_fusion.1.refs_0_.refs_1_ = bf16[4,256,1024]{2,1,0:T(8,128)(2,1)S(1)} fusion(bf16[8,256,1024]{2,1,0:T(8,128)(2,1)} %param.2, s32[]{:T(128)S(6)} %select_n.181), kind=kLoop, calls=%fused_computation.63 | loop fusion | bytes 4194308 | tf_op jit(solution)/shard_map/dynamic_slice | solution.py:374
  21.3 2.2 %collective-permute-done.4.refs_2_ = bf16[2,128,512]{2,1,0:T(8,128)(2,1)S(1)} collective-permute-done((bf16[2,128,512]{2,1,0:T(8,128)(2,1)S(1)}, bf16[2,128,512]{2,1,0:T(8,128)(2,1)S(1)}, u32[]{:S(2)}, u32[]{:S(2)}) %collective-permute-start.4) | collective-permute-done | bytes 262176 | tf_op jit(solution)/shard_map/ppermute | solution.py:35
  23.5 0.5 collective-permute-start.5
  24.0 3.5 %collective-permute-done.6.refs_4_ = bf16[2,128,512]{2,1,0:T(8,128)(2,1)S(1)} collective-permute-done((bf16[2,128,512]{2,1,0:T(8,128)(2,1)S(1)}, bf16[2,128,512]{2,1,0:T(8,128)(2,1)S(1)}, u32[]{:S(2)}, u32[]{:S(2)}) %collective-permute-start.6) | collective-permute-done | bytes 262176 | tf_op jit(solution)/shard_map/ppermute | solution.py:35
  27.5 0.5 collective-permute-start.7
  28.0 11.4 %collective-permute-done.8.refs_6_ = bf16[2,128,512]{2,1,0:T(8,128)(2,1)} collective-permute-done((bf16[2,128,512]{2,1,0:T(8,128)(2,1)S(1)}, bf16[2,128,512]{2,1,0:T(8,128)(2,1)}, u32[]{:S(2)}, u32[]{:S(2)}) %collective-permute-start.8) | collective-permute-done | bytes 262176 | tf_op jit(solution)/shard_map/ppermute | solution.py:35
  39.9 1.9 %constant_dynamic-slice_fusion = bf16[1,256,1024]{2,1,0:T(8,128)(2,1)} fusion(bf16[8,256,1024]{2,1,0:T(8,128)(2,1)} %param.2, s32[]{:T(128)S(6)} %select_n.182), kind=kLoop, calls=%fused_computation.62 | loop fusion | bytes 1048580 | tf_op jit(solution)/shard_map/dynamic_slice | solution.py:336
  41.8 6.1 %collective-permute-done.9.refs_7_ = bf16[2,128,512]{2,1,0:T(8,128)(2,1)S(1)} collective-permute-done((bf16[2,128,512]{2,1,0:T(8,128)(2,1)}, bf16[2,128,512]{2,1,0:T(8,128)(2,1)S(1)}, u32[]{:S(2)}, u32[]{:S(2)}) %collective-permute-start.9) | collective-permute-done | bytes 262176 | tf_op jit(solution)/shard_map/ppermute | solution.py:35
  47.9 0.6 collective-permute-start.10
  48.6 2.0 %assemble.1.refs_4_.refs_2_.refs_6_ = bf16[2,256,2048]{2,1,0:T(8,128)(2,1)S(1)} custom-call(s32[6]{0:T(128)S(1)} %stack.27.at, bf16[2,128,512]{2,1,0:T(8,128)(2,1)} %copy-done.1, bf16[2,128,512]{2,1,0:T(8,128)(2,1)} %collective-permute-done.2.refs_1_, bf16[2,128,512]{2,1,0:T(8,128)(2,1)} %copy-done.5, bf16[2,128,512]{2,1,0:T(8,128)(2,1)} %collective-permute-done.5.refs_3_, ...), custom_call_target="tpu_custom_call" | custom-call | bytes 2097152 | tf_op jit(solution)/shard_map/assemble/pallas_call | solution.py:80
  50.7 1.0 collective-permute-done.12.refs_3_
  51.7 8.4 %early_sums.1.refs_7_ = f32[2,256,2048]{2,1,0:T(8,128)S(1)} custom-call(bf16[4,256,1024]{2,1,0:T(8,128)(2,1)S(1)} %constant_dynamic-slice_fusion.1.refs_0_.refs_1_, bf16[3,256,1024]{2,1,0:T(8,128)(2,1)} %collective-permute-done.3.refs_1_, bf16[4,256,1024]{2,1,0:T(8,128)(2,1)} %collective-permute-done.11.refs_2_.refs_3_, ...), custom_call_target="tpu_custom_call" | custom-call | bytes 2097152 | tf_op jit(solution)/shard_map/early_sums/pallas_call | solution.py:149
  60.1 2.4 %collective-permute-done.10.refs_1_.refs_2_ = bf16[1,256,1024]{2,1,0:T(8,128)(2,1)S(1)} collective-permute-done((bf16[1,256,1024]{2,1,0:T(8,128)(2,1)}, bf16[1,256,1024]{2,1,0:T(8,128)(2,1)S(1)}, u32[]{:S(2)}, u32[]{:S(2)}) %collective-permute-start.10) | collective-permute-done | bytes 524320 | tf_op jit(solution)/shard_map/ppermute | solution.py:35
  62.5 0.8 step_pairs.1.refs_5_
  63.3 1.1 %collective-permute-done.13.refs_4_ = bf16[1,256,1024]{2,1,0:T(8,128)(2,1)S(1)} collective-permute-done((bf16[1,256,1024]{2,1,0:T(8,128)(2,1)S(1)}, bf16[1,256,1024]{2,1,0:T(8,128)(2,1)S(1)}, u32[]{:S(2)}, u32[]{:S(2)}) %collective-permute-start.13) | collective-permute-done | bytes 524320 | tf_op jit(solution)/shard_map/ppermute | solution.py:39
  64.4 4.3 %last_sums.1 = (bf16[1,2,32,2048]{3,2,1,0:T(8,128)(2,1)}, f32[1,2,32,2048]{3,2,1,0:T(8,128)}, bf16[1,2,32,2048]{3,2,1,0:T(8,128)(2,1)}, f32[2,32,2048]{2,1,0:T(8...) custom-call(s32[1]{0:T(128)} %bitcast.refs_0_, ...), custom_call_target="tpu_custom_call" | custom-call | bytes 3145728 | tf_op jit(solution)/shard_map/last_sums/pallas_call | solution.py:299
  68.7 0.6 collective-permute-start.23
  69.3 0.5 collective-permute-start.21
  69.9 1.5 %collective-permute-start.16 = (bf16[2,32,2048]{2,1,0:T(8,128)(2,1)}, bf16[2,32,2048]{2,1,0:T(8,128)(2,1)S(1)}, u32[]{:S(2)}, u32[]{:S(2)}) collective-permute-start(bf16[2,32,2048]{2,1,0:T(8,128)(2,1)} %bitcast.29), channel_id=1, source_target_pairs={{0,1},{1,0},{2,3},{3,2},{4,5},{5,4},{6,7},{7,6},{8,9},{9,8},{10,11... | collective-permute-start | bytes 786440 | tf_op jit(solution)/shard_map/ppermute | solution.py:35
  71.4 1.5 %collective-permute-start.14 = (bf16[1,2,32,2048]{3,2,1,0:T(8,128)(2,1)}, bf16[1,2,32,2048]{3,2,1,0:T(8,128)(2,1)S(1)}, u32[]{:S(2)}, u32[]{:S(2)}) collective-permute-start(bf16[1,2,32,2048]{3,2,1,0:T(8,128)(2,1)} %get-tuple-element.30), channel_id=1, source_target_pairs={{0,2},{2,0},{1,3},{3,1},{4,6},{6,4},{5,7},{7,5},{8,10},{10,8},{9,1... | collective-permute-start | bytes 786440 | tf_op jit(solution)/shard_map/ppermute | solution.py:35
  72.9 5.3 %collective-permute-done.23 = bf16[2,32,2048]{2,1,0:T(8,128)(2,1)S(1)} collective-permute-done((bf16[2,32,2048]{2,1,0:T(8,128)(2,1)}, bf16[2,32,2048]{2,1,0:T(8,128)(2,1)S(1)}, u32[]{:S(2)}, u32[]{:S(2)}) %collective-permute-start.23) | collective-permute-done | bytes 262176 | tf_op jit(solution)/shard_map/ppermute | solution.py:35
  78.2 1.1 %convert_add_fusion = f32[2,32,2048]{2,1,0:T(8,128)S(1)} fusion(f32[2,32,2048]{2,1,0:T(8,128)} %get-tuple-element.35, bf16[2,32,2048]{2,1,0:T(8,128)(2,1)S(1)} %collective-permute-done.23), kind=kLoop, calls=%fused_computation.16 | loop fusion | flops 262144 | bytes 1310720 | tf_op jit(solution)/shard_map/add | solution.py:401
  79.3 0.6 collective-permute-start.24
  80.1 0.6 collective-permute-start.22
  80.6 3.2 %collective-permute-done.16 = bf16[2,32,2048]{2,1,0:T(8,128)(2,1)S(1)} collective-permute-done((bf16[2,32,2048]{2,1,0:T(8,128)(2,1)}, bf16[2,32,2048]{2,1,0:T(8,128)(2,1)S(1)}, u32[]{:S(2)}, u32[]{:S(2)}) %collective-permute-start.16) | collective-permute-done | bytes 262176 | tf_op jit(solution)/shard_map/ppermute | solution.py:35
  83.9 0.6 collective-permute-start.17
  84.6 1.4 %collective-permute-start.15 = (bf16[1,32,2048]{2,1,0:T(8,128)(2,1)S(1)}, bf16[1,32,2048]{2,1,0:T(8,128)(2,1)S(1)}, u32[]{:S(2)}, u32[]{:S(2)}) collective-permute-start(bf16[1,32,2048]{2,1,0:T(8,128)(2,1)S(1)} %fusion), channel_id=1, source_target_pairs={{0,1},{1,0},{2,3},{3,2},{4,5},{5,4},{6,7},{7,6},{8,9},{9,8},{10,11... | collective-permute-start | bytes 393224 | tf_op jit(solution)/shard_map/ppermute | solution.py:35
  86.0 0.9 collective-permute-done.24
  87.2 0.6 collective-permute-start.25
  87.8 2.0 %collective-permute-start.26 = (bf16[1,64,512]{2,1,0:T(8,128)(2,1)S(1)}, bf16[1,64,512]{2,1,0:T(8,128)(2,1)S(1)}, u32[]{:S(2)}, u32[]{:S(2)}) collective-permute-start(bf16[1,64,512]{2,1,0:T(8,128)(2,1)S(1)} %get-tuple-element.38), channel_id=1, source_target_pairs={{0,16},{4,20},{8,24},{12,28},{16,0},{20,4},{24,8},{28,12},{1,17},{... | collective-permute-start | bytes 196616 | tf_op jit(solution)/shard_map/ppermute | solution.py:35
  89.8 2.8 %collective-permute-start.27 = (bf16[1,64,512]{2,1,0:T(8,128)(2,1)S(1)}, bf16[1,64,512]{2,1,0:T(8,128)(2,1)S(1)}, u32[]{:S(2)}, u32[]{:S(2)}) collective-permute-start(bf16[1,64,512]{2,1,0:T(8,128)(2,1)S(1)} %get-tuple-element.39), channel_id=1, source_target_pairs={{0,24},{4,28},{8,0},{12,4},{16,8},{20,12},{24,16},{28,20},{1,25},{... | collective-permute-start | bytes 196616 | tf_op jit(solution)/shard_map/ppermute | solution.py:35
  92.9 0.6 collective-permute-start.19
  93.5 3.3 %collective-permute-start.20 = (bf16[1,64,512]{2,1,0:T(8,128)(2,1)S(1)}, bf16[1,64,512]{2,1,0:T(8,128)(2,1)S(1)}, u32[]{:S(2)}, u32[]{:S(2)}) collective-permute-start(bf16[1,64,512]{2,1,0:T(8,128)(2,1)S(1)} %get-tuple-element.42), channel_id=1, source_target_pairs={{0,24},{4,28},{8,0},{12,4},{16,8},{20,12},{24,16},{28,20},{1,25},{... | collective-permute-start | bytes 196616 | tf_op jit(solution)/shard_map/ppermute | solution.py:35
  96.9 2.2 %collective-permute-done.18 = bf16[1,64,512]{2,1,0:T(8,128)(2,1)S(1)} collective-permute-done((bf16[1,64,512]{2,1,0:T(8,128)(2,1)S(1)}, bf16[1,64,512]{2,1,0:T(8,128)(2,1)S(1)}, u32[]{:S(2)}, u32[]{:S(2)}) %collective-permute-start.18) | collective-permute-done | bytes 65568 | tf_op jit(solution)/shard_map/ppermute | solution.py:35
  99.1 1.1 %collective-permute-done.19 = bf16[1,64,512]{2,1,0:T(8,128)(2,1)S(1)} collective-permute-done((bf16[1,64,512]{2,1,0:T(8,128)(2,1)S(1)}, bf16[1,64,512]{2,1,0:T(8,128)(2,1)S(1)}, u32[]{:S(2)}, u32[]{:S(2)}) %collective-permute-start.19) | collective-permute-done | bytes 65568 | tf_op jit(solution)/shard_map/ppermute | solution.py:35
  100.4 1.3 %collective-permute-done.28 = f32[1,128,256]{2,1,0:T(8,128)S(1)} collective-permute-done((f32[1,128,256]{2,1,0:T(8,128)S(1)}, f32[1,128,256]{2,1,0:T(8,128)S(1)}, u32[]{:S(2)}, u32[]{:S(2)}) %collective-permute-start.28) | collective-permute-done | bytes 131104 | tf_op jit(solution)/shard_map/ppermute | solution.py:39
  101.7 0.7 maximum_select_fusion.1
  (54 shorter events, 2.1 us)
Async XLA Ops:
  0.0 1.0 %copy-start = (f32[2,256,256]{2,1,0:T(8,128)S(1)}, f32[2,256,256]{2,1,0:T(8,128)}, u32[]{:S(2)}) copy-start(f32[2,256,256]{2,1,0:T(8,128)} %param.3) | copy-start | bytes 1572868
  1.1 6.5 %collective-permute-start = (bf16[2,128,256]{2,1,0:T(8,128)(2,1)S(1)}, bf16[2,128,256]{2,1,0:T(8,128)(2,1)S(1)}, u32[]{:S(2)}, u32[]{:S(2)}) collective-permute-start(bf16[2,128,256]{2,1,0:T(8,128)(2,1)S(1)} %dynamic-slice_convert_fusion.2), channel_id=1, source_target_pairs={{0,2},{2,0},{1,3},{3,1},{4,6},{6,4},{5,7},{7,5},{8,10},{10,8},{9,1... | collective-permute-start | bytes 393224 | tf_op jit(solution)/shard_map/ppermute | solution.py:35
  7.6 40.3 %collective-permute-start.3 = (bf16[3,256,1024]{2,1,0:T(8,128)(2,1)}, bf16[3,256,1024]{2,1,0:T(8,128)(2,1)}, u32[]{:S(2)}, u32[]{:S(2)}) collective-permute-start(bf16[3,256,1024]{2,1,0:T(8,128)(2,1)} %constant_dynamic-slice_fusion.2), channel_id=1, source_target_pairs={{0,2},{2,0},{1,3},{3,1},{4,6},{6,4},{5,7},{7,5},{8,10},{10,8},{9,1... | collective-permute-start | bytes 4718600 | tf_op jit(solution)/shard_map/ppermute | solution.py:35
  9.4 1.4 %collective-permute-start.1 = (bf16[2,1,128,256]{3,2,0,1:T(8,128)(2,1)S(1)}, bf16[2,1,128,256]{3,2,0,1:T(8,128)(2,1)S(1)}, u32[]{:S(2)}, u32[]{:S(2)}) collective-permute-start(bf16[2,1,128,256]{3,2,0,1:T(8,128)(2,1)S(1)} %get-tuple-element.46), channel_id=1, source_target_pairs={{0,4},{4,0},{8,12},{12,8},{16,20},{20,16},{24,28},{28,24},{1,5},{5... | collective-permute-start | bytes 393224 | tf_op jit(solution)/shard_map/ppermute | solution.py:39
  10.9 10.3 %copy-start.1 = (bf16[2,128,512]{2,1,0:T(8,128)(2,1)}, bf16[2,128,512]{2,1,0:T(8,128)(2,1)S(1)}, u32[]{:S(2)}) copy-start(bf16[2,128,512]{2,1,0:T(8,128)(2,1)S(1)} %maximum_select_fusion.refs_0_) | copy-start | bytes 786436
  10.9 8.5 %collective-permute-start.2 = (bf16[2,128,512]{2,1,0:T(8,128)(2,1)S(1)}, bf16[2,128,512]{2,1,0:T(8,128)(2,1)}, u32[]{:S(2)}, u32[]{:S(2)}) collective-permute-start(bf16[2,128,512]{2,1,0:T(8,128)(2,1)S(1)} %maximum_select_fusion.refs_0_), channel_id=1, source_target_pairs={{0,1},{1,0},{2,3},{3,2},{4,5},{5,4},{6,7},{7,6},{8,9},{9,8},{10,11... | collective-permute-start | bytes 786440 | tf_op jit(solution)/shard_map/ppermute | solution.py:35
  12.5 11.0 %collective-permute-start.4 = (bf16[2,128,512]{2,1,0:T(8,128)(2,1)S(1)}, bf16[2,128,512]{2,1,0:T(8,128)(2,1)S(1)}, u32[]{:S(2)}, u32[]{:S(2)}) collective-permute-start(bf16[2,128,512]{2,1,0:T(8,128)(2,1)S(1)} %maximum_select_fusion.refs_0_), channel_id=1, source_target_pairs={{0,8},{4,12},{8,16},{12,20},{16,24},{20,28},{24,0},{28,4},{1,9},{5... | collective-permute-start | bytes 786440 | tf_op jit(solution)/shard_map/ppermute | solution.py:35
  14.1 13.4 %collective-permute-start.6 = (bf16[2,128,512]{2,1,0:T(8,128)(2,1)S(1)}, bf16[2,128,512]{2,1,0:T(8,128)(2,1)S(1)}, u32[]{:S(2)}, u32[]{:S(2)}) collective-permute-start(bf16[2,128,512]{2,1,0:T(8,128)(2,1)S(1)} %maximum_select_fusion.refs_0_), channel_id=1, source_target_pairs={{0,24},{4,28},{8,0},{12,4},{16,8},{20,12},{24,16},{28,20},{1,25},{... | collective-permute-start | bytes 786440 | tf_op jit(solution)/shard_map/ppermute | solution.py:35
  16.3 23.1 %collective-permute-start.8 = (bf16[2,128,512]{2,1,0:T(8,128)(2,1)S(1)}, bf16[2,128,512]{2,1,0:T(8,128)(2,1)}, u32[]{:S(2)}, u32[]{:S(2)}) collective-permute-start(bf16[2,128,512]{2,1,0:T(8,128)(2,1)S(1)} %maximum_select_fusion.refs_0_), channel_id=1, source_target_pairs={{0,16},{4,20},{8,24},{12,28},{16,0},{20,4},{24,8},{28,12},{1,17},{... | collective-permute-start | bytes 786440 | tf_op jit(solution)/shard_map/ppermute | solution.py:35
  21.2 29.4 %collective-permute-start.11 = (bf16[4,256,1024]{2,1,0:T(8,128)(2,1)S(1)}, bf16[4,256,1024]{2,1,0:T(8,128)(2,1)}, u32[]{:S(2)}, u32[]{:S(2)}) collective-permute-start(bf16[4,256,1024]{2,1,0:T(8,128)(2,1)S(1)} %constant_dynamic-slice_fusion.1.refs_0_.refs_1_), channel_id=1, source_target_pairs={{0,4},{4,0},{8,12},{12,8},{16,20},{20,16},{24,28},{28,24},{1,5},{5... | collective-permute-start | bytes 6291464 | tf_op jit(solution)/shard_map/ppermute | solution.py:39
  23.5 24.3 %copy-start.5 = (bf16[2,128,512]{2,1,0:T(8,128)(2,1)}, bf16[2,128,512]{2,1,0:T(8,128)(2,1)S(1)}, u32[]{:S(2)}) copy-start(bf16[2,128,512]{2,1,0:T(8,128)(2,1)S(1)} %collective-permute-done.4.refs_2_) | copy-start | bytes 786436
  23.5 18.2 %collective-permute-start.5 = (bf16[2,128,512]{2,1,0:T(8,128)(2,1)S(1)}, bf16[2,128,512]{2,1,0:T(8,128)(2,1)}, u32[]{:S(2)}, u32[]{:S(2)}) collective-permute-start(bf16[2,128,512]{2,1,0:T(8,128)(2,1)S(1)} %collective-permute-done.4.refs_2_), channel_id=1, source_target_pairs={{0,1},{1,0},{2,3},{3,2},{4,5},{5,4},{6,7},{7,6},{8,9},{9,8},{10,11... | collective-permute-start | bytes 786440 | tf_op jit(solution)/shard_map/ppermute | solution.py:35
  27.5 20.3 %copy-start.6 = (bf16[2,128,512]{2,1,0:T(8,128)(2,1)}, bf16[2,128,512]{2,1,0:T(8,128)(2,1)S(1)}, u32[]{:S(2)}) copy-start(bf16[2,128,512]{2,1,0:T(8,128)(2,1)S(1)} %collective-permute-done.6.refs_4_) | copy-start | bytes 786436
  27.5 14.3 %collective-permute-start.7 = (bf16[2,128,512]{2,1,0:T(8,128)(2,1)S(1)}, bf16[2,128,512]{2,1,0:T(8,128)(2,1)}, u32[]{:S(2)}, u32[]{:S(2)}) collective-permute-start(bf16[2,128,512]{2,1,0:T(8,128)(2,1)S(1)} %collective-permute-done.6.refs_4_), channel_id=1, source_target_pairs={{0,1},{1,0},{2,3},{3,2},{4,5},{5,4},{6,7},{7,6},{8,9},{9,8},{10,11... | collective-permute-start | bytes 786440 | tf_op jit(solution)/shard_map/ppermute | solution.py:35
  39.4 8.4 %collective-permute-start.9 = (bf16[2,128,512]{2,1,0:T(8,128)(2,1)}, bf16[2,128,512]{2,1,0:T(8,128)(2,1)S(1)}, u32[]{:S(2)}, u32[]{:S(2)}) collective-permute-start(bf16[2,128,512]{2,1,0:T(8,128)(2,1)} %collective-permute-done.8.refs_6_), channel_id=1, source_target_pairs={{0,1},{1,0},{2,3},{3,2},{4,5},{5,4},{6,7},{7,6},{8,9},{9,8},{10,11... | collective-permute-start | bytes 786440 | tf_op jit(solution)/shard_map/ppermute | solution.py:35
  47.8 3.8 %collective-permute-start.12 = (bf16[3,256,1024]{2,1,0:T(8,128)(2,1)}, bf16[3,256,1024]{2,1,0:T(8,128)(2,1)}, u32[]{:S(2)}, u32[]{:S(2)}) collective-permute-start(bf16[3,256,1024]{2,1,0:T(8,128)(2,1)} %collective-permute-done.3.refs_1_), channel_id=1, source_target_pairs={{0,4},{4,0},{8,12},{12,8},{16,20},{20,16},{24,28},{28,24},{1,5},{5... | collective-permute-start | bytes 4718600 | tf_op jit(solution)/shard_map/ppermute | solution.py:39
  47.9 14.5 %collective-permute-start.10 = (bf16[1,256,1024]{2,1,0:T(8,128)(2,1)}, bf16[1,256,1024]{2,1,0:T(8,128)(2,1)S(1)}, u32[]{:S(2)}, u32[]{:S(2)}) collective-permute-start(bf16[1,256,1024]{2,1,0:T(8,128)(2,1)} %constant_dynamic-slice_fusion), channel_id=1, source_target_pairs={{0,2},{2,0},{1,3},{3,1},{4,6},{6,4},{5,7},{7,5},{8,10},{10,8},{9,1... | collective-permute-start | bytes 1572872 | tf_op jit(solution)/shard_map/ppermute | solution.py:35
  62.5 1.9 %collective-permute-start.13 = (bf16[1,256,1024]{2,1,0:T(8,128)(2,1)S(1)}, bf16[1,256,1024]{2,1,0:T(8,128)(2,1)S(1)}, u32[]{:S(2)}, u32[]{:S(2)}) collective-permute-start(bf16[1,256,1024]{2,1,0:T(8,128)(2,1)S(1)} %collective-permute-done.10.refs_1_.refs_2_), channel_id=1, source_target_pairs={{0,4},{4,0},{8,12},{12,8},{16,20},{20,16},{24,28},{28,24},{1,5},{5... | collective-permute-start | bytes 1572872 | tf_op jit(solution)/shard_map/ppermute | solution.py:39
  68.7 11.2 %copy-start.4 = (f32[1,2,32,2048]{3,2,1,0:T(8,128)S(1)}, f32[1,2,32,2048]{3,2,1,0:T(8,128)}, u32[]{:S(2)}) copy-start(f32[1,2,32,2048]{3,2,1,0:T(8,128)} %get-tuple-element.33) | copy-start | bytes 1572868
  68.7 15.1 %copy-start.3 = (f32[2,32,2048]{2,1,0:T(8,128)S(1)}, f32[2,32,2048]{2,1,0:T(8,128)}, u32[]{:S(2)}) copy-start(f32[2,32,2048]{2,1,0:T(8,128)} %get-tuple-element.31) | copy-start | bytes 1572868
  68.7 9.4 %collective-permute-start.23 = (bf16[2,32,2048]{2,1,0:T(8,128)(2,1)}, bf16[2,32,2048]{2,1,0:T(8,128)(2,1)S(1)}, u32[]{:S(2)}, u32[]{:S(2)}) collective-permute-start(bf16[2,32,2048]{2,1,0:T(8,128)(2,1)} %bitcast.30), channel_id=1, source_target_pairs={{0,1},{1,0},{2,3},{3,2},{4,5},{5,4},{6,7},{7,6},{8,9},{9,8},{10,11... | collective-permute-start | bytes 786440 | tf_op jit(solution)/shard_map/ppermute | solution.py:35
  69.3 10.6 %collective-permute-start.21 = (bf16[1,2,32,2048]{3,2,1,0:T(8,128)(2,1)}, bf16[1,2,32,2048]{3,2,1,0:T(8,128)(2,1)S(1)}, u32[]{:S(2)}, u32[]{:S(2)}) collective-permute-start(bf16[1,2,32,2048]{3,2,1,0:T(8,128)(2,1)} %get-tuple-element.34), channel_id=1, source_target_pairs={{0,2},{2,0},{1,3},{3,1},{4,6},{6,4},{5,7},{7,5},{8,10},{10,8},{9,1... | collective-permute-start | bytes 786440 | tf_op jit(solution)/shard_map/ppermute | solution.py:35
  69.9 13.9 %collective-permute-start.16 = (bf16[2,32,2048]{2,1,0:T(8,128)(2,1)}, bf16[2,32,2048]{2,1,0:T(8,128)(2,1)S(1)}, u32[]{:S(2)}, u32[]{:S(2)}) collective-permute-start(bf16[2,32,2048]{2,1,0:T(8,128)(2,1)} %bitcast.29), channel_id=1, source_target_pairs={{0,1},{1,0},{2,3},{3,2},{4,5},{5,4},{6,7},{7,6},{8,9},{9,8},{10,11... | collective-permute-start | bytes 786440 | tf_op jit(solution)/shard_map/ppermute | solution.py:35
  71.4 13.1 %collective-permute-start.14 = (bf16[1,2,32,2048]{3,2,1,0:T(8,128)(2,1)}, bf16[1,2,32,2048]{3,2,1,0:T(8,128)(2,1)S(1)}, u32[]{:S(2)}, u32[]{:S(2)}) collective-permute-start(bf16[1,2,32,2048]{3,2,1,0:T(8,128)(2,1)} %get-tuple-element.30), channel_id=1, source_target_pairs={{0,2},{2,0},{1,3},{3,1},{4,6},{6,4},{5,7},{7,5},{8,10},{10,8},{9,1... | collective-permute-start | bytes 786440 | tf_op jit(solution)/shard_map/ppermute | solution.py:35
  78.2 6.3 %copy-start.2 = (f32[1,2,32,2048]{3,2,1,0:T(8,128)S(1)}, f32[1,2,32,2048]{3,2,1,0:T(8,128)}, u32[]{:S(2)}) copy-start(f32[1,2,32,2048]{3,2,1,0:T(8,128)} %get-tuple-element.29) | copy-start | bytes 1572868
  79.3 7.6 %collective-permute-start.24 = (bf16[1,32,2048]{2,1,0:T(8,128)(2,1)S(1)}, bf16[1,32,2048]{2,1,0:T(8,128)(2,1)S(1)}, u32[]{:S(2)}, u32[]{:S(2)}) collective-permute-start(bf16[1,32,2048]{2,1,0:T(8,128)(2,1)S(1)} %slice.26), channel_id=1, source_target_pairs={{0,2},{2,0},{1,3},{3,1},{4,6},{6,4},{5,7},{7,5},{8,10},{10,8},{9,1... | collective-permute-start | bytes 393224 | tf_op jit(solution)/shard_map/ppermute | solution.py:35
  80.1 6.9 %collective-permute-start.22 = (bf16[1,32,2048]{2,1,0:T(8,128)(2,1)S(1)}, bf16[1,32,2048]{2,1,0:T(8,128)(2,1)S(1)}, u32[]{:S(2)}, u32[]{:S(2)}) collective-permute-start(bf16[1,32,2048]{2,1,0:T(8,128)(2,1)S(1)} %fusion.1), channel_id=1, source_target_pairs={{0,1},{1,0},{2,3},{3,2},{4,5},{5,4},{6,7},{7,6},{8,9},{9,8},{10,11... | collective-permute-start | bytes 393224 | tf_op jit(solution)/shard_map/ppermute | solution.py:35
  83.9 8.8 %collective-permute-start.17 = (bf16[1,32,2048]{2,1,0:T(8,128)(2,1)S(1)}, bf16[1,32,2048]{2,1,0:T(8,128)(2,1)S(1)}, u32[]{:S(2)}, u32[]{:S(2)}) collective-permute-start(bf16[1,32,2048]{2,1,0:T(8,128)(2,1)S(1)} %slice.27), channel_id=1, source_target_pairs={{0,2},{2,0},{1,3},{3,1},{4,6},{6,4},{5,7},{7,5},{8,10},{10,8},{9,1... | collective-permute-start | bytes 393224 | tf_op jit(solution)/shard_map/ppermute | solution.py:35
  84.6 8.1 %collective-permute-start.15 = (bf16[1,32,2048]{2,1,0:T(8,128)(2,1)S(1)}, bf16[1,32,2048]{2,1,0:T(8,128)(2,1)S(1)}, u32[]{:S(2)}, u32[]{:S(2)}) collective-permute-start(bf16[1,32,2048]{2,1,0:T(8,128)(2,1)S(1)} %fusion), channel_id=1, source_target_pairs={{0,1},{1,0},{2,3},{3,2},{4,5},{5,4},{6,7},{7,6},{8,9},{9,8},{10,11... | collective-permute-start | bytes 393224 | tf_op jit(solution)/shard_map/ppermute | solution.py:35
  87.2 6.3 %collective-permute-start.25 = (bf16[1,64,512]{2,1,0:T(8,128)(2,1)S(1)}, bf16[1,64,512]{2,1,0:T(8,128)(2,1)S(1)}, u32[]{:S(2)}, u32[]{:S(2)}) collective-permute-start(bf16[1,64,512]{2,1,0:T(8,128)(2,1)S(1)} %get-tuple-element.37), channel_id=1, source_target_pairs={{0,8},{4,12},{8,16},{12,20},{16,24},{20,28},{24,0},{28,4},{1,9},{5... | collective-permute-start | bytes 196616 | tf_op jit(solution)/shard_map/ppermute | solution.py:35
  87.8 9.0 %collective-permute-start.26 = (bf16[1,64,512]{2,1,0:T(8,128)(2,1)S(1)}, bf16[1,64,512]{2,1,0:T(8,128)(2,1)S(1)}, u32[]{:S(2)}, u32[]{:S(2)}) collective-permute-start(bf16[1,64,512]{2,1,0:T(8,128)(2,1)S(1)} %get-tuple-element.38), channel_id=1, source_target_pairs={{0,16},{4,20},{8,24},{12,28},{16,0},{20,4},{24,8},{28,12},{1,17},{... | collective-permute-start | bytes 196616 | tf_op jit(solution)/shard_map/ppermute | solution.py:35
  89.8 7.0 %collective-permute-start.27 = (bf16[1,64,512]{2,1,0:T(8,128)(2,1)S(1)}, bf16[1,64,512]{2,1,0:T(8,128)(2,1)S(1)}, u32[]{:S(2)}, u32[]{:S(2)}) collective-permute-start(bf16[1,64,512]{2,1,0:T(8,128)(2,1)S(1)} %get-tuple-element.39), channel_id=1, source_target_pairs={{0,24},{4,28},{8,0},{12,4},{16,8},{20,12},{24,16},{28,20},{1,25},{... | collective-permute-start | bytes 196616 | tf_op jit(solution)/shard_map/ppermute | solution.py:35
  92.9 6.2 %collective-permute-start.18 = (bf16[1,64,512]{2,1,0:T(8,128)(2,1)S(1)}, bf16[1,64,512]{2,1,0:T(8,128)(2,1)S(1)}, u32[]{:S(2)}, u32[]{:S(2)}) collective-permute-start(bf16[1,64,512]{2,1,0:T(8,128)(2,1)S(1)} %get-tuple-element.40), channel_id=1, source_target_pairs={{0,8},{4,12},{8,16},{12,20},{16,24},{20,28},{24,0},{28,4},{1,9},{5... | collective-permute-start | bytes 196616 | tf_op jit(solution)/shard_map/ppermute | solution.py:35
  92.9 7.2 %collective-permute-start.19 = (bf16[1,64,512]{2,1,0:T(8,128)(2,1)S(1)}, bf16[1,64,512]{2,1,0:T(8,128)(2,1)S(1)}, u32[]{:S(2)}, u32[]{:S(2)}) collective-permute-start(bf16[1,64,512]{2,1,0:T(8,128)(2,1)S(1)} %get-tuple-element.41), channel_id=1, source_target_pairs={{0,16},{4,20},{8,24},{12,28},{16,0},{20,4},{24,8},{28,12},{1,17},{... | collective-permute-start | bytes 196616 | tf_op jit(solution)/shard_map/ppermute | solution.py:35
  93.5 6.7 %collective-permute-start.20 = (bf16[1,64,512]{2,1,0:T(8,128)(2,1)S(1)}, bf16[1,64,512]{2,1,0:T(8,128)(2,1)S(1)}, u32[]{:S(2)}, u32[]{:S(2)}) collective-permute-start(bf16[1,64,512]{2,1,0:T(8,128)(2,1)S(1)} %get-tuple-element.42), channel_id=1, source_target_pairs={{0,24},{4,28},{8,0},{12,4},{16,8},{20,12},{24,16},{28,20},{1,25},{... | collective-permute-start | bytes 196616 | tf_op jit(solution)/shard_map/ppermute | solution.py:35
  100.3 1.4 %collective-permute-start.28 = (f32[1,128,256]{2,1,0:T(8,128)S(1)}, f32[1,128,256]{2,1,0:T(8,128)S(1)}, u32[]{:S(2)}, u32[]{:S(2)}) collective-permute-start(f32[1,128,256]{2,1,0:T(8,128)S(1)} %get-tuple-element.44), channel_id=1, source_target_pairs={{0,4},{4,0},{8,12},{12,8},{16,20},{20,16},{24,28},{28,24},{1,5},{5... | collective-permute-start | bytes 393224 | tf_op jit(solution)/shard_map/ppermute | solution.py:39

commit v12 on v11

--- a/solution.py
+++ b/solution.py
@@ -8,6 +8,7 @@
 CORES = 2
 PIECES = 2
 VMEM_LIMIT = 30 * 2**20
+VMEM_LARGE = 44 * 2**20
 F32, BF16 = jnp.float32, jnp.bfloat16
 VMEM = pl.BlockSpec(memory_space=pltpu.VMEM)
 ANY = pl.BlockSpec(memory_space=pl.ANY)
@@ -47,8 +48,9 @@
     return lax.dot_general(a, b, (((1,), (1,)), ((), ())), preferred_element_type=F32)
 
 
-def params():
-    return pltpu.CompilerParams(vmem_limit_bytes=VMEM_LIMIT)
+def params(sums=0):
+    large = 4 * sums > 8 * 2**20
+    return pltpu.CompilerParams(vmem_limit_bytes=VMEM_LARGE if large else VMEM_LIMIT)
 
 
 def in_hbm(x):
@@ -162,16 +164,20 @@
     )(*flat, vectors)
 
 
-def step_pairs(side, firsts, vectors):
+def own_sums(side, firsts, vectors, early):
     groups, rows, total = vectors.shape
-    shape = jax.ShapeDtypeStruct((groups, rows, rows), BF16)
     n = len(side)
     width = total // n
+    tile = min(width, 1024)
+    more = [] if early is None else [early]
+    shape = jax.ShapeDtypeStruct((groups, rows, total), F32)
 
     def body(*refs):
-        vec, out = refs[n : n + 2]
-        ins = refs[n + 2 : 2 * n + 2]
-        sems = refs[-1]
+        vec = refs[n]
+        out = refs[n + 1 + len(more)]
+        before = refs[n + 1] if more else None
+        ins = refs[n + 2 + len(more) : 2 * n + 2 + len(more)]
+        pairs, sems = refs[-2:]
         copies = [
             pltpu.make_async_copy(refs[i].at[pl.ds(firsts[i], 1)], ins[i], sems.at[i])
             for i in range(n)
@@ -182,72 +188,67 @@
             copy.wait()
 
         def store(g, _, pair):
-            out[g] = pair
+            pairs[g * rows : (g + 1) * rows] = pair
 
         pairs_of(ins, vec, store)
+        for i in range(total // tile):
+            r, at = i * tile // width, i * tile % width
+            cols = slice(i * tile, (i + 1) * tile)
+            got = jnp.dot(pairs[...], ins[r][0, :, at : at + tile], preferred_element_type=F32)
+            got = got.reshape(groups, rows, tile)
+            out[:, :, cols] = got if before is None else got + before[:, :, cols]
 
     return pl.pallas_call(
         body,
         out_shape=shape,
-        in_specs=[ANY] * n + [VMEM],
+        in_specs=[ANY] * n + [VMEM] * (1 + len(more)),
         out_specs=VMEM,
         scratch_shapes=[pltpu.VMEM((1, rows, width), BF16)] * n
-        + [pltpu.SemaphoreType.DMA((n,))],
+        + [pltpu.VMEM((groups * rows, rows), BF16), pltpu.SemaphoreType.DMA((n,))],
+        input_output_aliases={n + 1: 0} if more else {},
         cost_estimate=cost(0, vectors),
-        compiler_params=params(),
-        name="step_pairs",
-    )(*side, vectors)
-
-
-def last_sums(o, sides, firsts, pair_own, vectors, early, no, nv):
+        compiler_params=params(vectors.size),
+        name="own_sums",
+    )(*side, vectors, *more)
+
+
+def last_sums(o, side, firsts, vectors, sums, no, nv):
     groups, rows, total = vectors.shape
-    nr = len(sides[0])
+    nr = n = len(side)
     width = total // nr
-    flat = [p for side in sides for p in side]
-    n = len(flat)
     per = groups // nv
     own = rows // no
     small = own // (PIECES * 2)
-    more = [] if early is None else [early]
     tile = min(width, 1024)
     tiles = total // tile
 
     def body(*refs):
         me = refs[0][0]
         refs = refs[1:]
-        own_pair, vec = refs[n : n + 2]
-        before = refs[n + 2] if more else None
-        results = refs[n + 2 + len(more) : n + 2 + len(more) + 4 * PIECES]
-        outs = refs[n + 2 + len(more) + 4 * PIECES : n + 2 + len(more) + 8 * PIECES]
+        vec, before = refs[n : n + 2]
+        results = refs[n + 2 : n + 2 + 4 * PIECES]
+        outs = refs[n + 2 + 4 * PIECES : n + 2 + 8 * PIECES]
         ins = refs[-n - 3 : -3]
         their_pair, sems, out_sems = refs[-3:]
         copies = [
-            pltpu.make_async_copy(refs[i].at[pl.ds(firsts[i % nr], 1)], ins[i], sems.at[i])
+            pltpu.make_async_copy(refs[i].at[pl.ds(firsts[i], 1)], ins[i], sems.at[i])
             for i in range(n)
         ]
-        for copy in copies[nr:] + copies[:nr]:
+        for copy in copies:
             copy.start()
-        for copy in copies[nr:]:
+        for copy in copies:
             copy.wait()
 
         def store(g, _, pair):
             their_pair[g] = pair
 
-        pairs_of(ins[nr:], vec, store)
-        for copy in copies[:nr]:
-            copy.wait()
-        left = [p[...].reshape(groups * rows, rows) for p in (own_pair, their_pair)]
+        pairs_of(ins, vec, store)
+        left = their_pair[...].reshape(groups * rows, rows)
         sent = []
         for i in range(tiles):
             r, at = i * tile // width, i * tile % width
-            got = None
-            for s in range(len(sides)):
-                right = ins[s * nr + r][0, :, at : at + tile]
-                term = jnp.dot(left[s], right, preferred_element_type=F32)
-                got = term if got is None else got + term
-            got = got.reshape(groups, rows, tile)
-            if more:
-                got = got + before[:, :, i * tile : (i + 1) * tile]
+            got = jnp.dot(left, ins[r][0, :, at : at + tile], preferred_element_type=F32)
+            got = got.reshape(groups, rows, tile) + before[:, :, i * tile : (i + 1) * tile]
             got = got.reshape(groups, no, PIECES, 2, small, tile)
             for g in range(groups):
                 v = g // per
@@ -299,7 +300,7 @@
     outs = pl.pallas_call(
         body,
         out_shape=[pltpu.HBM(x.shape, x.dtype) for x in shapes],
-        in_specs=[SMEM] + [ANY] * n + [VMEM] * (2 + len(more)),
+        in_specs=[SMEM] + [ANY] * n + [VMEM] * 2,
         out_specs=[HBM] * len(shapes),
         scratch_shapes=[pltpu.VMEM(x, d) for x, d in held]
         + [pltpu.VMEM((1, rows, width), BF16)] * n
@@ -309,9 +310,9 @@
             pltpu.SemaphoreType.DMA((tiles * nv * PIECES * 3,)),
         ],
         cost_estimate=cost(0, *shapes),
-        compiler_params=params(),
+        compiler_params=params(vectors.size),
         name="last_sums",
-    )(o.reshape(1), *flat, pair_own, vectors, *more)
+    )(o.reshape(1), *side, vectors, sums)
     return [outs[4 * p : 4 * p + 4] for p in range(PIECES)]
 
 
@@ -357,6 +358,8 @@
 
     blocks = []
     for t in sorted(range(nz), key=lambda t: min(t, nz - t)):
+        if min(t, nz - t) == 2:
+            whole, _ = lax.optimization_barrier((whole, blocks[no - 1][0]))
         got = whole if t == 0 else shift(whole, "aux", na, t, CORES)
         blocks.append((got, 0, nz, t))
         for s in range(1, no):
@@ -383,10 +386,10 @@
     got, early = lax.optimization_barrier((come_last, early))
     sides = [[kept] + got, [shown] + [sibling(g, na) for g in got]]
     firsts = [early_steps] + [0] * (nv - 1)
-    pair_own = step_pairs(sides[0], firsts, vectors)
+    sums = own_sums(sides[0], firsts, vectors, early)
 
     out = []
-    for p in last_sums(o, sides, firsts, pair_own, vectors, early, no, nv):
+    for p in last_sums(o, sides[1], firsts, vectors, sums, no, nv):
         send_x, keep_x, send_y, keep_y = p
         one = keep_x
         for r in range(1, nv):

time: 103 us -> 102 us (level)
  waiting for transfers between devices: 46.1 us -> 41.9 us
  starting transfers between devices: 30 us -> 32.4 us
    ppermute x24, waiting for transfers between devices: 41.4 us -> 38 us  [shift(): return lax.ppermute(array, axis, pairs)]
    ppermute x24, starting transfers between devices: 29.7 us -> 32.1 us  [shift(): return lax.ppermute(array, axis, pairs)]
  transfers between devices with their start and end apart: 29 -> 29, of which waited for: 16 -> 15; matrix products, arithmetic and copies ran while one was open for 8% -> 8% of each run, Pallas kernels for 11% -> 12%
where the time goes in v12:
time: 102 us
  waiting for transfers between devices  41.9 us (41%)
  starting transfers between devices  32.4 us (32%)
  Pallas kernels  16 us (16%)
  local copies, waits for them, and re-layouts  8.29 us (8%)
  other arithmetic  2.81 us (3%)
    ppermute x24, waiting for transfers between devices, shift(): return lax.ppermute(array, axis, pairs)  38 us
    ppermute x24, starting transfers between devices, shift(): return lax.ppermute(array, axis, pairs)  32.1 us
    pallas_call x1, Pallas kernels, early_sums(): pl.pallas_call(body, out_shape=shape, in_specs=[ANY] * n + [VMEM], out_sp...  8.44 us
    dynamic_slice x2, local copies, waits for them, and re-layouts, sends(): lax.dynamic_slice_in_dim(source, (v - r) % nv * take + first, size, 0)  4.56 us
    ppermute x5, waiting for transfers between devices, sibling(): return lax.ppermute(array, 'aux', [(i, i ^ 1) for i in range(size)])  3.9 us
    pallas_call x1, Pallas kernels, last_sums(): pl.pallas_call(body, out_shape=[pltpu.HBM(x.shape, x.dtype) for x in shap...  3.9 us
    pallas_call x1, Pallas kernels, assemble(): pl.pallas_call(body, out_shape=shape, in_specs=[SMEM] + [ANY] * len(block...  2.05 us
  transfers between devices with their start and end apart: 29, of which 15 were waited for; matrix products, arithmetic and copies ran while one was open for 8% of the time, Pallas kernels for 12%

profile of v12, /device:TPU:0, one launch (start us, length us, event | category | flops | bytes accessed | tf_op | source)
XLA Modules:
  0.0 101.8 jit_solution(2278369403446524866)
XLA Ops:
  0.0 1.0 %copy-done = f32[2,256,256]{2,1,0:T(8,128)S(1)} copy-done((f32[2,256,256]{2,1,0:T(8,128)S(1)}, f32[2,256,256]{2,1,0:T(8,128)}, u32[]{:S(2)}) %copy-start) | copy-done | bytes 524312
  1.1 3.0 %collective-permute-start = (bf16[2,128,256]{2,1,0:T(8,128)(2,1)S(1)}, bf16[2,128,256]{2,1,0:T(8,128)(2,1)S(1)}, u32[]{:S(2)}, u32[]{:S(2)}) collective-permute-start(bf16[2,128,256]{2,1,0:T(8,128)(2,1)S(1)} %dynamic-slice_convert_fusion.2), channel_id=1, source_target_pairs={{0,2},{2,0},{1,3},{3,1},{4,6},{6,4},{5,7},{7,5},{8,10},{10,8},{9,1... | collective-permute-start | bytes 393224 | tf_op jit(solution)/shard_map/ppermute | solution.py:36
  4.1 2.7 %constant_dynamic-slice_fusion.2 = bf16[3,256,1024]{2,1,0:T(8,128)(2,1)} fusion(bf16[8,256,1024]{2,1,0:T(8,128)(2,1)} %param.2, s32[]{:T(128)S(6)} %select_n.177), kind=kLoop, calls=%fused_computation.64 | loop fusion | bytes 3145732 | tf_op jit(solution)/shard_map/dynamic_slice | solution.py:337
  6.8 0.8 collective-permute-done
  7.6 1.7 %collective-permute-start.4 = (bf16[3,256,1024]{2,1,0:T(8,128)(2,1)}, bf16[3,256,1024]{2,1,0:T(8,128)(2,1)}, u32[]{:S(2)}, u32[]{:S(2)}) collective-permute-start(bf16[3,256,1024]{2,1,0:T(8,128)(2,1)} %constant_dynamic-slice_fusion.2), channel_id=1, source_target_pairs={{0,2},{2,0},{1,3},{3,1},{4,6},{6,4},{5,7},{7,5},{8,10},{10,8},{9,1... | collective-permute-start | bytes 4718600 | tf_op jit(solution)/shard_map/ppermute | solution.py:36
  9.4 1.3 %collective-permute-done.1 = bf16[2,1,128,256]{3,2,0,1:T(8,128)(2,1)S(1)} collective-permute-done((bf16[2,1,128,256]{3,2,0,1:T(8,128)(2,1)S(1)}, bf16[2,1,128,256]{3,2,0,1:T(8,128)(2,1)S(1)}, u32[]{:S(2)}, u32[]{:S(2)}) %collective-permute-start.1) | collective-permute-done | bytes 131104 | tf_op jit(solution)/shard_map/ppermute | solution.py:40
  10.9 1.6 %collective-permute-start.2 = (bf16[2,128,512]{2,1,0:T(8,128)(2,1)S(1)}, bf16[2,128,512]{2,1,0:T(8,128)(2,1)S(1)}, u32[]{:S(2)}, u32[]{:S(2)}) collective-permute-start(bf16[2,128,512]{2,1,0:T(8,128)(2,1)S(1)} %maximum_select_fusion.refs_0_), channel_id=1, source_target_pairs={{0,1},{1,0},{2,3},{3,2},{4,5},{5,4},{6,7},{7,6},{8,9},{9,8},{10,11... | collective-permute-start | bytes 786440 | tf_op jit(solution)/shard_map/ppermute | solution.py:36
  12.5 1.6 %collective-permute-start.5 = (bf16[2,128,512]{2,1,0:T(8,128)(2,1)S(1)}, bf16[2,128,512]{2,1,0:T(8,128)(2,1)S(1)}, u32[]{:S(2)}, u32[]{:S(2)}) collective-permute-start(bf16[2,128,512]{2,1,0:T(8,128)(2,1)S(1)} %maximum_select_fusion.refs_0_), channel_id=1, source_target_pairs={{0,8},{4,12},{8,16},{12,20},{16,24},{20,28},{24,0},{28,4},{1,9},{5... | collective-permute-start | bytes 786440 | tf_op jit(solution)/shard_map/ppermute | solution.py:36
  14.1 2.2 %collective-permute-start.7 = (bf16[2,128,512]{2,1,0:T(8,128)(2,1)S(1)}, bf16[2,128,512]{2,1,0:T(8,128)(2,1)S(1)}, u32[]{:S(2)}, u32[]{:S(2)}) collective-permute-start(bf16[2,128,512]{2,1,0:T(8,128)(2,1)S(1)} %maximum_select_fusion.refs_0_), channel_id=1, source_target_pairs={{0,24},{4,28},{8,0},{12,4},{16,8},{20,12},{24,16},{28,20},{1,25},{... | collective-permute-start | bytes 786440 | tf_op jit(solution)/shard_map/ppermute | solution.py:36
  16.3 3.0 %collective-permute-done.2.refs_1_ = bf16[2,128,512]{2,1,0:T(8,128)(2,1)S(1)} collective-permute-done((bf16[2,128,512]{2,1,0:T(8,128)(2,1)S(1)}, bf16[2,128,512]{2,1,0:T(8,128)(2,1)S(1)}, u32[]{:S(2)}, u32[]{:S(2)}) %collective-permute-start.2) | collective-permute-done | bytes 262176 | tf_op jit(solution)/shard_map/ppermute | solution.py:36
  19.3 0.7 copy-done.5
  20.0 2.6 %collective-permute-start.9 = (bf16[2,128,512]{2,1,0:T(8,128)(2,1)S(1)}, bf16[2,128,512]{2,1,0:T(8,128)(2,1)}, u32[]{:S(2)}, u32[]{:S(2)}) collective-permute-start(bf16[2,128,512]{2,1,0:T(8,128)(2,1)S(1)} %maximum_select_fusion.refs_0_), channel_id=1, source_target_pairs={{0,16},{4,20},{8,24},{12,28},{16,0},{20,4},{24,8},{28,12},{1,17},{... | collective-permute-start | bytes 786440 | tf_op jit(solution)/shard_map/ppermute | solution.py:36
  22.6 1.8 %constant_dynamic-slice_fusion.1.refs_0_ = bf16[4,256,1024]{2,1,0:T(8,128)(2,1)S(1)} fusion(bf16[8,256,1024]{2,1,0:T(8,128)(2,1)} %param.2, s32[]{:T(128)S(6)} %select_n.181), kind=kLoop, calls=%fused_computation.63 | loop fusion | bytes 4194308 | tf_op jit(solution)/shard_map/dynamic_slice | solution.py:377
  24.5 1.6 %collective-permute-start.6 = (bf16[2,128,512]{2,1,0:T(8,128)(2,1)S(1)}, bf16[2,128,512]{2,1,0:T(8,128)(2,1)}, u32[]{:S(2)}, u32[]{:S(2)}) collective-permute-start(bf16[2,128,512]{2,1,0:T(8,128)(2,1)S(1)} %collective-permute-done.5.refs_2_), channel_id=1, source_target_pairs={{0,1},{1,0},{2,3},{3,2},{4,5},{5,4},{6,7},{7,6},{8,9},{9,8},{10,11... | collective-permute-start | bytes 786440 | tf_op jit(solution)/shard_map/ppermute | solution.py:36
  26.1 1.4 %collective-permute-done.7.refs_4_ = bf16[2,128,512]{2,1,0:T(8,128)(2,1)S(1)} collective-permute-done((bf16[2,128,512]{2,1,0:T(8,128)(2,1)S(1)}, bf16[2,128,512]{2,1,0:T(8,128)(2,1)S(1)}, u32[]{:S(2)}, u32[]{:S(2)}) %collective-permute-start.7) | collective-permute-done | bytes 262176 | tf_op jit(solution)/shard_map/ppermute | solution.py:36
  27.5 0.5 collective-permute-start.8
  28.0 11.4 %collective-permute-done.9.refs_6_ = bf16[2,128,512]{2,1,0:T(8,128)(2,1)} collective-permute-done((bf16[2,128,512]{2,1,0:T(8,128)(2,1)S(1)}, bf16[2,128,512]{2,1,0:T(8,128)(2,1)}, u32[]{:S(2)}, u32[]{:S(2)}) %collective-permute-start.9) | collective-permute-done | bytes 262176 | tf_op jit(solution)/shard_map/ppermute | solution.py:36
  39.4 0.5 collective-permute-start.10
  39.9 1.9 %constant_dynamic-slice_fusion = bf16[1,256,1024]{2,1,0:T(8,128)(2,1)} fusion(bf16[8,256,1024]{2,1,0:T(8,128)(2,1)} %param.2, s32[]{:T(128)S(6)} %select_n.182), kind=kLoop, calls=%fused_computation.62 | loop fusion | bytes 1048580 | tf_op jit(solution)/shard_map/dynamic_slice | solution.py:337
  41.8 6.1 %collective-permute-done.10.refs_7_ = bf16[2,128,512]{2,1,0:T(8,128)(2,1)S(1)} collective-permute-done((bf16[2,128,512]{2,1,0:T(8,128)(2,1)}, bf16[2,128,512]{2,1,0:T(8,128)(2,1)S(1)}, u32[]{:S(2)}, u32[]{:S(2)}) %collective-permute-start.10) | collective-permute-done | bytes 262176 | tf_op jit(solution)/shard_map/ppermute | solution.py:36
  47.9 0.6 collective-permute-start.11
  48.6 2.0 %assemble.1.refs_4_.refs_2_.refs_3_ = bf16[2,256,2048]{2,1,0:T(8,128)(2,1)S(1)} custom-call(s32[6]{0:T(128)S(1)} %stack.27.at, bf16[2,128,512]{2,1,0:T(8,128)(2,1)} %copy-done.1, bf16[2,128,512]{2,1,0:T(8,128)(2,1)} %copy-done.5, bf16[2,128,512]{2,1,0:T(8,128)(2,1)} %copy-done.6, bf16[2,128,512]{2,1,0:T(8,128)(2,1)} %collective-permute-done.6.refs_3_, ...), custom_call_target="tpu_custom_call" | custom-call | bytes 2097152 | tf_op jit(solution)/shard_map/assemble/pallas_call | solution.py:82
  50.7 1.0 collective-permute-done.12.refs_3_
  51.7 8.4 %early_sums.1.refs_3_ = f32[2,256,2048]{2,1,0:T(8,128)S(1)} custom-call(bf16[4,256,1024]{2,1,0:T(8,128)(2,1)S(1)} %constant_dynamic-slice_fusion.1.refs_0_, bf16[3,256,1024]{2,1,0:T(8,128)(2,1)} %collective-permute-done.4.refs_1_, bf16[4,256,1024]{2,1,0:T(8,128)(2,1)} %collective-permute-done.3.refs_2_.refs_1_, ...), custom_call_target="tpu_custom_call" | custom-call | bytes 2097152 | tf_op jit(solution)/shard_map/early_sums/pallas_call | solution.py:151
  60.1 2.4 %collective-permute-done.11.refs_1_ = bf16[1,256,1024]{2,1,0:T(8,128)(2,1)S(1)} collective-permute-done((bf16[1,256,1024]{2,1,0:T(8,128)(2,1)}, bf16[1,256,1024]{2,1,0:T(8,128)(2,1)S(1)}, u32[]{:S(2)}, u32[]{:S(2)}) %collective-permute-start.11) | collective-permute-done | bytes 524320 | tf_op jit(solution)/shard_map/ppermute | solution.py:36
  62.5 1.6 %own_sums.1.refs_4_ = f32[2,256,2048]{2,1,0:T(8,128)S(1)} custom-call(bf16[4,256,1024]{2,1,0:T(8,128)(2,1)S(1)} %constant_dynamic-slice_fusion.1.refs_0_, bf16[1,256,1024]{2,1,0:T(8,128)(2,1)S(1)} %collective-permute-done.11.refs_1_, bf16[2,256,2048]{2,1,0:T(8,128)(2,1)S(1)} %assemble.1.refs_4_.refs_2_.refs_3_, ...), custom_call_target="tpu_custom_call", output_to_operand_aliasing={{}: (3, {})} | custom-call | bytes 2097152 | tf_op jit(solution)/shard_map/own_sums/pallas_call | solution.py:201
  64.1 0.2 collective-permute-done.13.refs_2_
  64.4 3.9 %last_sums.1 = (bf16[1,2,32,2048]{3,2,1,0:T(8,128)(2,1)}, f32[1,2,32,2048]{3,2,1,0:T(8,128)}, bf16[1,2,32,2048]{3,2,1,0:T(8,128)(2,1)}, f32[2,32,2048]{2,1,0:T(8...) custom-call(s32[1]{0:T(128)} %bitcast.refs_0_, ...), custom_call_target="tpu_custom_call" | custom-call | bytes 3145728 | tf_op jit(solution)/shard_map/last_sums/pallas_call | solution.py:300
  68.3 0.6 collective-permute-start.23
  68.9 0.5 collective-permute-start.21
  69.4 1.5 %collective-permute-start.16 = (bf16[2,32,2048]{2,1,0:T(8,128)(2,1)}, bf16[2,32,2048]{2,1,0:T(8,128)(2,1)S(1)}, u32[]{:S(2)}, u32[]{:S(2)}) collective-permute-start(bf16[2,32,2048]{2,1,0:T(8,128)(2,1)} %bitcast.29), channel_id=1, source_target_pairs={{0,1},{1,0},{2,3},{3,2},{4,5},{5,4},{6,7},{7,6},{8,9},{9,8},{10,11... | collective-permute-start | bytes 786440 | tf_op jit(solution)/shard_map/ppermute | solution.py:36
  70.9 1.5 %collective-permute-start.14 = (bf16[1,2,32,2048]{3,2,1,0:T(8,128)(2,1)}, bf16[1,2,32,2048]{3,2,1,0:T(8,128)(2,1)S(1)}, u32[]{:S(2)}, u32[]{:S(2)}) collective-permute-start(bf16[1,2,32,2048]{3,2,1,0:T(8,128)(2,1)} %get-tuple-element.32), channel_id=1, source_target_pairs={{0,2},{2,0},{1,3},{3,1},{4,6},{6,4},{5,7},{7,5},{8,10},{10,8},{9,1... | collective-permute-start | bytes 786440 | tf_op jit(solution)/shard_map/ppermute | solution.py:36
  72.4 5.3 %collective-permute-done.23 = bf16[2,32,2048]{2,1,0:T(8,128)(2,1)S(1)} collective-permute-done((bf16[2,32,2048]{2,1,0:T(8,128)(2,1)}, bf16[2,32,2048]{2,1,0:T(8,128)(2,1)S(1)}, u32[]{:S(2)}, u32[]{:S(2)}) %collective-permute-start.23) | collective-permute-done | bytes 262176 | tf_op jit(solution)/shard_map/ppermute | solution.py:36
  77.7 1.1 %convert_add_fusion = f32[2,32,2048]{2,1,0:T(8,128)S(1)} fusion(f32[2,32,2048]{2,1,0:T(8,128)} %get-tuple-element.37, bf16[2,32,2048]{2,1,0:T(8,128)(2,1)S(1)} %collective-permute-done.23), kind=kLoop, calls=%fused_computation.16 | loop fusion | flops 262144 | bytes 1310720 | tf_op jit(solution)/shard_map/add | solution.py:404
  78.9 0.6 collective-permute-start.24
  79.6 0.6 collective-permute-start.22
  80.2 3.2 %collective-permute-done.16 = bf16[2,32,2048]{2,1,0:T(8,128)(2,1)S(1)} collective-permute-done((bf16[2,32,2048]{2,1,0:T(8,128)(2,1)}, bf16[2,32,2048]{2,1,0:T(8,128)(2,1)S(1)}, u32[]{:S(2)}, u32[]{:S(2)}) %collective-permute-start.16) | collective-permute-done | bytes 262176 | tf_op jit(solution)/shard_map/ppermute | solution.py:36
  83.4 0.6 collective-permute-start.17
  84.1 1.4 %collective-permute-start.15 = (bf16[1,32,2048]{2,1,0:T(8,128)(2,1)S(1)}, bf16[1,32,2048]{2,1,0:T(8,128)(2,1)S(1)}, u32[]{:S(2)}, u32[]{:S(2)}) collective-permute-start(bf16[1,32,2048]{2,1,0:T(8,128)(2,1)S(1)} %fusion), channel_id=1, source_target_pairs={{0,1},{1,0},{2,3},{3,2},{4,5},{5,4},{6,7},{7,6},{8,9},{9,8},{10,11... | collective-permute-start | bytes 393224 | tf_op jit(solution)/shard_map/ppermute | solution.py:36
  85.6 0.9 collective-permute-done.24
  86.8 2.2 %collective-permute-start.26 = (bf16[1,64,512]{2,1,0:T(8,128)(2,1)S(1)}, bf16[1,64,512]{2,1,0:T(8,128)(2,1)S(1)}, u32[]{:S(2)}, u32[]{:S(2)}) collective-permute-start(bf16[1,64,512]{2,1,0:T(8,128)(2,1)S(1)} %get-tuple-element.40), channel_id=1, source_target_pairs={{0,16},{4,20},{8,24},{12,28},{16,0},{20,4},{24,8},{28,12},{1,17},{... | collective-permute-start | bytes 196616 | tf_op jit(solution)/shard_map/ppermute | solution.py:36
  89.0 2.1 %collective-permute-start.27 = (bf16[1,64,512]{2,1,0:T(8,128)(2,1)S(1)}, bf16[1,64,512]{2,1,0:T(8,128)(2,1)S(1)}, u32[]{:S(2)}, u32[]{:S(2)}) collective-permute-start(bf16[1,64,512]{2,1,0:T(8,128)(2,1)S(1)} %get-tuple-element.41), channel_id=1, source_target_pairs={{0,24},{4,28},{8,0},{12,4},{16,8},{20,12},{24,16},{28,20},{1,25},{... | collective-permute-start | bytes 196616 | tf_op jit(solution)/shard_map/ppermute | solution.py:36
  91.4 1.5 %collective-permute-start.19 = (bf16[1,64,512]{2,1,0:T(8,128)(2,1)S(1)}, bf16[1,64,512]{2,1,0:T(8,128)(2,1)S(1)}, u32[]{:S(2)}, u32[]{:S(2)}) collective-permute-start(bf16[1,64,512]{2,1,0:T(8,128)(2,1)S(1)} %get-tuple-element.43), channel_id=1, source_target_pairs={{0,16},{4,20},{8,24},{12,28},{16,0},{20,4},{24,8},{28,12},{1,17},{... | collective-permute-start | bytes 196616 | tf_op jit(solution)/shard_map/ppermute | solution.py:36
  93.0 2.8 %collective-permute-start.20 = (bf16[1,64,512]{2,1,0:T(8,128)(2,1)S(1)}, bf16[1,64,512]{2,1,0:T(8,128)(2,1)S(1)}, u32[]{:S(2)}, u32[]{:S(2)}) collective-permute-start(bf16[1,64,512]{2,1,0:T(8,128)(2,1)S(1)} %get-tuple-element.44), channel_id=1, source_target_pairs={{0,24},{4,28},{8,0},{12,4},{16,8},{20,12},{24,16},{28,20},{1,25},{... | collective-permute-start | bytes 196616 | tf_op jit(solution)/shard_map/ppermute | solution.py:36
  96.0 1.6 %collective-permute-done.18 = bf16[1,64,512]{2,1,0:T(8,128)(2,1)S(1)} collective-permute-done((bf16[1,64,512]{2,1,0:T(8,128)(2,1)S(1)}, bf16[1,64,512]{2,1,0:T(8,128)(2,1)S(1)}, u32[]{:S(2)}, u32[]{:S(2)}) %collective-permute-start.18) | collective-permute-done | bytes 65568 | tf_op jit(solution)/shard_map/ppermute | solution.py:36
  97.5 1.9 %collective-permute-done.19 = bf16[1,64,512]{2,1,0:T(8,128)(2,1)S(1)} collective-permute-done((bf16[1,64,512]{2,1,0:T(8,128)(2,1)S(1)}, bf16[1,64,512]{2,1,0:T(8,128)(2,1)S(1)}, u32[]{:S(2)}, u32[]{:S(2)}) %collective-permute-start.19) | collective-permute-done | bytes 65568 | tf_op jit(solution)/shard_map/ppermute | solution.py:36
  99.7 1.3 %collective-permute-done.28 = f32[1,128,256]{2,1,0:T(8,128)S(1)} collective-permute-done((f32[1,128,256]{2,1,0:T(8,128)S(1)}, f32[1,128,256]{2,1,0:T(8,128)S(1)}, u32[]{:S(2)}, u32[]{:S(2)}) %collective-permute-start.28) | collective-permute-done | bytes 131104 | tf_op jit(solution)/shard_map/ppermute | solution.py:40
  101.0 0.7 maximum_select_fusion.1
  (56 shorter events, 1.7 us)
Async XLA Ops:
  0.0 1.0 %copy-start = (f32[2,256,256]{2,1,0:T(8,128)S(1)}, f32[2,256,256]{2,1,0:T(8,128)}, u32[]{:S(2)}) copy-start(f32[2,256,256]{2,1,0:T(8,128)} %param.3) | copy-start | bytes 1572868
  1.1 6.5 %collective-permute-start = (bf16[2,128,256]{2,1,0:T(8,128)(2,1)S(1)}, bf16[2,128,256]{2,1,0:T(8,128)(2,1)S(1)}, u32[]{:S(2)}, u32[]{:S(2)}) collective-permute-start(bf16[2,128,256]{2,1,0:T(8,128)(2,1)S(1)} %dynamic-slice_convert_fusion.2), channel_id=1, source_target_pairs={{0,2},{2,0},{1,3},{3,1},{4,6},{6,4},{5,7},{7,5},{8,10},{10,8},{9,1... | collective-permute-start | bytes 393224 | tf_op jit(solution)/shard_map/ppermute | solution.py:36
  7.6 40.3 %collective-permute-start.4 = (bf16[3,256,1024]{2,1,0:T(8,128)(2,1)}, bf16[3,256,1024]{2,1,0:T(8,128)(2,1)}, u32[]{:S(2)}, u32[]{:S(2)}) collective-permute-start(bf16[3,256,1024]{2,1,0:T(8,128)(2,1)} %constant_dynamic-slice_fusion.2), channel_id=1, source_target_pairs={{0,2},{2,0},{1,3},{3,1},{4,6},{6,4},{5,7},{7,5},{8,10},{10,8},{9,1... | collective-permute-start | bytes 4718600 | tf_op jit(solution)/shard_map/ppermute | solution.py:36
  9.4 1.4 %collective-permute-start.1 = (bf16[2,1,128,256]{3,2,0,1:T(8,128)(2,1)S(1)}, bf16[2,1,128,256]{3,2,0,1:T(8,128)(2,1)S(1)}, u32[]{:S(2)}, u32[]{:S(2)}) collective-permute-start(bf16[2,1,128,256]{3,2,0,1:T(8,128)(2,1)S(1)} %get-tuple-element.48), channel_id=1, source_target_pairs={{0,4},{4,0},{8,12},{12,8},{16,20},{20,16},{24,28},{28,24},{1,5},{5... | collective-permute-start | bytes 393224 | tf_op jit(solution)/shard_map/ppermute | solution.py:40
  10.9 13.5 %copy-start.1 = (bf16[2,128,512]{2,1,0:T(8,128)(2,1)}, bf16[2,128,512]{2,1,0:T(8,128)(2,1)S(1)}, u32[]{:S(2)}) copy-start(bf16[2,128,512]{2,1,0:T(8,128)(2,1)S(1)} %maximum_select_fusion.refs_0_) | copy-start | bytes 786436
  10.9 8.4 %collective-permute-start.2 = (bf16[2,128,512]{2,1,0:T(8,128)(2,1)S(1)}, bf16[2,128,512]{2,1,0:T(8,128)(2,1)S(1)}, u32[]{:S(2)}, u32[]{:S(2)}) collective-permute-start(bf16[2,128,512]{2,1,0:T(8,128)(2,1)S(1)} %maximum_select_fusion.refs_0_), channel_id=1, source_target_pairs={{0,1},{1,0},{2,3},{3,2},{4,5},{5,4},{6,7},{7,6},{8,9},{9,8},{10,11... | collective-permute-start | bytes 786440 | tf_op jit(solution)/shard_map/ppermute | solution.py:36
  12.5 12.0 %collective-permute-start.5 = (bf16[2,128,512]{2,1,0:T(8,128)(2,1)S(1)}, bf16[2,128,512]{2,1,0:T(8,128)(2,1)S(1)}, u32[]{:S(2)}, u32[]{:S(2)}) collective-permute-start(bf16[2,128,512]{2,1,0:T(8,128)(2,1)S(1)} %maximum_select_fusion.refs_0_), channel_id=1, source_target_pairs={{0,8},{4,12},{8,16},{12,20},{16,24},{20,28},{24,0},{28,4},{1,9},{5... | collective-permute-start | bytes 786440 | tf_op jit(solution)/shard_map/ppermute | solution.py:36
  14.1 13.4 %collective-permute-start.7 = (bf16[2,128,512]{2,1,0:T(8,128)(2,1)S(1)}, bf16[2,128,512]{2,1,0:T(8,128)(2,1)S(1)}, u32[]{:S(2)}, u32[]{:S(2)}) collective-permute-start(bf16[2,128,512]{2,1,0:T(8,128)(2,1)S(1)} %maximum_select_fusion.refs_0_), channel_id=1, source_target_pairs={{0,24},{4,28},{8,0},{12,4},{16,8},{20,12},{24,16},{28,20},{1,25},{... | collective-permute-start | bytes 786440 | tf_op jit(solution)/shard_map/ppermute | solution.py:36
  19.3 0.7 copy-start.5
  20.0 19.4 %collective-permute-start.9 = (bf16[2,128,512]{2,1,0:T(8,128)(2,1)S(1)}, bf16[2,128,512]{2,1,0:T(8,128)(2,1)}, u32[]{:S(2)}, u32[]{:S(2)}) collective-permute-start(bf16[2,128,512]{2,1,0:T(8,128)(2,1)S(1)} %maximum_select_fusion.refs_0_), channel_id=1, source_target_pairs={{0,16},{4,20},{8,24},{12,28},{16,0},{20,4},{24,8},{28,12},{1,17},{... | collective-permute-start | bytes 786440 | tf_op jit(solution)/shard_map/ppermute | solution.py:36
  24.4 26.3 %collective-permute-start.3 = (bf16[4,256,1024]{2,1,0:T(8,128)(2,1)S(1)}, bf16[4,256,1024]{2,1,0:T(8,128)(2,1)}, u32[]{:S(2)}, u32[]{:S(2)}) collective-permute-start(bf16[4,256,1024]{2,1,0:T(8,128)(2,1)S(1)} %constant_dynamic-slice_fusion.1.refs_0_), channel_id=1, source_target_pairs={{0,4},{4,0},{8,12},{12,8},{16,20},{20,16},{24,28},{28,24},{1,5},{5... | collective-permute-start | bytes 6291464 | tf_op jit(solution)/shard_map/ppermute | solution.py:40
  24.5 23.3 %copy-start.6 = (bf16[2,128,512]{2,1,0:T(8,128)(2,1)}, bf16[2,128,512]{2,1,0:T(8,128)(2,1)S(1)}, u32[]{:S(2)}) copy-start(bf16[2,128,512]{2,1,0:T(8,128)(2,1)S(1)} %collective-permute-done.5.refs_2_) | copy-start | bytes 786436
  24.5 17.3 %collective-permute-start.6 = (bf16[2,128,512]{2,1,0:T(8,128)(2,1)S(1)}, bf16[2,128,512]{2,1,0:T(8,128)(2,1)}, u32[]{:S(2)}, u32[]{:S(2)}) collective-permute-start(bf16[2,128,512]{2,1,0:T(8,128)(2,1)S(1)} %collective-permute-done.5.refs_2_), channel_id=1, source_target_pairs={{0,1},{1,0},{2,3},{3,2},{4,5},{5,4},{6,7},{7,6},{8,9},{9,8},{10,11... | collective-permute-start | bytes 786440 | tf_op jit(solution)/shard_map/ppermute | solution.py:36
  27.5 20.3 %copy-start.7 = (bf16[2,128,512]{2,1,0:T(8,128)(2,1)}, bf16[2,128,512]{2,1,0:T(8,128)(2,1)S(1)}, u32[]{:S(2)}) copy-start(bf16[2,128,512]{2,1,0:T(8,128)(2,1)S(1)} %collective-permute-done.7.refs_4_) | copy-start | bytes 786436
  27.5 14.3 %collective-permute-start.8 = (bf16[2,128,512]{2,1,0:T(8,128)(2,1)S(1)}, bf16[2,128,512]{2,1,0:T(8,128)(2,1)}, u32[]{:S(2)}, u32[]{:S(2)}) collective-permute-start(bf16[2,128,512]{2,1,0:T(8,128)(2,1)S(1)} %collective-permute-done.7.refs_4_), channel_id=1, source_target_pairs={{0,1},{1,0},{2,3},{3,2},{4,5},{5,4},{6,7},{7,6},{8,9},{9,8},{10,11... | collective-permute-start | bytes 786440 | tf_op jit(solution)/shard_map/ppermute | solution.py:36
  39.4 8.4 %collective-permute-start.10 = (bf16[2,128,512]{2,1,0:T(8,128)(2,1)}, bf16[2,128,512]{2,1,0:T(8,128)(2,1)S(1)}, u32[]{:S(2)}, u32[]{:S(2)}) collective-permute-start(bf16[2,128,512]{2,1,0:T(8,128)(2,1)} %collective-permute-done.9.refs_6_), channel_id=1, source_target_pairs={{0,1},{1,0},{2,3},{3,2},{4,5},{5,4},{6,7},{7,6},{8,9},{9,8},{10,11... | collective-permute-start | bytes 786440 | tf_op jit(solution)/shard_map/ppermute | solution.py:36
  47.8 3.8 %collective-permute-start.12 = (bf16[3,256,1024]{2,1,0:T(8,128)(2,1)}, bf16[3,256,1024]{2,1,0:T(8,128)(2,1)}, u32[]{:S(2)}, u32[]{:S(2)}) collective-permute-start(bf16[3,256,1024]{2,1,0:T(8,128)(2,1)} %collective-permute-done.4.refs_1_), channel_id=1, source_target_pairs={{0,4},{4,0},{8,12},{12,8},{16,20},{20,16},{24,28},{28,24},{1,5},{5... | collective-permute-start | bytes 4718600 | tf_op jit(solution)/shard_map/ppermute | solution.py:40
  47.9 14.5 %collective-permute-start.11 = (bf16[1,256,1024]{2,1,0:T(8,128)(2,1)}, bf16[1,256,1024]{2,1,0:T(8,128)(2,1)S(1)}, u32[]{:S(2)}, u32[]{:S(2)}) collective-permute-start(bf16[1,256,1024]{2,1,0:T(8,128)(2,1)} %constant_dynamic-slice_fusion), channel_id=1, source_target_pairs={{0,2},{2,0},{1,3},{3,1},{4,6},{6,4},{5,7},{7,5},{8,10},{10,8},{9,1... | collective-permute-start | bytes 1572872 | tf_op jit(solution)/shard_map/ppermute | solution.py:36
  62.5 1.9 %collective-permute-start.13 = (bf16[1,256,1024]{2,1,0:T(8,128)(2,1)S(1)}, bf16[1,256,1024]{2,1,0:T(8,128)(2,1)S(1)}, u32[]{:S(2)}, u32[]{:S(2)}) collective-permute-start(bf16[1,256,1024]{2,1,0:T(8,128)(2,1)S(1)} %collective-permute-done.11.refs_1_), channel_id=1, source_target_pairs={{0,4},{4,0},{8,12},{12,8},{16,20},{20,16},{24,28},{28,24},{1,5},{5... | collective-permute-start | bytes 1572872 | tf_op jit(solution)/shard_map/ppermute | solution.py:40
  68.3 11.2 %copy-start.4 = (f32[1,2,32,2048]{3,2,1,0:T(8,128)S(1)}, f32[1,2,32,2048]{3,2,1,0:T(8,128)}, u32[]{:S(2)}) copy-start(f32[1,2,32,2048]{3,2,1,0:T(8,128)} %get-tuple-element.35) | copy-start | bytes 1572868
  68.3 15.0 %copy-start.3 = (f32[2,32,2048]{2,1,0:T(8,128)S(1)}, f32[2,32,2048]{2,1,0:T(8,128)}, u32[]{:S(2)}) copy-start(f32[2,32,2048]{2,1,0:T(8,128)} %get-tuple-element.33) | copy-start | bytes 1572868
  68.3 9.4 %collective-permute-start.23 = (bf16[2,32,2048]{2,1,0:T(8,128)(2,1)}, bf16[2,32,2048]{2,1,0:T(8,128)(2,1)S(1)}, u32[]{:S(2)}, u32[]{:S(2)}) collective-permute-start(bf16[2,32,2048]{2,1,0:T(8,128)(2,1)} %bitcast.30), channel_id=1, source_target_pairs={{0,1},{1,0},{2,3},{3,2},{4,5},{5,4},{6,7},{7,6},{8,9},{9,8},{10,11... | collective-permute-start | bytes 786440 | tf_op jit(solution)/shard_map/ppermute | solution.py:36
  68.9 10.6 %collective-permute-start.21 = (bf16[1,2,32,2048]{3,2,1,0:T(8,128)(2,1)}, bf16[1,2,32,2048]{3,2,1,0:T(8,128)(2,1)S(1)}, u32[]{:S(2)}, u32[]{:S(2)}) collective-permute-start(bf16[1,2,32,2048]{3,2,1,0:T(8,128)(2,1)} %get-tuple-element.36), channel_id=1, source_target_pairs={{0,2},{2,0},{1,3},{3,1},{4,6},{6,4},{5,7},{7,5},{8,10},{10,8},{9,1... | collective-permute-start | bytes 786440 | tf_op jit(solution)/shard_map/ppermute | solution.py:36
  69.4 13.9 %collective-permute-start.16 = (bf16[2,32,2048]{2,1,0:T(8,128)(2,1)}, bf16[2,32,2048]{2,1,0:T(8,128)(2,1)S(1)}, u32[]{:S(2)}, u32[]{:S(2)}) collective-permute-start(bf16[2,32,2048]{2,1,0:T(8,128)(2,1)} %bitcast.29), channel_id=1, source_target_pairs={{0,1},{1,0},{2,3},{3,2},{4,5},{5,4},{6,7},{7,6},{8,9},{9,8},{10,11... | collective-permute-start | bytes 786440 | tf_op jit(solution)/shard_map/ppermute | solution.py:36
  70.9 13.1 %collective-permute-start.14 = (bf16[1,2,32,2048]{3,2,1,0:T(8,128)(2,1)}, bf16[1,2,32,2048]{3,2,1,0:T(8,128)(2,1)S(1)}, u32[]{:S(2)}, u32[]{:S(2)}) collective-permute-start(bf16[1,2,32,2048]{3,2,1,0:T(8,128)(2,1)} %get-tuple-element.32), channel_id=1, source_target_pairs={{0,2},{2,0},{1,3},{3,1},{4,6},{6,4},{5,7},{7,5},{8,10},{10,8},{9,1... | collective-permute-start | bytes 786440 | tf_op jit(solution)/shard_map/ppermute | solution.py:36
  77.7 6.3 %copy-start.2 = (f32[1,2,32,2048]{3,2,1,0:T(8,128)S(1)}, f32[1,2,32,2048]{3,2,1,0:T(8,128)}, u32[]{:S(2)}) copy-start(f32[1,2,32,2048]{3,2,1,0:T(8,128)} %get-tuple-element.31) | copy-start | bytes 1572868
  78.9 7.6 %collective-permute-start.24 = (bf16[1,32,2048]{2,1,0:T(8,128)(2,1)S(1)}, bf16[1,32,2048]{2,1,0:T(8,128)(2,1)S(1)}, u32[]{:S(2)}, u32[]{:S(2)}) collective-permute-start(bf16[1,32,2048]{2,1,0:T(8,128)(2,1)S(1)} %slice.26), channel_id=1, source_target_pairs={{0,2},{2,0},{1,3},{3,1},{4,6},{6,4},{5,7},{7,5},{8,10},{10,8},{9,1... | collective-permute-start | bytes 393224 | tf_op jit(solution)/shard_map/ppermute | solution.py:36
  79.6 6.9 %collective-permute-start.22 = (bf16[1,32,2048]{2,1,0:T(8,128)(2,1)S(1)}, bf16[1,32,2048]{2,1,0:T(8,128)(2,1)S(1)}, u32[]{:S(2)}, u32[]{:S(2)}) collective-permute-start(bf16[1,32,2048]{2,1,0:T(8,128)(2,1)S(1)} %fusion.1), channel_id=1, source_target_pairs={{0,1},{1,0},{2,3},{3,2},{4,5},{5,4},{6,7},{7,6},{8,9},{9,8},{10,11... | collective-permute-start | bytes 393224 | tf_op jit(solution)/shard_map/ppermute | solution.py:36
  83.4 7.6 %collective-permute-start.17 = (bf16[1,32,2048]{2,1,0:T(8,128)(2,1)S(1)}, bf16[1,32,2048]{2,1,0:T(8,128)(2,1)S(1)}, u32[]{:S(2)}, u32[]{:S(2)}) collective-permute-start(bf16[1,32,2048]{2,1,0:T(8,128)(2,1)S(1)} %slice.27), channel_id=1, source_target_pairs={{0,2},{2,0},{1,3},{3,1},{4,6},{6,4},{5,7},{7,5},{8,10},{10,8},{9,1... | collective-permute-start | bytes 393224 | tf_op jit(solution)/shard_map/ppermute | solution.py:36
  84.1 7.0 %collective-permute-start.15 = (bf16[1,32,2048]{2,1,0:T(8,128)(2,1)S(1)}, bf16[1,32,2048]{2,1,0:T(8,128)(2,1)S(1)}, u32[]{:S(2)}, u32[]{:S(2)}) collective-permute-start(bf16[1,32,2048]{2,1,0:T(8,128)(2,1)S(1)} %fusion), channel_id=1, source_target_pairs={{0,1},{1,0},{2,3},{3,2},{4,5},{5,4},{6,7},{7,6},{8,9},{9,8},{10,11... | collective-permute-start | bytes 393224 | tf_op jit(solution)/shard_map/ppermute | solution.py:36
  86.7 6.3 %collective-permute-start.25 = (bf16[1,64,512]{2,1,0:T(8,128)(2,1)S(1)}, bf16[1,64,512]{2,1,0:T(8,128)(2,1)S(1)}, u32[]{:S(2)}, u32[]{:S(2)}) collective-permute-start(bf16[1,64,512]{2,1,0:T(8,128)(2,1)S(1)} %get-tuple-element.39), channel_id=1, source_target_pairs={{0,8},{4,12},{8,16},{12,20},{16,24},{20,28},{24,0},{28,4},{1,9},{5... | collective-permute-start | bytes 196616 | tf_op jit(solution)/shard_map/ppermute | solution.py:36
  86.8 9.0 %collective-permute-start.26 = (bf16[1,64,512]{2,1,0:T(8,128)(2,1)S(1)}, bf16[1,64,512]{2,1,0:T(8,128)(2,1)S(1)}, u32[]{:S(2)}, u32[]{:S(2)}) collective-permute-start(bf16[1,64,512]{2,1,0:T(8,128)(2,1)S(1)} %get-tuple-element.40), channel_id=1, source_target_pairs={{0,16},{4,20},{8,24},{12,28},{16,0},{20,4},{24,8},{28,12},{1,17},{... | collective-permute-start | bytes 196616 | tf_op jit(solution)/shard_map/ppermute | solution.py:36
  89.0 6.8 %collective-permute-start.27 = (bf16[1,64,512]{2,1,0:T(8,128)(2,1)S(1)}, bf16[1,64,512]{2,1,0:T(8,128)(2,1)S(1)}, u32[]{:S(2)}, u32[]{:S(2)}) collective-permute-start(bf16[1,64,512]{2,1,0:T(8,128)(2,1)S(1)} %get-tuple-element.41), channel_id=1, source_target_pairs={{0,24},{4,28},{8,0},{12,4},{16,8},{20,12},{24,16},{28,20},{1,25},{... | collective-permute-start | bytes 196616 | tf_op jit(solution)/shard_map/ppermute | solution.py:36
  91.3 6.2 %collective-permute-start.18 = (bf16[1,64,512]{2,1,0:T(8,128)(2,1)S(1)}, bf16[1,64,512]{2,1,0:T(8,128)(2,1)S(1)}, u32[]{:S(2)}, u32[]{:S(2)}) collective-permute-start(bf16[1,64,512]{2,1,0:T(8,128)(2,1)S(1)} %get-tuple-element.42), channel_id=1, source_target_pairs={{0,8},{4,12},{8,16},{12,20},{16,24},{20,28},{24,0},{28,4},{1,9},{5... | collective-permute-start | bytes 196616 | tf_op jit(solution)/shard_map/ppermute | solution.py:36
  91.4 8.0 %collective-permute-start.19 = (bf16[1,64,512]{2,1,0:T(8,128)(2,1)S(1)}, bf16[1,64,512]{2,1,0:T(8,128)(2,1)S(1)}, u32[]{:S(2)}, u32[]{:S(2)}) collective-permute-start(bf16[1,64,512]{2,1,0:T(8,128)(2,1)S(1)} %get-tuple-element.43), channel_id=1, source_target_pairs={{0,16},{4,20},{8,24},{12,28},{16,0},{20,4},{24,8},{28,12},{1,17},{... | collective-permute-start | bytes 196616 | tf_op jit(solution)/shard_map/ppermute | solution.py:36
  93.0 6.5 %collective-permute-start.20 = (bf16[1,64,512]{2,1,0:T(8,128)(2,1)S(1)}, bf16[1,64,512]{2,1,0:T(8,128)(2,1)S(1)}, u32[]{:S(2)}, u32[]{:S(2)}) collective-permute-start(bf16[1,64,512]{2,1,0:T(8,128)(2,1)S(1)} %get-tuple-element.44), channel_id=1, source_target_pairs={{0,24},{4,28},{8,0},{12,4},{16,8},{20,12},{24,16},{28,20},{1,25},{... | collective-permute-start | bytes 196616 | tf_op jit(solution)/shard_map/ppermute | solution.py:36
  99.6 1.4 %collective-permute-start.28 = (f32[1,128,256]{2,1,0:T(8,128)S(1)}, f32[1,128,256]{2,1,0:T(8,128)S(1)}, u32[]{:S(2)}, u32[]{:S(2)}) collective-permute-start(f32[1,128,256]{2,1,0:T(8,128)S(1)} %get-tuple-element.46), channel_id=1, source_target_pairs={{0,4},{4,0},{8,12},{12,8},{16,20},{20,16},{24,28},{28,24},{1,5},{5... | collective-permute-start | bytes 393224 | tf_op jit(solution)/shard_map/ppermute | solution.py:40

commit v13 on v12

--- a/solution.py
+++ b/solution.py
@@ -412,7 +412,7 @@
             return lax.dynamic_slice_in_dim(u, (zz * block - v * width) % total, block, 2)
 
         got = to(z)
-        for t in range(1, nz):
+        for t in sorted(range(1, nz), key=lambda t: -min(t, nz - t)):
             got += shift(to((z + t) % nz).astype(BF16), "aux", na, t, CORES).astype(F32)
         out.append(got)
     done = jnp.concatenate(out, axis=1)

time: 102 us -> 102 us (level)
  waiting for transfers between devices: 41.9 us -> 43.4 us
  starting transfers between devices: 32.4 us -> 31 us
    ppermute x24, waiting for transfers between devices: 38 us -> 39.5 us  [shift(): return lax.ppermute(array, axis, pairs)]
    ppermute x24, starting transfers between devices: 32.1 us -> 30.7 us  [shift(): return lax.ppermute(array, axis, pairs)]
  transfers between devices with their start and end apart: 29 -> 29, of which waited for: 15 -> 16; matrix products, arithmetic and copies ran while one was open for 8% -> 8% of each run, Pallas kernels for 12% -> 12%
where the time goes in v13:
time: 102 us
  waiting for transfers between devices  43.4 us (43%)
  starting transfers between devices  31 us (30%)
  Pallas kernels  16 us (16%)
  local copies, waits for them, and re-layouts  8.29 us (8%)
  other arithmetic  2.81 us (3%)
    ppermute x24, waiting for transfers between devices, shift(): return lax.ppermute(array, axis, pairs)  39.5 us
    ppermute x24, starting transfers between devices, shift(): return lax.ppermute(array, axis, pairs)  30.7 us
    pallas_call x1, Pallas kernels, early_sums(): pl.pallas_call(body, out_shape=shape, in_specs=[ANY] * n + [VMEM], out_sp...  8.44 us
    dynamic_slice x2, local copies, waits for them, and re-layouts, sends(): lax.dynamic_slice_in_dim(source, (v - r) % nv * take + first, size, 0)  4.56 us
    ppermute x5, waiting for transfers between devices, sibling(): return lax.ppermute(array, 'aux', [(i, i ^ 1) for i in range(size)])  3.9 us
    pallas_call x1, Pallas kernels, last_sums(): pl.pallas_call(body, out_shape=[pltpu.HBM(x.shape, x.dtype) for x in shap...  3.9 us
    pallas_call x1, Pallas kernels, assemble(): pl.pallas_call(body, out_shape=shape, in_specs=[SMEM] + [ANY] * len(block...  2.05 us
  transfers between devices with their start and end apart: 29, of which 16 were waited for; matrix products, arithmetic and copies ran while one was open for 8% of the time, Pallas kernels for 12%

profile of v13, /device:TPU:0, one launch (start us, length us, event | category | flops | bytes accessed | tf_op | source)
XLA Modules:
  0.0 101.9 jit_solution(10145964811102013676)
XLA Ops:
  0.0 1.0 %copy-done = f32[2,256,256]{2,1,0:T(8,128)S(1)} copy-done((f32[2,256,256]{2,1,0:T(8,128)S(1)}, f32[2,256,256]{2,1,0:T(8,128)}, u32[]{:S(2)}) %copy-start) | copy-done | bytes 524312
  1.1 3.0 %collective-permute-start = (bf16[2,128,256]{2,1,0:T(8,128)(2,1)S(1)}, bf16[2,128,256]{2,1,0:T(8,128)(2,1)S(1)}, u32[]{:S(2)}, u32[]{:S(2)}) collective-permute-start(bf16[2,128,256]{2,1,0:T(8,128)(2,1)S(1)} %dynamic-slice_convert_fusion.2), channel_id=1, source_target_pairs={{0,2},{2,0},{1,3},{3,1},{4,6},{6,4},{5,7},{7,5},{8,10},{10,8},{9,1... | collective-permute-start | bytes 393224 | tf_op jit(solution)/shard_map/ppermute | solution.py:36
  4.1 2.7 %constant_dynamic-slice_fusion.2 = bf16[3,256,1024]{2,1,0:T(8,128)(2,1)} fusion(bf16[8,256,1024]{2,1,0:T(8,128)(2,1)} %param.2, s32[]{:T(128)S(6)} %select_n.177), kind=kLoop, calls=%fused_computation.64 | loop fusion | bytes 3145732 | tf_op jit(solution)/shard_map/dynamic_slice | solution.py:337
  6.8 0.8 collective-permute-done
  7.6 1.7 %collective-permute-start.4 = (bf16[3,256,1024]{2,1,0:T(8,128)(2,1)}, bf16[3,256,1024]{2,1,0:T(8,128)(2,1)}, u32[]{:S(2)}, u32[]{:S(2)}) collective-permute-start(bf16[3,256,1024]{2,1,0:T(8,128)(2,1)} %constant_dynamic-slice_fusion.2), channel_id=1, source_target_pairs={{0,2},{2,0},{1,3},{3,1},{4,6},{6,4},{5,7},{7,5},{8,10},{10,8},{9,1... | collective-permute-start | bytes 4718600 | tf_op jit(solution)/shard_map/ppermute | solution.py:36
  9.4 1.3 %collective-permute-done.1 = bf16[2,1,128,256]{3,2,0,1:T(8,128)(2,1)S(1)} collective-permute-done((bf16[2,1,128,256]{3,2,0,1:T(8,128)(2,1)S(1)}, bf16[2,1,128,256]{3,2,0,1:T(8,128)(2,1)S(1)}, u32[]{:S(2)}, u32[]{:S(2)}) %collective-permute-start.1) | collective-permute-done | bytes 131104 | tf_op jit(solution)/shard_map/ppermute | solution.py:40
  10.9 1.6 %collective-permute-start.2 = (bf16[2,128,512]{2,1,0:T(8,128)(2,1)S(1)}, bf16[2,128,512]{2,1,0:T(8,128)(2,1)S(1)}, u32[]{:S(2)}, u32[]{:S(2)}) collective-permute-start(bf16[2,128,512]{2,1,0:T(8,128)(2,1)S(1)} %maximum_select_fusion.refs_0_), channel_id=1, source_target_pairs={{0,1},{1,0},{2,3},{3,2},{4,5},{5,4},{6,7},{7,6},{8,9},{9,8},{10,11... | collective-permute-start | bytes 786440 | tf_op jit(solution)/shard_map/ppermute | solution.py:36
  12.5 1.6 %collective-permute-start.5 = (bf16[2,128,512]{2,1,0:T(8,128)(2,1)S(1)}, bf16[2,128,512]{2,1,0:T(8,128)(2,1)S(1)}, u32[]{:S(2)}, u32[]{:S(2)}) collective-permute-start(bf16[2,128,512]{2,1,0:T(8,128)(2,1)S(1)} %maximum_select_fusion.refs_0_), channel_id=1, source_target_pairs={{0,8},{4,12},{8,16},{12,20},{16,24},{20,28},{24,0},{28,4},{1,9},{5... | collective-permute-start | bytes 786440 | tf_op jit(solution)/shard_map/ppermute | solution.py:36
  14.1 2.2 %collective-permute-start.7 = (bf16[2,128,512]{2,1,0:T(8,128)(2,1)S(1)}, bf16[2,128,512]{2,1,0:T(8,128)(2,1)S(1)}, u32[]{:S(2)}, u32[]{:S(2)}) collective-permute-start(bf16[2,128,512]{2,1,0:T(8,128)(2,1)S(1)} %maximum_select_fusion.refs_0_), channel_id=1, source_target_pairs={{0,24},{4,28},{8,0},{12,4},{16,8},{20,12},{24,16},{28,20},{1,25},{... | collective-permute-start | bytes 786440 | tf_op jit(solution)/shard_map/ppermute | solution.py:36
  16.3 3.0 %collective-permute-done.2.refs_1_ = bf16[2,128,512]{2,1,0:T(8,128)(2,1)S(1)} collective-permute-done((bf16[2,128,512]{2,1,0:T(8,128)(2,1)S(1)}, bf16[2,128,512]{2,1,0:T(8,128)(2,1)S(1)}, u32[]{:S(2)}, u32[]{:S(2)}) %collective-permute-start.2) | collective-permute-done | bytes 262176 | tf_op jit(solution)/shard_map/ppermute | solution.py:36
  19.3 0.7 copy-done.5
  20.0 2.6 %collective-permute-start.9 = (bf16[2,128,512]{2,1,0:T(8,128)(2,1)S(1)}, bf16[2,128,512]{2,1,0:T(8,128)(2,1)}, u32[]{:S(2)}, u32[]{:S(2)}) collective-permute-start(bf16[2,128,512]{2,1,0:T(8,128)(2,1)S(1)} %maximum_select_fusion.refs_0_), channel_id=1, source_target_pairs={{0,16},{4,20},{8,24},{12,28},{16,0},{20,4},{24,8},{28,12},{1,17},{... | collective-permute-start | bytes 786440 | tf_op jit(solution)/shard_map/ppermute | solution.py:36
  22.6 1.8 %constant_dynamic-slice_fusion.1.refs_0_ = bf16[4,256,1024]{2,1,0:T(8,128)(2,1)S(1)} fusion(bf16[8,256,1024]{2,1,0:T(8,128)(2,1)} %param.2, s32[]{:T(128)S(6)} %select_n.181), kind=kLoop, calls=%fused_computation.63 | loop fusion | bytes 4194308 | tf_op jit(solution)/shard_map/dynamic_slice | solution.py:377
  24.5 1.6 %collective-permute-start.6 = (bf16[2,128,512]{2,1,0:T(8,128)(2,1)S(1)}, bf16[2,128,512]{2,1,0:T(8,128)(2,1)}, u32[]{:S(2)}, u32[]{:S(2)}) collective-permute-start(bf16[2,128,512]{2,1,0:T(8,128)(2,1)S(1)} %collective-permute-done.5.refs_2_), channel_id=1, source_target_pairs={{0,1},{1,0},{2,3},{3,2},{4,5},{5,4},{6,7},{7,6},{8,9},{9,8},{10,11... | collective-permute-start | bytes 786440 | tf_op jit(solution)/shard_map/ppermute | solution.py:36
  26.1 1.4 %collective-permute-done.7.refs_4_ = bf16[2,128,512]{2,1,0:T(8,128)(2,1)S(1)} collective-permute-done((bf16[2,128,512]{2,1,0:T(8,128)(2,1)S(1)}, bf16[2,128,512]{2,1,0:T(8,128)(2,1)S(1)}, u32[]{:S(2)}, u32[]{:S(2)}) %collective-permute-start.7) | collective-permute-done | bytes 262176 | tf_op jit(solution)/shard_map/ppermute | solution.py:36
  27.5 0.5 collective-permute-start.8
  28.0 11.4 %collective-permute-done.9.refs_6_ = bf16[2,128,512]{2,1,0:T(8,128)(2,1)} collective-permute-done((bf16[2,128,512]{2,1,0:T(8,128)(2,1)S(1)}, bf16[2,128,512]{2,1,0:T(8,128)(2,1)}, u32[]{:S(2)}, u32[]{:S(2)}) %collective-permute-start.9) | collective-permute-done | bytes 262176 | tf_op jit(solution)/shard_map/ppermute | solution.py:36
  39.4 0.5 collective-permute-start.10
  39.9 1.9 %constant_dynamic-slice_fusion = bf16[1,256,1024]{2,1,0:T(8,128)(2,1)} fusion(bf16[8,256,1024]{2,1,0:T(8,128)(2,1)} %param.2, s32[]{:T(128)S(6)} %select_n.182), kind=kLoop, calls=%fused_computation.62 | loop fusion | bytes 1048580 | tf_op jit(solution)/shard_map/dynamic_slice | solution.py:337
  41.8 6.1 %collective-permute-done.10.refs_7_ = bf16[2,128,512]{2,1,0:T(8,128)(2,1)S(1)} collective-permute-done((bf16[2,128,512]{2,1,0:T(8,128)(2,1)}, bf16[2,128,512]{2,1,0:T(8,128)(2,1)S(1)}, u32[]{:S(2)}, u32[]{:S(2)}) %collective-permute-start.10) | collective-permute-done | bytes 262176 | tf_op jit(solution)/shard_map/ppermute | solution.py:36
  47.9 0.6 collective-permute-start.11
  48.6 2.0 %assemble.1.refs_4_.refs_2_.refs_3_ = bf16[2,256,2048]{2,1,0:T(8,128)(2,1)S(1)} custom-call(s32[6]{0:T(128)S(1)} %stack.27.at, bf16[2,128,512]{2,1,0:T(8,128)(2,1)} %copy-done.1, bf16[2,128,512]{2,1,0:T(8,128)(2,1)} %copy-done.5, bf16[2,128,512]{2,1,0:T(8,128)(2,1)} %copy-done.6, bf16[2,128,512]{2,1,0:T(8,128)(2,1)} %collective-permute-done.6.refs_3_, ...), custom_call_target="tpu_custom_call" | custom-call | bytes 2097152 | tf_op jit(solution)/shard_map/assemble/pallas_call | solution.py:82
  50.7 1.0 collective-permute-done.12.refs_3_
  51.7 8.4 %early_sums.1.refs_3_ = f32[2,256,2048]{2,1,0:T(8,128)S(1)} custom-call(bf16[4,256,1024]{2,1,0:T(8,128)(2,1)S(1)} %constant_dynamic-slice_fusion.1.refs_0_, bf16[3,256,1024]{2,1,0:T(8,128)(2,1)} %collective-permute-done.4.refs_1_, bf16[4,256,1024]{2,1,0:T(8,128)(2,1)} %collective-permute-done.3.refs_2_.refs_1_, ...), custom_call_target="tpu_custom_call" | custom-call | bytes 2097152 | tf_op jit(solution)/shard_map/early_sums/pallas_call | solution.py:151
  60.1 2.4 %collective-permute-done.11.refs_1_ = bf16[1,256,1024]{2,1,0:T(8,128)(2,1)S(1)} collective-permute-done((bf16[1,256,1024]{2,1,0:T(8,128)(2,1)}, bf16[1,256,1024]{2,1,0:T(8,128)(2,1)S(1)}, u32[]{:S(2)}, u32[]{:S(2)}) %collective-permute-start.11) | collective-permute-done | bytes 524320 | tf_op jit(solution)/shard_map/ppermute | solution.py:36
  62.5 1.6 %own_sums.1.refs_4_ = f32[2,256,2048]{2,1,0:T(8,128)S(1)} custom-call(bf16[4,256,1024]{2,1,0:T(8,128)(2,1)S(1)} %constant_dynamic-slice_fusion.1.refs_0_, bf16[1,256,1024]{2,1,0:T(8,128)(2,1)S(1)} %collective-permute-done.11.refs_1_, bf16[2,256,2048]{2,1,0:T(8,128)(2,1)S(1)} %assemble.1.refs_4_.refs_2_.refs_3_, ...), custom_call_target="tpu_custom_call", output_to_operand_aliasing={{}: (3, {})} | custom-call | bytes 2097152 | tf_op jit(solution)/shard_map/own_sums/pallas_call | solution.py:201
  64.4 3.9 %last_sums.1 = (bf16[1,2,32,2048]{3,2,1,0:T(8,128)(2,1)}, f32[1,2,32,2048]{3,2,1,0:T(8,128)}, bf16[1,2,32,2048]{3,2,1,0:T(8,128)(2,1)}, f32[2,32,2048]{2,1,0:T(8...) custom-call(s32[1]{0:T(128)} %bitcast.refs_0_, ...), custom_call_target="tpu_custom_call" | custom-call | bytes 3145728 | tf_op jit(solution)/shard_map/last_sums/pallas_call | solution.py:300
  68.3 0.6 collective-permute-start.23
  68.9 0.5 collective-permute-start.21
  69.4 1.5 %collective-permute-start.16 = (bf16[2,32,2048]{2,1,0:T(8,128)(2,1)}, bf16[2,32,2048]{2,1,0:T(8,128)(2,1)S(1)}, u32[]{:S(2)}, u32[]{:S(2)}) collective-permute-start(bf16[2,32,2048]{2,1,0:T(8,128)(2,1)} %bitcast.29), channel_id=1, source_target_pairs={{0,1},{1,0},{2,3},{3,2},{4,5},{5,4},{6,7},{7,6},{8,9},{9,8},{10,11... | collective-permute-start | bytes 786440 | tf_op jit(solution)/shard_map/ppermute | solution.py:36
  70.9 1.5 %collective-permute-start.14 = (bf16[1,2,32,2048]{3,2,1,0:T(8,128)(2,1)}, bf16[1,2,32,2048]{3,2,1,0:T(8,128)(2,1)S(1)}, u32[]{:S(2)}, u32[]{:S(2)}) collective-permute-start(bf16[1,2,32,2048]{3,2,1,0:T(8,128)(2,1)} %get-tuple-element.32), channel_id=1, source_target_pairs={{0,2},{2,0},{1,3},{3,1},{4,6},{6,4},{5,7},{7,5},{8,10},{10,8},{9,1... | collective-permute-start | bytes 786440 | tf_op jit(solution)/shard_map/ppermute | solution.py:36
  72.4 5.3 %collective-permute-done.23 = bf16[2,32,2048]{2,1,0:T(8,128)(2,1)S(1)} collective-permute-done((bf16[2,32,2048]{2,1,0:T(8,128)(2,1)}, bf16[2,32,2048]{2,1,0:T(8,128)(2,1)S(1)}, u32[]{:S(2)}, u32[]{:S(2)}) %collective-permute-start.23) | collective-permute-done | bytes 262176 | tf_op jit(solution)/shard_map/ppermute | solution.py:36
  77.7 1.1 %convert_add_fusion = f32[2,32,2048]{2,1,0:T(8,128)S(1)} fusion(f32[2,32,2048]{2,1,0:T(8,128)} %get-tuple-element.37, bf16[2,32,2048]{2,1,0:T(8,128)(2,1)S(1)} %collective-permute-done.23), kind=kLoop, calls=%fused_computation.16 | loop fusion | flops 262144 | bytes 1310720 | tf_op jit(solution)/shard_map/add | solution.py:404
  78.9 0.6 collective-permute-start.24
  79.6 0.6 collective-permute-start.22
  80.2 3.2 %collective-permute-done.16 = bf16[2,32,2048]{2,1,0:T(8,128)(2,1)S(1)} collective-permute-done((bf16[2,32,2048]{2,1,0:T(8,128)(2,1)}, bf16[2,32,2048]{2,1,0:T(8,128)(2,1)S(1)}, u32[]{:S(2)}, u32[]{:S(2)}) %collective-permute-start.16) | collective-permute-done | bytes 262176 | tf_op jit(solution)/shard_map/ppermute | solution.py:36
  83.4 0.6 collective-permute-start.17
  84.1 1.4 %collective-permute-start.15 = (bf16[1,32,2048]{2,1,0:T(8,128)(2,1)S(1)}, bf16[1,32,2048]{2,1,0:T(8,128)(2,1)S(1)}, u32[]{:S(2)}, u32[]{:S(2)}) collective-permute-start(bf16[1,32,2048]{2,1,0:T(8,128)(2,1)S(1)} %fusion), channel_id=1, source_target_pairs={{0,1},{1,0},{2,3},{3,2},{4,5},{5,4},{6,7},{7,6},{8,9},{9,8},{10,11... | collective-permute-start | bytes 393224 | tf_op jit(solution)/shard_map/ppermute | solution.py:36
  85.6 0.9 collective-permute-done.24
  86.7 1.4 %collective-permute-start.25 = (bf16[1,64,512]{2,1,0:T(8,128)(2,1)S(1)}, bf16[1,64,512]{2,1,0:T(8,128)(2,1)S(1)}, u32[]{:S(2)}, u32[]{:S(2)}) collective-permute-start(bf16[1,64,512]{2,1,0:T(8,128)(2,1)S(1)} %get-tuple-element.39), channel_id=1, source_target_pairs={{0,16},{4,20},{8,24},{12,28},{16,0},{20,4},{24,8},{28,12},{1,17},{... | collective-permute-start | bytes 196616 | tf_op jit(solution)/shard_map/ppermute | solution.py:36
  88.2 0.9 collective-permute-start.26
  89.0 3.0 %collective-permute-start.27 = (bf16[1,64,512]{2,1,0:T(8,128)(2,1)S(1)}, bf16[1,64,512]{2,1,0:T(8,128)(2,1)S(1)}, u32[]{:S(2)}, u32[]{:S(2)}) collective-permute-start(bf16[1,64,512]{2,1,0:T(8,128)(2,1)S(1)} %get-tuple-element.41), channel_id=1, source_target_pairs={{0,24},{4,28},{8,0},{12,4},{16,8},{20,12},{24,16},{28,20},{1,25},{... | collective-permute-start | bytes 196616 | tf_op jit(solution)/shard_map/ppermute | solution.py:36
  92.3 0.6 collective-permute-start.19
  92.8 1.8 %collective-permute-done.25 = bf16[1,64,512]{2,1,0:T(8,128)(2,1)S(1)} collective-permute-done((bf16[1,64,512]{2,1,0:T(8,128)(2,1)S(1)}, bf16[1,64,512]{2,1,0:T(8,128)(2,1)S(1)}, u32[]{:S(2)}, u32[]{:S(2)}) %collective-permute-start.25) | collective-permute-done | bytes 65568 | tf_op jit(solution)/shard_map/ppermute | solution.py:36
  94.6 1.6 %collective-permute-start.20 = (bf16[1,64,512]{2,1,0:T(8,128)(2,1)S(1)}, bf16[1,64,512]{2,1,0:T(8,128)(2,1)S(1)}, u32[]{:S(2)}, u32[]{:S(2)}) collective-permute-start(bf16[1,64,512]{2,1,0:T(8,128)(2,1)S(1)} %get-tuple-element.44), channel_id=1, source_target_pairs={{0,24},{4,28},{8,0},{12,4},{16,8},{20,12},{24,16},{28,20},{1,25},{... | collective-permute-start | bytes 196616 | tf_op jit(solution)/shard_map/ppermute | solution.py:36
  96.3 2.9 %collective-permute-done.18 = bf16[1,64,512]{2,1,0:T(8,128)(2,1)S(1)} collective-permute-done((bf16[1,64,512]{2,1,0:T(8,128)(2,1)S(1)}, bf16[1,64,512]{2,1,0:T(8,128)(2,1)S(1)}, u32[]{:S(2)}, u32[]{:S(2)}) %collective-permute-start.18) | collective-permute-done | bytes 65568 | tf_op jit(solution)/shard_map/ppermute | solution.py:36
  99.8 1.3 %collective-permute-done.28 = f32[1,128,256]{2,1,0:T(8,128)S(1)} collective-permute-done((f32[1,128,256]{2,1,0:T(8,128)S(1)}, f32[1,128,256]{2,1,0:T(8,128)S(1)}, u32[]{:S(2)}, u32[]{:S(2)}) %collective-permute-start.28) | collective-permute-done | bytes 131104 | tf_op jit(solution)/shard_map/ppermute | solution.py:40
  101.2 0.7 maximum_select_fusion.1
  (56 shorter events, 2.2 us)
Async XLA Ops:
  0.0 1.0 %copy-start = (f32[2,256,256]{2,1,0:T(8,128)S(1)}, f32[2,256,256]{2,1,0:T(8,128)}, u32[]{:S(2)}) copy-start(f32[2,256,256]{2,1,0:T(8,128)} %param.3) | copy-start | bytes 1572868
  1.1 6.5 %collective-permute-start = (bf16[2,128,256]{2,1,0:T(8,128)(2,1)S(1)}, bf16[2,128,256]{2,1,0:T(8,128)(2,1)S(1)}, u32[]{:S(2)}, u32[]{:S(2)}) collective-permute-start(bf16[2,128,256]{2,1,0:T(8,128)(2,1)S(1)} %dynamic-slice_convert_fusion.2), channel_id=1, source_target_pairs={{0,2},{2,0},{1,3},{3,1},{4,6},{6,4},{5,7},{7,5},{8,10},{10,8},{9,1... | collective-permute-start | bytes 393224 | tf_op jit(solution)/shard_map/ppermute | solution.py:36
  7.6 40.3 %collective-permute-start.4 = (bf16[3,256,1024]{2,1,0:T(8,128)(2,1)}, bf16[3,256,1024]{2,1,0:T(8,128)(2,1)}, u32[]{:S(2)}, u32[]{:S(2)}) collective-permute-start(bf16[3,256,1024]{2,1,0:T(8,128)(2,1)} %constant_dynamic-slice_fusion.2), channel_id=1, source_target_pairs={{0,2},{2,0},{1,3},{3,1},{4,6},{6,4},{5,7},{7,5},{8,10},{10,8},{9,1... | collective-permute-start | bytes 4718600 | tf_op jit(solution)/shard_map/ppermute | solution.py:36
  9.4 1.4 %collective-permute-start.1 = (bf16[2,1,128,256]{3,2,0,1:T(8,128)(2,1)S(1)}, bf16[2,1,128,256]{3,2,0,1:T(8,128)(2,1)S(1)}, u32[]{:S(2)}, u32[]{:S(2)}) collective-permute-start(bf16[2,1,128,256]{3,2,0,1:T(8,128)(2,1)S(1)} %get-tuple-element.48), channel_id=1, source_target_pairs={{0,4},{4,0},{8,12},{12,8},{16,20},{20,16},{24,28},{28,24},{1,5},{5... | collective-permute-start | bytes 393224 | tf_op jit(solution)/shard_map/ppermute | solution.py:40
  10.9 13.5 %copy-start.1 = (bf16[2,128,512]{2,1,0:T(8,128)(2,1)}, bf16[2,128,512]{2,1,0:T(8,128)(2,1)S(1)}, u32[]{:S(2)}) copy-start(bf16[2,128,512]{2,1,0:T(8,128)(2,1)S(1)} %maximum_select_fusion.refs_0_) | copy-start | bytes 786436
  10.9 8.4 %collective-permute-start.2 = (bf16[2,128,512]{2,1,0:T(8,128)(2,1)S(1)}, bf16[2,128,512]{2,1,0:T(8,128)(2,1)S(1)}, u32[]{:S(2)}, u32[]{:S(2)}) collective-permute-start(bf16[2,128,512]{2,1,0:T(8,128)(2,1)S(1)} %maximum_select_fusion.refs_0_), channel_id=1, source_target_pairs={{0,1},{1,0},{2,3},{3,2},{4,5},{5,4},{6,7},{7,6},{8,9},{9,8},{10,11... | collective-permute-start | bytes 786440 | tf_op jit(solution)/shard_map/ppermute | solution.py:36
  12.5 12.0 %collective-permute-start.5 = (bf16[2,128,512]{2,1,0:T(8,128)(2,1)S(1)}, bf16[2,128,512]{2,1,0:T(8,128)(2,1)S(1)}, u32[]{:S(2)}, u32[]{:S(2)}) collective-permute-start(bf16[2,128,512]{2,1,0:T(8,128)(2,1)S(1)} %maximum_select_fusion.refs_0_), channel_id=1, source_target_pairs={{0,8},{4,12},{8,16},{12,20},{16,24},{20,28},{24,0},{28,4},{1,9},{5... | collective-permute-start | bytes 786440 | tf_op jit(solution)/shard_map/ppermute | solution.py:36
  14.1 13.4 %collective-permute-start.7 = (bf16[2,128,512]{2,1,0:T(8,128)(2,1)S(1)}, bf16[2,128,512]{2,1,0:T(8,128)(2,1)S(1)}, u32[]{:S(2)}, u32[]{:S(2)}) collective-permute-start(bf16[2,128,512]{2,1,0:T(8,128)(2,1)S(1)} %maximum_select_fusion.refs_0_), channel_id=1, source_target_pairs={{0,24},{4,28},{8,0},{12,4},{16,8},{20,12},{24,16},{28,20},{1,25},{... | collective-permute-start | bytes 786440 | tf_op jit(solution)/shard_map/ppermute | solution.py:36
  19.3 0.7 copy-start.5
  20.0 19.4 %collective-permute-start.9 = (bf16[2,128,512]{2,1,0:T(8,128)(2,1)S(1)}, bf16[2,128,512]{2,1,0:T(8,128)(2,1)}, u32[]{:S(2)}, u32[]{:S(2)}) collective-permute-start(bf16[2,128,512]{2,1,0:T(8,128)(2,1)S(1)} %maximum_select_fusion.refs_0_), channel_id=1, source_target_pairs={{0,16},{4,20},{8,24},{12,28},{16,0},{20,4},{24,8},{28,12},{1,17},{... | collective-permute-start | bytes 786440 | tf_op jit(solution)/shard_map/ppermute | solution.py:36
  24.4 26.3 %collective-permute-start.3 = (bf16[4,256,1024]{2,1,0:T(8,128)(2,1)S(1)}, bf16[4,256,1024]{2,1,0:T(8,128)(2,1)}, u32[]{:S(2)}, u32[]{:S(2)}) collective-permute-start(bf16[4,256,1024]{2,1,0:T(8,128)(2,1)S(1)} %constant_dynamic-slice_fusion.1.refs_0_), channel_id=1, source_target_pairs={{0,4},{4,0},{8,12},{12,8},{16,20},{20,16},{24,28},{28,24},{1,5},{5... | collective-permute-start | bytes 6291464 | tf_op jit(solution)/shard_map/ppermute | solution.py:40
  24.5 23.3 %copy-start.6 = (bf16[2,128,512]{2,1,0:T(8,128)(2,1)}, bf16[2,128,512]{2,1,0:T(8,128)(2,1)S(1)}, u32[]{:S(2)}) copy-start(bf16[2,128,512]{2,1,0:T(8,128)(2,1)S(1)} %collective-permute-done.5.refs_2_) | copy-start | bytes 786436
  24.5 17.3 %collective-permute-start.6 = (bf16[2,128,512]{2,1,0:T(8,128)(2,1)S(1)}, bf16[2,128,512]{2,1,0:T(8,128)(2,1)}, u32[]{:S(2)}, u32[]{:S(2)}) collective-permute-start(bf16[2,128,512]{2,1,0:T(8,128)(2,1)S(1)} %collective-permute-done.5.refs_2_), channel_id=1, source_target_pairs={{0,1},{1,0},{2,3},{3,2},{4,5},{5,4},{6,7},{7,6},{8,9},{9,8},{10,11... | collective-permute-start | bytes 786440 | tf_op jit(solution)/shard_map/ppermute | solution.py:36
  27.5 20.3 %copy-start.7 = (bf16[2,128,512]{2,1,0:T(8,128)(2,1)}, bf16[2,128,512]{2,1,0:T(8,128)(2,1)S(1)}, u32[]{:S(2)}) copy-start(bf16[2,128,512]{2,1,0:T(8,128)(2,1)S(1)} %collective-permute-done.7.refs_4_) | copy-start | bytes 786436
  27.5 14.3 %collective-permute-start.8 = (bf16[2,128,512]{2,1,0:T(8,128)(2,1)S(1)}, bf16[2,128,512]{2,1,0:T(8,128)(2,1)}, u32[]{:S(2)}, u32[]{:S(2)}) collective-permute-start(bf16[2,128,512]{2,1,0:T(8,128)(2,1)S(1)} %collective-permute-done.7.refs_4_), channel_id=1, source_target_pairs={{0,1},{1,0},{2,3},{3,2},{4,5},{5,4},{6,7},{7,6},{8,9},{9,8},{10,11... | collective-permute-start | bytes 786440 | tf_op jit(solution)/shard_map/ppermute | solution.py:36
  39.4 8.4 %collective-permute-start.10 = (bf16[2,128,512]{2,1,0:T(8,128)(2,1)}, bf16[2,128,512]{2,1,0:T(8,128)(2,1)S(1)}, u32[]{:S(2)}, u32[]{:S(2)}) collective-permute-start(bf16[2,128,512]{2,1,0:T(8,128)(2,1)} %collective-permute-done.9.refs_6_), channel_id=1, source_target_pairs={{0,1},{1,0},{2,3},{3,2},{4,5},{5,4},{6,7},{7,6},{8,9},{9,8},{10,11... | collective-permute-start | bytes 786440 | tf_op jit(solution)/shard_map/ppermute | solution.py:36
  47.8 3.8 %collective-permute-start.12 = (bf16[3,256,1024]{2,1,0:T(8,128)(2,1)}, bf16[3,256,1024]{2,1,0:T(8,128)(2,1)}, u32[]{:S(2)}, u32[]{:S(2)}) collective-permute-start(bf16[3,256,1024]{2,1,0:T(8,128)(2,1)} %collective-permute-done.4.refs_1_), channel_id=1, source_target_pairs={{0,4},{4,0},{8,12},{12,8},{16,20},{20,16},{24,28},{28,24},{1,5},{5... | collective-permute-start | bytes 4718600 | tf_op jit(solution)/shard_map/ppermute | solution.py:40
  47.9 14.5 %collective-permute-start.11 = (bf16[1,256,1024]{2,1,0:T(8,128)(2,1)}, bf16[1,256,1024]{2,1,0:T(8,128)(2,1)S(1)}, u32[]{:S(2)}, u32[]{:S(2)}) collective-permute-start(bf16[1,256,1024]{2,1,0:T(8,128)(2,1)} %constant_dynamic-slice_fusion), channel_id=1, source_target_pairs={{0,2},{2,0},{1,3},{3,1},{4,6},{6,4},{5,7},{7,5},{8,10},{10,8},{9,1... | collective-permute-start | bytes 1572872 | tf_op jit(solution)/shard_map/ppermute | solution.py:36
  62.5 1.9 %collective-permute-start.13 = (bf16[1,256,1024]{2,1,0:T(8,128)(2,1)S(1)}, bf16[1,256,1024]{2,1,0:T(8,128)(2,1)S(1)}, u32[]{:S(2)}, u32[]{:S(2)}) collective-permute-start(bf16[1,256,1024]{2,1,0:T(8,128)(2,1)S(1)} %collective-permute-done.11.refs_1_), channel_id=1, source_target_pairs={{0,4},{4,0},{8,12},{12,8},{16,20},{20,16},{24,28},{28,24},{1,5},{5... | collective-permute-start | bytes 1572872 | tf_op jit(solution)/shard_map/ppermute | solution.py:40
  68.3 11.2 %copy-start.4 = (f32[1,2,32,2048]{3,2,1,0:T(8,128)S(1)}, f32[1,2,32,2048]{3,2,1,0:T(8,128)}, u32[]{:S(2)}) copy-start(f32[1,2,32,2048]{3,2,1,0:T(8,128)} %get-tuple-element.35) | copy-start | bytes 1572868
  68.3 15.0 %copy-start.3 = (f32[2,32,2048]{2,1,0:T(8,128)S(1)}, f32[2,32,2048]{2,1,0:T(8,128)}, u32[]{:S(2)}) copy-start(f32[2,32,2048]{2,1,0:T(8,128)} %get-tuple-element.33) | copy-start | bytes 1572868
  68.3 9.4 %collective-permute-start.23 = (bf16[2,32,2048]{2,1,0:T(8,128)(2,1)}, bf16[2,32,2048]{2,1,0:T(8,128)(2,1)S(1)}, u32[]{:S(2)}, u32[]{:S(2)}) collective-permute-start(bf16[2,32,2048]{2,1,0:T(8,128)(2,1)} %bitcast.30), channel_id=1, source_target_pairs={{0,1},{1,0},{2,3},{3,2},{4,5},{5,4},{6,7},{7,6},{8,9},{9,8},{10,11... | collective-permute-start | bytes 786440 | tf_op jit(solution)/shard_map/ppermute | solution.py:36
  68.9 10.6 %collective-permute-start.21 = (bf16[1,2,32,2048]{3,2,1,0:T(8,128)(2,1)}, bf16[1,2,32,2048]{3,2,1,0:T(8,128)(2,1)S(1)}, u32[]{:S(2)}, u32[]{:S(2)}) collective-permute-start(bf16[1,2,32,2048]{3,2,1,0:T(8,128)(2,1)} %get-tuple-element.36), channel_id=1, source_target_pairs={{0,2},{2,0},{1,3},{3,1},{4,6},{6,4},{5,7},{7,5},{8,10},{10,8},{9,1... | collective-permute-start | bytes 786440 | tf_op jit(solution)/shard_map/ppermute | solution.py:36
  69.4 13.9 %collective-permute-start.16 = (bf16[2,32,2048]{2,1,0:T(8,128)(2,1)}, bf16[2,32,2048]{2,1,0:T(8,128)(2,1)S(1)}, u32[]{:S(2)}, u32[]{:S(2)}) collective-permute-start(bf16[2,32,2048]{2,1,0:T(8,128)(2,1)} %bitcast.29), channel_id=1, source_target_pairs={{0,1},{1,0},{2,3},{3,2},{4,5},{5,4},{6,7},{7,6},{8,9},{9,8},{10,11... | collective-permute-start | bytes 786440 | tf_op jit(solution)/shard_map/ppermute | solution.py:36
  70.9 13.1 %collective-permute-start.14 = (bf16[1,2,32,2048]{3,2,1,0:T(8,128)(2,1)}, bf16[1,2,32,2048]{3,2,1,0:T(8,128)(2,1)S(1)}, u32[]{:S(2)}, u32[]{:S(2)}) collective-permute-start(bf16[1,2,32,2048]{3,2,1,0:T(8,128)(2,1)} %get-tuple-element.32), channel_id=1, source_target_pairs={{0,2},{2,0},{1,3},{3,1},{4,6},{6,4},{5,7},{7,5},{8,10},{10,8},{9,1... | collective-permute-start | bytes 786440 | tf_op jit(solution)/shard_map/ppermute | solution.py:36
  77.7 6.3 %copy-start.2 = (f32[1,2,32,2048]{3,2,1,0:T(8,128)S(1)}, f32[1,2,32,2048]{3,2,1,0:T(8,128)}, u32[]{:S(2)}) copy-start(f32[1,2,32,2048]{3,2,1,0:T(8,128)} %get-tuple-element.31) | copy-start | bytes 1572868
  78.9 7.6 %collective-permute-start.24 = (bf16[1,32,2048]{2,1,0:T(8,128)(2,1)S(1)}, bf16[1,32,2048]{2,1,0:T(8,128)(2,1)S(1)}, u32[]{:S(2)}, u32[]{:S(2)}) collective-permute-start(bf16[1,32,2048]{2,1,0:T(8,128)(2,1)S(1)} %slice.26), channel_id=1, source_target_pairs={{0,2},{2,0},{1,3},{3,1},{4,6},{6,4},{5,7},{7,5},{8,10},{10,8},{9,1... | collective-permute-start | bytes 393224 | tf_op jit(solution)/shard_map/ppermute | solution.py:36
  79.6 6.9 %collective-permute-start.22 = (bf16[1,32,2048]{2,1,0:T(8,128)(2,1)S(1)}, bf16[1,32,2048]{2,1,0:T(8,128)(2,1)S(1)}, u32[]{:S(2)}, u32[]{:S(2)}) collective-permute-start(bf16[1,32,2048]{2,1,0:T(8,128)(2,1)S(1)} %fusion.1), channel_id=1, source_target_pairs={{0,1},{1,0},{2,3},{3,2},{4,5},{5,4},{6,7},{7,6},{8,9},{9,8},{10,11... | collective-permute-start | bytes 393224 | tf_op jit(solution)/shard_map/ppermute | solution.py:36
  83.4 8.6 %collective-permute-start.17 = (bf16[1,32,2048]{2,1,0:T(8,128)(2,1)S(1)}, bf16[1,32,2048]{2,1,0:T(8,128)(2,1)S(1)}, u32[]{:S(2)}, u32[]{:S(2)}) collective-permute-start(bf16[1,32,2048]{2,1,0:T(8,128)(2,1)S(1)} %slice.27), channel_id=1, source_target_pairs={{0,2},{2,0},{1,3},{3,1},{4,6},{6,4},{5,7},{7,5},{8,10},{10,8},{9,1... | collective-permute-start | bytes 393224 | tf_op jit(solution)/shard_map/ppermute | solution.py:36
  84.1 7.9 %collective-permute-start.15 = (bf16[1,32,2048]{2,1,0:T(8,128)(2,1)S(1)}, bf16[1,32,2048]{2,1,0:T(8,128)(2,1)S(1)}, u32[]{:S(2)}, u32[]{:S(2)}) collective-permute-start(bf16[1,32,2048]{2,1,0:T(8,128)(2,1)S(1)} %fusion), channel_id=1, source_target_pairs={{0,1},{1,0},{2,3},{3,2},{4,5},{5,4},{6,7},{7,6},{8,9},{9,8},{10,11... | collective-permute-start | bytes 393224 | tf_op jit(solution)/shard_map/ppermute | solution.py:36
  86.7 7.9 %collective-permute-start.25 = (bf16[1,64,512]{2,1,0:T(8,128)(2,1)S(1)}, bf16[1,64,512]{2,1,0:T(8,128)(2,1)S(1)}, u32[]{:S(2)}, u32[]{:S(2)}) collective-permute-start(bf16[1,64,512]{2,1,0:T(8,128)(2,1)S(1)} %get-tuple-element.39), channel_id=1, source_target_pairs={{0,16},{4,20},{8,24},{12,28},{16,0},{20,4},{24,8},{28,12},{1,17},{... | collective-permute-start | bytes 196616 | tf_op jit(solution)/shard_map/ppermute | solution.py:36
  88.2 8.0 %collective-permute-start.26 = (bf16[1,64,512]{2,1,0:T(8,128)(2,1)S(1)}, bf16[1,64,512]{2,1,0:T(8,128)(2,1)S(1)}, u32[]{:S(2)}, u32[]{:S(2)}) collective-permute-start(bf16[1,64,512]{2,1,0:T(8,128)(2,1)S(1)} %get-tuple-element.40), channel_id=1, source_target_pairs={{0,8},{4,12},{8,16},{12,20},{16,24},{20,28},{24,0},{28,4},{1,9},{5... | collective-permute-start | bytes 196616 | tf_op jit(solution)/shard_map/ppermute | solution.py:36
  89.0 7.1 %collective-permute-start.27 = (bf16[1,64,512]{2,1,0:T(8,128)(2,1)S(1)}, bf16[1,64,512]{2,1,0:T(8,128)(2,1)S(1)}, u32[]{:S(2)}, u32[]{:S(2)}) collective-permute-start(bf16[1,64,512]{2,1,0:T(8,128)(2,1)S(1)} %get-tuple-element.41), channel_id=1, source_target_pairs={{0,24},{4,28},{8,0},{12,4},{16,8},{20,12},{24,16},{28,20},{1,25},{... | collective-permute-start | bytes 196616 | tf_op jit(solution)/shard_map/ppermute | solution.py:36
  92.2 7.0 %collective-permute-start.18 = (bf16[1,64,512]{2,1,0:T(8,128)(2,1)S(1)}, bf16[1,64,512]{2,1,0:T(8,128)(2,1)S(1)}, u32[]{:S(2)}, u32[]{:S(2)}) collective-permute-start(bf16[1,64,512]{2,1,0:T(8,128)(2,1)S(1)} %get-tuple-element.42), channel_id=1, source_target_pairs={{0,16},{4,20},{8,24},{12,28},{16,0},{20,4},{24,8},{28,12},{1,17},{... | collective-permute-start | bytes 196616 | tf_op jit(solution)/shard_map/ppermute | solution.py:36
  92.3 6.9 %collective-permute-start.19 = (bf16[1,64,512]{2,1,0:T(8,128)(2,1)S(1)}, bf16[1,64,512]{2,1,0:T(8,128)(2,1)S(1)}, u32[]{:S(2)}, u32[]{:S(2)}) collective-permute-start(bf16[1,64,512]{2,1,0:T(8,128)(2,1)S(1)} %get-tuple-element.43), channel_id=1, source_target_pairs={{0,8},{4,12},{8,16},{12,20},{16,24},{20,28},{24,0},{28,4},{1,9},{5... | collective-permute-start | bytes 196616 | tf_op jit(solution)/shard_map/ppermute | solution.py:36
  94.6 5.0 %collective-permute-start.20 = (bf16[1,64,512]{2,1,0:T(8,128)(2,1)S(1)}, bf16[1,64,512]{2,1,0:T(8,128)(2,1)S(1)}, u32[]{:S(2)}, u32[]{:S(2)}) collective-permute-start(bf16[1,64,512]{2,1,0:T(8,128)(2,1)S(1)} %get-tuple-element.44), channel_id=1, source_target_pairs={{0,24},{4,28},{8,0},{12,4},{16,8},{20,12},{24,16},{28,20},{1,25},{... | collective-permute-start | bytes 196616 | tf_op jit(solution)/shard_map/ppermute | solution.py:36
  99.8 1.4 %collective-permute-start.28 = (f32[1,128,256]{2,1,0:T(8,128)S(1)}, f32[1,128,256]{2,1,0:T(8,128)S(1)}, u32[]{:S(2)}, u32[]{:S(2)}) collective-permute-start(f32[1,128,256]{2,1,0:T(8,128)S(1)} %get-tuple-element.46), channel_id=1, source_target_pairs={{0,4},{4,0},{8,12},{12,8},{16,20},{20,16},{24,28},{28,24},{1,5},{5... | collective-permute-start | bytes 393224 | tf_op jit(solution)/shard_map/ppermute | solution.py:40

commit v14 on v12

--- a/solution.py
+++ b/solution.py
@@ -219,7 +219,7 @@
     per = groups // nv
     own = rows // no
     small = own // (PIECES * 2)
-    tile = min(width, 1024)
+    tile = min(width, 512)
     tiles = total // tile
 
     def body(*refs):

time: 102 us -> 102 us (level)
  no operation moved by 1% of the time
where the time goes in v14:
time: 102 us
  waiting for transfers between devices  41.9 us (41%)
  starting transfers between devices  32.4 us (32%)
  Pallas kernels  16.2 us (16%)
  local copies, waits for them, and re-layouts  8.29 us (8%)
  other arithmetic  2.81 us (3%)
    ppermute x24, waiting for transfers between devices, shift(): return lax.ppermute(array, axis, pairs)  38 us
    ppermute x24, starting transfers between devices, shift(): return lax.ppermute(array, axis, pairs)  32.1 us
    pallas_call x1, Pallas kernels, early_sums(): pl.pallas_call(body, out_shape=shape, in_specs=[ANY] * n + [VMEM], out_sp...  8.44 us
    dynamic_slice x2, local copies, waits for them, and re-layouts, sends(): lax.dynamic_slice_in_dim(source, (v - r) % nv * take + first, size, 0)  4.56 us
    pallas_call x1, Pallas kernels, last_sums(): pl.pallas_call(body, out_shape=[pltpu.HBM(x.shape, x.dtype) for x in shap...  4.02 us
    ppermute x5, waiting for transfers between devices, sibling(): return lax.ppermute(array, 'aux', [(i, i ^ 1) for i in range(size)])  3.9 us
    pallas_call x1, Pallas kernels, assemble(): pl.pallas_call(body, out_shape=shape, in_specs=[SMEM] + [ANY] * len(block...  2.05 us
  transfers between devices with their start and end apart: 29, of which 15 were waited for; matrix products, arithmetic and copies ran while one was open for 8% of the time, Pallas kernels for 12%

profile of v14, /device:TPU:0, one launch (start us, length us, event | category | flops | bytes accessed | tf_op | source)
XLA Modules:
  0.0 101.9 jit_solution(1307238891240909649)
XLA Ops:
  0.0 1.0 %copy-done = f32[2,256,256]{2,1,0:T(8,128)S(1)} copy-done((f32[2,256,256]{2,1,0:T(8,128)S(1)}, f32[2,256,256]{2,1,0:T(8,128)}, u32[]{:S(2)}) %copy-start) | copy-done | bytes 524312
  1.1 3.0 %collective-permute-start = (bf16[2,128,256]{2,1,0:T(8,128)(2,1)S(1)}, bf16[2,128,256]{2,1,0:T(8,128)(2,1)S(1)}, u32[]{:S(2)}, u32[]{:S(2)}) collective-permute-start(bf16[2,128,256]{2,1,0:T(8,128)(2,1)S(1)} %dynamic-slice_convert_fusion.2), channel_id=1, source_target_pairs={{0,2},{2,0},{1,3},{3,1},{4,6},{6,4},{5,7},{7,5},{8,10},{10,8},{9,1... | collective-permute-start | bytes 393224 | tf_op jit(solution)/shard_map/ppermute | solution.py:36
  4.1 2.7 %constant_dynamic-slice_fusion.2 = bf16[3,256,1024]{2,1,0:T(8,128)(2,1)} fusion(bf16[8,256,1024]{2,1,0:T(8,128)(2,1)} %param.2, s32[]{:T(128)S(6)} %select_n.177), kind=kLoop, calls=%fused_computation.64 | loop fusion | bytes 3145732 | tf_op jit(solution)/shard_map/dynamic_slice | solution.py:337
  6.8 0.8 collective-permute-done
  7.6 1.7 %collective-permute-start.4 = (bf16[3,256,1024]{2,1,0:T(8,128)(2,1)}, bf16[3,256,1024]{2,1,0:T(8,128)(2,1)}, u32[]{:S(2)}, u32[]{:S(2)}) collective-permute-start(bf16[3,256,1024]{2,1,0:T(8,128)(2,1)} %constant_dynamic-slice_fusion.2), channel_id=1, source_target_pairs={{0,2},{2,0},{1,3},{3,1},{4,6},{6,4},{5,7},{7,5},{8,10},{10,8},{9,1... | collective-permute-start | bytes 4718600 | tf_op jit(solution)/shard_map/ppermute | solution.py:36
  9.4 1.3 %collective-permute-done.1 = bf16[2,1,128,256]{3,2,0,1:T(8,128)(2,1)S(1)} collective-permute-done((bf16[2,1,128,256]{3,2,0,1:T(8,128)(2,1)S(1)}, bf16[2,1,128,256]{3,2,0,1:T(8,128)(2,1)S(1)}, u32[]{:S(2)}, u32[]{:S(2)}) %collective-permute-start.1) | collective-permute-done | bytes 131104 | tf_op jit(solution)/shard_map/ppermute | solution.py:40
  10.9 1.6 %collective-permute-start.2 = (bf16[2,128,512]{2,1,0:T(8,128)(2,1)S(1)}, bf16[2,128,512]{2,1,0:T(8,128)(2,1)S(1)}, u32[]{:S(2)}, u32[]{:S(2)}) collective-permute-start(bf16[2,128,512]{2,1,0:T(8,128)(2,1)S(1)} %maximum_select_fusion.refs_0_), channel_id=1, source_target_pairs={{0,1},{1,0},{2,3},{3,2},{4,5},{5,4},{6,7},{7,6},{8,9},{9,8},{10,11... | collective-permute-start | bytes 786440 | tf_op jit(solution)/shard_map/ppermute | solution.py:36
  12.5 1.6 %collective-permute-start.5 = (bf16[2,128,512]{2,1,0:T(8,128)(2,1)S(1)}, bf16[2,128,512]{2,1,0:T(8,128)(2,1)S(1)}, u32[]{:S(2)}, u32[]{:S(2)}) collective-permute-start(bf16[2,128,512]{2,1,0:T(8,128)(2,1)S(1)} %maximum_select_fusion.refs_0_), channel_id=1, source_target_pairs={{0,8},{4,12},{8,16},{12,20},{16,24},{20,28},{24,0},{28,4},{1,9},{5... | collective-permute-start | bytes 786440 | tf_op jit(solution)/shard_map/ppermute | solution.py:36
  14.1 2.2 %collective-permute-start.7 = (bf16[2,128,512]{2,1,0:T(8,128)(2,1)S(1)}, bf16[2,128,512]{2,1,0:T(8,128)(2,1)S(1)}, u32[]{:S(2)}, u32[]{:S(2)}) collective-permute-start(bf16[2,128,512]{2,1,0:T(8,128)(2,1)S(1)} %maximum_select_fusion.refs_0_), channel_id=1, source_target_pairs={{0,24},{4,28},{8,0},{12,4},{16,8},{20,12},{24,16},{28,20},{1,25},{... | collective-permute-start | bytes 786440 | tf_op jit(solution)/shard_map/ppermute | solution.py:36
  16.3 3.0 %collective-permute-done.2.refs_1_ = bf16[2,128,512]{2,1,0:T(8,128)(2,1)S(1)} collective-permute-done((bf16[2,128,512]{2,1,0:T(8,128)(2,1)S(1)}, bf16[2,128,512]{2,1,0:T(8,128)(2,1)S(1)}, u32[]{:S(2)}, u32[]{:S(2)}) %collective-permute-start.2) | collective-permute-done | bytes 262176 | tf_op jit(solution)/shard_map/ppermute | solution.py:36
  19.3 0.7 copy-done.5
  20.0 2.6 %collective-permute-start.9 = (bf16[2,128,512]{2,1,0:T(8,128)(2,1)S(1)}, bf16[2,128,512]{2,1,0:T(8,128)(2,1)}, u32[]{:S(2)}, u32[]{:S(2)}) collective-permute-start(bf16[2,128,512]{2,1,0:T(8,128)(2,1)S(1)} %maximum_select_fusion.refs_0_), channel_id=1, source_target_pairs={{0,16},{4,20},{8,24},{12,28},{16,0},{20,4},{24,8},{28,12},{1,17},{... | collective-permute-start | bytes 786440 | tf_op jit(solution)/shard_map/ppermute | solution.py:36
  22.6 1.8 %constant_dynamic-slice_fusion.1.refs_0_ = bf16[4,256,1024]{2,1,0:T(8,128)(2,1)S(1)} fusion(bf16[8,256,1024]{2,1,0:T(8,128)(2,1)} %param.2, s32[]{:T(128)S(6)} %select_n.181), kind=kLoop, calls=%fused_computation.63 | loop fusion | bytes 4194308 | tf_op jit(solution)/shard_map/dynamic_slice | solution.py:377
  24.5 1.6 %collective-permute-start.6 = (bf16[2,128,512]{2,1,0:T(8,128)(2,1)S(1)}, bf16[2,128,512]{2,1,0:T(8,128)(2,1)}, u32[]{:S(2)}, u32[]{:S(2)}) collective-permute-start(bf16[2,128,512]{2,1,0:T(8,128)(2,1)S(1)} %collective-permute-done.5.refs_2_), channel_id=1, source_target_pairs={{0,1},{1,0},{2,3},{3,2},{4,5},{5,4},{6,7},{7,6},{8,9},{9,8},{10,11... | collective-permute-start | bytes 786440 | tf_op jit(solution)/shard_map/ppermute | solution.py:36
  26.1 1.4 %collective-permute-done.7.refs_4_ = bf16[2,128,512]{2,1,0:T(8,128)(2,1)S(1)} collective-permute-done((bf16[2,128,512]{2,1,0:T(8,128)(2,1)S(1)}, bf16[2,128,512]{2,1,0:T(8,128)(2,1)S(1)}, u32[]{:S(2)}, u32[]{:S(2)}) %collective-permute-start.7) | collective-permute-done | bytes 262176 | tf_op jit(solution)/shard_map/ppermute | solution.py:36
  27.5 0.5 collective-permute-start.8
  28.0 11.4 %collective-permute-done.9.refs_6_ = bf16[2,128,512]{2,1,0:T(8,128)(2,1)} collective-permute-done((bf16[2,128,512]{2,1,0:T(8,128)(2,1)S(1)}, bf16[2,128,512]{2,1,0:T(8,128)(2,1)}, u32[]{:S(2)}, u32[]{:S(2)}) %collective-permute-start.9) | collective-permute-done | bytes 262176 | tf_op jit(solution)/shard_map/ppermute | solution.py:36
  39.4 0.5 collective-permute-start.10
  39.9 1.9 %constant_dynamic-slice_fusion = bf16[1,256,1024]{2,1,0:T(8,128)(2,1)} fusion(bf16[8,256,1024]{2,1,0:T(8,128)(2,1)} %param.2, s32[]{:T(128)S(6)} %select_n.182), kind=kLoop, calls=%fused_computation.62 | loop fusion | bytes 1048580 | tf_op jit(solution)/shard_map/dynamic_slice | solution.py:337
  41.8 6.1 %collective-permute-done.10.refs_7_ = bf16[2,128,512]{2,1,0:T(8,128)(2,1)S(1)} collective-permute-done((bf16[2,128,512]{2,1,0:T(8,128)(2,1)}, bf16[2,128,512]{2,1,0:T(8,128)(2,1)S(1)}, u32[]{:S(2)}, u32[]{:S(2)}) %collective-permute-start.10) | collective-permute-done | bytes 262176 | tf_op jit(solution)/shard_map/ppermute | solution.py:36
  47.9 0.6 collective-permute-start.11
  48.6 2.0 %assemble.1.refs_4_.refs_2_.refs_3_ = bf16[2,256,2048]{2,1,0:T(8,128)(2,1)S(1)} custom-call(s32[6]{0:T(128)S(1)} %stack.27.at, bf16[2,128,512]{2,1,0:T(8,128)(2,1)} %copy-done.1, bf16[2,128,512]{2,1,0:T(8,128)(2,1)} %copy-done.5, bf16[2,128,512]{2,1,0:T(8,128)(2,1)} %copy-done.6, bf16[2,128,512]{2,1,0:T(8,128)(2,1)} %collective-permute-done.6.refs_3_, ...), custom_call_target="tpu_custom_call" | custom-call | bytes 2097152 | tf_op jit(solution)/shard_map/assemble/pallas_call | solution.py:82
  50.7 1.0 collective-permute-done.12.refs_3_
  51.7 8.4 %early_sums.1.refs_3_ = f32[2,256,2048]{2,1,0:T(8,128)S(1)} custom-call(bf16[4,256,1024]{2,1,0:T(8,128)(2,1)S(1)} %constant_dynamic-slice_fusion.1.refs_0_, bf16[3,256,1024]{2,1,0:T(8,128)(2,1)} %collective-permute-done.4.refs_1_, bf16[4,256,1024]{2,1,0:T(8,128)(2,1)} %collective-permute-done.3.refs_2_.refs_1_, ...), custom_call_target="tpu_custom_call" | custom-call | bytes 2097152 | tf_op jit(solution)/shard_map/early_sums/pallas_call | solution.py:151
  60.1 2.4 %collective-permute-done.11.refs_1_ = bf16[1,256,1024]{2,1,0:T(8,128)(2,1)S(1)} collective-permute-done((bf16[1,256,1024]{2,1,0:T(8,128)(2,1)}, bf16[1,256,1024]{2,1,0:T(8,128)(2,1)S(1)}, u32[]{:S(2)}, u32[]{:S(2)}) %collective-permute-start.11) | collective-permute-done | bytes 524320 | tf_op jit(solution)/shard_map/ppermute | solution.py:36
  62.5 1.6 %own_sums.1.refs_4_ = f32[2,256,2048]{2,1,0:T(8,128)S(1)} custom-call(bf16[4,256,1024]{2,1,0:T(8,128)(2,1)S(1)} %constant_dynamic-slice_fusion.1.refs_0_, bf16[1,256,1024]{2,1,0:T(8,128)(2,1)S(1)} %collective-permute-done.11.refs_1_, bf16[2,256,2048]{2,1,0:T(8,128)(2,1)S(1)} %assemble.1.refs_4_.refs_2_.refs_3_, ...), custom_call_target="tpu_custom_call", output_to_operand_aliasing={{}: (3, {})} | custom-call | bytes 2097152 | tf_op jit(solution)/shard_map/own_sums/pallas_call | solution.py:201
  64.1 0.2 collective-permute-done.13.refs_2_
  64.4 4.0 %last_sums.1 = (bf16[1,2,32,2048]{3,2,1,0:T(8,128)(2,1)}, f32[1,2,32,2048]{3,2,1,0:T(8,128)}, bf16[1,2,32,2048]{3,2,1,0:T(8,128)(2,1)}, f32[2,32,2048]{2,1,0:T(8...) custom-call(s32[1]{0:T(128)} %bitcast.refs_0_, ...), custom_call_target="tpu_custom_call" | custom-call | bytes 3145728 | tf_op jit(solution)/shard_map/last_sums/pallas_call | solution.py:300
  68.4 0.6 collective-permute-start.23
  69.0 0.5 collective-permute-start.21
  69.5 1.5 %collective-permute-start.16 = (bf16[2,32,2048]{2,1,0:T(8,128)(2,1)}, bf16[2,32,2048]{2,1,0:T(8,128)(2,1)S(1)}, u32[]{:S(2)}, u32[]{:S(2)}) collective-permute-start(bf16[2,32,2048]{2,1,0:T(8,128)(2,1)} %bitcast.29), channel_id=1, source_target_pairs={{0,1},{1,0},{2,3},{3,2},{4,5},{5,4},{6,7},{7,6},{8,9},{9,8},{10,11... | collective-permute-start | bytes 786440 | tf_op jit(solution)/shard_map/ppermute | solution.py:36
  71.1 1.5 %collective-permute-start.14 = (bf16[1,2,32,2048]{3,2,1,0:T(8,128)(2,1)}, bf16[1,2,32,2048]{3,2,1,0:T(8,128)(2,1)S(1)}, u32[]{:S(2)}, u32[]{:S(2)}) collective-permute-start(bf16[1,2,32,2048]{3,2,1,0:T(8,128)(2,1)} %get-tuple-element.32), channel_id=1, source_target_pairs={{0,2},{2,0},{1,3},{3,1},{4,6},{6,4},{5,7},{7,5},{8,10},{10,8},{9,1... | collective-permute-start | bytes 786440 | tf_op jit(solution)/shard_map/ppermute | solution.py:36
  72.5 5.3 %collective-permute-done.23 = bf16[2,32,2048]{2,1,0:T(8,128)(2,1)S(1)} collective-permute-done((bf16[2,32,2048]{2,1,0:T(8,128)(2,1)}, bf16[2,32,2048]{2,1,0:T(8,128)(2,1)S(1)}, u32[]{:S(2)}, u32[]{:S(2)}) %collective-permute-start.23) | collective-permute-done | bytes 262176 | tf_op jit(solution)/shard_map/ppermute | solution.py:36
  77.8 1.1 %convert_add_fusion = f32[2,32,2048]{2,1,0:T(8,128)S(1)} fusion(f32[2,32,2048]{2,1,0:T(8,128)} %get-tuple-element.37, bf16[2,32,2048]{2,1,0:T(8,128)(2,1)S(1)} %collective-permute-done.23), kind=kLoop, calls=%fused_computation.16 | loop fusion | flops 262144 | bytes 1310720 | tf_op jit(solution)/shard_map/add | solution.py:404
  79.0 0.6 collective-permute-start.24
  79.7 0.6 collective-permute-start.22
  80.3 3.2 %collective-permute-done.16 = bf16[2,32,2048]{2,1,0:T(8,128)(2,1)S(1)} collective-permute-done((bf16[2,32,2048]{2,1,0:T(8,128)(2,1)}, bf16[2,32,2048]{2,1,0:T(8,128)(2,1)S(1)}, u32[]{:S(2)}, u32[]{:S(2)}) %collective-permute-start.16) | collective-permute-done | bytes 262176 | tf_op jit(solution)/shard_map/ppermute | solution.py:36
  83.5 0.6 collective-permute-start.17
  84.2 1.4 %collective-permute-start.15 = (bf16[1,32,2048]{2,1,0:T(8,128)(2,1)S(1)}, bf16[1,32,2048]{2,1,0:T(8,128)(2,1)S(1)}, u32[]{:S(2)}, u32[]{:S(2)}) collective-permute-start(bf16[1,32,2048]{2,1,0:T(8,128)(2,1)S(1)} %fusion), channel_id=1, source_target_pairs={{0,1},{1,0},{2,3},{3,2},{4,5},{5,4},{6,7},{7,6},{8,9},{9,8},{10,11... | collective-permute-start | bytes 393224 | tf_op jit(solution)/shard_map/ppermute | solution.py:36
  85.7 0.9 collective-permute-done.24
  86.9 2.2 %collective-permute-start.26 = (bf16[1,64,512]{2,1,0:T(8,128)(2,1)S(1)}, bf16[1,64,512]{2,1,0:T(8,128)(2,1)S(1)}, u32[]{:S(2)}, u32[]{:S(2)}) collective-permute-start(bf16[1,64,512]{2,1,0:T(8,128)(2,1)S(1)} %get-tuple-element.40), channel_id=1, source_target_pairs={{0,16},{4,20},{8,24},{12,28},{16,0},{20,4},{24,8},{28,12},{1,17},{... | collective-permute-start | bytes 196616 | tf_op jit(solution)/shard_map/ppermute | solution.py:36
  89.1 2.1 %collective-permute-start.27 = (bf16[1,64,512]{2,1,0:T(8,128)(2,1)S(1)}, bf16[1,64,512]{2,1,0:T(8,128)(2,1)S(1)}, u32[]{:S(2)}, u32[]{:S(2)}) collective-permute-start(bf16[1,64,512]{2,1,0:T(8,128)(2,1)S(1)} %get-tuple-element.41), channel_id=1, source_target_pairs={{0,24},{4,28},{8,0},{12,4},{16,8},{20,12},{24,16},{28,20},{1,25},{... | collective-permute-start | bytes 196616 | tf_op jit(solution)/shard_map/ppermute | solution.py:36
  91.6 1.5 %collective-permute-start.19 = (bf16[1,64,512]{2,1,0:T(8,128)(2,1)S(1)}, bf16[1,64,512]{2,1,0:T(8,128)(2,1)S(1)}, u32[]{:S(2)}, u32[]{:S(2)}) collective-permute-start(bf16[1,64,512]{2,1,0:T(8,128)(2,1)S(1)} %get-tuple-element.43), channel_id=1, source_target_pairs={{0,16},{4,20},{8,24},{12,28},{16,0},{20,4},{24,8},{28,12},{1,17},{... | collective-permute-start | bytes 196616 | tf_op jit(solution)/shard_map/ppermute | solution.py:36
  93.1 2.8 %collective-permute-start.20 = (bf16[1,64,512]{2,1,0:T(8,128)(2,1)S(1)}, bf16[1,64,512]{2,1,0:T(8,128)(2,1)S(1)}, u32[]{:S(2)}, u32[]{:S(2)}) collective-permute-start(bf16[1,64,512]{2,1,0:T(8,128)(2,1)S(1)} %get-tuple-element.44), channel_id=1, source_target_pairs={{0,24},{4,28},{8,0},{12,4},{16,8},{20,12},{24,16},{28,20},{1,25},{... | collective-permute-start | bytes 196616 | tf_op jit(solution)/shard_map/ppermute | solution.py:36
  96.1 1.6 %collective-permute-done.18 = bf16[1,64,512]{2,1,0:T(8,128)(2,1)S(1)} collective-permute-done((bf16[1,64,512]{2,1,0:T(8,128)(2,1)S(1)}, bf16[1,64,512]{2,1,0:T(8,128)(2,1)S(1)}, u32[]{:S(2)}, u32[]{:S(2)}) %collective-permute-start.18) | collective-permute-done | bytes 65568 | tf_op jit(solution)/shard_map/ppermute | solution.py:36
  97.7 1.9 %collective-permute-done.19 = bf16[1,64,512]{2,1,0:T(8,128)(2,1)S(1)} collective-permute-done((bf16[1,64,512]{2,1,0:T(8,128)(2,1)S(1)}, bf16[1,64,512]{2,1,0:T(8,128)(2,1)S(1)}, u32[]{:S(2)}, u32[]{:S(2)}) %collective-permute-start.19) | collective-permute-done | bytes 65568 | tf_op jit(solution)/shard_map/ppermute | solution.py:36
  99.8 1.3 %collective-permute-done.28 = f32[1,128,256]{2,1,0:T(8,128)S(1)} collective-permute-done((f32[1,128,256]{2,1,0:T(8,128)S(1)}, f32[1,128,256]{2,1,0:T(8,128)S(1)}, u32[]{:S(2)}, u32[]{:S(2)}) %collective-permute-start.28) | collective-permute-done | bytes 131104 | tf_op jit(solution)/shard_map/ppermute | solution.py:40
  101.2 0.7 maximum_select_fusion.1
  (56 shorter events, 1.7 us)
Async XLA Ops:
  0.0 1.0 %copy-start = (f32[2,256,256]{2,1,0:T(8,128)S(1)}, f32[2,256,256]{2,1,0:T(8,128)}, u32[]{:S(2)}) copy-start(f32[2,256,256]{2,1,0:T(8,128)} %param.3) | copy-start | bytes 1572868
  1.1 6.5 %collective-permute-start = (bf16[2,128,256]{2,1,0:T(8,128)(2,1)S(1)}, bf16[2,128,256]{2,1,0:T(8,128)(2,1)S(1)}, u32[]{:S(2)}, u32[]{:S(2)}) collective-permute-start(bf16[2,128,256]{2,1,0:T(8,128)(2,1)S(1)} %dynamic-slice_convert_fusion.2), channel_id=1, source_target_pairs={{0,2},{2,0},{1,3},{3,1},{4,6},{6,4},{5,7},{7,5},{8,10},{10,8},{9,1... | collective-permute-start | bytes 393224 | tf_op jit(solution)/shard_map/ppermute | solution.py:36
  7.6 40.3 %collective-permute-start.4 = (bf16[3,256,1024]{2,1,0:T(8,128)(2,1)}, bf16[3,256,1024]{2,1,0:T(8,128)(2,1)}, u32[]{:S(2)}, u32[]{:S(2)}) collective-permute-start(bf16[3,256,1024]{2,1,0:T(8,128)(2,1)} %constant_dynamic-slice_fusion.2), channel_id=1, source_target_pairs={{0,2},{2,0},{1,3},{3,1},{4,6},{6,4},{5,7},{7,5},{8,10},{10,8},{9,1... | collective-permute-start | bytes 4718600 | tf_op jit(solution)/shard_map/ppermute | solution.py:36
  9.4 1.4 %collective-permute-start.1 = (bf16[2,1,128,256]{3,2,0,1:T(8,128)(2,1)S(1)}, bf16[2,1,128,256]{3,2,0,1:T(8,128)(2,1)S(1)}, u32[]{:S(2)}, u32[]{:S(2)}) collective-permute-start(bf16[2,1,128,256]{3,2,0,1:T(8,128)(2,1)S(1)} %get-tuple-element.48), channel_id=1, source_target_pairs={{0,4},{4,0},{8,12},{12,8},{16,20},{20,16},{24,28},{28,24},{1,5},{5... | collective-permute-start | bytes 393224 | tf_op jit(solution)/shard_map/ppermute | solution.py:40
  10.9 13.5 %copy-start.1 = (bf16[2,128,512]{2,1,0:T(8,128)(2,1)}, bf16[2,128,512]{2,1,0:T(8,128)(2,1)S(1)}, u32[]{:S(2)}) copy-start(bf16[2,128,512]{2,1,0:T(8,128)(2,1)S(1)} %maximum_select_fusion.refs_0_) | copy-start | bytes 786436
  10.9 8.4 %collective-permute-start.2 = (bf16[2,128,512]{2,1,0:T(8,128)(2,1)S(1)}, bf16[2,128,512]{2,1,0:T(8,128)(2,1)S(1)}, u32[]{:S(2)}, u32[]{:S(2)}) collective-permute-start(bf16[2,128,512]{2,1,0:T(8,128)(2,1)S(1)} %maximum_select_fusion.refs_0_), channel_id=1, source_target_pairs={{0,1},{1,0},{2,3},{3,2},{4,5},{5,4},{6,7},{7,6},{8,9},{9,8},{10,11... | collective-permute-start | bytes 786440 | tf_op jit(solution)/shard_map/ppermute | solution.py:36
  12.5 12.0 %collective-permute-start.5 = (bf16[2,128,512]{2,1,0:T(8,128)(2,1)S(1)}, bf16[2,128,512]{2,1,0:T(8,128)(2,1)S(1)}, u32[]{:S(2)}, u32[]{:S(2)}) collective-permute-start(bf16[2,128,512]{2,1,0:T(8,128)(2,1)S(1)} %maximum_select_fusion.refs_0_), channel_id=1, source_target_pairs={{0,8},{4,12},{8,16},{12,20},{16,24},{20,28},{24,0},{28,4},{1,9},{5... | collective-permute-start | bytes 786440 | tf_op jit(solution)/shard_map/ppermute | solution.py:36
  14.1 13.4 %collective-permute-start.7 = (bf16[2,128,512]{2,1,0:T(8,128)(2,1)S(1)}, bf16[2,128,512]{2,1,0:T(8,128)(2,1)S(1)}, u32[]{:S(2)}, u32[]{:S(2)}) collective-permute-start(bf16[2,128,512]{2,1,0:T(8,128)(2,1)S(1)} %maximum_select_fusion.refs_0_), channel_id=1, source_target_pairs={{0,24},{4,28},{8,0},{12,4},{16,8},{20,12},{24,16},{28,20},{1,25},{... | collective-permute-start | bytes 786440 | tf_op jit(solution)/shard_map/ppermute | solution.py:36
  19.3 0.7 copy-start.5
  20.0 19.4 %collective-permute-start.9 = (bf16[2,128,512]{2,1,0:T(8,128)(2,1)S(1)}, bf16[2,128,512]{2,1,0:T(8,128)(2,1)}, u32[]{:S(2)}, u32[]{:S(2)}) collective-permute-start(bf16[2,128,512]{2,1,0:T(8,128)(2,1)S(1)} %maximum_select_fusion.refs_0_), channel_id=1, source_target_pairs={{0,16},{4,20},{8,24},{12,28},{16,0},{20,4},{24,8},{28,12},{1,17},{... | collective-permute-start | bytes 786440 | tf_op jit(solution)/shard_map/ppermute | solution.py:36
  24.4 26.3 %collective-permute-start.3 = (bf16[4,256,1024]{2,1,0:T(8,128)(2,1)S(1)}, bf16[4,256,1024]{2,1,0:T(8,128)(2,1)}, u32[]{:S(2)}, u32[]{:S(2)}) collective-permute-start(bf16[4,256,1024]{2,1,0:T(8,128)(2,1)S(1)} %constant_dynamic-slice_fusion.1.refs_0_), channel_id=1, source_target_pairs={{0,4},{4,0},{8,12},{12,8},{16,20},{20,16},{24,28},{28,24},{1,5},{5... | collective-permute-start | bytes 6291464 | tf_op jit(solution)/shard_map/ppermute | solution.py:40
  24.5 23.3 %copy-start.6 = (bf16[2,128,512]{2,1,0:T(8,128)(2,1)}, bf16[2,128,512]{2,1,0:T(8,128)(2,1)S(1)}, u32[]{:S(2)}) copy-start(bf16[2,128,512]{2,1,0:T(8,128)(2,1)S(1)} %collective-permute-done.5.refs_2_) | copy-start | bytes 786436
  24.5 17.3 %collective-permute-start.6 = (bf16[2,128,512]{2,1,0:T(8,128)(2,1)S(1)}, bf16[2,128,512]{2,1,0:T(8,128)(2,1)}, u32[]{:S(2)}, u32[]{:S(2)}) collective-permute-start(bf16[2,128,512]{2,1,0:T(8,128)(2,1)S(1)} %collective-permute-done.5.refs_2_), channel_id=1, source_target_pairs={{0,1},{1,0},{2,3},{3,2},{4,5},{5,4},{6,7},{7,6},{8,9},{9,8},{10,11... | collective-permute-start | bytes 786440 | tf_op jit(solution)/shard_map/ppermute | solution.py:36
  27.5 20.3 %copy-start.7 = (bf16[2,128,512]{2,1,0:T(8,128)(2,1)}, bf16[2,128,512]{2,1,0:T(8,128)(2,1)S(1)}, u32[]{:S(2)}) copy-start(bf16[2,128,512]{2,1,0:T(8,128)(2,1)S(1)} %collective-permute-done.7.refs_4_) | copy-start | bytes 786436
  27.5 14.3 %collective-permute-start.8 = (bf16[2,128,512]{2,1,0:T(8,128)(2,1)S(1)}, bf16[2,128,512]{2,1,0:T(8,128)(2,1)}, u32[]{:S(2)}, u32[]{:S(2)}) collective-permute-start(bf16[2,128,512]{2,1,0:T(8,128)(2,1)S(1)} %collective-permute-done.7.refs_4_), channel_id=1, source_target_pairs={{0,1},{1,0},{2,3},{3,2},{4,5},{5,4},{6,7},{7,6},{8,9},{9,8},{10,11... | collective-permute-start | bytes 786440 | tf_op jit(solution)/shard_map/ppermute | solution.py:36
  39.4 8.4 %collective-permute-start.10 = (bf16[2,128,512]{2,1,0:T(8,128)(2,1)}, bf16[2,128,512]{2,1,0:T(8,128)(2,1)S(1)}, u32[]{:S(2)}, u32[]{:S(2)}) collective-permute-start(bf16[2,128,512]{2,1,0:T(8,128)(2,1)} %collective-permute-done.9.refs_6_), channel_id=1, source_target_pairs={{0,1},{1,0},{2,3},{3,2},{4,5},{5,4},{6,7},{7,6},{8,9},{9,8},{10,11... | collective-permute-start | bytes 786440 | tf_op jit(solution)/shard_map/ppermute | solution.py:36
  47.8 3.8 %collective-permute-start.12 = (bf16[3,256,1024]{2,1,0:T(8,128)(2,1)}, bf16[3,256,1024]{2,1,0:T(8,128)(2,1)}, u32[]{:S(2)}, u32[]{:S(2)}) collective-permute-start(bf16[3,256,1024]{2,1,0:T(8,128)(2,1)} %collective-permute-done.4.refs_1_), channel_id=1, source_target_pairs={{0,4},{4,0},{8,12},{12,8},{16,20},{20,16},{24,28},{28,24},{1,5},{5... | collective-permute-start | bytes 4718600 | tf_op jit(solution)/shard_map/ppermute | solution.py:40
  47.9 14.5 %collective-permute-start.11 = (bf16[1,256,1024]{2,1,0:T(8,128)(2,1)}, bf16[1,256,1024]{2,1,0:T(8,128)(2,1)S(1)}, u32[]{:S(2)}, u32[]{:S(2)}) collective-permute-start(bf16[1,256,1024]{2,1,0:T(8,128)(2,1)} %constant_dynamic-slice_fusion), channel_id=1, source_target_pairs={{0,2},{2,0},{1,3},{3,1},{4,6},{6,4},{5,7},{7,5},{8,10},{10,8},{9,1... | collective-permute-start | bytes 1572872 | tf_op jit(solution)/shard_map/ppermute | solution.py:36
  62.5 1.9 %collective-permute-start.13 = (bf16[1,256,1024]{2,1,0:T(8,128)(2,1)S(1)}, bf16[1,256,1024]{2,1,0:T(8,128)(2,1)S(1)}, u32[]{:S(2)}, u32[]{:S(2)}) collective-permute-start(bf16[1,256,1024]{2,1,0:T(8,128)(2,1)S(1)} %collective-permute-done.11.refs_1_), channel_id=1, source_target_pairs={{0,4},{4,0},{8,12},{12,8},{16,20},{20,16},{24,28},{28,24},{1,5},{5... | collective-permute-start | bytes 1572872 | tf_op jit(solution)/shard_map/ppermute | solution.py:40
  68.4 11.2 %copy-start.4 = (f32[1,2,32,2048]{3,2,1,0:T(8,128)S(1)}, f32[1,2,32,2048]{3,2,1,0:T(8,128)}, u32[]{:S(2)}) copy-start(f32[1,2,32,2048]{3,2,1,0:T(8,128)} %get-tuple-element.35) | copy-start | bytes 1572868
  68.4 15.0 %copy-start.3 = (f32[2,32,2048]{2,1,0:T(8,128)S(1)}, f32[2,32,2048]{2,1,0:T(8,128)}, u32[]{:S(2)}) copy-start(f32[2,32,2048]{2,1,0:T(8,128)} %get-tuple-element.33) | copy-start | bytes 1572868
  68.4 9.4 %collective-permute-start.23 = (bf16[2,32,2048]{2,1,0:T(8,128)(2,1)}, bf16[2,32,2048]{2,1,0:T(8,128)(2,1)S(1)}, u32[]{:S(2)}, u32[]{:S(2)}) collective-permute-start(bf16[2,32,2048]{2,1,0:T(8,128)(2,1)} %bitcast.30), channel_id=1, source_target_pairs={{0,1},{1,0},{2,3},{3,2},{4,5},{5,4},{6,7},{7,6},{8,9},{9,8},{10,11... | collective-permute-start | bytes 786440 | tf_op jit(solution)/shard_map/ppermute | solution.py:36
  69.0 10.6 %collective-permute-start.21 = (bf16[1,2,32,2048]{3,2,1,0:T(8,128)(2,1)}, bf16[1,2,32,2048]{3,2,1,0:T(8,128)(2,1)S(1)}, u32[]{:S(2)}, u32[]{:S(2)}) collective-permute-start(bf16[1,2,32,2048]{3,2,1,0:T(8,128)(2,1)} %get-tuple-element.36), channel_id=1, source_target_pairs={{0,2},{2,0},{1,3},{3,1},{4,6},{6,4},{5,7},{7,5},{8,10},{10,8},{9,1... | collective-permute-start | bytes 786440 | tf_op jit(solution)/shard_map/ppermute | solution.py:36
  69.5 13.9 %collective-permute-start.16 = (bf16[2,32,2048]{2,1,0:T(8,128)(2,1)}, bf16[2,32,2048]{2,1,0:T(8,128)(2,1)S(1)}, u32[]{:S(2)}, u32[]{:S(2)}) collective-permute-start(bf16[2,32,2048]{2,1,0:T(8,128)(2,1)} %bitcast.29), channel_id=1, source_target_pairs={{0,1},{1,0},{2,3},{3,2},{4,5},{5,4},{6,7},{7,6},{8,9},{9,8},{10,11... | collective-permute-start | bytes 786440 | tf_op jit(solution)/shard_map/ppermute | solution.py:36
  71.1 13.1 %collective-permute-start.14 = (bf16[1,2,32,2048]{3,2,1,0:T(8,128)(2,1)}, bf16[1,2,32,2048]{3,2,1,0:T(8,128)(2,1)S(1)}, u32[]{:S(2)}, u32[]{:S(2)}) collective-permute-start(bf16[1,2,32,2048]{3,2,1,0:T(8,128)(2,1)} %get-tuple-element.32), channel_id=1, source_target_pairs={{0,2},{2,0},{1,3},{3,1},{4,6},{6,4},{5,7},{7,5},{8,10},{10,8},{9,1... | collective-permute-start | bytes 786440 | tf_op jit(solution)/shard_map/ppermute | solution.py:36
  77.8 6.3 %copy-start.2 = (f32[1,2,32,2048]{3,2,1,0:T(8,128)S(1)}, f32[1,2,32,2048]{3,2,1,0:T(8,128)}, u32[]{:S(2)}) copy-start(f32[1,2,32,2048]{3,2,1,0:T(8,128)} %get-tuple-element.31) | copy-start | bytes 1572868
  79.0 7.6 %collective-permute-start.24 = (bf16[1,32,2048]{2,1,0:T(8,128)(2,1)S(1)}, bf16[1,32,2048]{2,1,0:T(8,128)(2,1)S(1)}, u32[]{:S(2)}, u32[]{:S(2)}) collective-permute-start(bf16[1,32,2048]{2,1,0:T(8,128)(2,1)S(1)} %slice.26), channel_id=1, source_target_pairs={{0,2},{2,0},{1,3},{3,1},{4,6},{6,4},{5,7},{7,5},{8,10},{10,8},{9,1... | collective-permute-start | bytes 393224 | tf_op jit(solution)/shard_map/ppermute | solution.py:36
  79.7 6.9 %collective-permute-start.22 = (bf16[1,32,2048]{2,1,0:T(8,128)(2,1)S(1)}, bf16[1,32,2048]{2,1,0:T(8,128)(2,1)S(1)}, u32[]{:S(2)}, u32[]{:S(2)}) collective-permute-start(bf16[1,32,2048]{2,1,0:T(8,128)(2,1)S(1)} %fusion.1), channel_id=1, source_target_pairs={{0,1},{1,0},{2,3},{3,2},{4,5},{5,4},{6,7},{7,6},{8,9},{9,8},{10,11... | collective-permute-start | bytes 393224 | tf_op jit(solution)/shard_map/ppermute | solution.py:36
  83.5 7.6 %collective-permute-start.17 = (bf16[1,32,2048]{2,1,0:T(8,128)(2,1)S(1)}, bf16[1,32,2048]{2,1,0:T(8,128)(2,1)S(1)}, u32[]{:S(2)}, u32[]{:S(2)}) collective-permute-start(bf16[1,32,2048]{2,1,0:T(8,128)(2,1)S(1)} %slice.27), channel_id=1, source_target_pairs={{0,2},{2,0},{1,3},{3,1},{4,6},{6,4},{5,7},{7,5},{8,10},{10,8},{9,1... | collective-permute-start | bytes 393224 | tf_op jit(solution)/shard_map/ppermute | solution.py:36
  84.2 7.0 %collective-permute-start.15 = (bf16[1,32,2048]{2,1,0:T(8,128)(2,1)S(1)}, bf16[1,32,2048]{2,1,0:T(8,128)(2,1)S(1)}, u32[]{:S(2)}, u32[]{:S(2)}) collective-permute-start(bf16[1,32,2048]{2,1,0:T(8,128)(2,1)S(1)} %fusion), channel_id=1, source_target_pairs={{0,1},{1,0},{2,3},{3,2},{4,5},{5,4},{6,7},{7,6},{8,9},{9,8},{10,11... | collective-permute-start | bytes 393224 | tf_op jit(solution)/shard_map/ppermute | solution.py:36
  86.8 6.3 %collective-permute-start.25 = (bf16[1,64,512]{2,1,0:T(8,128)(2,1)S(1)}, bf16[1,64,512]{2,1,0:T(8,128)(2,1)S(1)}, u32[]{:S(2)}, u32[]{:S(2)}) collective-permute-start(bf16[1,64,512]{2,1,0:T(8,128)(2,1)S(1)} %get-tuple-element.39), channel_id=1, source_target_pairs={{0,8},{4,12},{8,16},{12,20},{16,24},{20,28},{24,0},{28,4},{1,9},{5... | collective-permute-start | bytes 196616 | tf_op jit(solution)/shard_map/ppermute | solution.py:36
  86.9 9.0 %collective-permute-start.26 = (bf16[1,64,512]{2,1,0:T(8,128)(2,1)S(1)}, bf16[1,64,512]{2,1,0:T(8,128)(2,1)S(1)}, u32[]{:S(2)}, u32[]{:S(2)}) collective-permute-start(bf16[1,64,512]{2,1,0:T(8,128)(2,1)S(1)} %get-tuple-element.40), channel_id=1, source_target_pairs={{0,16},{4,20},{8,24},{12,28},{16,0},{20,4},{24,8},{28,12},{1,17},{... | collective-permute-start | bytes 196616 | tf_op jit(solution)/shard_map/ppermute | solution.py:36
  89.1 6.8 %collective-permute-start.27 = (bf16[1,64,512]{2,1,0:T(8,128)(2,1)S(1)}, bf16[1,64,512]{2,1,0:T(8,128)(2,1)S(1)}, u32[]{:S(2)}, u32[]{:S(2)}) collective-permute-start(bf16[1,64,512]{2,1,0:T(8,128)(2,1)S(1)} %get-tuple-element.41), channel_id=1, source_target_pairs={{0,24},{4,28},{8,0},{12,4},{16,8},{20,12},{24,16},{28,20},{1,25},{... | collective-permute-start | bytes 196616 | tf_op jit(solution)/shard_map/ppermute | solution.py:36
  91.4 6.2 %collective-permute-start.18 = (bf16[1,64,512]{2,1,0:T(8,128)(2,1)S(1)}, bf16[1,64,512]{2,1,0:T(8,128)(2,1)S(1)}, u32[]{:S(2)}, u32[]{:S(2)}) collective-permute-start(bf16[1,64,512]{2,1,0:T(8,128)(2,1)S(1)} %get-tuple-element.42), channel_id=1, source_target_pairs={{0,8},{4,12},{8,16},{12,20},{16,24},{20,28},{24,0},{28,4},{1,9},{5... | collective-permute-start | bytes 196616 | tf_op jit(solution)/shard_map/ppermute | solution.py:36
  91.6 8.0 %collective-permute-start.19 = (bf16[1,64,512]{2,1,0:T(8,128)(2,1)S(1)}, bf16[1,64,512]{2,1,0:T(8,128)(2,1)S(1)}, u32[]{:S(2)}, u32[]{:S(2)}) collective-permute-start(bf16[1,64,512]{2,1,0:T(8,128)(2,1)S(1)} %get-tuple-element.43), channel_id=1, source_target_pairs={{0,16},{4,20},{8,24},{12,28},{16,0},{20,4},{24,8},{28,12},{1,17},{... | collective-permute-start | bytes 196616 | tf_op jit(solution)/shard_map/ppermute | solution.py:36
  93.1 6.5 %collective-permute-start.20 = (bf16[1,64,512]{2,1,0:T(8,128)(2,1)S(1)}, bf16[1,64,512]{2,1,0:T(8,128)(2,1)S(1)}, u32[]{:S(2)}, u32[]{:S(2)}) collective-permute-start(bf16[1,64,512]{2,1,0:T(8,128)(2,1)S(1)} %get-tuple-element.44), channel_id=1, source_target_pairs={{0,24},{4,28},{8,0},{12,4},{16,8},{20,12},{24,16},{28,20},{1,25},{... | collective-permute-start | bytes 196616 | tf_op jit(solution)/shard_map/ppermute | solution.py:36
  99.7 1.4 %collective-permute-start.28 = (f32[1,128,256]{2,1,0:T(8,128)S(1)}, f32[1,128,256]{2,1,0:T(8,128)S(1)}, u32[]{:S(2)}, u32[]{:S(2)}) collective-permute-start(f32[1,128,256]{2,1,0:T(8,128)S(1)} %get-tuple-element.46), channel_id=1, source_target_pairs={{0,4},{4,0},{8,12},{12,8},{16,20},{20,16},{24,28},{28,24},{1,5},{5... | collective-permute-start | bytes 393224 | tf_op jit(solution)/shard_map/ppermute | solution.py:40
